TPU v7x, 32 devices: a whole 2x2x4 slice. The times are simulated.
32 devices in a mesh: tile: 8 (over z, y), cond: 4 (over x, core).
Axes of the slice: x: 2, y: 2, z: 4, core: 2. Of those that a mesh axis runs over, the one named last changes fastest.
Arguments:
- theta: float32 [4096, 512], P(('tile', 'cond')), may hold values from -6 to 6
- target: int32 [4096, 512], P('tile'), may hold values 0 or 1
- kernel_real: float32 [8, 2, 65, 65], P('cond'), may hold values from -24 to 24
- kernel_imag: float32 [8, 2, 65, 65], P('cond'), may hold values from -24 to 24
- weights: int32 [8], replicated, may hold values from 1 to 4
- thresholds: float32 [8], P('cond'), may hold values from 0.5 to 1.5
Outputs:
- gradient: float32 [4096, 512], P(('tile', 'cond'))
Inputs may be any that keep to these rules, and one draw needn't show every extreme that they name: Each pixel of the target is 0 or 1. Condition weights are small positive integers.
All inputs are finite; a program needn't handle non-finite values. No bound on the sum of `target` on one device may be relied on, other than what follows from the above.
Results may differ from a plain program's by a relative error of at most 0.00021.
Values sent between devices are 32-bit elements; how exact they have to be, the bound alone decides.
No kernel may reach another device: no remote copies, remote signals or barrier semaphores. Data moves between devices by JAX's collectives and lax.ppermute only.
A program may use at most 64 MiB of HBM per device.

v0:
```python
import functools

import jax
import jax.numpy as jnp
import ml_dtypes
import numpy as np
from jax import lax
from jax.experimental import pallas as pl
from jax.experimental.pallas import tpu as pltpu
from jax.sharding import PartitionSpec as P

TP = 512
HALO = 32
KSUP = 65
HALF = KSUP // 2
KERNELS = 2
CONDS = 8
FULL = TP + 2 * HALO
PARTS = 4
ROWS = TP // PARTS
FA = 40
FB = 64
BF = jnp.bfloat16
F32 = jnp.float32

mask_steep = 2.0
resist_steep = 4.0
band_weight = 1.0


def waves(positions):
    angles = (np.outer(np.asarray(positions, np.int64), np.arange(HALF + 1)) % FULL) * (2.0 * np.pi / FULL)
    return np.cos(angles), np.sin(angles)


def halves(table):
    high = table.astype(np.float32).astype(ml_dtypes.bfloat16)
    low = (table - high.astype(np.float64)).astype(np.float32).astype(ml_dtypes.bfloat16)
    return high, low


def row_table(positions):
    cosine, sine = waves(positions)
    table = np.zeros((len(positions), 2 * FA))
    table[:, : HALF + 1] = cosine
    table[:, FA : FA + HALF + 1] = sine
    return table


def pair_table(positions):
    table = row_table(positions)
    return np.concatenate([table, np.concatenate([-table[:, FA:], table[:, :FA]], axis=1)])


def column_table(positions):
    cosine, sine = waves(positions)
    table = np.zeros((len(positions), 4 * FB))
    for block, values in enumerate((cosine, cosine, sine, -sine)):
        table[:, block * FB : block * FB + HALF] = values[:, 1:]
    table[:, HALF] = 1.0
    return table


@functools.cache
def tables():
    pixels = np.arange(TP) + HALO
    column = column_table(pixels)
    column_high, column_low = halves(column)
    turned = np.concatenate([column[:, : 2 * FB].T, column[:, 2 * FB :].T], axis=1)
    turned_high, turned_low = halves(turned)
    row = row_table(pixels)
    row_high, row_low = halves(row)
    out = {}
    out["column"] = np.stack([column_high, column_low])
    spectrum_rows = []
    rim_rows = []
    halo_rows = []
    own_rows = []
    forward = []
    backward = []
    for part in range(PARTS):
        own = np.arange(ROWS) + part * ROWS + HALO
        rim = np.arange(HALO) + (0 if part == PARTS - 1 else FULL - HALO)
        for rows, positions in ((spectrum_rows, own), (rim_rows, rim)):
            high, low = halves(row_table(positions).T)
            rows.append(np.concatenate([high, low, high], axis=1))
        high, low = halves(pair_table(rim))
        halo_rows.append(np.concatenate([high, low, high], axis=1))
        high, low = halves(pair_table(own))
        own_rows.append(np.concatenate([high, low, high], axis=1))
        cols = slice(part * ROWS, (part + 1) * ROWS)
        high = np.concatenate([turned_high[:, :TP][:, cols], turned_high[:, TP:][:, cols]], axis=1)
        low = np.concatenate([turned_low[:, :TP][:, cols], turned_low[:, TP:][:, cols]], axis=1)
        forward.append(np.concatenate([high, high, low]))
        backward.append(np.concatenate([column_high[cols], column_high[cols], column_low[cols]]))
    out["spectrum_rows"] = np.stack(spectrum_rows)
    out["own_rows"] = np.stack(own_rows)
    out["rim_rows"] = np.stack(rim_rows)
    out["halo_rows"] = np.stack(halo_rows)
    out["forward"] = np.stack(forward)
    out["backward"] = np.stack(backward)
    out["turned"] = np.stack([column_high.T, column_low.T])
    out["row"] = np.concatenate([row_high, row_low, row_high], axis=1)
    out["row_turned"] = np.concatenate([row_high.T, row_low.T])
    return out


def part_of(ref):
    return ref[0] % PARTS


def has_mask_halo(ref):
    return ref[0] // PARTS % 2 > 0


def has_adjoint_halo(ref):
    return ref[0] // (2 * PARTS) > 0


def dot(left, right):
    return jnp.dot(left, right, preferred_element_type=F32)


def split(value):
    high = value.astype(BF)
    return high, (value - high.astype(F32)).astype(BF)


def spectrum_of(mask, column_ref, rows):
    high, low = split(mask)
    across = dot(high, column_ref[0]) + dot(low, column_ref[0]) + dot(high, column_ref[1])
    high, low = split(across)
    both = dot(rows, jnp.concatenate([high, high, low], axis=0))
    even = both[:FA, : 2 * FB] - both[FA:, 2 * FB :]
    odd = both[FA:, : 2 * FB] + both[:FA, 2 * FB :]
    return even, odd


def open_kernel(
    part_ref, theta_hbm, real_hbm, imag_hbm, thresholds_hbm, weights_hbm, forward_hbm, backward_hbm,
    out_ref, rim_ref, shares_ref, forward_ref, backward_ref, real_ref, imag_ref, thresholds_ref, weights_ref, stage, sems,
):
    part = part_of(part_ref)
    moves = [
        (real_hbm, real_ref),
        (imag_hbm, imag_ref),
        (thresholds_hbm, thresholds_ref),
        (weights_hbm, weights_ref),
        (theta_hbm.at[pl.ds(pl.multiple_of(jnp.where(part == 0, 0, ROWS - HALO), HALO), HALO)], rim_ref),
        (forward_hbm.at[part], forward_ref),
        (backward_hbm.at[part], backward_ref),
    ]
    copies = [pltpu.make_async_copy(source, target, sems.at[i]) for i, (source, target) in enumerate(moves)]
    for copy in copies:
        copy.start()
    local_conds = real_ref.shape[0]
    mats = local_conds * KERNELS * 2
    stage[...] = jnp.zeros_like(stage)
    for copy in copies[:4]:
        copy.wait()
    for cond in range(local_conds):
        for kern in range(KERNELS):
            for piece, ref in enumerate((real_ref, imag_ref)):
                stage[(cond * KERNELS + kern) * 2 + piece, :KSUP, :KSUP] = ref[cond, :, kern, :]
    rows = stage.shape[1]
    source = lax.broadcasted_iota(jnp.int32, (2 * FB, 4 * FB), 0)
    target = lax.broadcasted_iota(jnp.int32, (2 * FB, 4 * FB), 1)
    lane = target % FB
    block = target // FB
    plus = (block == 0) | (block == 3)
    freq = jnp.where(lane < HALF, lane + 1, 0)
    used = (lane < HALF) | ((lane == HALF) & (block % 2 == 0))
    pick = (used & (source == jnp.where(plus, HALF + freq, HALF - freq))).astype(F32).astype(BF)
    high, low = split(stage[...].reshape(mats * rows, 2 * FB))
    picked = [dot(piece, pick) for piece in (high, low)]
    source = lax.broadcasted_iota(jnp.int32, (FA, 2 * rows), 1) % rows
    target = lax.broadcasted_iota(jnp.int32, (FA, 2 * rows), 0)
    turn = ((source == HALF - target) & (target <= HALF)).astype(F32).astype(BF)
    lane = lax.broadcasted_iota(jnp.int32, (FA, 2 * FB), 1)
    row = lax.broadcasted_iota(jnp.int32, (FA, 2 * FB), 0)
    valid = (row <= HALF) & ((lane <= HALF) | ((row > 0) & (lane >= FB) & (lane < FB + HALF)))
    scale = 1.0 / (FULL * FULL)
    keep_top = jnp.where(valid, scale, 0.0)
    keep_bottom = jnp.where((row == 0) & (lane == HALF), 0.0, keep_top)
    first = lane % FB < HALF
    extra = jnp.zeros((FA, 2 * FB), F32)
    for kern in range(local_conds * KERNELS):
        arrays = [[], []]
        for piece in range(2):
            start = (kern * 2 + piece) * rows
            top = picked[0][start + HALF : start + HALF + FA, : 2 * FB] + picked[1][start + HALF : start + HALF + FA, : 2 * FB]
            pieces = jnp.concatenate([half[start : start + rows, 2 * FB :] for half in picked], axis=0)
            bottom = dot(turn, pieces.astype(BF)) * keep_bottom
            top = top * keep_top
            arrays[0].append(top + bottom)
            arrays[1].append(top - bottom)
        for which, (real, imag) in enumerate(arrays):
            packed = jnp.where(first, real, pltpu.roll(imag, HALF, 1))
            if which == 0:
                packed = jnp.where(row == FA - 1, thresholds_ref[kern // KERNELS], packed)
            out_ref[kern * 2 + which] = packed
            for piece, value in enumerate((real, imag)):
                place = kern * 4 + which * 2 + piece
                extra = jnp.where(lane == place, pltpu.roll(value, (place - HALF) % (2 * FB), 1), extra)
    out_ref[local_conds * KERNELS * 2] = extra
    weight_sum = weights_ref[0]
    for i in range(1, CONDS):
        weight_sum = weight_sum + weights_ref[i]
    row = lax.broadcasted_iota(jnp.int32, shares_ref.shape, 0)
    shares = jnp.zeros(shares_ref.shape, F32)
    for group, step in enumerate((0, 3, 1, 2)):
        for i in range(local_conds):
            weight = weights_ref[lax.bitwise_xor(part, step) * local_conds + i]
            shares = jnp.where(row == group * local_conds + i, weight.astype(F32), shares)
    shares_ref[...] = shares / weight_sum.astype(F32)
    for copy in copies[4:]:
        copy.wait()


def spectrum_kernel(part_ref, theta_ref, column_ref, rows_ref, out_ref):
    even, odd = spectrum_of(jnp.tanh(mask_steep * theta_ref[...]), column_ref, rows_ref[0])
    out_ref[0] = even
    out_ref[1] = odd


def rim_kernel(part_ref, spectrum_ref, rim_ref, column_ref, rows_ref, out_ref):
    mask = jnp.where(has_mask_halo(part_ref), jnp.tanh(mask_steep * rim_ref[...]), 0.0)
    even, odd = spectrum_of(mask, column_ref, rows_ref[0])
    out_ref[0] = even + spectrum_ref[0]
    out_ref[1] = odd + spectrum_ref[1]


def fields_kernel(
    part_ref, own_ref, side_ref, core_ref, cross_ref, shares_ref, target_ref, forward_ref, backward_ref, row_ref,
    row_turned_ref, out_ref, kernels_ref, lines, folded, amps, tanhs, total, signs, turned, backs,
):
    count = kernels_ref.shape[0]
    local = count // PARTS
    tall = 4 * FA
    even = side_ref[2 * local + 1] + cross_ref[2 * local + 1]
    odd = side_ref[2 * local + 2] + cross_ref[2 * local + 2]
    lane = lax.broadcasted_iota(jnp.int32, (FA, 2 * FB), 1)
    row = lax.broadcasted_iota(jnp.int32, (FA, 2 * FB), 0)
    zero_lane = (lane == HALF) & (row <= HALF)
    for group, ref in enumerate((own_ref, side_ref, core_ref, cross_ref)):
        extra = ref[2 * local]
        for kern in range(local):
            values = []
            for which in range(2):
                packed = ref[2 * kern + which]
                for part, value in enumerate((packed, pltpu.roll(packed, 2 * FB - HALF, 1))):
                    place = kern * 4 + which * 2 + part
                    zeroth = pltpu.roll(extra, (HALF - place) % (2 * FB), 1)
                    value = jnp.where(zero_lane, zeroth, value)
                    kernels_ref[group * local + kern, which * 2 + part] = value
                    values.append(value)
            he_real, he_imag, ho_real, ho_imag = values
            start = (group * local + kern) * tall
            for i, value in enumerate(
                (
                    even * he_real + odd * ho_imag,
                    odd * he_real - even * ho_imag,
                    even * he_imag - odd * ho_real,
                    odd * he_imag + even * ho_real,
                )
            ):
                lines[start + i * FA : start + (i + 1) * FA] = value

    high, low = split(lines[...])
    lines_folded = dot(jnp.concatenate([high, low], axis=1), forward_ref[: 4 * FB]) + dot(high, forward_ref[4 * FB :])
    for kern in range(count):
        parts = []
        for i in range(2):
            x_part = lines_folded[tall * kern + 2 * FA * i : tall * kern + 2 * FA * i + FA]
            y_part = lines_folded[tall * kern + 2 * FA * i + FA : tall * kern + 2 * FA * (i + 1)]
            parts.append(
                jnp.concatenate(
                    [x_part[:, :ROWS] + y_part[:, ROWS:], y_part[:, :ROWS] - x_part[:, ROWS:]], axis=0
                )
            )
        high, low = split(jnp.concatenate(parts, axis=1))
        folded[kern] = jnp.concatenate([high, high, low], axis=0)
    total[...] = jnp.zeros_like(total)
    signs[...] = 1.0 - 2.0 * target_ref[...].astype(F32)

    def expose(cond, carry):
        intensity = None
        for kern in range(KERNELS):
            index = cond * KERNELS + kern
            amp = dot(row_ref[...], folded[index])
            amps[index] = amp
            power = amp[:, :ROWS] * amp[:, :ROWS] + amp[:, ROWS:] * amp[:, ROWS:]
            intensity = power if intensity is None else intensity + power
        level = kernels_ref[cond * KERNELS, 0, FA - 1 :, :]
        value = jnp.tanh((0.5 * resist_steep) * (intensity - level))
        tanhs[cond] = value
        total[...] += value
        return carry

    lax.fori_loop(0, CONDS, expose, 0, unroll=4)
    total[...] = total[...] * (band_weight / (CONDS * CONDS))

    def drive(cond, carry):
        weight = shares_ref[pl.ds(cond, 1), :]
        value = tanhs[cond]
        slope = (weight + band_weight / CONDS) * value + weight * signs[...] - total[...]
        field = (0.5 * resist_steep) * (1.0 - value * value) * slope
        field = jnp.concatenate([field, field], axis=1)
        for kern in range(KERNELS):
            index = cond * KERNELS + kern
            high, low = split(field * amps[index])
            long = dot(row_turned_ref[...], high)
            back = long[: 2 * FA] + long[2 * FA :] + dot(row_turned_ref[: 2 * FA], low)
            turned[pl.ds(index * 2, 2)] = jnp.stack([back[:, :ROWS], back[:, ROWS:]])
        return carry

    lax.fori_loop(0, CONDS, drive, 0, unroll=4)
    high, low = split(turned[...].reshape(count * tall, ROWS))
    backs[...] = dot(jnp.concatenate([high, low], axis=1), backward_ref[: 2 * ROWS]) + dot(high, backward_ref[2 * ROWS :])

    sum_even = jnp.zeros((FA, 2 * FB), F32)
    sum_odd = jnp.zeros((FA, 2 * FB), F32)
    for kern in range(count):
        grads = []
        for i in range(2):
            c_part = backs[tall * kern + 2 * FA * i : tall * kern + 2 * FA * i + FA]
            s_part = backs[tall * kern + 2 * FA * i + FA : tall * kern + 2 * FA * (i + 1)]
            grads.append(
                (
                    c_part[:, : 2 * FB] - s_part[:, 2 * FB :],
                    s_part[:, : 2 * FB] + c_part[:, 2 * FB :],
                )
            )
        (x_real, y_real), (x_imag, y_imag) = grads
        he_real, he_imag, ho_real, ho_imag = (kernels_ref[kern, i] for i in range(4))
        sum_even = sum_even + x_real * he_real + x_imag * he_imag - y_real * ho_imag + y_imag * ho_real
        sum_odd = sum_odd + x_real * ho_imag - x_imag * ho_real + y_real * he_real + y_imag * he_imag
    out_ref[:FA] = sum_even
    out_ref[FA:] = sum_odd


def image_rows(value, rows, turned_ref):
    high, low = split(value)
    pair = dot(rows, jnp.concatenate([high, high, low], axis=0))
    count = pair.shape[0] // 2
    high, low = split(jnp.concatenate([pair[:count], pair[count:]], axis=1))
    return dot(high, turned_ref[0]) + dot(low, turned_ref[0]) + dot(high, turned_ref[1])


def edge_start(part_ref):
    return pl.multiple_of(jnp.where(part_of(part_ref) == PARTS - 1, ROWS - HALO, 0), HALO)


def gradient_kernel(part_ref, theta_ref, sum_ref, chip_ref, back_ref, turned_ref, rows_ref, out_ref, edge_ref, scale_ref):
    part = part_of(part_ref)
    middle = (part == 1) | (part == 2)
    mask = jnp.tanh(mask_steep * theta_ref[...])
    scale = mask_steep * (1.0 - mask * mask)
    mine = jnp.where(middle, sum_ref[...], chip_ref[...] + back_ref[...])
    gradient = image_rows(mine, rows_ref[0], turned_ref) * scale
    out_ref[...] = gradient
    last = part == PARTS - 1
    edge_ref[...] = jnp.where(last, gradient[ROWS - HALO :], gradient[:HALO])
    scale_ref[...] = jnp.where(last, scale[ROWS - HALO :], scale[:HALO])


def edge_kernel(part_ref, gradient_hbm, edge_ref, scale_ref, near_ref, turned_ref, rows_ref, out_hbm, stage, sem):
    rim = image_rows(near_ref[...], rows_ref[0], turned_ref) * scale_ref[...]
    stage[...] = edge_ref[...] + jnp.where(has_adjoint_halo(part_ref), rim, 0.0)
    copy = pltpu.make_async_copy(stage, out_hbm.at[pl.ds(edge_start(part_ref), HALO)], sem)
    copy.start()
    copy.wait()


def whole_spec(array):
    rank = len(array.shape)
    return pl.BlockSpec(array.shape, lambda i, *refs: (0,) * rank)


def part_spec(array):
    rank = len(array.shape)
    return pl.BlockSpec((1,) + array.shape[1:], lambda i, part, *refs: (part_of(part),) + (0,) * (rank - 1))


def call(kernel, scalars, operands, specs, out_shapes, scratch=(), name=None, flops=1 << 28, out_specs=None, aliases=None):
    many = isinstance(out_shapes, list)
    if out_specs is None:
        out_specs = [whole_spec(shape) for shape in out_shapes] if many else whole_spec(out_shapes)
    return pl.pallas_call(
        kernel,
        grid_spec=pltpu.PrefetchScalarGridSpec(
            num_scalar_prefetch=len(scalars),
            grid=(1,),
            in_specs=specs,
            out_specs=out_specs,
            scratch_shapes=list(scratch),
        ),
        out_shape=out_shapes,
        input_output_aliases=aliases or {},
        compiler_params=pltpu.CompilerParams(vmem_limit_bytes=48 * 1024 * 1024),
        cost_estimate=pl.CostEstimate(flops=flops, bytes_accessed=1 << 20, transcendentals=0),
        name=name,
    )(*scalars, *operands)


def floats(*shape):
    return jax.ShapeDtypeStruct(shape, F32)


def shards(theta, target, kernel_real, kernel_imag, weights, thresholds):
    table = {name: jnp.asarray(value) for name, value in tables().items()}
    tiles = lax.axis_size("tile")
    part = lax.axis_index("cond")
    tile = lax.axis_index("tile")
    last = PARTS - 1
    above = ((part == 0) & (tile > 0)) | ((part == last) & (tile < tiles - 1))
    below = ((part == 0) & (tile < tiles - 1)) | ((part == last) & (tile > 0))
    parts = (part + PARTS * below.astype(jnp.int32) + 2 * PARTS * above.astype(jnp.int32)).reshape(1).astype(jnp.int32)
    local_conds = kernel_real.shape[0]
    local = local_conds * KERNELS
    count = CONDS * KERNELS
    hbm = pl.BlockSpec(memory_space=pltpu.HBM)

    def across(value, within, down, up):
        pairs = [(PARTS * i + a, PARTS * i + b) for i in range(tiles) for a, b in within]
        pairs += [(PARTS * (i + 1) + down[0], PARTS * i + down[1]) for i in range(tiles - 1)]
        pairs += [(PARTS * i + up[0], PARTS * (i + 1) + up[1]) for i in range(tiles - 1)]
        pairs += [(down[0], up[1]), (PARTS * (tiles - 1) + up[0], PARTS * (tiles - 1) + down[1])]
        return lax.ppermute(value, ("tile", "cond"), pairs)

    def partner(value, step):
        return lax.ppermute(value, "cond", [(i, i ^ step) for i in range(PARTS)])

    kernel_shape = (local_conds, KSUP, KERNELS, KSUP)
    own, rim, shares, forward, backward = call(
        open_kernel,
        (parts,),
        tuple(
            pltpu.with_memory_space_constraint(value, pltpu.HBM)
            for value in (
                theta, kernel_real.transpose(0, 2, 1, 3), kernel_imag.transpose(0, 2, 1, 3), thresholds, weights,
                table["forward"], table["backward"],
            )
        ),
        [hbm] * 7,
        [
            floats(2 * local + 1, FA, 2 * FB),
            floats(HALO, TP),
            floats(CONDS, ROWS),
            jax.ShapeDtypeStruct(table["forward"].shape[1:], BF),
            jax.ShapeDtypeStruct(table["backward"].shape[1:], BF),
        ],
        scratch=(
            pltpu.VMEM(kernel_shape, F32),
            pltpu.VMEM(kernel_shape, F32),
            pltpu.SMEM(thresholds.shape, F32),
            pltpu.SMEM(weights.shape, jnp.int32),
            pltpu.VMEM((2 * local, 72, 2 * FB), F32),
            pltpu.SemaphoreType.DMA((7,)),
        ),
        name="open_parts",
    )
    rim = across(rim, [(1, 1), (2, 2)], (0, 0), (last, last))
    spectrum = call(
        spectrum_kernel,
        (parts,),
        (theta, table["column"], table["spectrum_rows"]),
        [whole_spec(theta), whole_spec(table["column"]), part_spec(table["spectrum_rows"])],
        floats(2, FA, 2 * FB),
        name="own_spectrum",
        flops=1 << 31,
    )
    side = partner(own, 3)
    core = partner(own, 1)
    spectrum = call(
        rim_kernel,
        (parts,),
        (spectrum, rim, table["column"], table["rim_rows"]),
        [whole_spec(spectrum), whole_spec(rim), whole_spec(table["column"]), part_spec(table["rim_rows"])],
        floats(2, FA, 2 * FB),
        name="add_rim",
    )
    mixed = jnp.concatenate([side, spectrum + partner(spectrum, 3)], axis=0)
    adjoint = call(
        fields_kernel,
        (parts,),
        (own, mixed, core, partner(mixed, 1), shares, target, forward, backward, table["row"], table["row_turned"]),
        [
            whole_spec(own),
            whole_spec(mixed),
            whole_spec(core),
            whole_spec(mixed),
            whole_spec(shares),
            pl.BlockSpec((TP, ROWS), lambda i, part, *refs: (0, part_of(part))),
            whole_spec(forward),
            whole_spec(backward),
            whole_spec(table["row"]),
            whole_spec(table["row_turned"]),
        ],
        floats(2 * FA, 2 * FB),
        scratch=(
            pltpu.VMEM((count, 4, FA, 2 * FB), F32),
            pltpu.VMEM((count * 4 * FA, 2 * FB), F32),
            pltpu.VMEM((count, 6 * FA, 2 * ROWS), BF),
            pltpu.VMEM((count, TP, 2 * ROWS), F32),
            pltpu.VMEM((CONDS, TP, ROWS), F32),
            pltpu.VMEM((TP, ROWS), F32),
            pltpu.VMEM((TP, ROWS), F32),
            pltpu.VMEM((count * 2, 2 * FA, ROWS), F32),
            pltpu.VMEM((count * 4 * FA, 4 * FB), F32),
        ),
        name="coherent_fields",
        flops=1 << 33,
    )
    chip = adjoint + partner(adjoint, 1)
    adjoint = chip + lax.ppermute(chip, "cond", [(0, 0), (1, 2), (2, 1), (last, last)])
    back = lax.ppermute(chip, "cond", [(0, last), (1, 1), (2, 2), (last, 0)])
    near = across(adjoint, [(0, 1), (last, 2)], (2, last), (1, 0))
    gradient, edge, scale = call(
        gradient_kernel,
        (parts,),
        (theta, adjoint, chip, back, table["turned"], table["own_rows"]),
        [
            whole_spec(theta),
            whole_spec(adjoint),
            whole_spec(chip),
            whole_spec(back),
            whole_spec(table["turned"]),
            part_spec(table["own_rows"]),
        ],
        [floats(ROWS, TP), floats(HALO, TP), floats(HALO, TP)],
        name="own_gradient",
        flops=1 << 31,
    )
    return call(
        edge_kernel,
        (parts,),
        (gradient, edge, scale, near, table["turned"], table["halo_rows"]),
        [
            hbm,
            whole_spec(edge),
            whole_spec(scale),
            whole_spec(near),
            whole_spec(table["turned"]),
            part_spec(table["halo_rows"]),
        ],
        floats(ROWS, TP),
        scratch=(pltpu.VMEM((HALO, TP), F32), pltpu.SemaphoreType.DMA),
        name="edge_gradient",
        out_specs=hbm,
        aliases={1: 0},
    )


def solution(mesh):
    in_specs = (
        P(("tile", "cond"), None),
        P("tile", None),
        P("cond", None, None, None),
        P("cond", None, None, None),
        P(),
        P("cond"),
    )
    out_specs = P(("tile", "cond"), None)
    return jax.shard_map(shards, mesh=mesh, in_specs=in_specs, out_specs=out_specs, check_vma=False)
```

profile of v0, /device:TPU:0, one launch (start us, length us, event | category | flops | bytes accessed | tf_op | source)
XLA Modules:
  0.0 32.2 jit_solution(14694938987399880067)
XLA Ops:
  0.0 0.0 copy-start.1
  0.0 0.0 copy-start.5
  0.0 0.0 copy-start.7
  0.0 1.7 %open_parts.1 = (f32[9,40,128]{2,1,0:T(8,128)S(1)}, f32[32,512]{1,0:T(8,128)S(1)}, f32[8,128]{1,0:T(8,128)S(1)}, bf16[384,256]{1,0:T(8,128)(2,1)S(1)}, bf16[384,256]{1,0:T(8,128)(2,1)S(1)}) custom-call(s32[1]{0:T(128)} %bitcast.part_ref, f32[128,512]{1,0:T(8,128)} %theta_ref.3, f32[2,65,2,65]{3,2,1,0:T(2,128)} %bitcast.3, f32[2,65,2,65]{3,2,1,0:T(2,128)} %bitcast.4, ...), custom_call_target="tpu_custom_call" | custom-call | flops 268435456 | bytes 1048576 | tf_op jit(solution)/shard_map/open_parts/pallas_call | solution.py:389
  1.7 4.3 %collective-permute-start.1 = (f32[32,512]{1,0:T(8,128)S(1)}, f32[32,512]{1,0:T(8,128)S(1)}, u32[]{:S(2)}, u32[]{:S(2)}) collective-permute-start(f32[32,512]{1,0:T(8,128)S(1)} %get-tuple-element.14), channel_id=1, source_target_pairs={{1,1},{2,2},{5,5},{6,6},{9,9},{10,10},{13,13},{14,14},{17,17},{18,... | collective-permute-start | bytes 196616 | tf_op jit(solution)/shard_map/ppermute | solution.py:429
  6.0 0.0 copy-start.9
  6.0 1.3 %collective-permute-start = (f32[9,40,128]{2,1,0:T(8,128)S(1)}, f32[9,40,128]{2,1,0:T(8,128)S(1)}, u32[]{:S(2)}, u32[]{:S(2)}) collective-permute-start(f32[9,40,128]{2,1,0:T(8,128)S(1)} %get-tuple-element.13.own_ref), channel_id=1, source_target_pairs={{0,3},{1,2},{2,1},{3,0},{4,7},{5,6},{6,5},{7,4},{8,11},{9,10},{10,... | collective-permute-start | bytes 552968 | tf_op jit(solution)/shard_map/ppermute | solution.py:432
  7.3 0.0 copy-done.1
  7.3 0.0 copy-done.5
  7.3 0.0 copy-done.7
  7.4 0.5 %own_spectrum.1.spectrum_ref = f32[2,40,128]{2,1,0:T(8,128)S(1)} custom-call(s32[1]{0:T(128)} %bitcast.part_ref, f32[128,512]{1,0:T(8,128)S(1)} %copy-done.1, bf16[2,512,256]{2,1,0:T(8,128)(2,1)S(1)} %copy-done.5, bf16[4,80,384]{2,1,0:T(8,128)(2,1)S(1)} %copy-done.7), custom_call_target="tpu_custom_call" | custom-call | flops 2147483648 | bytes 1048576 | tf_op jit(solution)/shard_map/own_spectrum/pallas_call | solution.py:389
  7.8 0.0 copy-start.3
  7.9 1.0 %collective-permute-done.1.rim_ref = f32[32,512]{1,0:T(8,128)S(1)} collective-permute-done((f32[32,512]{1,0:T(8,128)S(1)}, f32[32,512]{1,0:T(8,128)S(1)}, u32[]{:S(2)}, u32[]{:S(2)}) %collective-permute-start.1) | collective-permute-done | bytes 65568 | tf_op jit(solution)/shard_map/ppermute | solution.py:429
  8.8 0.0 copy-done.9
  8.8 0.4 %add_rim.1 = f32[2,40,128]{2,1,0:T(8,128)S(1)} custom-call(s32[1]{0:T(128)} %bitcast.part_ref, f32[2,40,128]{2,1,0:T(8,128)S(1)} %own_spectrum.1.spectrum_ref, f32[32,512]{1,0:T(8,128)S(1)} %collective-permute-done.1.rim_ref, bf16[2,512,256]{2,1,0:T(8,128)(2,1)S(1)} %copy-done.5, bf16[4,80,96]{2,1,0:T(8,128)(2,1)S(1)} %copy-done.9), custom_call_target="tpu_custom_call" | custom-call | flops 268435456 | bytes 1048576 | tf_op jit(solution)/shard_map/add_rim/pallas_call | solution.py:389
  9.2 0.0 copy-start.6
  9.2 1.9 %collective-permute-start.2 = (f32[2,40,128]{2,1,0:T(8,128)S(1)}, f32[2,40,128]{2,1,0:T(8,128)S(1)}, u32[]{:S(2)}, u32[]{:S(2)}) collective-permute-start(f32[2,40,128]{2,1,0:T(8,128)S(1)} %add_rim.1), channel_id=1, source_target_pairs={{0,3},{1,2},{2,1},{3,0},{4,7},{5,6},{6,5},{7,4},{8,11},{9,10},{10,... | collective-permute-start | bytes 122888 | tf_op jit(solution)/shard_map/ppermute | solution.py:432
  11.2 1.7 %collective-permute-done.2 = f32[2,40,128]{2,1,0:T(8,128)S(1)} collective-permute-done((f32[2,40,128]{2,1,0:T(8,128)S(1)}, f32[2,40,128]{2,1,0:T(8,128)S(1)}, u32[]{:S(2)}, u32[]{:S(2)}) %collective-permute-start.2) | collective-permute-done | bytes 40992 | tf_op jit(solution)/shard_map/ppermute | solution.py:432
  12.9 0.0 copy-start.8
  12.9 0.0 collective-permute-done
  12.9 0.1 collective-permute-start.4
  13.0 0.5 %collective-permute-start.3 = (f32[9,40,128]{2,1,0:T(8,128)S(1)}, f32[9,40,128]{2,1,0:T(8,128)S(1)}, u32[]{:S(2)}, u32[]{:S(2)}) collective-permute-start(f32[9,40,128]{2,1,0:T(8,128)S(1)} %get-tuple-element.13.own_ref), channel_id=1, source_target_pairs={{0,1},{1,0},{2,3},{3,2},{4,5},{5,4},{6,7},{7,6},{8,9},{9,8},{10,11... | collective-permute-start | bytes 552968 | tf_op jit(solution)/shard_map/ppermute | solution.py:432
  13.5 1.2 %collective-permute-done.3.core_ref = f32[9,40,128]{2,1,0:T(8,128)S(1)} collective-permute-done((f32[9,40,128]{2,1,0:T(8,128)S(1)}, f32[9,40,128]{2,1,0:T(8,128)S(1)}, u32[]{:S(2)}, u32[]{:S(2)}) %collective-permute-start.3) | collective-permute-done | bytes 184352 | tf_op jit(solution)/shard_map/ppermute | solution.py:432
  14.7 0.0 collective-permute-done.4.cross_ref
  14.7 0.0 copy-done.3
  14.7 0.0 copy-done.6
  14.7 0.0 copy-done.8
  14.7 0.0 copy-start
  14.8 0.0 copy-start.4
  14.8 5.9 %coherent_fields.1 = f32[80,128]{1,0:T(8,128)S(1)} custom-call(s32[1]{0:T(128)} %bitcast.part_ref, f32[9,40,128]{2,1,0:T(8,128)S(1)} %get-tuple-element.13.own_ref, f32[11,40,128]{2,1,0:T(8,128)S(1)} %pad_maximum_fusion.side_ref, f32[9,40,128]{2,1,0:T(8,128)S(1)} %collective-permute-done.3.core_ref, f32[11,40,128]{2,1,0:T(8,128)S(1)} %collective-permute-done.4.cross_ref, ...), custom_call_target="tpu_custom_call" | custom-call | flops 8589934592 | bytes 1048576 | tf_op jit(solution)/shard_map/coherent_fields/pallas_call | solution.py:389
  20.7 0.2 collective-permute-start.5
  20.9 1.0 %collective-permute-done.5 = f32[80,128]{1,0:T(8,128)S(1)} collective-permute-done((f32[80,128]{1,0:T(8,128)S(1)}, f32[80,128]{1,0:T(8,128)S(1)}, u32[]{:S(2)}, u32[]{:S(2)}) %collective-permute-start.5) | collective-permute-done | bytes 40992 | tf_op jit(solution)/shard_map/ppermute | solution.py:432
  22.0 0.7 %collective-permute-start.6 = (f32[80,128]{1,0:T(8,128)S(1)}, f32[80,128]{1,0:T(8,128)S(1)}, u32[]{:S(2)}, u32[]{:S(2)}) collective-permute-start(f32[80,128]{1,0:T(8,128)S(1)} %add.18.chip_ref), channel_id=1, source_target_pairs={{0,0},{1,2},{2,1},{3,3},{4,4},{5,6},{6,5},{7,7},{8,8},{9,10},{10,9... | collective-permute-start | bytes 122888 | tf_op jit(solution)/shard_map/ppermute | solution.py:516
  22.6 3.6 %collective-permute-start.7 = (f32[80,128]{1,0:T(8,128)S(1)}, f32[80,128]{1,0:T(8,128)S(1)}, u32[]{:S(2)}, u32[]{:S(2)}) collective-permute-start(f32[80,128]{1,0:T(8,128)S(1)} %add.18.chip_ref), channel_id=1, source_target_pairs={{0,3},{1,1},{2,2},{3,0},{4,7},{5,5},{6,6},{7,4},{8,11},{9,9},{10,1... | collective-permute-start | bytes 122888 | tf_op jit(solution)/shard_map/ppermute | solution.py:517
  26.3 0.0 collective-permute-done.6
  26.3 0.0 copy-start.2
  26.3 1.7 %collective-permute-start.8 = (f32[80,128]{1,0:T(8,128)S(1)}, f32[80,128]{1,0:T(8,128)S(1)}, u32[]{:S(2)}, u32[]{:S(2)}) collective-permute-start(f32[80,128]{1,0:T(8,128)S(1)} %add.19.sum_ref), channel_id=1, source_target_pairs={{0,1},{3,2},{4,5},{7,6},{8,9},{11,10},{12,13},{15,14},{16,17},{19,... | collective-permute-start | bytes 122888 | tf_op jit(solution)/shard_map/ppermute | solution.py:429
  28.0 0.1 collective-permute-done.7.back_ref
  28.1 0.0 copy-done
  28.1 0.0 copy-done.4
  28.1 1.2 %own_gradient.1 = (f32[128,512]{1,0:T(8,128)}, f32[32,512]{1,0:T(8,128)S(1)}, f32[32,512]{1,0:T(8,128)S(1)}) custom-call(s32[1]{0:T(128)} %bitcast.part_ref, f32[128,512]{1,0:T(8,128)S(1)} %copy-done.1, f32[80,128]{1,0:T(8,128)S(1)} %add.19.sum_ref, f32[80,128]{1,0:T(8,128)S(1)} %add.18.chip_ref, f32[80,128]{1,0:T(8,128)S(1)} %collective-permute-done.7.back_ref, ...), custom_call_target="tpu_custom_call" | custom-call | flops 2147483648 | bytes 1048576 | tf_op jit(solution)/shard_map/own_gradient/pallas_call | solution.py:389
  29.3 1.9 %collective-permute-done.8.near_ref = f32[80,128]{1,0:T(8,128)S(1)} collective-permute-done((f32[80,128]{1,0:T(8,128)S(1)}, f32[80,128]{1,0:T(8,128)S(1)}, u32[]{:S(2)}, u32[]{:S(2)}) %collective-permute-start.8) | collective-permute-done | bytes 40992 | tf_op jit(solution)/shard_map/ppermute | solution.py:429
  31.1 0.0 copy-done.2
  31.1 1.0 %edge_gradient.1 = f32[128,512]{1,0:T(8,128)} custom-call(s32[1]{0:T(128)} %bitcast.part_ref, f32[128,512]{1,0:T(8,128)} %get-tuple-element.18.gradient_hbm, f32[32,512]{1,0:T(8,128)S(1)} %get-tuple-element.19.edge_ref, f32[32,512]{1,0:T(8,128)S(1)} %get-tuple-element.20.scale_ref, ...), custom_call_target="tpu_custom_call", output_to_operand_aliasing={{}: (1, {})} | custom-call | flops 268435456 | bytes 1048576 | tf_op jit(solution)/shard_map/edge_gradient/pallas_call | solution.py:389
  (4 shorter events, 0.0 us)
Async XLA Ops:
  0.0 7.3 %copy-start.1 = (f32[128,512]{1,0:T(8,128)S(1)}, f32[128,512]{1,0:T(8,128)}, u32[]{:S(2)}) copy-start(f32[128,512]{1,0:T(8,128)} %theta_ref.3) | copy-start | bytes 786436
  0.0 7.3 %copy-start.5 = (bf16[2,512,256]{2,1,0:T(8,128)(2,1)S(1)}, bf16[2,512,256]{2,1,0:T(8,128)(2,1)}, u32[]{:S(2)}) copy-start(bf16[2,512,256]{2,1,0:T(8,128)(2,1)} %constant.41.clone.column_ref) | copy-start | bytes 1572868
  0.0 7.3 %copy-start.7 = (bf16[4,80,384]{2,1,0:T(8,128)(2,1)S(1)}, bf16[4,80,384]{2,1,0:T(8,128)(2,1)}, u32[]{:S(2)}) copy-start(bf16[4,80,384]{2,1,0:T(8,128)(2,1)} %constant.42.clone.rows_ref) | copy-start | bytes 737284
  1.7 7.1 %collective-permute-start.1 = (f32[32,512]{1,0:T(8,128)S(1)}, f32[32,512]{1,0:T(8,128)S(1)}, u32[]{:S(2)}, u32[]{:S(2)}) collective-permute-start(f32[32,512]{1,0:T(8,128)S(1)} %get-tuple-element.14), channel_id=1, source_target_pairs={{1,1},{2,2},{5,5},{6,6},{9,9},{10,10},{13,13},{14,14},{17,17},{18,... | collective-permute-start | bytes 196616 | tf_op jit(solution)/shard_map/ppermute | solution.py:429
  6.0 2.8 %copy-start.9 = (bf16[4,80,96]{2,1,0:T(8,128)(2,1)S(1)}, bf16[4,80,96]{2,1,0:T(8,128)(2,1)}, u32[]{:S(2)}) copy-start(bf16[4,80,96]{2,1,0:T(8,128)(2,1)} %constant.44.clone.rows_ref) | copy-start | bytes 184324
  6.0 6.8 %collective-permute-start = (f32[9,40,128]{2,1,0:T(8,128)S(1)}, f32[9,40,128]{2,1,0:T(8,128)S(1)}, u32[]{:S(2)}, u32[]{:S(2)}) collective-permute-start(f32[9,40,128]{2,1,0:T(8,128)S(1)} %get-tuple-element.13.own_ref), channel_id=1, source_target_pairs={{0,3},{1,2},{2,1},{3,0},{4,7},{5,6},{6,5},{7,4},{8,11},{9,10},{10,... | collective-permute-start | bytes 552968 | tf_op jit(solution)/shard_map/ppermute | solution.py:432
  7.8 6.9 %copy-start.3 = (s32[512,512]{1,0:T(8,128)S(1)}, s32[512,512]{1,0:T(8,128)}, u32[]{:S(2)}) copy-start(s32[512,512]{1,0:T(8,128)} %target_ref.1) | copy-start | bytes 3145732
  9.2 5.5 %copy-start.6 = (bf16[512,240]{1,0:T(8,128)(2,1)S(1)}, bf16[512,240]{1,0:T(8,128)(2,1)}, u32[]{:S(2)}) copy-start(bf16[512,240]{1,0:T(8,128)(2,1)} %constant.49.clone.row_ref) | copy-start | bytes 737284
  9.2 3.6 %collective-permute-start.2 = (f32[2,40,128]{2,1,0:T(8,128)S(1)}, f32[2,40,128]{2,1,0:T(8,128)S(1)}, u32[]{:S(2)}, u32[]{:S(2)}) collective-permute-start(f32[2,40,128]{2,1,0:T(8,128)S(1)} %add_rim.1), channel_id=1, source_target_pairs={{0,3},{1,2},{2,1},{3,0},{4,7},{5,6},{6,5},{7,4},{8,11},{9,10},{10,... | collective-permute-start | bytes 122888 | tf_op jit(solution)/shard_map/ppermute | solution.py:432
  12.9 1.9 %copy-start.8 = (bf16[160,512]{1,0:T(8,128)(2,1)S(1)}, bf16[160,512]{1,0:T(8,128)(2,1)}, u32[]{:S(2)}) copy-start(bf16[160,512]{1,0:T(8,128)(2,1)} %constant.50.clone.row_turned_ref) | copy-start | bytes 491524
  12.9 1.8 %collective-permute-start.4 = (f32[11,40,128]{2,1,0:T(8,128)S(1)}, f32[11,40,128]{2,1,0:T(8,128)S(1)}, u32[]{:S(2)}, u32[]{:S(2)}) collective-permute-start(f32[11,40,128]{2,1,0:T(8,128)S(1)} %pad_maximum_fusion.side_ref), channel_id=1, source_target_pairs={{0,1},{1,0},{2,3},{3,2},{4,5},{5,4},{6,7},{7,6},{8,9},{9,8},{10,11... | collective-permute-start | bytes 675848 | tf_op jit(solution)/shard_map/ppermute | solution.py:432
  13.0 1.7 %collective-permute-start.3 = (f32[9,40,128]{2,1,0:T(8,128)S(1)}, f32[9,40,128]{2,1,0:T(8,128)S(1)}, u32[]{:S(2)}, u32[]{:S(2)}) collective-permute-start(f32[9,40,128]{2,1,0:T(8,128)S(1)} %get-tuple-element.13.own_ref), channel_id=1, source_target_pairs={{0,1},{1,0},{2,3},{3,2},{4,5},{5,4},{6,7},{7,6},{8,9},{9,8},{10,11... | collective-permute-start | bytes 552968 | tf_op jit(solution)/shard_map/ppermute | solution.py:432
  14.7 13.3 %copy-start = (bf16[2,256,512]{2,1,0:T(8,128)(2,1)S(1)}, bf16[2,256,512]{2,1,0:T(8,128)(2,1)}, u32[]{:S(2)}) copy-start(bf16[2,256,512]{2,1,0:T(8,128)(2,1)} %constant.48.clone.turned_ref) | copy-start | bytes 1572868
  14.8 13.3 %copy-start.4 = (bf16[4,256,240]{2,1,0:T(8,128)(2,1)S(1)}, bf16[4,256,240]{2,1,0:T(8,128)(2,1)}, u32[]{:S(2)}) copy-start(bf16[4,256,240]{2,1,0:T(8,128)(2,1)} %constant.43.clone.rows_ref) | copy-start | bytes 1474564
  20.7 1.3 %collective-permute-start.5 = (f32[80,128]{1,0:T(8,128)S(1)}, f32[80,128]{1,0:T(8,128)S(1)}, u32[]{:S(2)}, u32[]{:S(2)}) collective-permute-start(f32[80,128]{1,0:T(8,128)S(1)} %coherent_fields.1), channel_id=1, source_target_pairs={{0,1},{1,0},{2,3},{3,2},{4,5},{5,4},{6,7},{7,6},{8,9},{9,8},{10,11... | collective-permute-start | bytes 122888 | tf_op jit(solution)/shard_map/ppermute | solution.py:432
  22.0 4.3 %collective-permute-start.6 = (f32[80,128]{1,0:T(8,128)S(1)}, f32[80,128]{1,0:T(8,128)S(1)}, u32[]{:S(2)}, u32[]{:S(2)}) collective-permute-start(f32[80,128]{1,0:T(8,128)S(1)} %add.18.chip_ref), channel_id=1, source_target_pairs={{0,0},{1,2},{2,1},{3,3},{4,4},{5,6},{6,5},{7,7},{8,8},{9,10},{10,9... | collective-permute-start | bytes 122888 | tf_op jit(solution)/shard_map/ppermute | solution.py:516
  22.6 5.5 %collective-permute-start.7 = (f32[80,128]{1,0:T(8,128)S(1)}, f32[80,128]{1,0:T(8,128)S(1)}, u32[]{:S(2)}, u32[]{:S(2)}) collective-permute-start(f32[80,128]{1,0:T(8,128)S(1)} %add.18.chip_ref), channel_id=1, source_target_pairs={{0,3},{1,1},{2,2},{3,0},{4,7},{5,5},{6,6},{7,4},{8,11},{9,9},{10,1... | collective-permute-start | bytes 122888 | tf_op jit(solution)/shard_map/ppermute | solution.py:517
  26.3 4.8 %copy-start.2 = (bf16[4,64,240]{2,1,0:T(8,128)(2,1)S(1)}, bf16[4,64,240]{2,1,0:T(8,128)(2,1)}, u32[]{:S(2)}) copy-start(bf16[4,64,240]{2,1,0:T(8,128)(2,1)} %constant.45.clone.rows_ref) | copy-start | bytes 368644
  26.3 4.8 %collective-permute-start.8 = (f32[80,128]{1,0:T(8,128)S(1)}, f32[80,128]{1,0:T(8,128)S(1)}, u32[]{:S(2)}, u32[]{:S(2)}) collective-permute-start(f32[80,128]{1,0:T(8,128)S(1)} %add.19.sum_ref), channel_id=1, source_target_pairs={{0,1},{3,2},{4,5},{7,6},{8,9},{11,10},{12,13},{15,14},{16,17},{19,... | collective-permute-start | bytes 122888 | tf_op jit(solution)/shard_map/ppermute | solution.py:429
where the time goes:
time: 32.4 us; the launch traced here: 32.2 us
  starting transfers between devices  14.3 us (44%)
  Pallas kernels  10.7 us (33%)
  waiting for transfers between devices  6.95 us (21%)
    pallas_call x6, Pallas kernels, call(): pl.pallas_call(kernel, grid_spec=pltpu.PrefetchScalarGridSpec(num_scalar_...  10.7 us
    ppermute x2, starting transfers between devices, across(): return lax.ppermute(value, ('tile', 'cond'), pairs)  5.95 us
    ppermute x5, starting transfers between devices, partner(): return lax.ppermute(value, 'cond', [(i, i ^ step) for i in range(PARTS)])  4.04 us
    ppermute x5, waiting for transfers between devices, partner(): return lax.ppermute(value, 'cond', [(i, i ^ step) for i in range(PARTS)])  3.97 us
    ppermute x1, starting transfers between devices, shards(): back = lax.ppermute(chip, 'cond', [(0, last), (1, 1), (2, 2), (last, 0)])  3.63 us
    ppermute x2, waiting for transfers between devices, across(): return lax.ppermute(value, ('tile', 'cond'), pairs)  2.86 us
    ppermute x1, starting transfers between devices, shards(): lax.ppermute(chip, 'cond', [(0, 0), (1, 2), (2, 1), (last, last)])  0.65 us
  transfers between devices with their start and end apart: 9, of which 6 were waited for; matrix products, arithmetic and copies ran while one was open for 0% of the time, Pallas kernels for 6%

commit v1 on v0

--- a/solution.py
+++ b/solution.py
@@ -137,8 +137,8 @@
 
 
 def open_kernel(
-    part_ref, theta_hbm, real_hbm, imag_hbm, thresholds_hbm, weights_hbm, forward_hbm, backward_hbm,
-    out_ref, rim_ref, shares_ref, forward_ref, backward_ref, real_ref, imag_ref, thresholds_ref, weights_ref, stage, sems,
+    part_ref, real_hbm, imag_hbm, thresholds_hbm, weights_hbm, forward_hbm, backward_hbm,
+    out_ref, shares_ref, forward_ref, backward_ref, real_ref, imag_ref, thresholds_ref, weights_ref, stage, sems,
 ):
     part = part_of(part_ref)
     moves = [
@@ -146,7 +146,6 @@
         (imag_hbm, imag_ref),
         (thresholds_hbm, thresholds_ref),
         (weights_hbm, weights_ref),
-        (theta_hbm.at[pl.ds(pl.multiple_of(jnp.where(part == 0, 0, ROWS - HALO), HALO), HALO)], rim_ref),
         (forward_hbm.at[part], forward_ref),
         (backward_hbm.at[part], backward_ref),
     ]
@@ -432,20 +431,19 @@
         return lax.ppermute(value, "cond", [(i, i ^ step) for i in range(PARTS)])
 
     kernel_shape = (local_conds, KSUP, KERNELS, KSUP)
-    own, rim, shares, forward, backward = call(
+    own, shares, forward, backward = call(
         open_kernel,
         (parts,),
         tuple(
             pltpu.with_memory_space_constraint(value, pltpu.HBM)
             for value in (
-                theta, kernel_real.transpose(0, 2, 1, 3), kernel_imag.transpose(0, 2, 1, 3), thresholds, weights,
+                kernel_real.transpose(0, 2, 1, 3), kernel_imag.transpose(0, 2, 1, 3), thresholds, weights,
                 table["forward"], table["backward"],
             )
         ),
-        [hbm] * 7,
+        [hbm] * 6,
         [
             floats(2 * local + 1, FA, 2 * FB),
-            floats(HALO, TP),
             floats(CONDS, ROWS),
             jax.ShapeDtypeStruct(table["forward"].shape[1:], BF),
             jax.ShapeDtypeStruct(table["backward"].shape[1:], BF),
@@ -456,10 +454,11 @@
             pltpu.SMEM(thresholds.shape, F32),
             pltpu.SMEM(weights.shape, jnp.int32),
             pltpu.VMEM((2 * local, 72, 2 * FB), F32),
-            pltpu.SemaphoreType.DMA((7,)),
+            pltpu.SemaphoreType.DMA((6,)),
         ),
         name="open_parts",
     )
+    rim = lax.dynamic_slice_in_dim(theta, jnp.where(part == 0, 0, ROWS - HALO), HALO, axis=0)
     rim = across(rim, [(1, 1), (2, 2)], (0, 0), (last, last))
     spectrum = call(
         spectrum_kernel,

time: 32.4 us -> 31.4 us (0.969)
  starting transfers between devices: 14.3 us -> 12.9 us
  local copies, waits for them, and re-layouts: 0.06 us -> 0.91 us
  waiting for transfers between devices: 6.95 us -> 6.44 us
    ppermute x2, waiting for transfers between devices: 2.86 us -> 0.93 us  [across(): return lax.ppermute(value, ('tile', 'cond'), pairs)]
    ppermute x5, waiting for transfers between devices: 3.97 us -> 5.38 us  [partner(): return lax.ppermute(value, 'cond', [(i, i ^ step) for i in range(PARTS)])]
    ppermute x5, starting transfers between devices: 4.04 us -> 2.69 us  [partner(): return lax.ppermute(value, 'cond', [(i, i ^ step) for i in range(PARTS)])]
    ppermute x1, starting transfers between devices: 3.63 us -> 2.71 us  [shards(): back = lax.ppermute(chip, 'cond', [(0, last), (1, 1), (2, 2), (last, 0)])]
    ppermute x2, starting transfers between devices: 5.95 us -> 6.84 us  [across(): return lax.ppermute(value, ('tile', 'cond'), pairs)]
    dynamic_slice x0 -> x1, local copies, waits for them, and re-layouts: none -> 0.84 us  [shards(): lax.dynamic_slice_in_dim(theta, jnp.where(part == 0, 0, ROWS - HALO), HAL...]
  transfers between devices with their start and end apart: 9 -> 9, of which waited for: 6 -> 5; matrix products, arithmetic and copies ran while one was open for 0% -> 0% of each run, Pallas kernels for 6% -> 12%
where the time goes in v1:
time: 31.4 us; the launch traced here: 31.2 us
  starting transfers between devices  12.9 us (41%)
  Pallas kernels  10.7 us (34%)
  waiting for transfers between devices  6.44 us (21%)
  local copies, waits for them, and re-layouts  0.91 us (3%)
    pallas_call x6, Pallas kernels, call(): pl.pallas_call(kernel, grid_spec=pltpu.PrefetchScalarGridSpec(num_scalar_...  10.7 us
    ppermute x2, starting transfers between devices, across(): return lax.ppermute(value, ('tile', 'cond'), pairs)  6.84 us
    ppermute x5, waiting for transfers between devices, partner(): return lax.ppermute(value, 'cond', [(i, i ^ step) for i in range(PARTS)])  5.38 us
    ppermute x1, starting transfers between devices, shards(): back = lax.ppermute(chip, 'cond', [(0, last), (1, 1), (2, 2), (last, 0)])  2.71 us
    ppermute x5, starting transfers between devices, partner(): return lax.ppermute(value, 'cond', [(i, i ^ step) for i in range(PARTS)])  2.69 us
    ppermute x2, waiting for transfers between devices, across(): return lax.ppermute(value, ('tile', 'cond'), pairs)  0.93 us
    dynamic_slice x1, local copies, waits for them, and re-layouts, shards(): lax.dynamic_slice_in_dim(theta, jnp.where(part == 0, 0, ROWS - HALO), HAL...  0.84 us
    ppermute x1, starting transfers between devices, shards(): lax.ppermute(chip, 'cond', [(0, 0), (1, 2), (2, 1), (last, last)])  0.65 us
  transfers between devices with their start and end apart: 9, of which 5 were waited for; matrix products, arithmetic and copies ran while one was open for 0% of the time, Pallas kernels for 12%

profile of v1, /device:TPU:0, one launch (start us, length us, event | category | flops | bytes accessed | tf_op | source)
XLA Modules:
  0.0 31.2 jit_solution(17557432871146024604)
XLA Ops:
  0.0 0.8 %constant_dynamic-slice_fusion = f32[32,512]{1,0:T(8,128)S(1)} fusion(f32[128,512]{1,0:T(8,128)} %theta_ref.3, s32[]{:T(128)S(6)} %select_n.5), kind=kLoop, calls=%fused_computation.1 | loop fusion | bytes 131076 | tf_op jit(solution)/shard_map/dynamic_slice | solution.py:461
  0.8 4.3 %collective-permute-start.1 = (f32[32,512]{1,0:T(8,128)S(1)}, f32[32,512]{1,0:T(8,128)S(1)}, u32[]{:S(2)}, u32[]{:S(2)}) collective-permute-start(f32[32,512]{1,0:T(8,128)S(1)} %constant_dynamic-slice_fusion), channel_id=1, source_target_pairs={{1,1},{2,2},{5,5},{6,6},{9,9},{10,10},{13,13},{14,14},{17,17},{18,... | collective-permute-start | bytes 196616 | tf_op jit(solution)/shard_map/ppermute | solution.py:428
  5.2 0.0 copy-start.2
  5.2 0.0 copy-start.5
  5.2 0.0 copy-start.7
  5.2 1.7 %open_parts.1 = (f32[9,40,128]{2,1,0:T(8,128)S(1)}, f32[8,128]{1,0:T(8,128)S(1)}, bf16[384,256]{1,0:T(8,128)(2,1)S(1)}, bf16[384,256]{1,0:T(8,128)(2,1)S(1)}) custom-call(s32[1]{0:T(128)} %bitcast.part_ref, f32[2,65,2,65]{3,2,1,0:T(2,128)} %bitcast.3, f32[2,65,2,65]{3,2,1,0:T(2,128)} %bitcast.4, f32[2]{0:T(128)} %thresholds_hbm.1, s32[8]{0:T(128)} %weights_hbm.1, ...), custom_call_target="tpu_custom_call" | custom-call | flops 268435456 | bytes 1048576 | tf_op jit(solution)/shard_map/open_parts/pallas_call | solution.py:388
  6.9 0.0 copy-start.9
  6.9 1.3 %collective-permute-start = (f32[9,40,128]{2,1,0:T(8,128)S(1)}, f32[9,40,128]{2,1,0:T(8,128)S(1)}, u32[]{:S(2)}, u32[]{:S(2)}) collective-permute-start(f32[9,40,128]{2,1,0:T(8,128)S(1)} %get-tuple-element.12.own_ref), channel_id=1, source_target_pairs={{0,3},{1,2},{2,1},{3,0},{4,7},{5,6},{6,5},{7,4},{8,11},{9,10},{10,... | collective-permute-start | bytes 552968 | tf_op jit(solution)/shard_map/ppermute | solution.py:431
  8.2 0.0 copy-done.2
  8.2 0.0 copy-done.5
  8.2 0.0 copy-done.7
  8.2 0.5 %own_spectrum.1.spectrum_ref = f32[2,40,128]{2,1,0:T(8,128)S(1)} custom-call(s32[1]{0:T(128)} %bitcast.part_ref, f32[128,512]{1,0:T(8,128)S(1)} %copy-done.2, bf16[2,512,256]{2,1,0:T(8,128)(2,1)S(1)} %copy-done.5, bf16[4,80,384]{2,1,0:T(8,128)(2,1)S(1)} %copy-done.7), custom_call_target="tpu_custom_call" | custom-call | flops 2147483648 | bytes 1048576 | tf_op jit(solution)/shard_map/own_spectrum/pallas_call | solution.py:388
  8.7 0.0 copy-start.3
  8.7 0.0 collective-permute-done.1.rim_ref
  8.7 0.0 copy-done.9
  8.8 0.4 %add_rim.1 = f32[2,40,128]{2,1,0:T(8,128)S(1)} custom-call(s32[1]{0:T(128)} %bitcast.part_ref, f32[2,40,128]{2,1,0:T(8,128)S(1)} %own_spectrum.1.spectrum_ref, f32[32,512]{1,0:T(8,128)S(1)} %collective-permute-done.1.rim_ref, bf16[2,512,256]{2,1,0:T(8,128)(2,1)S(1)} %copy-done.5, bf16[4,80,96]{2,1,0:T(8,128)(2,1)S(1)} %copy-done.9), custom_call_target="tpu_custom_call" | custom-call | flops 268435456 | bytes 1048576 | tf_op jit(solution)/shard_map/add_rim/pallas_call | solution.py:388
  9.1 0.0 copy-start.6
  9.2 0.6 %collective-permute-start.2 = (f32[2,40,128]{2,1,0:T(8,128)S(1)}, f32[2,40,128]{2,1,0:T(8,128)S(1)}, u32[]{:S(2)}, u32[]{:S(2)}) collective-permute-start(f32[2,40,128]{2,1,0:T(8,128)S(1)} %add_rim.1), channel_id=1, source_target_pairs={{0,3},{1,2},{2,1},{3,0},{4,7},{5,6},{6,5},{7,4},{8,11},{9,10},{10,... | collective-permute-start | bytes 122888 | tf_op jit(solution)/shard_map/ppermute | solution.py:431
  9.7 3.1 %collective-permute-done.2 = f32[2,40,128]{2,1,0:T(8,128)S(1)} collective-permute-done((f32[2,40,128]{2,1,0:T(8,128)S(1)}, f32[2,40,128]{2,1,0:T(8,128)S(1)}, u32[]{:S(2)}, u32[]{:S(2)}) %collective-permute-start.2) | collective-permute-done | bytes 40992 | tf_op jit(solution)/shard_map/ppermute | solution.py:431
  12.8 0.0 copy-start.8
  12.8 0.0 collective-permute-done
  12.9 0.1 collective-permute-start.4
  13.0 0.5 %collective-permute-start.3 = (f32[9,40,128]{2,1,0:T(8,128)S(1)}, f32[9,40,128]{2,1,0:T(8,128)S(1)}, u32[]{:S(2)}, u32[]{:S(2)}) collective-permute-start(f32[9,40,128]{2,1,0:T(8,128)S(1)} %get-tuple-element.12.own_ref), channel_id=1, source_target_pairs={{0,1},{1,0},{2,3},{3,2},{4,5},{5,4},{6,7},{7,6},{8,9},{9,8},{10,11... | collective-permute-start | bytes 552968 | tf_op jit(solution)/shard_map/ppermute | solution.py:431
  13.5 1.2 %collective-permute-done.3.core_ref = f32[9,40,128]{2,1,0:T(8,128)S(1)} collective-permute-done((f32[9,40,128]{2,1,0:T(8,128)S(1)}, f32[9,40,128]{2,1,0:T(8,128)S(1)}, u32[]{:S(2)}, u32[]{:S(2)}) %collective-permute-start.3) | collective-permute-done | bytes 184352 | tf_op jit(solution)/shard_map/ppermute | solution.py:431
  14.7 0.0 collective-permute-done.4.cross_ref
  14.7 0.0 copy-done.3
  14.7 0.0 copy-done.6
  14.7 0.0 copy-done.8
  14.7 0.0 copy-start
  14.7 0.0 copy-start.4
  14.7 5.9 %coherent_fields.1 = f32[80,128]{1,0:T(8,128)S(1)} custom-call(s32[1]{0:T(128)} %bitcast.part_ref, f32[9,40,128]{2,1,0:T(8,128)S(1)} %get-tuple-element.12.own_ref, f32[11,40,128]{2,1,0:T(8,128)S(1)} %pad_maximum_fusion.side_ref, f32[9,40,128]{2,1,0:T(8,128)S(1)} %collective-permute-done.3.core_ref, f32[11,40,128]{2,1,0:T(8,128)S(1)} %collective-permute-done.4.cross_ref, ...), custom_call_target="tpu_custom_call" | custom-call | flops 8589934592 | bytes 1048576 | tf_op jit(solution)/shard_map/coherent_fields/pallas_call | solution.py:388
  20.6 0.2 collective-permute-start.5
  20.9 1.0 %collective-permute-done.5 = f32[80,128]{1,0:T(8,128)S(1)} collective-permute-done((f32[80,128]{1,0:T(8,128)S(1)}, f32[80,128]{1,0:T(8,128)S(1)}, u32[]{:S(2)}, u32[]{:S(2)}) %collective-permute-start.5) | collective-permute-done | bytes 40992 | tf_op jit(solution)/shard_map/ppermute | solution.py:431
  21.9 0.7 %collective-permute-start.6 = (f32[80,128]{1,0:T(8,128)S(1)}, f32[80,128]{1,0:T(8,128)S(1)}, u32[]{:S(2)}, u32[]{:S(2)}) collective-permute-start(f32[80,128]{1,0:T(8,128)S(1)} %add.19.chip_ref), channel_id=1, source_target_pairs={{0,0},{1,2},{2,1},{3,3},{4,4},{5,6},{6,5},{7,7},{8,8},{9,10},{10,9... | collective-permute-start | bytes 122888 | tf_op jit(solution)/shard_map/ppermute | solution.py:515
  22.6 2.7 %collective-permute-start.7 = (f32[80,128]{1,0:T(8,128)S(1)}, f32[80,128]{1,0:T(8,128)S(1)}, u32[]{:S(2)}, u32[]{:S(2)}) collective-permute-start(f32[80,128]{1,0:T(8,128)S(1)} %add.19.chip_ref), channel_id=1, source_target_pairs={{0,3},{1,1},{2,2},{3,0},{4,7},{5,5},{6,6},{7,4},{8,11},{9,9},{10,1... | collective-permute-start | bytes 122888 | tf_op jit(solution)/shard_map/ppermute | solution.py:516
  25.3 0.0 collective-permute-done.6
  25.3 0.0 copy-start.1
  25.3 2.6 %collective-permute-start.8 = (f32[80,128]{1,0:T(8,128)S(1)}, f32[80,128]{1,0:T(8,128)S(1)}, u32[]{:S(2)}, u32[]{:S(2)}) collective-permute-start(f32[80,128]{1,0:T(8,128)S(1)} %add.20.sum_ref), channel_id=1, source_target_pairs={{0,1},{3,2},{4,5},{7,6},{8,9},{11,10},{12,13},{15,14},{16,17},{19,... | collective-permute-start | bytes 122888 | tf_op jit(solution)/shard_map/ppermute | solution.py:428
  27.9 0.1 collective-permute-done.7.back_ref
  28.0 0.0 copy-done
  28.0 0.0 copy-done.4
  28.0 1.2 %own_gradient.1 = (f32[128,512]{1,0:T(8,128)}, f32[32,512]{1,0:T(8,128)S(1)}, f32[32,512]{1,0:T(8,128)S(1)}) custom-call(s32[1]{0:T(128)} %bitcast.part_ref, f32[128,512]{1,0:T(8,128)S(1)} %copy-done.2, f32[80,128]{1,0:T(8,128)S(1)} %add.20.sum_ref, f32[80,128]{1,0:T(8,128)S(1)} %add.19.chip_ref, f32[80,128]{1,0:T(8,128)S(1)} %collective-permute-done.7.back_ref, ...), custom_call_target="tpu_custom_call" | custom-call | flops 2147483648 | bytes 1048576 | tf_op jit(solution)/shard_map/own_gradient/pallas_call | solution.py:388
  29.2 0.9 %collective-permute-done.8.near_ref = f32[80,128]{1,0:T(8,128)S(1)} collective-permute-done((f32[80,128]{1,0:T(8,128)S(1)}, f32[80,128]{1,0:T(8,128)S(1)}, u32[]{:S(2)}, u32[]{:S(2)}) %collective-permute-start.8) | collective-permute-done | bytes 40992 | tf_op jit(solution)/shard_map/ppermute | solution.py:428
  30.1 0.0 copy-done.1
  30.1 1.0 %edge_gradient.1 = f32[128,512]{1,0:T(8,128)} custom-call(s32[1]{0:T(128)} %bitcast.part_ref, f32[128,512]{1,0:T(8,128)} %get-tuple-element.16.gradient_hbm, f32[32,512]{1,0:T(8,128)S(1)} %get-tuple-element.17.edge_ref, f32[32,512]{1,0:T(8,128)S(1)} %get-tuple-element.18.scale_ref, ...), custom_call_target="tpu_custom_call", output_to_operand_aliasing={{}: (1, {})} | custom-call | flops 268435456 | bytes 1048576 | tf_op jit(solution)/shard_map/edge_gradient/pallas_call | solution.py:388
  (4 shorter events, 0.0 us)
Async XLA Ops:
  0.8 7.9 %collective-permute-start.1 = (f32[32,512]{1,0:T(8,128)S(1)}, f32[32,512]{1,0:T(8,128)S(1)}, u32[]{:S(2)}, u32[]{:S(2)}) collective-permute-start(f32[32,512]{1,0:T(8,128)S(1)} %constant_dynamic-slice_fusion), channel_id=1, source_target_pairs={{1,1},{2,2},{5,5},{6,6},{9,9},{10,10},{13,13},{14,14},{17,17},{18,... | collective-permute-start | bytes 196616 | tf_op jit(solution)/shard_map/ppermute | solution.py:428
  5.2 3.1 %copy-start.2 = (f32[128,512]{1,0:T(8,128)S(1)}, f32[128,512]{1,0:T(8,128)}, u32[]{:S(2)}) copy-start(f32[128,512]{1,0:T(8,128)} %theta_ref.3) | copy-start | bytes 786436
  5.2 3.1 %copy-start.5 = (bf16[2,512,256]{2,1,0:T(8,128)(2,1)S(1)}, bf16[2,512,256]{2,1,0:T(8,128)(2,1)}, u32[]{:S(2)}) copy-start(bf16[2,512,256]{2,1,0:T(8,128)(2,1)} %constant.45.clone.column_ref) | copy-start | bytes 1572868
  5.2 3.0 %copy-start.7 = (bf16[4,80,384]{2,1,0:T(8,128)(2,1)S(1)}, bf16[4,80,384]{2,1,0:T(8,128)(2,1)}, u32[]{:S(2)}) copy-start(bf16[4,80,384]{2,1,0:T(8,128)(2,1)} %constant.46.clone.rows_ref) | copy-start | bytes 737284
  6.9 1.8 %copy-start.9 = (bf16[4,80,96]{2,1,0:T(8,128)(2,1)S(1)}, bf16[4,80,96]{2,1,0:T(8,128)(2,1)}, u32[]{:S(2)}) copy-start(bf16[4,80,96]{2,1,0:T(8,128)(2,1)} %constant.48.clone.rows_ref) | copy-start | bytes 184324
  6.9 5.9 %collective-permute-start = (f32[9,40,128]{2,1,0:T(8,128)S(1)}, f32[9,40,128]{2,1,0:T(8,128)S(1)}, u32[]{:S(2)}, u32[]{:S(2)}) collective-permute-start(f32[9,40,128]{2,1,0:T(8,128)S(1)} %get-tuple-element.12.own_ref), channel_id=1, source_target_pairs={{0,3},{1,2},{2,1},{3,0},{4,7},{5,6},{6,5},{7,4},{8,11},{9,10},{10,... | collective-permute-start | bytes 552968 | tf_op jit(solution)/shard_map/ppermute | solution.py:431
  8.7 6.0 %copy-start.3 = (s32[512,512]{1,0:T(8,128)S(1)}, s32[512,512]{1,0:T(8,128)}, u32[]{:S(2)}) copy-start(s32[512,512]{1,0:T(8,128)} %target_ref.1) | copy-start | bytes 3145732
  9.1 5.6 %copy-start.6 = (bf16[512,240]{1,0:T(8,128)(2,1)S(1)}, bf16[512,240]{1,0:T(8,128)(2,1)}, u32[]{:S(2)}) copy-start(bf16[512,240]{1,0:T(8,128)(2,1)} %constant.53.clone.row_ref) | copy-start | bytes 737284
  9.2 3.7 %collective-permute-start.2 = (f32[2,40,128]{2,1,0:T(8,128)S(1)}, f32[2,40,128]{2,1,0:T(8,128)S(1)}, u32[]{:S(2)}, u32[]{:S(2)}) collective-permute-start(f32[2,40,128]{2,1,0:T(8,128)S(1)} %add_rim.1), channel_id=1, source_target_pairs={{0,3},{1,2},{2,1},{3,0},{4,7},{5,6},{6,5},{7,4},{8,11},{9,10},{10,... | collective-permute-start | bytes 122888 | tf_op jit(solution)/shard_map/ppermute | solution.py:431
  12.8 1.9 %copy-start.8 = (bf16[160,512]{1,0:T(8,128)(2,1)S(1)}, bf16[160,512]{1,0:T(8,128)(2,1)}, u32[]{:S(2)}) copy-start(bf16[160,512]{1,0:T(8,128)(2,1)} %constant.54.clone.row_turned_ref) | copy-start | bytes 491524
  12.9 1.8 %collective-permute-start.4 = (f32[11,40,128]{2,1,0:T(8,128)S(1)}, f32[11,40,128]{2,1,0:T(8,128)S(1)}, u32[]{:S(2)}, u32[]{:S(2)}) collective-permute-start(f32[11,40,128]{2,1,0:T(8,128)S(1)} %pad_maximum_fusion.side_ref), channel_id=1, source_target_pairs={{0,1},{1,0},{2,3},{3,2},{4,5},{5,4},{6,7},{7,6},{8,9},{9,8},{10,11... | collective-permute-start | bytes 675848 | tf_op jit(solution)/shard_map/ppermute | solution.py:431
  13.0 1.7 %collective-permute-start.3 = (f32[9,40,128]{2,1,0:T(8,128)S(1)}, f32[9,40,128]{2,1,0:T(8,128)S(1)}, u32[]{:S(2)}, u32[]{:S(2)}) collective-permute-start(f32[9,40,128]{2,1,0:T(8,128)S(1)} %get-tuple-element.12.own_ref), channel_id=1, source_target_pairs={{0,1},{1,0},{2,3},{3,2},{4,5},{5,4},{6,7},{7,6},{8,9},{9,8},{10,11... | collective-permute-start | bytes 552968 | tf_op jit(solution)/shard_map/ppermute | solution.py:431
  14.7 13.3 %copy-start = (bf16[2,256,512]{2,1,0:T(8,128)(2,1)S(1)}, bf16[2,256,512]{2,1,0:T(8,128)(2,1)}, u32[]{:S(2)}) copy-start(bf16[2,256,512]{2,1,0:T(8,128)(2,1)} %constant.52.clone.turned_ref) | copy-start | bytes 1572868
  14.7 13.3 %copy-start.4 = (bf16[4,256,240]{2,1,0:T(8,128)(2,1)S(1)}, bf16[4,256,240]{2,1,0:T(8,128)(2,1)}, u32[]{:S(2)}) copy-start(bf16[4,256,240]{2,1,0:T(8,128)(2,1)} %constant.47.clone.rows_ref) | copy-start | bytes 1474564
  20.6 1.3 %collective-permute-start.5 = (f32[80,128]{1,0:T(8,128)S(1)}, f32[80,128]{1,0:T(8,128)S(1)}, u32[]{:S(2)}, u32[]{:S(2)}) collective-permute-start(f32[80,128]{1,0:T(8,128)S(1)} %coherent_fields.1), channel_id=1, source_target_pairs={{0,1},{1,0},{2,3},{3,2},{4,5},{5,4},{6,7},{7,6},{8,9},{9,8},{10,11... | collective-permute-start | bytes 122888 | tf_op jit(solution)/shard_map/ppermute | solution.py:431
  21.9 3.4 %collective-permute-start.6 = (f32[80,128]{1,0:T(8,128)S(1)}, f32[80,128]{1,0:T(8,128)S(1)}, u32[]{:S(2)}, u32[]{:S(2)}) collective-permute-start(f32[80,128]{1,0:T(8,128)S(1)} %add.19.chip_ref), channel_id=1, source_target_pairs={{0,0},{1,2},{2,1},{3,3},{4,4},{5,6},{6,5},{7,7},{8,8},{9,10},{10,9... | collective-permute-start | bytes 122888 | tf_op jit(solution)/shard_map/ppermute | solution.py:515
  22.6 5.4 %collective-permute-start.7 = (f32[80,128]{1,0:T(8,128)S(1)}, f32[80,128]{1,0:T(8,128)S(1)}, u32[]{:S(2)}, u32[]{:S(2)}) collective-permute-start(f32[80,128]{1,0:T(8,128)S(1)} %add.19.chip_ref), channel_id=1, source_target_pairs={{0,3},{1,1},{2,2},{3,0},{4,7},{5,5},{6,6},{7,4},{8,11},{9,9},{10,1... | collective-permute-start | bytes 122888 | tf_op jit(solution)/shard_map/ppermute | solution.py:516
  25.3 4.8 %copy-start.1 = (bf16[4,64,240]{2,1,0:T(8,128)(2,1)S(1)}, bf16[4,64,240]{2,1,0:T(8,128)(2,1)}, u32[]{:S(2)}) copy-start(bf16[4,64,240]{2,1,0:T(8,128)(2,1)} %constant.49.clone.rows_ref) | copy-start | bytes 368644
  25.3 4.8 %collective-permute-start.8 = (f32[80,128]{1,0:T(8,128)S(1)}, f32[80,128]{1,0:T(8,128)S(1)}, u32[]{:S(2)}, u32[]{:S(2)}) collective-permute-start(f32[80,128]{1,0:T(8,128)S(1)} %add.20.sum_ref), channel_id=1, source_target_pairs={{0,1},{3,2},{4,5},{7,6},{8,9},{11,10},{12,13},{15,14},{16,17},{19,... | collective-permute-start | bytes 122888 | tf_op jit(solution)/shard_map/ppermute | solution.py:428

commit v2 on v1

--- a/solution.py
+++ b/solution.py
@@ -109,12 +109,8 @@
     return ref[0] % PARTS
 
 
-def has_mask_halo(ref):
-    return ref[0] // PARTS % 2 > 0
-
-
-def has_adjoint_halo(ref):
-    return ref[0] // (2 * PARTS) > 0
+def has_halo(ref):
+    return ref[0] // PARTS > 0
 
 
 def dot(left, right):
@@ -223,25 +219,26 @@
 
 
 def rim_kernel(part_ref, spectrum_ref, rim_ref, column_ref, rows_ref, out_ref):
-    mask = jnp.where(has_mask_halo(part_ref), jnp.tanh(mask_steep * rim_ref[...]), 0.0)
-    even, odd = spectrum_of(mask, column_ref, rows_ref[0])
+    even, odd = spectrum_of(jnp.tanh(mask_steep * rim_ref[...]), column_ref, rows_ref[0])
     out_ref[0] = even + spectrum_ref[0]
     out_ref[1] = odd + spectrum_ref[1]
 
 
 def fields_kernel(
-    part_ref, own_ref, side_ref, core_ref, cross_ref, shares_ref, target_ref, forward_ref, backward_ref, row_ref,
+    part_ref, mixed_ref, other_ref, shares_ref, target_ref, forward_ref, backward_ref, row_ref,
     row_turned_ref, out_ref, kernels_ref, lines, folded, amps, tanhs, total, signs, turned, backs,
 ):
     count = kernels_ref.shape[0]
     local = count // PARTS
     tall = 4 * FA
-    even = side_ref[2 * local + 1] + cross_ref[2 * local + 1]
-    odd = side_ref[2 * local + 2] + cross_ref[2 * local + 2]
+    each = 2 * local + 1
+    even = mixed_ref[2 * each] + other_ref[2 * each]
+    odd = mixed_ref[2 * each + 1] + other_ref[2 * each + 1]
     lane = lax.broadcasted_iota(jnp.int32, (FA, 2 * FB), 1)
     row = lax.broadcasted_iota(jnp.int32, (FA, 2 * FB), 0)
     zero_lane = (lane == HALF) & (row <= HALF)
-    for group, ref in enumerate((own_ref, side_ref, core_ref, cross_ref)):
+    for group in range(PARTS):
+        ref = (mixed_ref, other_ref)[group // 2].at[pl.ds(group % 2 * each, each)]
         extra = ref[2 * local]
         for kern in range(local):
             values = []
@@ -296,7 +293,7 @@
         total[...] += value
         return carry
 
-    lax.fori_loop(0, CONDS, expose, 0, unroll=4)
+    lax.fori_loop(0, CONDS, expose, 0, unroll=8)
     total[...] = total[...] * (band_weight / (CONDS * CONDS))
 
     def drive(cond, carry):
@@ -313,7 +310,7 @@
             turned[pl.ds(index * 2, 2)] = jnp.stack([back[:, :ROWS], back[:, ROWS:]])
         return carry
 
-    lax.fori_loop(0, CONDS, drive, 0, unroll=4)
+    lax.fori_loop(0, CONDS, drive, 0, unroll=8)
     high, low = split(turned[...].reshape(count * tall, ROWS))
     backs[...] = dot(jnp.concatenate([high, low], axis=1), backward_ref[: 2 * ROWS]) + dot(high, backward_ref[2 * ROWS :])
 
@@ -365,7 +362,7 @@
 
 def edge_kernel(part_ref, gradient_hbm, edge_ref, scale_ref, near_ref, turned_ref, rows_ref, out_hbm, stage, sem):
     rim = image_rows(near_ref[...], rows_ref[0], turned_ref) * scale_ref[...]
-    stage[...] = edge_ref[...] + jnp.where(has_adjoint_halo(part_ref), rim, 0.0)
+    stage[...] = edge_ref[...] + jnp.where(has_halo(part_ref), rim, 0.0)
     copy = pltpu.make_async_copy(stage, out_hbm.at[pl.ds(edge_start(part_ref), HALO)], sem)
     copy.start()
     copy.wait()
@@ -413,18 +410,18 @@
     tile = lax.axis_index("tile")
     last = PARTS - 1
     above = ((part == 0) & (tile > 0)) | ((part == last) & (tile < tiles - 1))
-    below = ((part == 0) & (tile < tiles - 1)) | ((part == last) & (tile > 0))
-    parts = (part + PARTS * below.astype(jnp.int32) + 2 * PARTS * above.astype(jnp.int32)).reshape(1).astype(jnp.int32)
+    parts = (part + PARTS * above.astype(jnp.int32)).reshape(1).astype(jnp.int32)
     local_conds = kernel_real.shape[0]
     local = local_conds * KERNELS
     count = CONDS * KERNELS
     hbm = pl.BlockSpec(memory_space=pltpu.HBM)
 
-    def across(value, within, down, up):
+    def across(value, down, up, within=()):
         pairs = [(PARTS * i + a, PARTS * i + b) for i in range(tiles) for a, b in within]
         pairs += [(PARTS * (i + 1) + down[0], PARTS * i + down[1]) for i in range(tiles - 1)]
         pairs += [(PARTS * i + up[0], PARTS * (i + 1) + up[1]) for i in range(tiles - 1)]
-        pairs += [(down[0], up[1]), (PARTS * (tiles - 1) + up[0], PARTS * (tiles - 1) + down[1])]
+        if within:
+            pairs += [(down[0], up[1]), (PARTS * (tiles - 1) + up[0], PARTS * (tiles - 1) + down[1])]
         return lax.ppermute(value, ("tile", "cond"), pairs)
 
     def partner(value, step):
@@ -459,7 +456,7 @@
         name="open_parts",
     )
     rim = lax.dynamic_slice_in_dim(theta, jnp.where(part == 0, 0, ROWS - HALO), HALO, axis=0)
-    rim = across(rim, [(1, 1), (2, 2)], (0, 0), (last, last))
+    rim = across(rim, (0, 0), (last, last))
     spectrum = call(
         spectrum_kernel,
         (parts,),
@@ -470,7 +467,6 @@
         flops=1 << 31,
     )
     side = partner(own, 3)
-    core = partner(own, 1)
     spectrum = call(
         rim_kernel,
         (parts,),
@@ -479,15 +475,13 @@
         floats(2, FA, 2 * FB),
         name="add_rim",
     )
-    mixed = jnp.concatenate([side, spectrum + partner(spectrum, 3)], axis=0)
+    mixed = jnp.concatenate([own, side, spectrum + partner(spectrum, 3)], axis=0)
     adjoint = call(
         fields_kernel,
         (parts,),
-        (own, mixed, core, partner(mixed, 1), shares, target, forward, backward, table["row"], table["row_turned"]),
+        (mixed, partner(mixed, 1), shares, target, forward, backward, table["row"], table["row_turned"]),
         [
-            whole_spec(own),
             whole_spec(mixed),
-            whole_spec(core),
             whole_spec(mixed),
             whole_spec(shares),
             pl.BlockSpec((TP, ROWS), lambda i, part, *refs: (0, part_of(part))),
@@ -514,7 +508,7 @@
     chip = adjoint + partner(adjoint, 1)
     adjoint = chip + lax.ppermute(chip, "cond", [(0, 0), (1, 2), (2, 1), (last, last)])
     back = lax.ppermute(chip, "cond", [(0, last), (1, 1), (2, 2), (last, 0)])
-    near = across(adjoint, [(0, 1), (last, 2)], (2, last), (1, 0))
+    near = across(adjoint, (2, last), (1, 0), within=[(0, 1), (last, 2)])
     gradient, edge, scale = call(
         gradient_kernel,
         (parts,),

time: 31.4 us -> 31.6 us (level)
  waiting for transfers between devices: 6.44 us -> 7.26 us
  starting transfers between devices: 12.9 us -> 12.1 us
    ppermute x2, starting transfers between devices: 6.84 us -> 3.66 us  [across(): return lax.ppermute(value, ('tile', 'cond'), pairs)]
    ppermute x5 -> x4, starting transfers between devices: 2.69 us -> 4.91 us  [partner(): return lax.ppermute(value, 'cond', [(i, i ^ step) for i in range(PARTS)])]
    ppermute x5 -> x4, waiting for transfers between devices: 5.38 us -> 6.02 us  [partner(): return lax.ppermute(value, 'cond', [(i, i ^ step) for i in range(PARTS)])]
  transfers between devices with their start and end apart: 9 -> 8, of which waited for: 5 -> 5; matrix products, arithmetic and copies ran while one was open for 0% -> 0% of each run, Pallas kernels for 12% -> 12%
where the time goes in v2:
time: 31.6 us; the launch traced here: 31.4 us
  starting transfers between devices  12.1 us (38%)
  Pallas kernels  10.9 us (34%)
  waiting for transfers between devices  7.26 us (23%)
  local copies, waits for them, and re-layouts  0.91 us (3%)
    pallas_call x6, Pallas kernels, call(): pl.pallas_call(kernel, grid_spec=pltpu.PrefetchScalarGridSpec(num_scalar_...  10.9 us
    ppermute x4, waiting for transfers between devices, partner(): return lax.ppermute(value, 'cond', [(i, i ^ step) for i in range(PARTS)])  6.02 us
    ppermute x4, starting transfers between devices, partner(): return lax.ppermute(value, 'cond', [(i, i ^ step) for i in range(PARTS)])  4.91 us
    ppermute x2, starting transfers between devices, across(): return lax.ppermute(value, ('tile', 'cond'), pairs)  3.66 us
    ppermute x1, starting transfers between devices, shards(): back = lax.ppermute(chip, 'cond', [(0, last), (1, 1), (2, 2), (last, 0)])  2.86 us
    ppermute x2, waiting for transfers between devices, across(): return lax.ppermute(value, ('tile', 'cond'), pairs)  1.09 us
    dynamic_slice x1, local copies, waits for them, and re-layouts, shards(): lax.dynamic_slice_in_dim(theta, jnp.where(part == 0, 0, ROWS - HALO), HAL...  0.84 us
    ppermute x1, starting transfers between devices, shards(): lax.ppermute(chip, 'cond', [(0, 0), (1, 2), (2, 1), (last, last)])  0.65 us
  transfers between devices with their start and end apart: 8, of which 5 were waited for; matrix products, arithmetic and copies ran while one was open for 0% of the time, Pallas kernels for 12%

profile of v2, /device:TPU:0, one launch (start us, length us, event | category | flops | bytes accessed | tf_op | source)
XLA Modules:
  0.0 31.4 jit_solution(9231030223136316455)
XLA Ops:
  0.0 0.8 %constant_dynamic-slice_fusion = f32[32,512]{1,0:T(8,128)S(1)} fusion(f32[128,512]{1,0:T(8,128)} %theta_ref.3, s32[]{:T(128)S(6)} %select_n.5), kind=kLoop, calls=%fused_computation.1 | loop fusion | bytes 131076 | tf_op jit(solution)/shard_map/dynamic_slice | solution.py:458
  0.8 1.3 %collective-permute-start.1 = (f32[32,512]{1,0:T(8,128)S(1)}, f32[32,512]{1,0:T(8,128)S(1)}, u32[]{:S(2)}, u32[]{:S(2)}) collective-permute-start(f32[32,512]{1,0:T(8,128)S(1)} %constant_dynamic-slice_fusion), channel_id=1, source_target_pairs={{4,0},{8,4},{12,8},{16,12},{20,16},{24,20},{28,24},{3,7},{7,11},{1... | collective-permute-start | bytes 196616 | tf_op jit(solution)/shard_map/ppermute | solution.py:425
  2.2 0.0 copy-start.2
  2.2 0.0 copy-start.5
  2.2 0.0 copy-start.7
  2.2 1.7 %open_parts.1 = (f32[9,40,128]{2,1,0:T(8,128)S(1)}, f32[8,128]{1,0:T(8,128)S(1)}, bf16[384,256]{1,0:T(8,128)(2,1)S(1)}, bf16[384,256]{1,0:T(8,128)(2,1)S(1)}) custom-call(s32[1]{0:T(128)} %bitcast.part_ref, f32[2,65,2,65]{3,2,1,0:T(2,128)} %bitcast.3, f32[2,65,2,65]{3,2,1,0:T(2,128)} %bitcast.4, f32[2]{0:T(128)} %thresholds_hbm.1, s32[8]{0:T(128)} %weights_hbm.1, ...), custom_call_target="tpu_custom_call" | custom-call | flops 268435456 | bytes 1048576 | tf_op jit(solution)/shard_map/open_parts/pallas_call | solution.py:385
  3.9 0.0 copy-start.9
  3.9 4.3 %collective-permute-start = (f32[9,40,128]{2,1,0:T(8,128)S(1)}, f32[9,40,128]{2,1,0:T(8,128)S(1)}, u32[]{:S(2)}, u32[]{:S(2)}) collective-permute-start(f32[9,40,128]{2,1,0:T(8,128)S(1)} %get-tuple-element.12), channel_id=1, source_target_pairs={{0,3},{1,2},{2,1},{3,0},{4,7},{5,6},{6,5},{7,4},{8,11},{9,10},{10,... | collective-permute-start | bytes 552968 | tf_op jit(solution)/shard_map/ppermute | solution.py:428
  8.2 0.0 copy-done.2
  8.2 0.0 copy-done.5
  8.2 0.0 copy-done.7
  8.2 0.5 %own_spectrum.1.spectrum_ref = f32[2,40,128]{2,1,0:T(8,128)S(1)} custom-call(s32[1]{0:T(128)} %bitcast.part_ref, f32[128,512]{1,0:T(8,128)S(1)} %copy-done.2, bf16[2,512,256]{2,1,0:T(8,128)(2,1)S(1)} %copy-done.5, bf16[4,80,384]{2,1,0:T(8,128)(2,1)S(1)} %copy-done.7), custom_call_target="tpu_custom_call" | custom-call | flops 2147483648 | bytes 1048576 | tf_op jit(solution)/shard_map/own_spectrum/pallas_call | solution.py:385
  8.7 0.0 copy-start.3
  8.7 0.0 collective-permute-done.1.rim_ref
  8.7 0.0 copy-done.9
  8.7 0.4 %add_rim.1 = f32[2,40,128]{2,1,0:T(8,128)S(1)} custom-call(s32[1]{0:T(128)} %bitcast.part_ref, f32[2,40,128]{2,1,0:T(8,128)S(1)} %own_spectrum.1.spectrum_ref, f32[32,512]{1,0:T(8,128)S(1)} %collective-permute-done.1.rim_ref, bf16[2,512,256]{2,1,0:T(8,128)(2,1)S(1)} %copy-done.5, bf16[4,80,96]{2,1,0:T(8,128)(2,1)S(1)} %copy-done.9), custom_call_target="tpu_custom_call" | custom-call | flops 268435456 | bytes 1048576 | tf_op jit(solution)/shard_map/add_rim/pallas_call | solution.py:385
  9.1 0.3 %collective-permute-start.2 = (f32[2,40,128]{2,1,0:T(8,128)S(1)}, f32[2,40,128]{2,1,0:T(8,128)S(1)}, u32[]{:S(2)}, u32[]{:S(2)}) collective-permute-start(f32[2,40,128]{2,1,0:T(8,128)S(1)} %add_rim.1), channel_id=1, source_target_pairs={{0,3},{1,2},{2,1},{3,0},{4,7},{5,6},{6,5},{7,4},{8,11},{9,10},{10,... | collective-permute-start | bytes 122888 | tf_op jit(solution)/shard_map/ppermute | solution.py:428
  9.5 3.2 %collective-permute-done.2 = f32[2,40,128]{2,1,0:T(8,128)S(1)} collective-permute-done((f32[2,40,128]{2,1,0:T(8,128)S(1)}, f32[2,40,128]{2,1,0:T(8,128)S(1)}, u32[]{:S(2)}, u32[]{:S(2)}) %collective-permute-start.2) | collective-permute-done | bytes 40992 | tf_op jit(solution)/shard_map/ppermute | solution.py:428
  12.7 0.0 copy-start.6
  12.7 0.0 copy-start.8
  12.7 0.0 collective-permute-done
  12.7 0.1 collective-permute-start.3
  12.8 1.7 %collective-permute-done.3.other_ref = f32[20,40,128]{2,1,0:T(8,128)S(1)} collective-permute-done((f32[20,40,128]{2,1,0:T(8,128)S(1)}, f32[20,40,128]{2,1,0:T(8,128)S(1)}, u32[]{:S(2)}, u32[]{:S(2)}) %collective-permute-start.3) | collective-permute-done | bytes 409632 | tf_op jit(solution)/shard_map/ppermute | solution.py:428
  14.6 0.0 copy-done.3
  14.6 0.0 copy-done.6
  14.6 0.0 copy-done.8
  14.6 0.0 copy-start
  14.6 0.0 copy-start.4
  14.6 6.1 %coherent_fields.1 = f32[80,128]{1,0:T(8,128)S(1)} custom-call(s32[1]{0:T(128)} %bitcast.part_ref, f32[20,40,128]{2,1,0:T(8,128)S(1)} %pad_maximum_fusion.mixed_ref, f32[20,40,128]{2,1,0:T(8,128)S(1)} %collective-permute-done.3.other_ref, f32[8,128]{1,0:T(8,128)S(1)} %get-tuple-element.13.shares_ref, s32[512,512]{1,0:T(8,128)S(1)} %copy-done.3, ...), custom_call_target="tpu_custom_call" | custom-call | flops 8589934592 | bytes 1048576 | tf_op jit(solution)/shard_map/coherent_fields/pallas_call | solution.py:385
  20.7 0.2 collective-permute-start.4
  20.9 1.1 %collective-permute-done.4 = f32[80,128]{1,0:T(8,128)S(1)} collective-permute-done((f32[80,128]{1,0:T(8,128)S(1)}, f32[80,128]{1,0:T(8,128)S(1)}, u32[]{:S(2)}, u32[]{:S(2)}) %collective-permute-start.4) | collective-permute-done | bytes 40992 | tf_op jit(solution)/shard_map/ppermute | solution.py:428
  22.0 0.7 %collective-permute-start.5 = (f32[80,128]{1,0:T(8,128)S(1)}, f32[80,128]{1,0:T(8,128)S(1)}, u32[]{:S(2)}, u32[]{:S(2)}) collective-permute-start(f32[80,128]{1,0:T(8,128)S(1)} %add.15.chip_ref), channel_id=1, source_target_pairs={{0,0},{1,2},{2,1},{3,3},{4,4},{5,6},{6,5},{7,7},{8,8},{9,10},{10,9... | collective-permute-start | bytes 122888 | tf_op jit(solution)/shard_map/ppermute | solution.py:509
  22.7 2.9 %collective-permute-start.6 = (f32[80,128]{1,0:T(8,128)S(1)}, f32[80,128]{1,0:T(8,128)S(1)}, u32[]{:S(2)}, u32[]{:S(2)}) collective-permute-start(f32[80,128]{1,0:T(8,128)S(1)} %add.15.chip_ref), channel_id=1, source_target_pairs={{0,3},{1,1},{2,2},{3,0},{4,7},{5,5},{6,6},{7,4},{8,11},{9,9},{10,1... | collective-permute-start | bytes 122888 | tf_op jit(solution)/shard_map/ppermute | solution.py:510
  25.5 0.0 collective-permute-done.5
  25.5 0.0 copy-start.1
  25.6 2.4 %collective-permute-start.7 = (f32[80,128]{1,0:T(8,128)S(1)}, f32[80,128]{1,0:T(8,128)S(1)}, u32[]{:S(2)}, u32[]{:S(2)}) collective-permute-start(f32[80,128]{1,0:T(8,128)S(1)} %add.16.sum_ref), channel_id=1, source_target_pairs={{0,1},{3,2},{4,5},{7,6},{8,9},{11,10},{12,13},{15,14},{16,17},{19,... | collective-permute-start | bytes 122888 | tf_op jit(solution)/shard_map/ppermute | solution.py:425
  27.9 0.1 collective-permute-done.6.back_ref
  28.1 0.0 copy-done
  28.1 0.0 copy-done.4
  28.1 1.2 %own_gradient.1 = (f32[128,512]{1,0:T(8,128)}, f32[32,512]{1,0:T(8,128)S(1)}, f32[32,512]{1,0:T(8,128)S(1)}) custom-call(s32[1]{0:T(128)} %bitcast.part_ref, f32[128,512]{1,0:T(8,128)S(1)} %copy-done.2, f32[80,128]{1,0:T(8,128)S(1)} %add.16.sum_ref, f32[80,128]{1,0:T(8,128)S(1)} %add.15.chip_ref, f32[80,128]{1,0:T(8,128)S(1)} %collective-permute-done.6.back_ref, ...), custom_call_target="tpu_custom_call" | custom-call | flops 2147483648 | bytes 1048576 | tf_op jit(solution)/shard_map/own_gradient/pallas_call | solution.py:385
  29.3 1.1 %collective-permute-done.7.near_ref = f32[80,128]{1,0:T(8,128)S(1)} collective-permute-done((f32[80,128]{1,0:T(8,128)S(1)}, f32[80,128]{1,0:T(8,128)S(1)}, u32[]{:S(2)}, u32[]{:S(2)}) %collective-permute-start.7) | collective-permute-done | bytes 40992 | tf_op jit(solution)/shard_map/ppermute | solution.py:425
  30.3 0.0 copy-done.1
  30.4 1.0 %edge_gradient.1 = f32[128,512]{1,0:T(8,128)} custom-call(s32[1]{0:T(128)} %bitcast.part_ref, f32[128,512]{1,0:T(8,128)} %get-tuple-element.16.gradient_hbm, f32[32,512]{1,0:T(8,128)S(1)} %get-tuple-element.17.edge_ref, f32[32,512]{1,0:T(8,128)S(1)} %get-tuple-element.18.scale_ref, ...), custom_call_target="tpu_custom_call", output_to_operand_aliasing={{}: (1, {})} | custom-call | flops 268435456 | bytes 1048576 | tf_op jit(solution)/shard_map/edge_gradient/pallas_call | solution.py:385
  (4 shorter events, 0.1 us)
Async XLA Ops:
  0.8 7.9 %collective-permute-start.1 = (f32[32,512]{1,0:T(8,128)S(1)}, f32[32,512]{1,0:T(8,128)S(1)}, u32[]{:S(2)}, u32[]{:S(2)}) collective-permute-start(f32[32,512]{1,0:T(8,128)S(1)} %constant_dynamic-slice_fusion), channel_id=1, source_target_pairs={{4,0},{8,4},{12,8},{16,12},{20,16},{24,20},{28,24},{3,7},{7,11},{1... | collective-permute-start | bytes 196616 | tf_op jit(solution)/shard_map/ppermute | solution.py:425
  2.2 6.1 %copy-start.2 = (f32[128,512]{1,0:T(8,128)S(1)}, f32[128,512]{1,0:T(8,128)}, u32[]{:S(2)}) copy-start(f32[128,512]{1,0:T(8,128)} %theta_ref.3) | copy-start | bytes 786436
  2.2 6.0 %copy-start.5 = (bf16[2,512,256]{2,1,0:T(8,128)(2,1)S(1)}, bf16[2,512,256]{2,1,0:T(8,128)(2,1)}, u32[]{:S(2)}) copy-start(bf16[2,512,256]{2,1,0:T(8,128)(2,1)} %constant.42.clone.column_ref) | copy-start | bytes 1572868
  2.2 6.0 %copy-start.7 = (bf16[4,80,384]{2,1,0:T(8,128)(2,1)S(1)}, bf16[4,80,384]{2,1,0:T(8,128)(2,1)}, u32[]{:S(2)}) copy-start(bf16[4,80,384]{2,1,0:T(8,128)(2,1)} %constant.43.clone.rows_ref) | copy-start | bytes 737284
  3.9 4.8 %copy-start.9 = (bf16[4,80,96]{2,1,0:T(8,128)(2,1)S(1)}, bf16[4,80,96]{2,1,0:T(8,128)(2,1)}, u32[]{:S(2)}) copy-start(bf16[4,80,96]{2,1,0:T(8,128)(2,1)} %constant.45.clone.rows_ref) | copy-start | bytes 184324
  3.9 8.8 %collective-permute-start = (f32[9,40,128]{2,1,0:T(8,128)S(1)}, f32[9,40,128]{2,1,0:T(8,128)S(1)}, u32[]{:S(2)}, u32[]{:S(2)}) collective-permute-start(f32[9,40,128]{2,1,0:T(8,128)S(1)} %get-tuple-element.12), channel_id=1, source_target_pairs={{0,3},{1,2},{2,1},{3,0},{4,7},{5,6},{6,5},{7,4},{8,11},{9,10},{10,... | collective-permute-start | bytes 552968 | tf_op jit(solution)/shard_map/ppermute | solution.py:428
  8.7 5.8 %copy-start.3 = (s32[512,512]{1,0:T(8,128)S(1)}, s32[512,512]{1,0:T(8,128)}, u32[]{:S(2)}) copy-start(s32[512,512]{1,0:T(8,128)} %target_ref.1) | copy-start | bytes 3145732
  9.1 3.5 %collective-permute-start.2 = (f32[2,40,128]{2,1,0:T(8,128)S(1)}, f32[2,40,128]{2,1,0:T(8,128)S(1)}, u32[]{:S(2)}, u32[]{:S(2)}) collective-permute-start(f32[2,40,128]{2,1,0:T(8,128)S(1)} %add_rim.1), channel_id=1, source_target_pairs={{0,3},{1,2},{2,1},{3,0},{4,7},{5,6},{6,5},{7,4},{8,11},{9,10},{10,... | collective-permute-start | bytes 122888 | tf_op jit(solution)/shard_map/ppermute | solution.py:428
  12.7 1.9 %copy-start.6 = (bf16[512,240]{1,0:T(8,128)(2,1)S(1)}, bf16[512,240]{1,0:T(8,128)(2,1)}, u32[]{:S(2)}) copy-start(bf16[512,240]{1,0:T(8,128)(2,1)} %constant.50.clone.row_ref) | copy-start | bytes 737284
  12.7 1.9 %copy-start.8 = (bf16[160,512]{1,0:T(8,128)(2,1)S(1)}, bf16[160,512]{1,0:T(8,128)(2,1)}, u32[]{:S(2)}) copy-start(bf16[160,512]{1,0:T(8,128)(2,1)} %constant.51.clone.row_turned_ref) | copy-start | bytes 491524
  12.7 1.8 %collective-permute-start.3 = (f32[20,40,128]{2,1,0:T(8,128)S(1)}, f32[20,40,128]{2,1,0:T(8,128)S(1)}, u32[]{:S(2)}, u32[]{:S(2)}) collective-permute-start(f32[20,40,128]{2,1,0:T(8,128)S(1)} %pad_maximum_fusion.mixed_ref), channel_id=1, source_target_pairs={{0,1},{1,0},{2,3},{3,2},{4,5},{5,4},{6,7},{7,6},{8,9},{9,8},{10,11... | collective-permute-start | bytes 1228808 | tf_op jit(solution)/shard_map/ppermute | solution.py:428
  14.6 13.5 %copy-start = (bf16[2,256,512]{2,1,0:T(8,128)(2,1)S(1)}, bf16[2,256,512]{2,1,0:T(8,128)(2,1)}, u32[]{:S(2)}) copy-start(bf16[2,256,512]{2,1,0:T(8,128)(2,1)} %constant.49.clone.turned_ref) | copy-start | bytes 1572868
  14.6 13.5 %copy-start.4 = (bf16[4,256,240]{2,1,0:T(8,128)(2,1)S(1)}, bf16[4,256,240]{2,1,0:T(8,128)(2,1)}, u32[]{:S(2)}) copy-start(bf16[4,256,240]{2,1,0:T(8,128)(2,1)} %constant.44.clone.rows_ref) | copy-start | bytes 1474564
  20.7 1.3 %collective-permute-start.4 = (f32[80,128]{1,0:T(8,128)S(1)}, f32[80,128]{1,0:T(8,128)S(1)}, u32[]{:S(2)}, u32[]{:S(2)}) collective-permute-start(f32[80,128]{1,0:T(8,128)S(1)} %coherent_fields.1), channel_id=1, source_target_pairs={{0,1},{1,0},{2,3},{3,2},{4,5},{5,4},{6,7},{7,6},{8,9},{9,8},{10,11... | collective-permute-start | bytes 122888 | tf_op jit(solution)/shard_map/ppermute | solution.py:428
  22.0 3.5 %collective-permute-start.5 = (f32[80,128]{1,0:T(8,128)S(1)}, f32[80,128]{1,0:T(8,128)S(1)}, u32[]{:S(2)}, u32[]{:S(2)}) collective-permute-start(f32[80,128]{1,0:T(8,128)S(1)} %add.15.chip_ref), channel_id=1, source_target_pairs={{0,0},{1,2},{2,1},{3,3},{4,4},{5,6},{6,5},{7,7},{8,8},{9,10},{10,9... | collective-permute-start | bytes 122888 | tf_op jit(solution)/shard_map/ppermute | solution.py:509
  22.7 5.4 %collective-permute-start.6 = (f32[80,128]{1,0:T(8,128)S(1)}, f32[80,128]{1,0:T(8,128)S(1)}, u32[]{:S(2)}, u32[]{:S(2)}) collective-permute-start(f32[80,128]{1,0:T(8,128)S(1)} %add.15.chip_ref), channel_id=1, source_target_pairs={{0,3},{1,1},{2,2},{3,0},{4,7},{5,5},{6,6},{7,4},{8,11},{9,9},{10,1... | collective-permute-start | bytes 122888 | tf_op jit(solution)/shard_map/ppermute | solution.py:510
  25.5 4.8 %copy-start.1 = (bf16[4,64,240]{2,1,0:T(8,128)(2,1)S(1)}, bf16[4,64,240]{2,1,0:T(8,128)(2,1)}, u32[]{:S(2)}) copy-start(bf16[4,64,240]{2,1,0:T(8,128)(2,1)} %constant.46.clone.rows_ref) | copy-start | bytes 368644
  25.6 4.8 %collective-permute-start.7 = (f32[80,128]{1,0:T(8,128)S(1)}, f32[80,128]{1,0:T(8,128)S(1)}, u32[]{:S(2)}, u32[]{:S(2)}) collective-permute-start(f32[80,128]{1,0:T(8,128)S(1)} %add.16.sum_ref), channel_id=1, source_target_pairs={{0,1},{3,2},{4,5},{7,6},{8,9},{11,10},{12,13},{15,14},{16,17},{19,... | collective-permute-start | bytes 122888 | tf_op jit(solution)/shard_map/ppermute | solution.py:425

commit v3 on v2

--- a/solution.py
+++ b/solution.py
@@ -72,6 +72,8 @@
     row_high, row_low = halves(row)
     out = {}
     out["column"] = np.stack([column_high, column_low])
+    waves_only = np.s_[:, np.r_[0:FB, 2 * FB : 3 * FB]]
+    out["waves"] = np.stack([column_high[waves_only], column_low[waves_only]])
     spectrum_rows = []
     rim_rows = []
     halo_rows = []
@@ -122,9 +124,36 @@
     return high, (value - high.astype(F32)).astype(BF)
 
 
-def spectrum_of(mask, column_ref, rows):
+def lanes_and_rows():
+    shape = (FA, 2 * FB)
+    return lax.broadcasted_iota(jnp.int32, shape, 1), lax.broadcasted_iota(jnp.int32, shape, 0)
+
+
+def pack(even, odd):
+    lane, row = lanes_and_rows()
+    packed = jnp.where(lane % FB < HALF, even, pltpu.roll(odd, HALF, 1))
+    for place, value in ((FA - 2, even), (FA - 3, odd)):
+        line = jnp.sum(jnp.where(lane == row, value[:, HALF : HALF + 1], 0.0), axis=0, keepdims=True)
+        packed = jnp.where(row == place, line, packed)
+    return packed
+
+
+def unpack(packed):
+    lane, row = lanes_and_rows()
+    values = []
+    for place, value in ((FA - 2, packed), (FA - 3, pltpu.roll(packed, 2 * FB - HALF, 1))):
+        column = jnp.sum(jnp.where((lane == row) & (row <= HALF), packed[place : place + 1], 0.0), axis=1, keepdims=True)
+        value = jnp.where(lane == HALF, column, jnp.where(lane % FB < HALF, value, 0.0))
+        values.append(jnp.where(row <= HALF, value, 0.0))
+    return values
+
+
+def columns_of(mask, column_ref):
     high, low = split(mask)
-    across = dot(high, column_ref[0]) + dot(low, column_ref[0]) + dot(high, column_ref[1])
+    return dot(high, column_ref[0]) + dot(low, column_ref[0]) + dot(high, column_ref[1])
+
+
+def spectrum_of(across, rows):
     high, low = split(across)
     both = dot(rows, jnp.concatenate([high, high, low], axis=0))
     even = both[:FA, : 2 * FB] - both[FA:, 2 * FB :]
@@ -212,16 +241,34 @@
         copy.wait()
 
 
+def send_rim_kernel(part_ref, theta_hbm, waves_hbm, out_ref, theta_ref, waves_ref, sems):
+    rows = pl.ds(pl.multiple_of(jnp.where(part_of(part_ref) == 0, 0, ROWS - HALO), HALO), HALO)
+    copies = [
+        pltpu.make_async_copy(theta_hbm.at[rows], theta_ref, sems.at[0]),
+        pltpu.make_async_copy(waves_hbm, waves_ref, sems.at[1]),
+    ]
+    for copy in copies:
+        copy.start()
+    copies[0].wait()
+    mask = jnp.tanh(mask_steep * theta_ref[...])
+    copies[1].wait()
+    out_ref[...] = columns_of(mask, waves_ref)
+
+
 def spectrum_kernel(part_ref, theta_ref, column_ref, rows_ref, out_ref):
-    even, odd = spectrum_of(jnp.tanh(mask_steep * theta_ref[...]), column_ref, rows_ref[0])
+    across = columns_of(jnp.tanh(mask_steep * theta_ref[...]), column_ref)
+    even, odd = spectrum_of(across, rows_ref[0])
     out_ref[0] = even
     out_ref[1] = odd
 
 
-def rim_kernel(part_ref, spectrum_ref, rim_ref, column_ref, rows_ref, out_ref):
-    even, odd = spectrum_of(jnp.tanh(mask_steep * rim_ref[...]), column_ref, rows_ref[0])
-    out_ref[0] = even + spectrum_ref[0]
-    out_ref[1] = odd + spectrum_ref[1]
+def rim_kernel(part_ref, spectrum_ref, rim_ref, rows_ref, out_ref):
+    rim = rim_ref[...]
+    turned = pltpu.roll(rim, FB, 1)
+    first = lax.broadcasted_iota(jnp.int32, rim.shape, 1) < FB
+    across = jnp.concatenate([jnp.where(first, rim, turned), jnp.where(first, turned, -rim)], axis=1)
+    even, odd = spectrum_of(across, rows_ref[0])
+    out_ref[0] = pack(even + spectrum_ref[0], odd + spectrum_ref[1])
 
 
 def fields_kernel(
@@ -232,10 +279,8 @@
     local = count // PARTS
     tall = 4 * FA
     each = 2 * local + 1
-    even = mixed_ref[2 * each] + other_ref[2 * each]
-    odd = mixed_ref[2 * each + 1] + other_ref[2 * each + 1]
-    lane = lax.broadcasted_iota(jnp.int32, (FA, 2 * FB), 1)
-    row = lax.broadcasted_iota(jnp.int32, (FA, 2 * FB), 0)
+    even, odd = unpack(mixed_ref[2 * each] + other_ref[2 * each])
+    lane, row = lanes_and_rows()
     zero_lane = (lane == HALF) & (row <= HALF)
     for group in range(PARTS):
         ref = (mixed_ref, other_ref)[group // 2].at[pl.ds(group % 2 * each, each)]
@@ -293,7 +338,7 @@
         total[...] += value
         return carry
 
-    lax.fori_loop(0, CONDS, expose, 0, unroll=8)
+    lax.fori_loop(0, CONDS, expose, 0, unroll=4)
     total[...] = total[...] * (band_weight / (CONDS * CONDS))
 
     def drive(cond, carry):
@@ -310,7 +355,7 @@
             turned[pl.ds(index * 2, 2)] = jnp.stack([back[:, :ROWS], back[:, ROWS:]])
         return carry
 
-    lax.fori_loop(0, CONDS, drive, 0, unroll=8)
+    lax.fori_loop(0, CONDS, drive, 0, unroll=4)
     high, low = split(turned[...].reshape(count * tall, ROWS))
     backs[...] = dot(jnp.concatenate([high, low], axis=1), backward_ref[: 2 * ROWS]) + dot(high, backward_ref[2 * ROWS :])
 
@@ -331,12 +376,11 @@
         he_real, he_imag, ho_real, ho_imag = (kernels_ref[kern, i] for i in range(4))
         sum_even = sum_even + x_real * he_real + x_imag * he_imag - y_real * ho_imag + y_imag * ho_real
         sum_odd = sum_odd + x_real * ho_imag - x_imag * ho_real + y_real * he_real + y_imag * he_imag
-    out_ref[:FA] = sum_even
-    out_ref[FA:] = sum_odd
-
-
-def image_rows(value, rows, turned_ref):
-    high, low = split(value)
+    out_ref[...] = pack(sum_even, sum_odd)
+
+
+def image_rows(packed, rows, turned_ref):
+    high, low = split(jnp.concatenate(unpack(packed), axis=0))
     pair = dot(rows, jnp.concatenate([high, high, low], axis=0))
     count = pair.shape[0] // 2
     high, low = split(jnp.concatenate([pair[:count], pair[count:]], axis=1))
@@ -455,7 +499,19 @@
         ),
         name="open_parts",
     )
-    rim = lax.dynamic_slice_in_dim(theta, jnp.where(part == 0, 0, ROWS - HALO), HALO, axis=0)
+    rim = call(
+        send_rim_kernel,
+        (parts,),
+        tuple(pltpu.with_memory_space_constraint(value, pltpu.HBM) for value in (theta, table["waves"])),
+        [hbm, hbm],
+        floats(HALO, 2 * FB),
+        scratch=(
+            pltpu.VMEM((HALO, TP), F32),
+            pltpu.VMEM(table["waves"].shape, BF),
+            pltpu.SemaphoreType.DMA((2,)),
+        ),
+        name="edge_columns",
+    )
     rim = across(rim, (0, 0), (last, last))
     spectrum = call(
         spectrum_kernel,
@@ -470,9 +526,9 @@
     spectrum = call(
         rim_kernel,
         (parts,),
-        (spectrum, rim, table["column"], table["rim_rows"]),
-        [whole_spec(spectrum), whole_spec(rim), whole_spec(table["column"]), part_spec(table["rim_rows"])],
-        floats(2, FA, 2 * FB),
+        (spectrum, rim, table["rim_rows"]),
+        [whole_spec(spectrum), whole_spec(rim), part_spec(table["rim_rows"])],
+        floats(1, FA, 2 * FB),
         name="add_rim",
     )
     mixed = jnp.concatenate([own, side, spectrum + partner(spectrum, 3)], axis=0)
@@ -490,7 +546,7 @@
             whole_spec(table["row"]),
             whole_spec(table["row_turned"]),
         ],
-        floats(2 * FA, 2 * FB),
+        floats(FA, 2 * FB),
         scratch=(
             pltpu.VMEM((count, 4, FA, 2 * FB), F32),
             pltpu.VMEM((count * 4 * FA, 2 * FB), F32),

time: 31.6 us -> 31.2 us (0.987)
  Pallas kernels: 10.9 us -> 12.1 us
  local copies, waits for them, and re-layouts: 0.91 us -> 0.06 us
  starting transfers between devices: 12.1 us -> 11.4 us
    pallas_call x6 -> x7, Pallas kernels: 10.9 us -> 12.1 us  [call(): pl.pallas_call(kernel, grid_spec=pltpu.PrefetchScalarGridSpec(num_scalar_...]
    dynamic_slice x1 -> x0, local copies, waits for them, and re-layouts: 0.84 us -> none  [shards(): lax.dynamic_slice_in_dim(theta, jnp.where(part == 0, 0, ROWS - HALO), HAL...]
    ppermute x2, starting transfers between devices: 3.66 us -> 2.87 us  [across(): return lax.ppermute(value, ('tile', 'cond'), pairs)]
    ppermute x1, waiting for transfers between devices: 0.15 us -> 0.5 us  [shards(): back = lax.ppermute(chip, 'cond', [(0, last), (1, 1), (2, 2), (last, 0)])]
    ppermute x4, waiting for transfers between devices: 6.02 us -> 5.7 us  [partner(): return lax.ppermute(value, 'cond', [(i, i ^ step) for i in range(PARTS)])]
where the time goes in v3:
time: 31.2 us; the launch traced here: 31 us
  Pallas kernels  12.1 us (39%)
  starting transfers between devices  11.4 us (37%)
  waiting for transfers between devices  7.16 us (23%)
    pallas_call x7, Pallas kernels, call(): pl.pallas_call(kernel, grid_spec=pltpu.PrefetchScalarGridSpec(num_scalar_...  12.1 us
    ppermute x4, waiting for transfers between devices, partner(): return lax.ppermute(value, 'cond', [(i, i ^ step) for i in range(PARTS)])  5.7 us
    ppermute x4, starting transfers between devices, partner(): return lax.ppermute(value, 'cond', [(i, i ^ step) for i in range(PARTS)])  4.9 us
    ppermute x1, starting transfers between devices, shards(): back = lax.ppermute(chip, 'cond', [(0, last), (1, 1), (2, 2), (last, 0)])  2.98 us
    ppermute x2, starting transfers between devices, across(): return lax.ppermute(value, ('tile', 'cond'), pairs)  2.87 us
    ppermute x2, waiting for transfers between devices, across(): return lax.ppermute(value, ('tile', 'cond'), pairs)  0.96 us
    ppermute x1, starting transfers between devices, shards(): lax.ppermute(chip, 'cond', [(0, 0), (1, 2), (2, 1), (last, last)])  0.65 us
  transfers between devices with their start and end apart: 8, of which 5 were waited for; matrix products, arithmetic and copies ran while one was open for 0% of the time, Pallas kernels for 12%

profile of v3, /device:TPU:0, one launch (start us, length us, event | category | flops | bytes accessed | tf_op | source)
XLA Modules:
  0.0 31.0 jit_solution(13261691279602477184)
XLA Ops:
  0.0 1.2 %edge_columns.1 = f32[32,128]{1,0:T(8,128)S(1)} custom-call(s32[1]{0:T(128)} %bitcast.part_ref, f32[128,512]{1,0:T(8,128)} %theta_ref.3, bf16[2,512,128]{2,1,0:T(8,128)(2,1)} %constant.41.clone.waves_hbm), custom_call_target="tpu_custom_call" | custom-call | flops 268435456 | bytes 1048576 | tf_op jit(solution)/shard_map/edge_columns/pallas_call | solution.py:429
  1.2 1.3 %collective-permute-start.1 = (f32[32,128]{1,0:T(8,128)S(1)}, f32[32,128]{1,0:T(8,128)S(1)}, u32[]{:S(2)}, u32[]{:S(2)}) collective-permute-start(f32[32,128]{1,0:T(8,128)S(1)} %edge_columns.1), channel_id=1, source_target_pairs={{4,0},{8,4},{12,8},{16,12},{20,16},{24,20},{28,24},{3,7},{7,11},{1... | collective-permute-start | bytes 49160 | tf_op jit(solution)/shard_map/ppermute | solution.py:469
  2.5 0.0 copy-start.3
  2.5 0.0 copy-start.5
  2.5 0.0 copy-start.7
  2.5 1.7 %open_parts.1 = (f32[9,40,128]{2,1,0:T(8,128)S(1)}, f32[8,128]{1,0:T(8,128)S(1)}, bf16[384,256]{1,0:T(8,128)(2,1)S(1)}, bf16[384,256]{1,0:T(8,128)(2,1)S(1)}) custom-call(s32[1]{0:T(128)} %bitcast.part_ref, f32[2,65,2,65]{3,2,1,0:T(2,128)} %bitcast.3, f32[2,65,2,65]{3,2,1,0:T(2,128)} %bitcast.4, f32[2]{0:T(128)} %thresholds_hbm.1, s32[8]{0:T(128)} %weights_hbm.1, ...), custom_call_target="tpu_custom_call" | custom-call | flops 268435456 | bytes 1048576 | tf_op jit(solution)/shard_map/open_parts/pallas_call | solution.py:429
  4.2 0.0 copy-start.9
  4.3 4.3 %collective-permute-start = (f32[9,40,128]{2,1,0:T(8,128)S(1)}, f32[9,40,128]{2,1,0:T(8,128)S(1)}, u32[]{:S(2)}, u32[]{:S(2)}) collective-permute-start(f32[9,40,128]{2,1,0:T(8,128)S(1)} %get-tuple-element.12), channel_id=1, source_target_pairs={{0,3},{1,2},{2,1},{3,0},{4,7},{5,6},{6,5},{7,4},{8,11},{9,10},{10,... | collective-permute-start | bytes 552968 | tf_op jit(solution)/shard_map/ppermute | solution.py:472
  8.6 0.0 copy-done.3
  8.6 0.0 copy-done.5
  8.6 0.0 copy-done.7
  8.6 0.5 %own_spectrum.1.spectrum_ref = f32[2,40,128]{2,1,0:T(8,128)S(1)} custom-call(s32[1]{0:T(128)} %bitcast.part_ref, f32[128,512]{1,0:T(8,128)S(1)} %copy-done.3, bf16[2,512,256]{2,1,0:T(8,128)(2,1)S(1)} %copy-done.5, bf16[4,80,384]{2,1,0:T(8,128)(2,1)S(1)} %copy-done.7), custom_call_target="tpu_custom_call" | custom-call | flops 2147483648 | bytes 1048576 | tf_op jit(solution)/shard_map/own_spectrum/pallas_call | solution.py:429
  9.1 0.0 copy-start.2
  9.1 0.0 collective-permute-done.1.rim_ref
  9.1 0.0 copy-done.9
  9.1 0.3 add_rim.1
  9.4 0.3 %collective-permute-start.2 = (f32[1,40,128]{2,1,0:T(8,128)S(1)}, f32[1,40,128]{2,1,0:T(8,128)S(1)}, u32[]{:S(2)}, u32[]{:S(2)}) collective-permute-start(f32[1,40,128]{2,1,0:T(8,128)S(1)} %add_rim.1), channel_id=1, source_target_pairs={{0,3},{1,2},{2,1},{3,0},{4,7},{5,6},{6,5},{7,4},{8,11},{9,10},{10,... | collective-permute-start | bytes 61448 | tf_op jit(solution)/shard_map/ppermute | solution.py:472
  9.7 2.9 %collective-permute-done.2 = f32[1,40,128]{2,1,0:T(8,128)S(1)} collective-permute-done((f32[1,40,128]{2,1,0:T(8,128)S(1)}, f32[1,40,128]{2,1,0:T(8,128)S(1)}, u32[]{:S(2)}, u32[]{:S(2)}) %collective-permute-start.2) | collective-permute-done | bytes 20512 | tf_op jit(solution)/shard_map/ppermute | solution.py:472
  12.7 0.0 copy-start.6
  12.7 0.0 copy-start.8
  12.7 0.0 collective-permute-done
  12.7 0.1 collective-permute-start.3
  12.8 1.7 %collective-permute-done.3.other_ref = f32[19,40,128]{2,1,0:T(8,128)S(1)} collective-permute-done((f32[19,40,128]{2,1,0:T(8,128)S(1)}, f32[19,40,128]{2,1,0:T(8,128)S(1)}, u32[]{:S(2)}, u32[]{:S(2)}) %collective-permute-start.3) | collective-permute-done | bytes 389152 | tf_op jit(solution)/shard_map/ppermute | solution.py:472
  14.5 0.0 copy-done.2
  14.5 0.0 copy-done.6
  14.5 0.0 copy-done.8
  14.5 0.0 copy-start
  14.5 0.0 copy-start.4
  14.5 6.1 %coherent_fields.1 = f32[40,128]{1,0:T(8,128)S(1)} custom-call(s32[1]{0:T(128)} %bitcast.part_ref, f32[19,40,128]{2,1,0:T(8,128)S(1)} %pad_maximum_fusion.mixed_ref, f32[19,40,128]{2,1,0:T(8,128)S(1)} %collective-permute-done.3.other_ref, f32[8,128]{1,0:T(8,128)S(1)} %get-tuple-element.13.shares_ref, s32[512,512]{1,0:T(8,128)S(1)} %copy-done.2, ...), custom_call_target="tpu_custom_call" | custom-call | flops 8589934592 | bytes 1048576 | tf_op jit(solution)/shard_map/coherent_fields/pallas_call | solution.py:429
  20.7 0.2 collective-permute-start.4
  20.8 1.1 %collective-permute-done.4 = f32[40,128]{1,0:T(8,128)S(1)} collective-permute-done((f32[40,128]{1,0:T(8,128)S(1)}, f32[40,128]{1,0:T(8,128)S(1)}, u32[]{:S(2)}, u32[]{:S(2)}) %collective-permute-start.4) | collective-permute-done | bytes 20512 | tf_op jit(solution)/shard_map/ppermute | solution.py:472
  21.9 0.7 %collective-permute-start.5 = (f32[40,128]{1,0:T(8,128)S(1)}, f32[40,128]{1,0:T(8,128)S(1)}, u32[]{:S(2)}, u32[]{:S(2)}) collective-permute-start(f32[40,128]{1,0:T(8,128)S(1)} %add.14.chip_ref), channel_id=1, source_target_pairs={{0,0},{1,2},{2,1},{3,3},{4,4},{5,6},{6,5},{7,7},{8,8},{9,10},{10,9... | collective-permute-start | bytes 61448 | tf_op jit(solution)/shard_map/ppermute | solution.py:565
  22.6 3.0 %collective-permute-start.6 = (f32[40,128]{1,0:T(8,128)S(1)}, f32[40,128]{1,0:T(8,128)S(1)}, u32[]{:S(2)}, u32[]{:S(2)}) collective-permute-start(f32[40,128]{1,0:T(8,128)S(1)} %add.14.chip_ref), channel_id=1, source_target_pairs={{0,3},{1,1},{2,2},{3,0},{4,7},{5,5},{6,6},{7,4},{8,11},{9,9},{10,1... | collective-permute-start | bytes 61448 | tf_op jit(solution)/shard_map/ppermute | solution.py:566
  25.6 0.0 collective-permute-done.5
  25.6 0.0 copy-start.1
  25.6 1.6 %collective-permute-start.7 = (f32[40,128]{1,0:T(8,128)S(1)}, f32[40,128]{1,0:T(8,128)S(1)}, u32[]{:S(2)}, u32[]{:S(2)}) collective-permute-start(f32[40,128]{1,0:T(8,128)S(1)} %add.15.sum_ref), channel_id=1, source_target_pairs={{0,1},{3,2},{4,5},{7,6},{8,9},{11,10},{12,13},{15,14},{16,17},{19,... | collective-permute-start | bytes 61448 | tf_op jit(solution)/shard_map/ppermute | solution.py:469
  27.2 0.5 %collective-permute-done.6.back_ref = f32[40,128]{1,0:T(8,128)S(1)} collective-permute-done((f32[40,128]{1,0:T(8,128)S(1)}, f32[40,128]{1,0:T(8,128)S(1)}, u32[]{:S(2)}, u32[]{:S(2)}) %collective-permute-start.6) | collective-permute-done | bytes 20512 | tf_op jit(solution)/shard_map/ppermute | solution.py:566
  27.7 0.0 copy-done
  27.7 0.0 copy-done.4
  27.7 1.3 %own_gradient.1 = (f32[128,512]{1,0:T(8,128)}, f32[32,512]{1,0:T(8,128)S(1)}, f32[32,512]{1,0:T(8,128)S(1)}) custom-call(s32[1]{0:T(128)} %bitcast.part_ref, f32[128,512]{1,0:T(8,128)S(1)} %copy-done.3, f32[40,128]{1,0:T(8,128)S(1)} %add.15.sum_ref, f32[40,128]{1,0:T(8,128)S(1)} %add.14.chip_ref, f32[40,128]{1,0:T(8,128)S(1)} %collective-permute-done.6.back_ref, ...), custom_call_target="tpu_custom_call" | custom-call | flops 2147483648 | bytes 1048576 | tf_op jit(solution)/shard_map/own_gradient/pallas_call | solution.py:429
  28.9 1.0 %collective-permute-done.7.near_ref = f32[40,128]{1,0:T(8,128)S(1)} collective-permute-done((f32[40,128]{1,0:T(8,128)S(1)}, f32[40,128]{1,0:T(8,128)S(1)}, u32[]{:S(2)}, u32[]{:S(2)}) %collective-permute-start.7) | collective-permute-done | bytes 20512 | tf_op jit(solution)/shard_map/ppermute | solution.py:469
  29.9 0.0 copy-done.1
  29.9 1.1 %edge_gradient.1 = f32[128,512]{1,0:T(8,128)} custom-call(s32[1]{0:T(128)} %bitcast.part_ref, f32[128,512]{1,0:T(8,128)} %get-tuple-element.16.gradient_hbm, f32[32,512]{1,0:T(8,128)S(1)} %get-tuple-element.17.edge_ref, f32[32,512]{1,0:T(8,128)S(1)} %get-tuple-element.18.scale_ref, ...), custom_call_target="tpu_custom_call", output_to_operand_aliasing={{}: (1, {})} | custom-call | flops 268435456 | bytes 1048576 | tf_op jit(solution)/shard_map/edge_gradient/pallas_call | solution.py:429
  (4 shorter events, 0.0 us)
Async XLA Ops:
  1.2 7.9 %collective-permute-start.1 = (f32[32,128]{1,0:T(8,128)S(1)}, f32[32,128]{1,0:T(8,128)S(1)}, u32[]{:S(2)}, u32[]{:S(2)}) collective-permute-start(f32[32,128]{1,0:T(8,128)S(1)} %edge_columns.1), channel_id=1, source_target_pairs={{4,0},{8,4},{12,8},{16,12},{20,16},{24,20},{28,24},{3,7},{7,11},{1... | collective-permute-start | bytes 49160 | tf_op jit(solution)/shard_map/ppermute | solution.py:469
  2.5 6.1 %copy-start.3 = (f32[128,512]{1,0:T(8,128)S(1)}, f32[128,512]{1,0:T(8,128)}, u32[]{:S(2)}) copy-start(f32[128,512]{1,0:T(8,128)} %theta_ref.3) | copy-start | bytes 786436
  2.5 6.0 %copy-start.5 = (bf16[2,512,256]{2,1,0:T(8,128)(2,1)S(1)}, bf16[2,512,256]{2,1,0:T(8,128)(2,1)}, u32[]{:S(2)}) copy-start(bf16[2,512,256]{2,1,0:T(8,128)(2,1)} %constant.40.clone.column_ref) | copy-start | bytes 1572868
  2.5 6.0 %copy-start.7 = (bf16[4,80,384]{2,1,0:T(8,128)(2,1)S(1)}, bf16[4,80,384]{2,1,0:T(8,128)(2,1)}, u32[]{:S(2)}) copy-start(bf16[4,80,384]{2,1,0:T(8,128)(2,1)} %constant.42.clone.rows_ref) | copy-start | bytes 737284
  4.2 4.8 %copy-start.9 = (bf16[4,80,96]{2,1,0:T(8,128)(2,1)S(1)}, bf16[4,80,96]{2,1,0:T(8,128)(2,1)}, u32[]{:S(2)}) copy-start(bf16[4,80,96]{2,1,0:T(8,128)(2,1)} %constant.44.clone.rows_ref) | copy-start | bytes 184324
  4.3 8.4 %collective-permute-start = (f32[9,40,128]{2,1,0:T(8,128)S(1)}, f32[9,40,128]{2,1,0:T(8,128)S(1)}, u32[]{:S(2)}, u32[]{:S(2)}) collective-permute-start(f32[9,40,128]{2,1,0:T(8,128)S(1)} %get-tuple-element.12), channel_id=1, source_target_pairs={{0,3},{1,2},{2,1},{3,0},{4,7},{5,6},{6,5},{7,4},{8,11},{9,10},{10,... | collective-permute-start | bytes 552968 | tf_op jit(solution)/shard_map/ppermute | solution.py:472
  9.1 5.5 %copy-start.2 = (s32[512,512]{1,0:T(8,128)S(1)}, s32[512,512]{1,0:T(8,128)}, u32[]{:S(2)}) copy-start(s32[512,512]{1,0:T(8,128)} %target_ref.1) | copy-start | bytes 3145732
  9.4 3.3 %collective-permute-start.2 = (f32[1,40,128]{2,1,0:T(8,128)S(1)}, f32[1,40,128]{2,1,0:T(8,128)S(1)}, u32[]{:S(2)}, u32[]{:S(2)}) collective-permute-start(f32[1,40,128]{2,1,0:T(8,128)S(1)} %add_rim.1), channel_id=1, source_target_pairs={{0,3},{1,2},{2,1},{3,0},{4,7},{5,6},{6,5},{7,4},{8,11},{9,10},{10,... | collective-permute-start | bytes 61448 | tf_op jit(solution)/shard_map/ppermute | solution.py:472
  12.7 1.8 %copy-start.6 = (bf16[512,240]{1,0:T(8,128)(2,1)S(1)}, bf16[512,240]{1,0:T(8,128)(2,1)}, u32[]{:S(2)}) copy-start(bf16[512,240]{1,0:T(8,128)(2,1)} %constant.49.clone.row_ref) | copy-start | bytes 737284
  12.7 1.8 %copy-start.8 = (bf16[160,512]{1,0:T(8,128)(2,1)S(1)}, bf16[160,512]{1,0:T(8,128)(2,1)}, u32[]{:S(2)}) copy-start(bf16[160,512]{1,0:T(8,128)(2,1)} %constant.50.clone.row_turned_ref) | copy-start | bytes 491524
  12.7 1.8 %collective-permute-start.3 = (f32[19,40,128]{2,1,0:T(8,128)S(1)}, f32[19,40,128]{2,1,0:T(8,128)S(1)}, u32[]{:S(2)}, u32[]{:S(2)}) collective-permute-start(f32[19,40,128]{2,1,0:T(8,128)S(1)} %pad_maximum_fusion.mixed_ref), channel_id=1, source_target_pairs={{0,1},{1,0},{2,3},{3,2},{4,5},{5,4},{6,7},{7,6},{8,9},{9,8},{10,11... | collective-permute-start | bytes 1167368 | tf_op jit(solution)/shard_map/ppermute | solution.py:472
  14.5 13.2 %copy-start = (bf16[2,256,512]{2,1,0:T(8,128)(2,1)S(1)}, bf16[2,256,512]{2,1,0:T(8,128)(2,1)}, u32[]{:S(2)}) copy-start(bf16[2,256,512]{2,1,0:T(8,128)(2,1)} %constant.48.clone.turned_ref) | copy-start | bytes 1572868
  14.5 13.2 %copy-start.4 = (bf16[4,256,240]{2,1,0:T(8,128)(2,1)S(1)}, bf16[4,256,240]{2,1,0:T(8,128)(2,1)}, u32[]{:S(2)}) copy-start(bf16[4,256,240]{2,1,0:T(8,128)(2,1)} %constant.43.clone.rows_ref) | copy-start | bytes 1474564
  20.7 1.3 %collective-permute-start.4 = (f32[40,128]{1,0:T(8,128)S(1)}, f32[40,128]{1,0:T(8,128)S(1)}, u32[]{:S(2)}, u32[]{:S(2)}) collective-permute-start(f32[40,128]{1,0:T(8,128)S(1)} %coherent_fields.1), channel_id=1, source_target_pairs={{0,1},{1,0},{2,3},{3,2},{4,5},{5,4},{6,7},{7,6},{8,9},{9,8},{10,11... | collective-permute-start | bytes 61448 | tf_op jit(solution)/shard_map/ppermute | solution.py:472
  21.9 3.7 %collective-permute-start.5 = (f32[40,128]{1,0:T(8,128)S(1)}, f32[40,128]{1,0:T(8,128)S(1)}, u32[]{:S(2)}, u32[]{:S(2)}) collective-permute-start(f32[40,128]{1,0:T(8,128)S(1)} %add.14.chip_ref), channel_id=1, source_target_pairs={{0,0},{1,2},{2,1},{3,3},{4,4},{5,6},{6,5},{7,7},{8,8},{9,10},{10,9... | collective-permute-start | bytes 61448 | tf_op jit(solution)/shard_map/ppermute | solution.py:565
  22.6 5.1 %collective-permute-start.6 = (f32[40,128]{1,0:T(8,128)S(1)}, f32[40,128]{1,0:T(8,128)S(1)}, u32[]{:S(2)}, u32[]{:S(2)}) collective-permute-start(f32[40,128]{1,0:T(8,128)S(1)} %add.14.chip_ref), channel_id=1, source_target_pairs={{0,3},{1,1},{2,2},{3,0},{4,7},{5,5},{6,6},{7,4},{8,11},{9,9},{10,1... | collective-permute-start | bytes 61448 | tf_op jit(solution)/shard_map/ppermute | solution.py:566
  25.6 4.3 %copy-start.1 = (bf16[4,64,240]{2,1,0:T(8,128)(2,1)S(1)}, bf16[4,64,240]{2,1,0:T(8,128)(2,1)}, u32[]{:S(2)}) copy-start(bf16[4,64,240]{2,1,0:T(8,128)(2,1)} %constant.45.clone.rows_ref) | copy-start | bytes 368644
  25.6 4.3 %collective-permute-start.7 = (f32[40,128]{1,0:T(8,128)S(1)}, f32[40,128]{1,0:T(8,128)S(1)}, u32[]{:S(2)}, u32[]{:S(2)}) collective-permute-start(f32[40,128]{1,0:T(8,128)S(1)} %add.15.sum_ref), channel_id=1, source_target_pairs={{0,1},{3,2},{4,5},{7,6},{8,9},{11,10},{12,13},{15,14},{16,17},{19,... | collective-permute-start | bytes 61448 | tf_op jit(solution)/shard_map/ppermute | solution.py:469

commit v4 on v3

--- a/solution.py
+++ b/solution.py
@@ -20,6 +20,8 @@
 ROWS = TP // PARTS
 FA = 40
 FB = 64
+SPARE = FA - HALF - 1
+SPARE_BLOCKS = -(-(HALF + 1) // SPARE)
 BF = jnp.bfloat16
 F32 = jnp.float32
 
@@ -208,6 +210,7 @@
     keep_bottom = jnp.where((row == 0) & (lane == HALF), 0.0, keep_top)
     first = lane % FB < HALF
     extra = jnp.zeros((FA, 2 * FB), F32)
+    blocks = []
     for kern in range(local_conds * KERNELS):
         arrays = [[], []]
         for piece in range(2):
@@ -219,14 +222,16 @@
             arrays[0].append(top + bottom)
             arrays[1].append(top - bottom)
         for which, (real, imag) in enumerate(arrays):
-            packed = jnp.where(first, real, pltpu.roll(imag, HALF, 1))
-            if which == 0:
-                packed = jnp.where(row == FA - 1, thresholds_ref[kern // KERNELS], packed)
-            out_ref[kern * 2 + which] = packed
+            blocks.append(jnp.where(first, real, pltpu.roll(imag, HALF, 1)))
             for piece, value in enumerate((real, imag)):
                 place = kern * 4 + which * 2 + piece
                 extra = jnp.where(lane == place, pltpu.roll(value, (place - HALF) % (2 * FB), 1), extra)
-    out_ref[local_conds * KERNELS * 2] = extra
+    for i, block in enumerate(blocks):
+        if i < SPARE_BLOCKS:
+            block = jnp.concatenate([block[: HALF + 1], extra[SPARE * i : SPARE * (i + 1)]], axis=0)
+        elif i < SPARE_BLOCKS + local_conds:
+            block = jnp.where(row == FA - 1, thresholds_ref[i - SPARE_BLOCKS], block)
+        out_ref[i] = block
     weight_sum = weights_ref[0]
     for i in range(1, CONDS):
         weight_sum = weight_sum + weights_ref[i]
@@ -273,18 +278,22 @@
 
 def fields_kernel(
     part_ref, mixed_ref, other_ref, shares_ref, target_ref, forward_ref, backward_ref, row_ref,
-    row_turned_ref, out_ref, kernels_ref, lines, folded, amps, tanhs, total, signs, turned, backs,
+    row_turned_ref, out_ref, kernels_ref, levels_ref, lines, folded, amps, tanhs, total, signs, turned, backs,
 ):
     count = kernels_ref.shape[0]
     local = count // PARTS
     tall = 4 * FA
-    each = 2 * local + 1
+    each = 2 * local
     even, odd = unpack(mixed_ref[2 * each] + other_ref[2 * each])
     lane, row = lanes_and_rows()
     zero_lane = (lane == HALF) & (row <= HALF)
     for group in range(PARTS):
         ref = (mixed_ref, other_ref)[group // 2].at[pl.ds(group % 2 * each, each)]
-        extra = ref[2 * local]
+        extra = [ref[i][HALF + 1 :] for i in range(SPARE_BLOCKS)]
+        extra = jnp.concatenate(extra + [jnp.zeros((FA - SPARE * SPARE_BLOCKS, 2 * FB), F32)], axis=0)
+        for i in range(CONDS // PARTS):
+            place = group * (CONDS // PARTS) + i
+            levels_ref[place : place + 1] = ref[SPARE_BLOCKS + i][FA - 1 :]
         for kern in range(local):
             values = []
             for which in range(2):
@@ -332,7 +341,7 @@
             amps[index] = amp
             power = amp[:, :ROWS] * amp[:, :ROWS] + amp[:, ROWS:] * amp[:, ROWS:]
             intensity = power if intensity is None else intensity + power
-        level = kernels_ref[cond * KERNELS, 0, FA - 1 :, :]
+        level = levels_ref[pl.ds(cond, 1), :]
         value = jnp.tanh((0.5 * resist_steep) * (intensity - level))
         tanhs[cond] = value
         total[...] += value
@@ -391,13 +400,11 @@
     return pl.multiple_of(jnp.where(part_of(part_ref) == PARTS - 1, ROWS - HALO, 0), HALO)
 
 
-def gradient_kernel(part_ref, theta_ref, sum_ref, chip_ref, back_ref, turned_ref, rows_ref, out_ref, edge_ref, scale_ref):
+def gradient_kernel(part_ref, theta_ref, sum_ref, turned_ref, rows_ref, out_ref, edge_ref, scale_ref):
     part = part_of(part_ref)
-    middle = (part == 1) | (part == 2)
     mask = jnp.tanh(mask_steep * theta_ref[...])
     scale = mask_steep * (1.0 - mask * mask)
-    mine = jnp.where(middle, sum_ref[...], chip_ref[...] + back_ref[...])
-    gradient = image_rows(mine, rows_ref[0], turned_ref) * scale
+    gradient = image_rows(sum_ref[...], rows_ref[0], turned_ref) * scale
     out_ref[...] = gradient
     last = part == PARTS - 1
     edge_ref[...] = jnp.where(last, gradient[ROWS - HALO :], gradient[:HALO])
@@ -484,7 +491,7 @@
         ),
         [hbm] * 6,
         [
-            floats(2 * local + 1, FA, 2 * FB),
+            floats(2 * local, FA, 2 * FB),
             floats(CONDS, ROWS),
             jax.ShapeDtypeStruct(table["forward"].shape[1:], BF),
             jax.ShapeDtypeStruct(table["backward"].shape[1:], BF),
@@ -549,6 +556,7 @@
         floats(FA, 2 * FB),
         scratch=(
             pltpu.VMEM((count, 4, FA, 2 * FB), F32),
+            pltpu.VMEM((CONDS, ROWS), F32),
             pltpu.VMEM((count * 4 * FA, 2 * FB), F32),
             pltpu.VMEM((count, 6 * FA, 2 * ROWS), BF),
             pltpu.VMEM((count, TP, 2 * ROWS), F32),
@@ -561,19 +569,16 @@
         name="coherent_fields",
         flops=1 << 33,
     )
-    chip = adjoint + partner(adjoint, 1)
-    adjoint = chip + lax.ppermute(chip, "cond", [(0, 0), (1, 2), (2, 1), (last, last)])
-    back = lax.ppermute(chip, "cond", [(0, last), (1, 1), (2, 2), (last, 0)])
+    adjoint = adjoint + partner(adjoint, 1)
+    adjoint = adjoint + partner(adjoint, 3)
     near = across(adjoint, (2, last), (1, 0), within=[(0, 1), (last, 2)])
     gradient, edge, scale = call(
         gradient_kernel,
         (parts,),
-        (theta, adjoint, chip, back, table["turned"], table["own_rows"]),
+        (theta, adjoint, table["turned"], table["own_rows"]),
         [
             whole_spec(theta),
             whole_spec(adjoint),
-            whole_spec(chip),
-            whole_spec(back),
             whole_spec(table["turned"]),
             part_spec(table["own_rows"]),
         ],

time: 31.2 us -> 30.2 us (0.968)
  starting transfers between devices: 11.4 us -> 7.23 us
  waiting for transfers between devices: 7.16 us -> 10.3 us
    ppermute x2 -> x0, starting transfers between devices: 3.63 us -> none  [the longest x1 2.98 us: shards(): back = lax.ppermute(chip, 'cond', [(0, last), (1, 1), (2, 2), (last, 0)])]
    ppermute x4 -> x5, waiting for transfers between devices: 5.7 us -> 7.98 us  [partner(): return lax.ppermute(value, 'cond', [(i, i ^ step) for i in range(PARTS)])]
    ppermute x2, starting transfers between devices: 2.87 us -> 1.46 us  [across(): return lax.ppermute(value, ('tile', 'cond'), pairs)]
    ppermute x2, waiting for transfers between devices: 0.96 us -> 2.37 us  [across(): return lax.ppermute(value, ('tile', 'cond'), pairs)]
    ppermute x4 -> x5, starting transfers between devices: 4.9 us -> 5.77 us  [partner(): return lax.ppermute(value, 'cond', [(i, i ^ step) for i in range(PARTS)])]
    ppermute x2 -> x0, waiting for transfers between devices: 0.5 us -> none  [the longest x1 0.5 us: shards(): back = lax.ppermute(chip, 'cond', [(0, last), (1, 1), (2, 2), (last, 0)])]
  transfers between devices with their start and end apart: 8 -> 7, of which waited for: 5 -> 5; matrix products, arithmetic and copies ran while one was open for 0% -> 0% of each run, Pallas kernels for 12% -> 12%
where the time goes in v4:
time: 30.2 us; the launch traced here: 30.1 us
  Pallas kernels  12.2 us (40%)
  waiting for transfers between devices  10.3 us (34%)
  starting transfers between devices  7.23 us (24%)
    pallas_call x7, Pallas kernels, call(): pl.pallas_call(kernel, grid_spec=pltpu.PrefetchScalarGridSpec(num_scalar_...  12.2 us
    ppermute x5, waiting for transfers between devices, partner(): return lax.ppermute(value, 'cond', [(i, i ^ step) for i in range(PARTS)])  7.98 us
    ppermute x5, starting transfers between devices, partner(): return lax.ppermute(value, 'cond', [(i, i ^ step) for i in range(PARTS)])  5.77 us
    ppermute x2, waiting for transfers between devices, across(): return lax.ppermute(value, ('tile', 'cond'), pairs)  2.37 us
    ppermute x2, starting transfers between devices, across(): return lax.ppermute(value, ('tile', 'cond'), pairs)  1.46 us
  transfers between devices with their start and end apart: 7, of which 5 were waited for; matrix products, arithmetic and copies ran while one was open for 0% of the time, Pallas kernels for 12%

profile of v4, /device:TPU:0, one launch (start us, length us, event | category | flops | bytes accessed | tf_op | source)
XLA Modules:
  0.0 30.1 jit_solution(5752827588212453601)
XLA Ops:
  0.0 1.2 %edge_columns.1 = f32[32,128]{1,0:T(8,128)S(1)} custom-call(s32[1]{0:T(128)} %bitcast.part_ref, f32[128,512]{1,0:T(8,128)} %theta_ref.3, bf16[2,512,128]{2,1,0:T(8,128)(2,1)} %constant.41.clone.waves_hbm), custom_call_target="tpu_custom_call" | custom-call | flops 268435456 | bytes 1048576 | tf_op jit(solution)/shard_map/edge_columns/pallas_call | solution.py:436
  1.2 1.3 %collective-permute-start.1 = (f32[32,128]{1,0:T(8,128)S(1)}, f32[32,128]{1,0:T(8,128)S(1)}, u32[]{:S(2)}, u32[]{:S(2)}) collective-permute-start(f32[32,128]{1,0:T(8,128)S(1)} %edge_columns.1), channel_id=1, source_target_pairs={{4,0},{8,4},{12,8},{16,12},{20,16},{24,20},{28,24},{3,7},{7,11},{1... | collective-permute-start | bytes 49160 | tf_op jit(solution)/shard_map/ppermute | solution.py:476
  2.5 0.0 copy-start.3
  2.5 0.0 copy-start.5
  2.5 0.0 copy-start.7
  2.5 1.7 %open_parts.1 = (f32[8,40,128]{2,1,0:T(8,128)S(1)}, f32[8,128]{1,0:T(8,128)S(1)}, bf16[384,256]{1,0:T(8,128)(2,1)S(1)}, bf16[384,256]{1,0:T(8,128)(2,1)S(1)}) custom-call(s32[1]{0:T(128)} %bitcast.part_ref, f32[2,65,2,65]{3,2,1,0:T(2,128)} %bitcast.3, f32[2,65,2,65]{3,2,1,0:T(2,128)} %bitcast.4, f32[2]{0:T(128)} %thresholds_hbm.1, s32[8]{0:T(128)} %weights_hbm.1, ...), custom_call_target="tpu_custom_call" | custom-call | flops 268435456 | bytes 1048576 | tf_op jit(solution)/shard_map/open_parts/pallas_call | solution.py:436
  4.2 0.0 copy-start.9
  4.3 4.3 %collective-permute-start = (f32[8,40,128]{2,1,0:T(8,128)S(1)}, f32[8,40,128]{2,1,0:T(8,128)S(1)}, u32[]{:S(2)}, u32[]{:S(2)}) collective-permute-start(f32[8,40,128]{2,1,0:T(8,128)S(1)} %get-tuple-element.12), channel_id=1, source_target_pairs={{0,3},{1,2},{2,1},{3,0},{4,7},{5,6},{6,5},{7,4},{8,11},{9,10},{10,... | collective-permute-start | bytes 491528 | tf_op jit(solution)/shard_map/ppermute | solution.py:479
  8.6 0.0 copy-done.3
  8.6 0.0 copy-done.5
  8.6 0.0 copy-done.7
  8.6 0.5 %own_spectrum.1.spectrum_ref = f32[2,40,128]{2,1,0:T(8,128)S(1)} custom-call(s32[1]{0:T(128)} %bitcast.part_ref, f32[128,512]{1,0:T(8,128)S(1)} %copy-done.3, bf16[2,512,256]{2,1,0:T(8,128)(2,1)S(1)} %copy-done.5, bf16[4,80,384]{2,1,0:T(8,128)(2,1)S(1)} %copy-done.7), custom_call_target="tpu_custom_call" | custom-call | flops 2147483648 | bytes 1048576 | tf_op jit(solution)/shard_map/own_spectrum/pallas_call | solution.py:436
  9.1 0.0 copy-start.2
  9.1 0.0 collective-permute-done.1.rim_ref
  9.1 0.0 copy-done.9
  9.1 0.3 add_rim.1
  9.4 0.3 %collective-permute-start.2 = (f32[1,40,128]{2,1,0:T(8,128)S(1)}, f32[1,40,128]{2,1,0:T(8,128)S(1)}, u32[]{:S(2)}, u32[]{:S(2)}) collective-permute-start(f32[1,40,128]{2,1,0:T(8,128)S(1)} %add_rim.1), channel_id=1, source_target_pairs={{0,3},{1,2},{2,1},{3,0},{4,7},{5,6},{6,5},{7,4},{8,11},{9,10},{10,... | collective-permute-start | bytes 61448 | tf_op jit(solution)/shard_map/ppermute | solution.py:479
  9.7 2.9 %collective-permute-done.2 = f32[1,40,128]{2,1,0:T(8,128)S(1)} collective-permute-done((f32[1,40,128]{2,1,0:T(8,128)S(1)}, f32[1,40,128]{2,1,0:T(8,128)S(1)}, u32[]{:S(2)}, u32[]{:S(2)}) %collective-permute-start.2) | collective-permute-done | bytes 20512 | tf_op jit(solution)/shard_map/ppermute | solution.py:479
  12.7 0.0 copy-start.6
  12.7 0.0 copy-start.8
  12.7 0.0 collective-permute-done
  12.7 0.1 collective-permute-start.3
  12.8 1.6 %collective-permute-done.3.other_ref = f32[17,40,128]{2,1,0:T(8,128)S(1)} collective-permute-done((f32[17,40,128]{2,1,0:T(8,128)S(1)}, f32[17,40,128]{2,1,0:T(8,128)S(1)}, u32[]{:S(2)}, u32[]{:S(2)}) %collective-permute-start.3) | collective-permute-done | bytes 348192 | tf_op jit(solution)/shard_map/ppermute | solution.py:479
  14.4 0.0 copy-done.2
  14.4 0.0 copy-done.6
  14.4 0.0 copy-done.8
  14.5 0.0 copy-start
  14.5 0.0 copy-start.4
  14.5 6.2 %coherent_fields.1 = f32[40,128]{1,0:T(8,128)S(1)} custom-call(s32[1]{0:T(128)} %bitcast.part_ref, f32[17,40,128]{2,1,0:T(8,128)S(1)} %pad_maximum_fusion.mixed_ref, f32[17,40,128]{2,1,0:T(8,128)S(1)} %collective-permute-done.3.other_ref, f32[8,128]{1,0:T(8,128)S(1)} %get-tuple-element.13.shares_ref, s32[512,512]{1,0:T(8,128)S(1)} %copy-done.2, ...), custom_call_target="tpu_custom_call" | custom-call | flops 8589934592 | bytes 1048576 | tf_op jit(solution)/shard_map/coherent_fields/pallas_call | solution.py:436
  20.7 0.2 collective-permute-start.4
  20.9 1.1 %collective-permute-done.4 = f32[40,128]{1,0:T(8,128)S(1)} collective-permute-done((f32[40,128]{1,0:T(8,128)S(1)}, f32[40,128]{1,0:T(8,128)S(1)}, u32[]{:S(2)}, u32[]{:S(2)}) %collective-permute-start.4) | collective-permute-done | bytes 20512 | tf_op jit(solution)/shard_map/ppermute | solution.py:479
  21.9 0.9 %collective-permute-start.5 = (f32[40,128]{1,0:T(8,128)S(1)}, f32[40,128]{1,0:T(8,128)S(1)}, u32[]{:S(2)}, u32[]{:S(2)}) collective-permute-start(f32[40,128]{1,0:T(8,128)S(1)} %add.14), channel_id=1, source_target_pairs={{0,3},{1,2},{2,1},{3,0},{4,7},{5,6},{6,5},{7,4},{8,11},{9,10},{10,... | collective-permute-start | bytes 61448 | tf_op jit(solution)/shard_map/ppermute | solution.py:479
  22.8 2.3 %collective-permute-done.5 = f32[40,128]{1,0:T(8,128)S(1)} collective-permute-done((f32[40,128]{1,0:T(8,128)S(1)}, f32[40,128]{1,0:T(8,128)S(1)}, u32[]{:S(2)}, u32[]{:S(2)}) %collective-permute-start.5) | collective-permute-done | bytes 20512 | tf_op jit(solution)/shard_map/ppermute | solution.py:479
  25.1 0.0 copy-start.1
  25.1 0.2 collective-permute-start.6
  25.3 0.0 copy-done
  25.3 0.0 copy-done.4
  25.3 1.2 %own_gradient.1 = (f32[128,512]{1,0:T(8,128)}, f32[32,512]{1,0:T(8,128)S(1)}, f32[32,512]{1,0:T(8,128)S(1)}) custom-call(s32[1]{0:T(128)} %bitcast.part_ref, f32[128,512]{1,0:T(8,128)S(1)} %copy-done.3, f32[40,128]{1,0:T(8,128)S(1)} %add.15.sum_ref, bf16[2,256,512]{2,1,0:T(8,128)(2,1)S(1)} %copy-done, bf16[4,256,240]{2,1,0:T(8,128)(2,1)S(1)} %copy-done.4), custom_call_target="tpu_custom_call" | custom-call | flops 2147483648 | bytes 1048576 | tf_op jit(solution)/shard_map/own_gradient/pallas_call | solution.py:436
  26.6 2.4 %collective-permute-done.6.near_ref = f32[40,128]{1,0:T(8,128)S(1)} collective-permute-done((f32[40,128]{1,0:T(8,128)S(1)}, f32[40,128]{1,0:T(8,128)S(1)}, u32[]{:S(2)}, u32[]{:S(2)}) %collective-permute-start.6) | collective-permute-done | bytes 20512 | tf_op jit(solution)/shard_map/ppermute | solution.py:476
  28.9 0.0 copy-done.1
  28.9 1.1 %edge_gradient.1 = f32[128,512]{1,0:T(8,128)} custom-call(s32[1]{0:T(128)} %bitcast.part_ref, f32[128,512]{1,0:T(8,128)} %get-tuple-element.16.gradient_hbm, f32[32,512]{1,0:T(8,128)S(1)} %get-tuple-element.17.edge_ref, f32[32,512]{1,0:T(8,128)S(1)} %get-tuple-element.18.scale_ref, ...), custom_call_target="tpu_custom_call", output_to_operand_aliasing={{}: (1, {})} | custom-call | flops 268435456 | bytes 1048576 | tf_op jit(solution)/shard_map/edge_gradient/pallas_call | solution.py:436
  (4 shorter events, 0.0 us)
Async XLA Ops:
  1.2 7.9 %collective-permute-start.1 = (f32[32,128]{1,0:T(8,128)S(1)}, f32[32,128]{1,0:T(8,128)S(1)}, u32[]{:S(2)}, u32[]{:S(2)}) collective-permute-start(f32[32,128]{1,0:T(8,128)S(1)} %edge_columns.1), channel_id=1, source_target_pairs={{4,0},{8,4},{12,8},{16,12},{20,16},{24,20},{28,24},{3,7},{7,11},{1... | collective-permute-start | bytes 49160 | tf_op jit(solution)/shard_map/ppermute | solution.py:476
  2.5 6.1 %copy-start.3 = (f32[128,512]{1,0:T(8,128)S(1)}, f32[128,512]{1,0:T(8,128)}, u32[]{:S(2)}) copy-start(f32[128,512]{1,0:T(8,128)} %theta_ref.3) | copy-start | bytes 786436
  2.5 6.0 %copy-start.5 = (bf16[2,512,256]{2,1,0:T(8,128)(2,1)S(1)}, bf16[2,512,256]{2,1,0:T(8,128)(2,1)}, u32[]{:S(2)}) copy-start(bf16[2,512,256]{2,1,0:T(8,128)(2,1)} %constant.40.clone.column_ref) | copy-start | bytes 1572868
  2.5 6.0 %copy-start.7 = (bf16[4,80,384]{2,1,0:T(8,128)(2,1)S(1)}, bf16[4,80,384]{2,1,0:T(8,128)(2,1)}, u32[]{:S(2)}) copy-start(bf16[4,80,384]{2,1,0:T(8,128)(2,1)} %constant.42.clone.rows_ref) | copy-start | bytes 737284
  4.2 4.8 %copy-start.9 = (bf16[4,80,96]{2,1,0:T(8,128)(2,1)S(1)}, bf16[4,80,96]{2,1,0:T(8,128)(2,1)}, u32[]{:S(2)}) copy-start(bf16[4,80,96]{2,1,0:T(8,128)(2,1)} %constant.44.clone.rows_ref) | copy-start | bytes 184324
  4.3 8.4 %collective-permute-start = (f32[8,40,128]{2,1,0:T(8,128)S(1)}, f32[8,40,128]{2,1,0:T(8,128)S(1)}, u32[]{:S(2)}, u32[]{:S(2)}) collective-permute-start(f32[8,40,128]{2,1,0:T(8,128)S(1)} %get-tuple-element.12), channel_id=1, source_target_pairs={{0,3},{1,2},{2,1},{3,0},{4,7},{5,6},{6,5},{7,4},{8,11},{9,10},{10,... | collective-permute-start | bytes 491528 | tf_op jit(solution)/shard_map/ppermute | solution.py:479
  9.1 5.4 %copy-start.2 = (s32[512,512]{1,0:T(8,128)S(1)}, s32[512,512]{1,0:T(8,128)}, u32[]{:S(2)}) copy-start(s32[512,512]{1,0:T(8,128)} %target_ref.1) | copy-start | bytes 3145732
  9.4 3.3 %collective-permute-start.2 = (f32[1,40,128]{2,1,0:T(8,128)S(1)}, f32[1,40,128]{2,1,0:T(8,128)S(1)}, u32[]{:S(2)}, u32[]{:S(2)}) collective-permute-start(f32[1,40,128]{2,1,0:T(8,128)S(1)} %add_rim.1), channel_id=1, source_target_pairs={{0,3},{1,2},{2,1},{3,0},{4,7},{5,6},{6,5},{7,4},{8,11},{9,10},{10,... | collective-permute-start | bytes 61448 | tf_op jit(solution)/shard_map/ppermute | solution.py:479
  12.7 1.8 %copy-start.6 = (bf16[512,240]{1,0:T(8,128)(2,1)S(1)}, bf16[512,240]{1,0:T(8,128)(2,1)}, u32[]{:S(2)}) copy-start(bf16[512,240]{1,0:T(8,128)(2,1)} %constant.49.clone.row_ref) | copy-start | bytes 737284
  12.7 1.8 %copy-start.8 = (bf16[160,512]{1,0:T(8,128)(2,1)S(1)}, bf16[160,512]{1,0:T(8,128)(2,1)}, u32[]{:S(2)}) copy-start(bf16[160,512]{1,0:T(8,128)(2,1)} %constant.50.clone.row_turned_ref) | copy-start | bytes 491524
  12.7 1.7 %collective-permute-start.3 = (f32[17,40,128]{2,1,0:T(8,128)S(1)}, f32[17,40,128]{2,1,0:T(8,128)S(1)}, u32[]{:S(2)}, u32[]{:S(2)}) collective-permute-start(f32[17,40,128]{2,1,0:T(8,128)S(1)} %pad_maximum_fusion.mixed_ref), channel_id=1, source_target_pairs={{0,1},{1,0},{2,3},{3,2},{4,5},{5,4},{6,7},{7,6},{8,9},{9,8},{10,11... | collective-permute-start | bytes 1044488 | tf_op jit(solution)/shard_map/ppermute | solution.py:479
  14.5 10.9 %copy-start = (bf16[2,256,512]{2,1,0:T(8,128)(2,1)S(1)}, bf16[2,256,512]{2,1,0:T(8,128)(2,1)}, u32[]{:S(2)}) copy-start(bf16[2,256,512]{2,1,0:T(8,128)(2,1)} %constant.48.clone.turned_ref) | copy-start | bytes 1572868
  14.5 10.9 %copy-start.4 = (bf16[4,256,240]{2,1,0:T(8,128)(2,1)S(1)}, bf16[4,256,240]{2,1,0:T(8,128)(2,1)}, u32[]{:S(2)}) copy-start(bf16[4,256,240]{2,1,0:T(8,128)(2,1)} %constant.43.clone.rows_ref) | copy-start | bytes 1474564
  20.7 1.3 %collective-permute-start.4 = (f32[40,128]{1,0:T(8,128)S(1)}, f32[40,128]{1,0:T(8,128)S(1)}, u32[]{:S(2)}, u32[]{:S(2)}) collective-permute-start(f32[40,128]{1,0:T(8,128)S(1)} %coherent_fields.1), channel_id=1, source_target_pairs={{0,1},{1,0},{2,3},{3,2},{4,5},{5,4},{6,7},{7,6},{8,9},{9,8},{10,11... | collective-permute-start | bytes 61448 | tf_op jit(solution)/shard_map/ppermute | solution.py:479
  21.9 3.2 %collective-permute-start.5 = (f32[40,128]{1,0:T(8,128)S(1)}, f32[40,128]{1,0:T(8,128)S(1)}, u32[]{:S(2)}, u32[]{:S(2)}) collective-permute-start(f32[40,128]{1,0:T(8,128)S(1)} %add.14), channel_id=1, source_target_pairs={{0,3},{1,2},{2,1},{3,0},{4,7},{5,6},{6,5},{7,4},{8,11},{9,10},{10,... | collective-permute-start | bytes 61448 | tf_op jit(solution)/shard_map/ppermute | solution.py:479
  25.1 3.8 %copy-start.1 = (bf16[4,64,240]{2,1,0:T(8,128)(2,1)S(1)}, bf16[4,64,240]{2,1,0:T(8,128)(2,1)}, u32[]{:S(2)}) copy-start(bf16[4,64,240]{2,1,0:T(8,128)(2,1)} %constant.45.clone.rows_ref) | copy-start | bytes 368644
  25.1 3.8 %collective-permute-start.6 = (f32[40,128]{1,0:T(8,128)S(1)}, f32[40,128]{1,0:T(8,128)S(1)}, u32[]{:S(2)}, u32[]{:S(2)}) collective-permute-start(f32[40,128]{1,0:T(8,128)S(1)} %add.15.sum_ref), channel_id=1, source_target_pairs={{0,1},{3,2},{4,5},{7,6},{8,9},{11,10},{12,13},{15,14},{16,17},{19,... | collective-permute-start | bytes 61448 | tf_op jit(solution)/shard_map/ppermute | solution.py:476

commit v5 on v4

--- a/solution.py
+++ b/solution.py
@@ -63,13 +63,32 @@
     return table
 
 
+def folded_table(positions):
+    cosine, sine = waves(positions)
+    count = len(positions)
+    table = np.zeros((2, count, 2, 2, 2, HALF))
+    for part in range(2):
+        for block, sign in enumerate((1.0, -1.0)):
+            table[part, :, 0, block, part] = cosine[:, 1:]
+            table[part, :, 1, block, part] = sign * sine[:, 1:]
+    return table.reshape(2 * count, 4 * FB)
+
+
+def forward_table(positions):
+    count = len(positions)
+    table = folded_table(positions).reshape(2, count, 2, 2 * FB).transpose(3, 2, 0, 1).reshape(2 * FB, 4 * count)
+    high, low = halves(table)
+    zeroth = np.zeros((2 * FB, 4, count), ml_dtypes.bfloat16)
+    for lane in range(4):
+        zeroth[lane, lane % 2] = 1
+    return np.concatenate([high, high, low, zeroth.reshape(2 * FB, 4 * count)])
+
+
 @functools.cache
 def tables():
     pixels = np.arange(TP) + HALO
     column = column_table(pixels)
     column_high, column_low = halves(column)
-    turned = np.concatenate([column[:, : 2 * FB].T, column[:, 2 * FB :].T], axis=1)
-    turned_high, turned_low = halves(turned)
     row = row_table(pixels)
     row_high, row_low = halves(row)
     out = {}
@@ -92,11 +111,8 @@
         halo_rows.append(np.concatenate([high, low, high], axis=1))
         high, low = halves(pair_table(own))
         own_rows.append(np.concatenate([high, low, high], axis=1))
-        cols = slice(part * ROWS, (part + 1) * ROWS)
-        high = np.concatenate([turned_high[:, :TP][:, cols], turned_high[:, TP:][:, cols]], axis=1)
-        low = np.concatenate([turned_low[:, :TP][:, cols], turned_low[:, TP:][:, cols]], axis=1)
-        forward.append(np.concatenate([high, high, low]))
-        backward.append(np.concatenate([column_high[cols], column_high[cols], column_low[cols]]))
+        forward.append(forward_table(own))
+        backward.append(np.concatenate(halves(folded_table(own))))
     out["spectrum_rows"] = np.stack(spectrum_rows)
     out["own_rows"] = np.stack(own_rows)
     out["rim_rows"] = np.stack(rim_rows)
@@ -221,10 +237,11 @@
             top = top * keep_top
             arrays[0].append(top + bottom)
             arrays[1].append(top - bottom)
-        for which, (real, imag) in enumerate(arrays):
-            blocks.append(jnp.where(first, real, pltpu.roll(imag, HALF, 1)))
-            for piece, value in enumerate((real, imag)):
-                place = kern * 4 + which * 2 + piece
+        (he_real, he_imag), (ho_real, ho_imag) = arrays
+        for which, pair in enumerate(((he_real, he_imag), (ho_imag, -ho_real))):
+            blocks.append(jnp.where(first, pair[0], pltpu.roll(pair[1], HALF, 1)))
+            for piece, value in enumerate(pair):
+                place = which * FB + kern * 4 + piece
                 extra = jnp.where(lane == place, pltpu.roll(value, (place - HALF) % (2 * FB), 1), extra)
     for i, block in enumerate(blocks):
         if i < SPARE_BLOCKS:
@@ -278,57 +295,63 @@
 
 def fields_kernel(
     part_ref, mixed_ref, other_ref, shares_ref, target_ref, forward_ref, backward_ref, row_ref,
-    row_turned_ref, out_ref, kernels_ref, levels_ref, lines, folded, amps, tanhs, total, signs, turned, backs,
+    row_turned_ref, out_ref, extras_ref, levels_ref, lines, zeroth, folded, amps, tanhs, total, signs, turned,
 ):
-    count = kernels_ref.shape[0]
+    count = folded.shape[0]
     local = count // PARTS
-    tall = 4 * FA
+    tall = 2 * FA
     each = 2 * local
-    even, odd = unpack(mixed_ref[2 * each] + other_ref[2 * each])
     lane, row = lanes_and_rows()
-    zero_lane = (lane == HALF) & (row <= HALF)
+    first = lane % FB < HALF
+    packed = mixed_ref[2 * each] + other_ref[2 * each]
+    even_0, odd_0 = (
+        jnp.sum(jnp.where((lane == row) & (row <= HALF), packed[place : place + 1], 0.0), axis=1, keepdims=True)
+        for place in (FA - 2, FA - 3)
+    )
+    packed = jnp.where(row <= HALF, packed, 0.0)
+    even = jnp.where(first, packed, pltpu.roll(packed, HALF, 1))
+    odd = jnp.where(first, pltpu.roll(packed, 2 * FB - HALF, 1), packed)
+
+    def blocks_of(group):
+        return (mixed_ref, other_ref)[group // 2].at[pl.ds(group % 2 * each, each)]
+
     for group in range(PARTS):
-        ref = (mixed_ref, other_ref)[group // 2].at[pl.ds(group % 2 * each, each)]
+        ref = blocks_of(group)
         extra = [ref[i][HALF + 1 :] for i in range(SPARE_BLOCKS)]
         extra = jnp.concatenate(extra + [jnp.zeros((FA - SPARE * SPARE_BLOCKS, 2 * FB), F32)], axis=0)
+        extra_b = pltpu.roll(extra, FB, 1)
+        extras_ref[group, 0] = extra
+        extras_ref[group, 1] = extra_b
         for i in range(CONDS // PARTS):
             place = group * (CONDS // PARTS) + i
             levels_ref[place : place + 1] = ref[SPARE_BLOCKS + i][FA - 1 :]
+        columns = []
+        for value in (even_0 * extra + odd_0 * extra_b, odd_0 * extra - even_0 * extra_b):
+            high = value.astype(BF).astype(F32)
+            columns.append(jnp.where(lane % 4 < 2, high, pltpu.roll(value - high, 2, 1)))
         for kern in range(local):
-            values = []
-            for which in range(2):
-                packed = ref[2 * kern + which]
-                for part, value in enumerate((packed, pltpu.roll(packed, 2 * FB - HALF, 1))):
-                    place = kern * 4 + which * 2 + part
-                    zeroth = pltpu.roll(extra, (HALF - place) % (2 * FB), 1)
-                    value = jnp.where(zero_lane, zeroth, value)
-                    kernels_ref[group * local + kern, which * 2 + part] = value
-                    values.append(value)
-            he_real, he_imag, ho_real, ho_imag = values
             start = (group * local + kern) * tall
-            for i, value in enumerate(
-                (
-                    even * he_real + odd * ho_imag,
-                    odd * he_real - even * ho_imag,
-                    even * he_imag - odd * ho_real,
-                    odd * he_imag + even * ho_real,
-                )
-            ):
-                lines[start + i * FA : start + (i + 1) * FA] = value
+            a_block, b_block = ref[2 * kern], ref[2 * kern + 1]
+            lines[start : start + FA] = even * a_block + odd * b_block
+            lines[start + FA : start + tall] = odd * a_block - even * b_block
+            for i, value in enumerate(columns):
+                value = pltpu.roll(value, 2 * FB - 4 * kern, 1) if kern else value
+                zeroth[start + FA * i : start + FA * (i + 1)] = value
 
     high, low = split(lines[...])
-    lines_folded = dot(jnp.concatenate([high, low], axis=1), forward_ref[: 4 * FB]) + dot(high, forward_ref[4 * FB :])
+    lines_folded = dot(jnp.concatenate([high, low], axis=1), forward_ref[: 4 * FB])
+    lines_folded += dot(jnp.concatenate([high, zeroth[...].astype(BF)], axis=1), forward_ref[4 * FB :])
     for kern in range(count):
-        parts = []
-        for i in range(2):
-            x_part = lines_folded[tall * kern + 2 * FA * i : tall * kern + 2 * FA * i + FA]
-            y_part = lines_folded[tall * kern + 2 * FA * i + FA : tall * kern + 2 * FA * (i + 1)]
-            parts.append(
-                jnp.concatenate(
-                    [x_part[:, :ROWS] + y_part[:, ROWS:], y_part[:, :ROWS] - x_part[:, ROWS:]], axis=0
-                )
-            )
-        high, low = split(jnp.concatenate(parts, axis=1))
+        x_part = lines_folded[tall * kern : tall * kern + FA]
+        y_part = lines_folded[tall * kern + FA : tall * (kern + 1)]
+        both = jnp.concatenate(
+            [
+                x_part[:, : 2 * ROWS] + y_part[:, 2 * ROWS :],
+                y_part[:, : 2 * ROWS] - x_part[:, 2 * ROWS :],
+            ],
+            axis=0,
+        )
+        high, low = split(both)
         folded[kern] = jnp.concatenate([high, high, low], axis=0)
     total[...] = jnp.zeros_like(total)
     signs[...] = 1.0 - 2.0 * target_ref[...].astype(F32)
@@ -361,31 +384,41 @@
             high, low = split(field * amps[index])
             long = dot(row_turned_ref[...], high)
             back = long[: 2 * FA] + long[2 * FA :] + dot(row_turned_ref[: 2 * FA], low)
-            turned[pl.ds(index * 2, 2)] = jnp.stack([back[:, :ROWS], back[:, ROWS:]])
+            turned[index] = back
         return carry
 
     lax.fori_loop(0, CONDS, drive, 0, unroll=4)
-    high, low = split(turned[...].reshape(count * tall, ROWS))
-    backs[...] = dot(jnp.concatenate([high, low], axis=1), backward_ref[: 2 * ROWS]) + dot(high, backward_ref[2 * ROWS :])
-
+    high, low = split(turned[...].reshape(count * tall, 2 * ROWS))
+    backs = dot(high, backward_ref[: 2 * ROWS]) + dot(low, backward_ref[: 2 * ROWS]) + dot(high, backward_ref[2 * ROWS :])
     sum_even = jnp.zeros((FA, 2 * FB), F32)
     sum_odd = jnp.zeros((FA, 2 * FB), F32)
-    for kern in range(count):
-        grads = []
-        for i in range(2):
-            c_part = backs[tall * kern + 2 * FA * i : tall * kern + 2 * FA * i + FA]
-            s_part = backs[tall * kern + 2 * FA * i + FA : tall * kern + 2 * FA * (i + 1)]
-            grads.append(
-                (
-                    c_part[:, : 2 * FB] - s_part[:, 2 * FB :],
-                    s_part[:, : 2 * FB] + c_part[:, 2 * FB :],
-                )
-            )
-        (x_real, y_real), (x_imag, y_imag) = grads
-        he_real, he_imag, ho_real, ho_imag = (kernels_ref[kern, i] for i in range(4))
-        sum_even = sum_even + x_real * he_real + x_imag * he_imag - y_real * ho_imag + y_imag * ho_real
-        sum_odd = sum_odd + x_real * ho_imag - x_imag * ho_real + y_real * he_real + y_imag * he_imag
-    out_ref[...] = pack(sum_even, sum_odd)
+    lines_even = jnp.zeros((FA, 2 * FB), F32)
+    lines_odd = jnp.zeros((FA, 2 * FB), F32)
+    for group in range(PARTS):
+        ref = blocks_of(group)
+        sums = [jnp.zeros((FA, 2 * FB), F32)] * 2
+        for kern in range(local):
+            start = (group * local + kern) * tall
+            c_part, s_part = backs[start : start + FA], backs[start + FA : start + tall]
+            x_grad = c_part[:, : 2 * FB] - s_part[:, 2 * FB :]
+            y_grad = s_part[:, : 2 * FB] + c_part[:, 2 * FB :]
+            a_block, b_block = ref[2 * kern], ref[2 * kern + 1]
+            sum_even = sum_even + x_grad * a_block - y_grad * b_block
+            sum_odd = sum_odd + x_grad * b_block + y_grad * a_block
+            back = turned[group * local + kern]
+            for i in range(2):
+                for piece in range(2):
+                    whole = back[FA * i : FA * (i + 1), ROWS * piece : ROWS * (piece + 1)]
+                    whole = jnp.sum(whole, axis=1, keepdims=True)
+                    sums[i] = jnp.where(lane == 4 * kern + piece, whole, sums[i])
+        lines_even = lines_even + sums[0] * extras_ref[group, 0] - sums[1] * extras_ref[group, 1]
+        lines_odd = lines_odd + sums[0] * extras_ref[group, 1] + sums[1] * extras_ref[group, 0]
+    value = jnp.where(first, sum_even + pltpu.roll(sum_even, 2 * FB - HALF, 1), sum_odd + pltpu.roll(sum_odd, HALF, 1))
+    for place, columns in ((FA - 2, lines_even), (FA - 3, lines_odd)):
+        column = jnp.sum(columns, axis=1, keepdims=True)
+        line = jnp.sum(jnp.where((lane == row) & (row <= HALF), column, 0.0), axis=0, keepdims=True)
+        value = jnp.where(row == place, line, value)
+    out_ref[...] = value
 
 
 def image_rows(packed, rows, turned_ref):
@@ -555,16 +588,16 @@
         ],
         floats(FA, 2 * FB),
         scratch=(
-            pltpu.VMEM((count, 4, FA, 2 * FB), F32),
+            pltpu.VMEM((PARTS, 2, FA, 2 * FB), F32),
             pltpu.VMEM((CONDS, ROWS), F32),
-            pltpu.VMEM((count * 4 * FA, 2 * FB), F32),
+            pltpu.VMEM((count * 2 * FA, 2 * FB), F32),
+            pltpu.VMEM((count * 2 * FA, 2 * FB), F32),
             pltpu.VMEM((count, 6 * FA, 2 * ROWS), BF),
             pltpu.VMEM((count, TP, 2 * ROWS), F32),
             pltpu.VMEM((CONDS, TP, ROWS), F32),
             pltpu.VMEM((TP, ROWS), F32),
             pltpu.VMEM((TP, ROWS), F32),
-            pltpu.VMEM((count * 2, 2 * FA, ROWS), F32),
-            pltpu.VMEM((count * 4 * FA, 4 * FB), F32),
+            pltpu.VMEM((count, 2 * FA, 2 * ROWS), F32),
         ),
         name="coherent_fields",
         flops=1 << 33,

time: 30.2 us -> 30.2 us (level)
  no operation moved by 1% of the time
where the time goes in v5:
time: 30.2 us; the launch traced here: 30 us
  Pallas kernels  12.2 us (40%)
  waiting for transfers between devices  10.3 us (34%)
  starting transfers between devices  7.25 us (24%)
    pallas_call x7, Pallas kernels, call(): pl.pallas_call(kernel, grid_spec=pltpu.PrefetchScalarGridSpec(num_scalar_...  12.2 us
    ppermute x5, waiting for transfers between devices, partner(): return lax.ppermute(value, 'cond', [(i, i ^ step) for i in range(PARTS)])  7.98 us
    ppermute x5, starting transfers between devices, partner(): return lax.ppermute(value, 'cond', [(i, i ^ step) for i in range(PARTS)])  5.79 us
    ppermute x2, waiting for transfers between devices, across(): return lax.ppermute(value, ('tile', 'cond'), pairs)  2.37 us
    ppermute x2, starting transfers between devices, across(): return lax.ppermute(value, ('tile', 'cond'), pairs)  1.46 us
  transfers between devices with their start and end apart: 7, of which 5 were waited for; matrix products, arithmetic and copies ran while one was open for 0% of the time, Pallas kernels for 12%

profile of v5, /device:TPU:0, one launch (start us, length us, event | category | flops | bytes accessed | tf_op | source)
XLA Modules:
  0.0 30.0 jit_solution(3679528342171969892)
XLA Ops:
  0.0 0.0 copy-start.3
  0.0 0.0 copy-start.5
  0.0 0.0 copy-start.7
  0.0 1.3 %edge_columns.1 = f32[32,128]{1,0:T(8,128)S(1)} custom-call(s32[1]{0:T(128)} %bitcast.part_ref, f32[128,512]{1,0:T(8,128)} %theta_ref.3, bf16[2,512,128]{2,1,0:T(8,128)(2,1)} %constant.41.clone.waves_hbm), custom_call_target="tpu_custom_call" | custom-call | flops 268435456 | bytes 1048576 | tf_op jit(solution)/shard_map/edge_columns/pallas_call | solution.py:469
  1.3 1.3 %collective-permute-start.1 = (f32[32,128]{1,0:T(8,128)S(1)}, f32[32,128]{1,0:T(8,128)S(1)}, u32[]{:S(2)}, u32[]{:S(2)}) collective-permute-start(f32[32,128]{1,0:T(8,128)S(1)} %edge_columns.1), channel_id=1, source_target_pairs={{4,0},{8,4},{12,8},{16,12},{20,16},{24,20},{28,24},{3,7},{7,11},{1... | collective-permute-start | bytes 49160 | tf_op jit(solution)/shard_map/ppermute | solution.py:509
  2.6 1.6 %open_parts.1 = (f32[8,40,128]{2,1,0:T(8,128)S(1)}, f32[8,128]{1,0:T(8,128)S(1)}, bf16[512,512]{1,0:T(8,128)(2,1)S(1)}, bf16[512,256]{1,0:T(8,128)(2,1)S(1)}) custom-call(s32[1]{0:T(128)} %bitcast.part_ref, f32[2,65,2,65]{3,2,1,0:T(2,128)} %bitcast.3, f32[2,65,2,65]{3,2,1,0:T(2,128)} %bitcast.4, f32[2]{0:T(128)} %thresholds_hbm.1, s32[8]{0:T(128)} %weights_hbm.1, ...), custom_call_target="tpu_custom_call" | custom-call | flops 268435456 | bytes 1048576 | tf_op jit(solution)/shard_map/open_parts/pallas_call | solution.py:469
  4.2 0.0 copy-start.9
  4.2 0.0 copy-start.2
  4.2 0.0 copy-start.6
  4.2 0.0 copy-start.8
  4.3 4.3 %collective-permute-start = (f32[8,40,128]{2,1,0:T(8,128)S(1)}, f32[8,40,128]{2,1,0:T(8,128)S(1)}, u32[]{:S(2)}, u32[]{:S(2)}) collective-permute-start(f32[8,40,128]{2,1,0:T(8,128)S(1)} %get-tuple-element.12), channel_id=1, source_target_pairs={{0,3},{1,2},{2,1},{3,0},{4,7},{5,6},{6,5},{7,4},{8,11},{9,10},{10,... | collective-permute-start | bytes 491528 | tf_op jit(solution)/shard_map/ppermute | solution.py:512
  8.6 0.0 copy-done.3
  8.6 0.0 copy-done.5
  8.6 0.0 copy-done.7
  8.6 0.5 %own_spectrum.1.spectrum_ref = f32[2,40,128]{2,1,0:T(8,128)S(1)} custom-call(s32[1]{0:T(128)} %bitcast.part_ref, f32[128,512]{1,0:T(8,128)S(1)} %copy-done.3, bf16[2,512,256]{2,1,0:T(8,128)(2,1)S(1)} %copy-done.5, bf16[4,80,384]{2,1,0:T(8,128)(2,1)S(1)} %copy-done.7), custom_call_target="tpu_custom_call" | custom-call | flops 2147483648 | bytes 1048576 | tf_op jit(solution)/shard_map/own_spectrum/pallas_call | solution.py:469
  9.1 0.0 collective-permute-done.1.rim_ref
  9.1 0.0 copy-done.9
  9.1 0.3 add_rim.1
  9.4 0.3 %collective-permute-start.2 = (f32[1,40,128]{2,1,0:T(8,128)S(1)}, f32[1,40,128]{2,1,0:T(8,128)S(1)}, u32[]{:S(2)}, u32[]{:S(2)}) collective-permute-start(f32[1,40,128]{2,1,0:T(8,128)S(1)} %add_rim.1), channel_id=1, source_target_pairs={{0,3},{1,2},{2,1},{3,0},{4,7},{5,6},{6,5},{7,4},{8,11},{9,10},{10,... | collective-permute-start | bytes 61448 | tf_op jit(solution)/shard_map/ppermute | solution.py:512
  9.7 3.0 %collective-permute-done.2 = f32[1,40,128]{2,1,0:T(8,128)S(1)} collective-permute-done((f32[1,40,128]{2,1,0:T(8,128)S(1)}, f32[1,40,128]{2,1,0:T(8,128)S(1)}, u32[]{:S(2)}, u32[]{:S(2)}) %collective-permute-start.2) | collective-permute-done | bytes 20512 | tf_op jit(solution)/shard_map/ppermute | solution.py:512
  12.7 0.0 collective-permute-done
  12.7 0.1 collective-permute-start.3
  12.8 1.6 %collective-permute-done.3.other_ref = f32[17,40,128]{2,1,0:T(8,128)S(1)} collective-permute-done((f32[17,40,128]{2,1,0:T(8,128)S(1)}, f32[17,40,128]{2,1,0:T(8,128)S(1)}, u32[]{:S(2)}, u32[]{:S(2)}) %collective-permute-start.3) | collective-permute-done | bytes 348192 | tf_op jit(solution)/shard_map/ppermute | solution.py:512
  14.4 0.0 copy-done.2
  14.4 0.0 copy-done.6
  14.4 0.0 copy-done.8
  14.4 0.0 copy-start
  14.5 0.0 copy-start.4
  14.5 6.2 %coherent_fields.1 = f32[40,128]{1,0:T(8,128)S(1)} custom-call(s32[1]{0:T(128)} %bitcast.part_ref, f32[17,40,128]{2,1,0:T(8,128)S(1)} %pad_maximum_fusion.mixed_ref, f32[17,40,128]{2,1,0:T(8,128)S(1)} %collective-permute-done.3.other_ref, f32[8,128]{1,0:T(8,128)S(1)} %get-tuple-element.13.shares_ref, s32[512,512]{1,0:T(8,128)S(1)} %copy-done.2, ...), custom_call_target="tpu_custom_call" | custom-call | flops 8589934592 | bytes 1048576 | tf_op jit(solution)/shard_map/coherent_fields/pallas_call | solution.py:469
  20.7 0.2 collective-permute-start.4
  20.9 1.0 %collective-permute-done.4 = f32[40,128]{1,0:T(8,128)S(1)} collective-permute-done((f32[40,128]{1,0:T(8,128)S(1)}, f32[40,128]{1,0:T(8,128)S(1)}, u32[]{:S(2)}, u32[]{:S(2)}) %collective-permute-start.4) | collective-permute-done | bytes 20512 | tf_op jit(solution)/shard_map/ppermute | solution.py:512
  21.9 0.9 %collective-permute-start.5 = (f32[40,128]{1,0:T(8,128)S(1)}, f32[40,128]{1,0:T(8,128)S(1)}, u32[]{:S(2)}, u32[]{:S(2)}) collective-permute-start(f32[40,128]{1,0:T(8,128)S(1)} %add.14), channel_id=1, source_target_pairs={{0,3},{1,2},{2,1},{3,0},{4,7},{5,6},{6,5},{7,4},{8,11},{9,10},{10,... | collective-permute-start | bytes 61448 | tf_op jit(solution)/shard_map/ppermute | solution.py:512
  22.8 2.3 %collective-permute-done.5 = f32[40,128]{1,0:T(8,128)S(1)} collective-permute-done((f32[40,128]{1,0:T(8,128)S(1)}, f32[40,128]{1,0:T(8,128)S(1)}, u32[]{:S(2)}, u32[]{:S(2)}) %collective-permute-start.5) | collective-permute-done | bytes 20512 | tf_op jit(solution)/shard_map/ppermute | solution.py:512
  25.1 0.0 copy-start.1
  25.1 0.2 collective-permute-start.6
  25.3 0.0 copy-done
  25.3 0.0 copy-done.4
  25.3 1.2 %own_gradient.1 = (f32[128,512]{1,0:T(8,128)}, f32[32,512]{1,0:T(8,128)S(1)}, f32[32,512]{1,0:T(8,128)S(1)}) custom-call(s32[1]{0:T(128)} %bitcast.part_ref, f32[128,512]{1,0:T(8,128)S(1)} %copy-done.3, f32[40,128]{1,0:T(8,128)S(1)} %add.15.sum_ref, bf16[2,256,512]{2,1,0:T(8,128)(2,1)S(1)} %copy-done, bf16[4,256,240]{2,1,0:T(8,128)(2,1)S(1)} %copy-done.4), custom_call_target="tpu_custom_call" | custom-call | flops 2147483648 | bytes 1048576 | tf_op jit(solution)/shard_map/own_gradient/pallas_call | solution.py:469
  26.5 2.4 %collective-permute-done.6.near_ref = f32[40,128]{1,0:T(8,128)S(1)} collective-permute-done((f32[40,128]{1,0:T(8,128)S(1)}, f32[40,128]{1,0:T(8,128)S(1)}, u32[]{:S(2)}, u32[]{:S(2)}) %collective-permute-start.6) | collective-permute-done | bytes 20512 | tf_op jit(solution)/shard_map/ppermute | solution.py:509
  28.9 0.0 copy-done.1
  28.9 1.1 %edge_gradient.1 = f32[128,512]{1,0:T(8,128)} custom-call(s32[1]{0:T(128)} %bitcast.part_ref, f32[128,512]{1,0:T(8,128)} %get-tuple-element.16.gradient_hbm, f32[32,512]{1,0:T(8,128)S(1)} %get-tuple-element.17.edge_ref, f32[32,512]{1,0:T(8,128)S(1)} %get-tuple-element.18.scale_ref, ...), custom_call_target="tpu_custom_call", output_to_operand_aliasing={{}: (1, {})} | custom-call | flops 268435456 | bytes 1048576 | tf_op jit(solution)/shard_map/edge_gradient/pallas_call | solution.py:469
  (4 shorter events, 0.0 us)
Async XLA Ops:
  0.0 8.6 %copy-start.3 = (f32[128,512]{1,0:T(8,128)S(1)}, f32[128,512]{1,0:T(8,128)}, u32[]{:S(2)}) copy-start(f32[128,512]{1,0:T(8,128)} %theta_ref.3) | copy-start | bytes 786436
  0.0 8.6 %copy-start.5 = (bf16[2,512,256]{2,1,0:T(8,128)(2,1)S(1)}, bf16[2,512,256]{2,1,0:T(8,128)(2,1)}, u32[]{:S(2)}) copy-start(bf16[2,512,256]{2,1,0:T(8,128)(2,1)} %constant.40.clone.column_ref) | copy-start | bytes 1572868
  0.0 8.6 %copy-start.7 = (bf16[4,80,384]{2,1,0:T(8,128)(2,1)S(1)}, bf16[4,80,384]{2,1,0:T(8,128)(2,1)}, u32[]{:S(2)}) copy-start(bf16[4,80,384]{2,1,0:T(8,128)(2,1)} %constant.42.clone.rows_ref) | copy-start | bytes 737284
  1.3 7.8 %collective-permute-start.1 = (f32[32,128]{1,0:T(8,128)S(1)}, f32[32,128]{1,0:T(8,128)S(1)}, u32[]{:S(2)}, u32[]{:S(2)}) collective-permute-start(f32[32,128]{1,0:T(8,128)S(1)} %edge_columns.1), channel_id=1, source_target_pairs={{4,0},{8,4},{12,8},{16,12},{20,16},{24,20},{28,24},{3,7},{7,11},{1... | collective-permute-start | bytes 49160 | tf_op jit(solution)/shard_map/ppermute | solution.py:509
  4.2 4.9 %copy-start.9 = (bf16[4,80,96]{2,1,0:T(8,128)(2,1)S(1)}, bf16[4,80,96]{2,1,0:T(8,128)(2,1)}, u32[]{:S(2)}) copy-start(bf16[4,80,96]{2,1,0:T(8,128)(2,1)} %constant.44.clone.rows_ref) | copy-start | bytes 184324
  4.2 10.2 %copy-start.2 = (s32[512,512]{1,0:T(8,128)S(1)}, s32[512,512]{1,0:T(8,128)}, u32[]{:S(2)}) copy-start(s32[512,512]{1,0:T(8,128)} %target_ref.1) | copy-start | bytes 3145732
  4.2 10.2 %copy-start.6 = (bf16[512,240]{1,0:T(8,128)(2,1)S(1)}, bf16[512,240]{1,0:T(8,128)(2,1)}, u32[]{:S(2)}) copy-start(bf16[512,240]{1,0:T(8,128)(2,1)} %constant.49.clone.row_ref) | copy-start | bytes 737284
  4.2 10.2 %copy-start.8 = (bf16[160,512]{1,0:T(8,128)(2,1)S(1)}, bf16[160,512]{1,0:T(8,128)(2,1)}, u32[]{:S(2)}) copy-start(bf16[160,512]{1,0:T(8,128)(2,1)} %constant.50.clone.row_turned_ref) | copy-start | bytes 491524
  4.3 8.4 %collective-permute-start = (f32[8,40,128]{2,1,0:T(8,128)S(1)}, f32[8,40,128]{2,1,0:T(8,128)S(1)}, u32[]{:S(2)}, u32[]{:S(2)}) collective-permute-start(f32[8,40,128]{2,1,0:T(8,128)S(1)} %get-tuple-element.12), channel_id=1, source_target_pairs={{0,3},{1,2},{2,1},{3,0},{4,7},{5,6},{6,5},{7,4},{8,11},{9,10},{10,... | collective-permute-start | bytes 491528 | tf_op jit(solution)/shard_map/ppermute | solution.py:512
  9.4 3.3 %collective-permute-start.2 = (f32[1,40,128]{2,1,0:T(8,128)S(1)}, f32[1,40,128]{2,1,0:T(8,128)S(1)}, u32[]{:S(2)}, u32[]{:S(2)}) collective-permute-start(f32[1,40,128]{2,1,0:T(8,128)S(1)} %add_rim.1), channel_id=1, source_target_pairs={{0,3},{1,2},{2,1},{3,0},{4,7},{5,6},{6,5},{7,4},{8,11},{9,10},{10,... | collective-permute-start | bytes 61448 | tf_op jit(solution)/shard_map/ppermute | solution.py:512
  12.7 1.7 %collective-permute-start.3 = (f32[17,40,128]{2,1,0:T(8,128)S(1)}, f32[17,40,128]{2,1,0:T(8,128)S(1)}, u32[]{:S(2)}, u32[]{:S(2)}) collective-permute-start(f32[17,40,128]{2,1,0:T(8,128)S(1)} %pad_maximum_fusion.mixed_ref), channel_id=1, source_target_pairs={{0,1},{1,0},{2,3},{3,2},{4,5},{5,4},{6,7},{7,6},{8,9},{9,8},{10,11... | collective-permute-start | bytes 1044488 | tf_op jit(solution)/shard_map/ppermute | solution.py:512
  14.4 10.9 %copy-start = (bf16[2,256,512]{2,1,0:T(8,128)(2,1)S(1)}, bf16[2,256,512]{2,1,0:T(8,128)(2,1)}, u32[]{:S(2)}) copy-start(bf16[2,256,512]{2,1,0:T(8,128)(2,1)} %constant.48.clone.turned_ref) | copy-start | bytes 1572868
  14.5 10.8 %copy-start.4 = (bf16[4,256,240]{2,1,0:T(8,128)(2,1)S(1)}, bf16[4,256,240]{2,1,0:T(8,128)(2,1)}, u32[]{:S(2)}) copy-start(bf16[4,256,240]{2,1,0:T(8,128)(2,1)} %constant.43.clone.rows_ref) | copy-start | bytes 1474564
  20.7 1.3 %collective-permute-start.4 = (f32[40,128]{1,0:T(8,128)S(1)}, f32[40,128]{1,0:T(8,128)S(1)}, u32[]{:S(2)}, u32[]{:S(2)}) collective-permute-start(f32[40,128]{1,0:T(8,128)S(1)} %coherent_fields.1), channel_id=1, source_target_pairs={{0,1},{1,0},{2,3},{3,2},{4,5},{5,4},{6,7},{7,6},{8,9},{9,8},{10,11... | collective-permute-start | bytes 61448 | tf_op jit(solution)/shard_map/ppermute | solution.py:512
  21.9 3.2 %collective-permute-start.5 = (f32[40,128]{1,0:T(8,128)S(1)}, f32[40,128]{1,0:T(8,128)S(1)}, u32[]{:S(2)}, u32[]{:S(2)}) collective-permute-start(f32[40,128]{1,0:T(8,128)S(1)} %add.14), channel_id=1, source_target_pairs={{0,3},{1,2},{2,1},{3,0},{4,7},{5,6},{6,5},{7,4},{8,11},{9,10},{10,... | collective-permute-start | bytes 61448 | tf_op jit(solution)/shard_map/ppermute | solution.py:512
  25.1 3.8 %copy-start.1 = (bf16[4,64,240]{2,1,0:T(8,128)(2,1)S(1)}, bf16[4,64,240]{2,1,0:T(8,128)(2,1)}, u32[]{:S(2)}) copy-start(bf16[4,64,240]{2,1,0:T(8,128)(2,1)} %constant.45.clone.rows_ref) | copy-start | bytes 368644
  25.1 3.8 %collective-permute-start.6 = (f32[40,128]{1,0:T(8,128)S(1)}, f32[40,128]{1,0:T(8,128)S(1)}, u32[]{:S(2)}, u32[]{:S(2)}) collective-permute-start(f32[40,128]{1,0:T(8,128)S(1)} %add.15.sum_ref), channel_id=1, source_target_pairs={{0,1},{3,2},{4,5},{7,6},{8,9},{11,10},{12,13},{15,14},{16,17},{19,... | collective-permute-start | bytes 61448 | tf_op jit(solution)/shard_map/ppermute | solution.py:509

commit v6 on v4

--- a/solution.py
+++ b/solution.py
@@ -113,8 +113,12 @@
     return ref[0] % PARTS
 
 
-def has_halo(ref):
-    return ref[0] // PARTS > 0
+def has_adjoint_halo(ref):
+    return ref[0] // PARTS % 2 > 0
+
+
+def has_mask_halo(ref):
+    return ref[0] // (2 * PARTS) > 0
 
 
 def dot(left, right):
@@ -268,7 +272,7 @@
 
 
 def rim_kernel(part_ref, spectrum_ref, rim_ref, rows_ref, out_ref):
-    rim = rim_ref[...]
+    rim = jnp.where(has_mask_halo(part_ref), rim_ref[...], 0.0)
     turned = pltpu.roll(rim, FB, 1)
     first = lax.broadcasted_iota(jnp.int32, rim.shape, 1) < FB
     across = jnp.concatenate([jnp.where(first, rim, turned), jnp.where(first, turned, -rim)], axis=1)
@@ -413,7 +417,7 @@
 
 def edge_kernel(part_ref, gradient_hbm, edge_ref, scale_ref, near_ref, turned_ref, rows_ref, out_hbm, stage, sem):
     rim = image_rows(near_ref[...], rows_ref[0], turned_ref) * scale_ref[...]
-    stage[...] = edge_ref[...] + jnp.where(has_halo(part_ref), rim, 0.0)
+    stage[...] = edge_ref[...] + jnp.where(has_adjoint_halo(part_ref), rim, 0.0)
     copy = pltpu.make_async_copy(stage, out_hbm.at[pl.ds(edge_start(part_ref), HALO)], sem)
     copy.start()
     copy.wait()
@@ -461,18 +465,18 @@
     tile = lax.axis_index("tile")
     last = PARTS - 1
     above = ((part == 0) & (tile > 0)) | ((part == last) & (tile < tiles - 1))
-    parts = (part + PARTS * above.astype(jnp.int32)).reshape(1).astype(jnp.int32)
+    below = ((part == 0) & (tile < tiles - 1)) | ((part == last) & (tile > 0))
+    parts = (part + PARTS * above.astype(jnp.int32) + 2 * PARTS * below.astype(jnp.int32)).reshape(1).astype(jnp.int32)
     local_conds = kernel_real.shape[0]
     local = local_conds * KERNELS
     count = CONDS * KERNELS
     hbm = pl.BlockSpec(memory_space=pltpu.HBM)
 
-    def across(value, down, up, within=()):
+    def across(value, down, up, within):
         pairs = [(PARTS * i + a, PARTS * i + b) for i in range(tiles) for a, b in within]
         pairs += [(PARTS * (i + 1) + down[0], PARTS * i + down[1]) for i in range(tiles - 1)]
         pairs += [(PARTS * i + up[0], PARTS * (i + 1) + up[1]) for i in range(tiles - 1)]
-        if within:
-            pairs += [(down[0], up[1]), (PARTS * (tiles - 1) + up[0], PARTS * (tiles - 1) + down[1])]
+        pairs += [(down[0], up[1]), (PARTS * (tiles - 1) + up[0], PARTS * (tiles - 1) + down[1])]
         return lax.ppermute(value, ("tile", "cond"), pairs)
 
     def partner(value, step):
@@ -519,7 +523,7 @@
         ),
         name="edge_columns",
     )
-    rim = across(rim, (0, 0), (last, last))
+    rim = across(rim, (0, 0), (last, last), [(1, 2), (2, 1)])
     spectrum = call(
         spectrum_kernel,
         (parts,),
@@ -571,7 +575,7 @@
     )
     adjoint = adjoint + partner(adjoint, 1)
     adjoint = adjoint + partner(adjoint, 3)
-    near = across(adjoint, (2, last), (1, 0), within=[(0, 1), (last, 2)])
+    near = across(adjoint, (2, last), (1, 0), [(0, 1), (last, 2)])
     gradient, edge, scale = call(
         gradient_kernel,
         (parts,),

time: 30.2 us -> 29.4 us (0.974)
  the two profiles are of different devices: /device:TPU:0 before, /device:TPU:24 now
where the time goes in v6:
time: 29.4 us; the launch traced here: 28.8 us
  waiting for transfers between devices  12.5 us (43%)
  Pallas kernels  12.2 us (41%)
  starting transfers between devices  3.89 us (13%)
    pallas_call x7, Pallas kernels, call(): pl.pallas_call(kernel, grid_spec=pltpu.PrefetchScalarGridSpec(num_scalar_...  12.2 us
    ppermute x5, waiting for transfers between devices, partner(): return lax.ppermute(value, 'cond', [(i, i ^ step) for i in range(PARTS)])  9.8 us
    ppermute x2, waiting for transfers between devices, across(): return lax.ppermute(value, ('tile', 'cond'), pairs)  2.69 us
    ppermute x5, starting transfers between devices, partner(): return lax.ppermute(value, 'cond', [(i, i ^ step) for i in range(PARTS)])  2.26 us
    ppermute x2, starting transfers between devices, across(): return lax.ppermute(value, ('tile', 'cond'), pairs)  1.63 us
  transfers between devices with their start and end apart: 7, of which 5 were waited for; matrix products, arithmetic and copies ran while one was open for 0% of the time, Pallas kernels for 13%

profile of v6, /device:TPU:24, one launch (start us, length us, event | category | flops | bytes accessed | tf_op | source)
XLA Modules:
  0.0 28.8 jit_solution(17290553899544666411)
XLA Ops:
  0.0 1.2 %edge_columns.1 = f32[32,128]{1,0:T(8,128)S(1)} custom-call(s32[1]{0:T(128)} %bitcast.part_ref, f32[128,512]{1,0:T(8,128)} %theta_ref.3, bf16[2,512,128]{2,1,0:T(8,128)(2,1)} %constant.44.clone.waves_hbm), custom_call_target="tpu_custom_call" | custom-call | flops 268435456 | bytes 1048576 | tf_op jit(solution)/shard_map/edge_columns/pallas_call | solution.py:440
  1.2 1.5 %collective-permute-start.1 = (f32[32,128]{1,0:T(8,128)S(1)}, f32[32,128]{1,0:T(8,128)S(1)}, u32[]{:S(2)}, u32[]{:S(2)}) collective-permute-start(f32[32,128]{1,0:T(8,128)S(1)} %edge_columns.1), channel_id=1, source_target_pairs={{1,2},{2,1},{5,6},{6,5},{9,10},{10,9},{13,14},{14,13},{17,18},{18,... | collective-permute-start | bytes 49160 | tf_op jit(solution)/shard_map/ppermute | solution.py:480
  2.7 0.0 copy-start.3
  2.7 0.0 copy-start.5
  2.7 0.0 copy-start.7
  2.7 1.7 %open_parts.1 = (f32[8,40,128]{2,1,0:T(8,128)S(1)}, f32[8,128]{1,0:T(8,128)S(1)}, bf16[384,256]{1,0:T(8,128)(2,1)S(1)}, bf16[384,256]{1,0:T(8,128)(2,1)S(1)}) custom-call(s32[1]{0:T(128)} %bitcast.part_ref, f32[2,65,2,65]{3,2,1,0:T(2,128)} %bitcast.3, f32[2,65,2,65]{3,2,1,0:T(2,128)} %bitcast.4, f32[2]{0:T(128)} %thresholds_hbm.1, s32[8]{0:T(128)} %weights_hbm.1, ...), custom_call_target="tpu_custom_call" | custom-call | flops 268435456 | bytes 1048576 | tf_op jit(solution)/shard_map/open_parts/pallas_call | solution.py:440
  4.4 0.0 copy-start.9
  4.4 0.8 %collective-permute-start = (f32[8,40,128]{2,1,0:T(8,128)S(1)}, f32[8,40,128]{2,1,0:T(8,128)S(1)}, u32[]{:S(2)}, u32[]{:S(2)}) collective-permute-start(f32[8,40,128]{2,1,0:T(8,128)S(1)} %get-tuple-element.12), channel_id=1, source_target_pairs={{0,3},{1,2},{2,1},{3,0},{4,7},{5,6},{6,5},{7,4},{8,11},{9,10},{10,... | collective-permute-start | bytes 491528 | tf_op jit(solution)/shard_map/ppermute | solution.py:483
  5.2 0.0 copy-done.3
  5.2 0.0 copy-done.5
  5.2 0.0 copy-done.7
  5.2 0.5 %own_spectrum.1.spectrum_ref = f32[2,40,128]{2,1,0:T(8,128)S(1)} custom-call(s32[1]{0:T(128)} %bitcast.part_ref, f32[128,512]{1,0:T(8,128)S(1)} %copy-done.3, bf16[2,512,256]{2,1,0:T(8,128)(2,1)S(1)} %copy-done.5, bf16[4,80,384]{2,1,0:T(8,128)(2,1)S(1)} %copy-done.7), custom_call_target="tpu_custom_call" | custom-call | flops 2147483648 | bytes 1048576 | tf_op jit(solution)/shard_map/own_spectrum/pallas_call | solution.py:440
  5.7 0.0 copy-start.2
  5.7 0.0 collective-permute-done.1.rim_ref
  5.7 0.0 copy-done.9
  5.8 0.3 %add_rim.1 = f32[1,40,128]{2,1,0:T(8,128)S(1)} custom-call(s32[1]{0:T(128)} %bitcast.part_ref, f32[2,40,128]{2,1,0:T(8,128)S(1)} %own_spectrum.1.spectrum_ref, f32[32,128]{1,0:T(8,128)S(1)} %collective-permute-done.1.rim_ref, bf16[4,80,96]{2,1,0:T(8,128)(2,1)S(1)} %copy-done.9), custom_call_target="tpu_custom_call" | custom-call | flops 268435456 | bytes 1048576 | tf_op jit(solution)/shard_map/add_rim/pallas_call | solution.py:440
  6.1 1.0 %collective-permute-start.2 = (f32[1,40,128]{2,1,0:T(8,128)S(1)}, f32[1,40,128]{2,1,0:T(8,128)S(1)}, u32[]{:S(2)}, u32[]{:S(2)}) collective-permute-start(f32[1,40,128]{2,1,0:T(8,128)S(1)} %add_rim.1), channel_id=1, source_target_pairs={{0,3},{1,2},{2,1},{3,0},{4,7},{5,6},{6,5},{7,4},{8,11},{9,10},{10,... | collective-permute-start | bytes 61448 | tf_op jit(solution)/shard_map/ppermute | solution.py:483
  7.1 4.0 %collective-permute-done.2 = f32[1,40,128]{2,1,0:T(8,128)S(1)} collective-permute-done((f32[1,40,128]{2,1,0:T(8,128)S(1)}, f32[1,40,128]{2,1,0:T(8,128)S(1)}, u32[]{:S(2)}, u32[]{:S(2)}) %collective-permute-start.2) | collective-permute-done | bytes 20512 | tf_op jit(solution)/shard_map/ppermute | solution.py:483
  11.1 0.0 copy-start.6
  11.1 0.0 copy-start.8
  11.1 0.0 collective-permute-done
  11.2 0.2 collective-permute-start.3
  11.3 1.5 %collective-permute-done.3.other_ref = f32[17,40,128]{2,1,0:T(8,128)S(1)} collective-permute-done((f32[17,40,128]{2,1,0:T(8,128)S(1)}, f32[17,40,128]{2,1,0:T(8,128)S(1)}, u32[]{:S(2)}, u32[]{:S(2)}) %collective-permute-start.3) | collective-permute-done | bytes 348192 | tf_op jit(solution)/shard_map/ppermute | solution.py:483
  12.9 0.0 copy-done.2
  12.9 0.0 copy-done.6
  12.9 0.0 copy-done.8
  12.9 0.0 copy-start
  12.9 0.0 copy-start.4
  12.9 6.2 %coherent_fields.1 = f32[40,128]{1,0:T(8,128)S(1)} custom-call(s32[1]{0:T(128)} %bitcast.part_ref, f32[17,40,128]{2,1,0:T(8,128)S(1)} %pad_maximum_fusion.mixed_ref, f32[17,40,128]{2,1,0:T(8,128)S(1)} %collective-permute-done.3.other_ref, f32[8,128]{1,0:T(8,128)S(1)} %get-tuple-element.13.shares_ref, s32[512,512]{1,0:T(8,128)S(1)} %copy-done.2, ...), custom_call_target="tpu_custom_call" | custom-call | flops 8589934592 | bytes 1048576 | tf_op jit(solution)/shard_map/coherent_fields/pallas_call | solution.py:440
  19.1 0.2 collective-permute-start.4
  19.3 1.1 %collective-permute-done.4 = f32[40,128]{1,0:T(8,128)S(1)} collective-permute-done((f32[40,128]{1,0:T(8,128)S(1)}, f32[40,128]{1,0:T(8,128)S(1)}, u32[]{:S(2)}, u32[]{:S(2)}) %collective-permute-start.4) | collective-permute-done | bytes 20512 | tf_op jit(solution)/shard_map/ppermute | solution.py:483
  20.4 0.0 collective-permute-start.5
  20.4 3.2 %collective-permute-done.5 = f32[40,128]{1,0:T(8,128)S(1)} collective-permute-done((f32[40,128]{1,0:T(8,128)S(1)}, f32[40,128]{1,0:T(8,128)S(1)}, u32[]{:S(2)}, u32[]{:S(2)}) %collective-permute-start.5) | collective-permute-done | bytes 20512 | tf_op jit(solution)/shard_map/ppermute | solution.py:483
  23.6 0.0 copy-start.1
  23.6 0.2 collective-permute-start.6
  23.8 0.0 copy-done
  23.8 0.0 copy-done.4
  23.8 1.2 %own_gradient.1 = (f32[128,512]{1,0:T(8,128)}, f32[32,512]{1,0:T(8,128)S(1)}, f32[32,512]{1,0:T(8,128)S(1)}) custom-call(s32[1]{0:T(128)} %bitcast.part_ref, f32[128,512]{1,0:T(8,128)S(1)} %copy-done.3, f32[40,128]{1,0:T(8,128)S(1)} %add.19.sum_ref, bf16[2,256,512]{2,1,0:T(8,128)(2,1)S(1)} %copy-done, bf16[4,256,240]{2,1,0:T(8,128)(2,1)S(1)} %copy-done.4), custom_call_target="tpu_custom_call" | custom-call | flops 2147483648 | bytes 1048576 | tf_op jit(solution)/shard_map/own_gradient/pallas_call | solution.py:440
  25.0 2.7 %collective-permute-done.6.near_ref = f32[40,128]{1,0:T(8,128)S(1)} collective-permute-done((f32[40,128]{1,0:T(8,128)S(1)}, f32[40,128]{1,0:T(8,128)S(1)}, u32[]{:S(2)}, u32[]{:S(2)}) %collective-permute-start.6) | collective-permute-done | bytes 20512 | tf_op jit(solution)/shard_map/ppermute | solution.py:480
  27.7 0.0 copy-done.1
  27.7 1.1 %edge_gradient.1 = f32[128,512]{1,0:T(8,128)} custom-call(s32[1]{0:T(128)} %bitcast.part_ref, f32[128,512]{1,0:T(8,128)} %get-tuple-element.16.gradient_hbm, f32[32,512]{1,0:T(8,128)S(1)} %get-tuple-element.17.edge_ref, f32[32,512]{1,0:T(8,128)S(1)} %get-tuple-element.18.scale_ref, ...), custom_call_target="tpu_custom_call", output_to_operand_aliasing={{}: (1, {})} | custom-call | flops 268435456 | bytes 1048576 | tf_op jit(solution)/shard_map/edge_gradient/pallas_call | solution.py:440
  (4 shorter events, 0.0 us)
Async XLA Ops:
  1.2 4.5 %collective-permute-start.1 = (f32[32,128]{1,0:T(8,128)S(1)}, f32[32,128]{1,0:T(8,128)S(1)}, u32[]{:S(2)}, u32[]{:S(2)}) collective-permute-start(f32[32,128]{1,0:T(8,128)S(1)} %edge_columns.1), channel_id=1, source_target_pairs={{1,2},{2,1},{5,6},{6,5},{9,10},{10,9},{13,14},{14,13},{17,18},{18,... | collective-permute-start | bytes 49160 | tf_op jit(solution)/shard_map/ppermute | solution.py:480
  2.7 2.6 %copy-start.3 = (f32[128,512]{1,0:T(8,128)S(1)}, f32[128,512]{1,0:T(8,128)}, u32[]{:S(2)}) copy-start(f32[128,512]{1,0:T(8,128)} %theta_ref.3) | copy-start | bytes 786436
  2.7 2.6 %copy-start.5 = (bf16[2,512,256]{2,1,0:T(8,128)(2,1)S(1)}, bf16[2,512,256]{2,1,0:T(8,128)(2,1)}, u32[]{:S(2)}) copy-start(bf16[2,512,256]{2,1,0:T(8,128)(2,1)} %constant.43.clone.column_ref) | copy-start | bytes 1572868
  2.7 2.6 %copy-start.7 = (bf16[4,80,384]{2,1,0:T(8,128)(2,1)S(1)}, bf16[4,80,384]{2,1,0:T(8,128)(2,1)}, u32[]{:S(2)}) copy-start(bf16[4,80,384]{2,1,0:T(8,128)(2,1)} %constant.45.clone.rows_ref) | copy-start | bytes 737284
  4.4 1.4 %copy-start.9 = (bf16[4,80,96]{2,1,0:T(8,128)(2,1)S(1)}, bf16[4,80,96]{2,1,0:T(8,128)(2,1)}, u32[]{:S(2)}) copy-start(bf16[4,80,96]{2,1,0:T(8,128)(2,1)} %constant.47.clone.rows_ref) | copy-start | bytes 184324
  4.4 6.7 %collective-permute-start = (f32[8,40,128]{2,1,0:T(8,128)S(1)}, f32[8,40,128]{2,1,0:T(8,128)S(1)}, u32[]{:S(2)}, u32[]{:S(2)}) collective-permute-start(f32[8,40,128]{2,1,0:T(8,128)S(1)} %get-tuple-element.12), channel_id=1, source_target_pairs={{0,3},{1,2},{2,1},{3,0},{4,7},{5,6},{6,5},{7,4},{8,11},{9,10},{10,... | collective-permute-start | bytes 491528 | tf_op jit(solution)/shard_map/ppermute | solution.py:483
  5.7 7.2 %copy-start.2 = (s32[512,512]{1,0:T(8,128)S(1)}, s32[512,512]{1,0:T(8,128)}, u32[]{:S(2)}) copy-start(s32[512,512]{1,0:T(8,128)} %target_ref.1) | copy-start | bytes 3145732
  6.1 5.0 %collective-permute-start.2 = (f32[1,40,128]{2,1,0:T(8,128)S(1)}, f32[1,40,128]{2,1,0:T(8,128)S(1)}, u32[]{:S(2)}, u32[]{:S(2)}) collective-permute-start(f32[1,40,128]{2,1,0:T(8,128)S(1)} %add_rim.1), channel_id=1, source_target_pairs={{0,3},{1,2},{2,1},{3,0},{4,7},{5,6},{6,5},{7,4},{8,11},{9,10},{10,... | collective-permute-start | bytes 61448 | tf_op jit(solution)/shard_map/ppermute | solution.py:483
  11.1 1.8 %copy-start.6 = (bf16[512,240]{1,0:T(8,128)(2,1)S(1)}, bf16[512,240]{1,0:T(8,128)(2,1)}, u32[]{:S(2)}) copy-start(bf16[512,240]{1,0:T(8,128)(2,1)} %constant.52.clone.row_ref) | copy-start | bytes 737284
  11.1 1.8 %copy-start.8 = (bf16[160,512]{1,0:T(8,128)(2,1)S(1)}, bf16[160,512]{1,0:T(8,128)(2,1)}, u32[]{:S(2)}) copy-start(bf16[160,512]{1,0:T(8,128)(2,1)} %constant.53.clone.row_turned_ref) | copy-start | bytes 491524
  11.2 1.7 %collective-permute-start.3 = (f32[17,40,128]{2,1,0:T(8,128)S(1)}, f32[17,40,128]{2,1,0:T(8,128)S(1)}, u32[]{:S(2)}, u32[]{:S(2)}) collective-permute-start(f32[17,40,128]{2,1,0:T(8,128)S(1)} %pad_maximum_fusion.mixed_ref), channel_id=1, source_target_pairs={{0,1},{1,0},{2,3},{3,2},{4,5},{5,4},{6,7},{7,6},{8,9},{9,8},{10,11... | collective-permute-start | bytes 1044488 | tf_op jit(solution)/shard_map/ppermute | solution.py:483
  12.9 10.9 %copy-start = (bf16[2,256,512]{2,1,0:T(8,128)(2,1)S(1)}, bf16[2,256,512]{2,1,0:T(8,128)(2,1)}, u32[]{:S(2)}) copy-start(bf16[2,256,512]{2,1,0:T(8,128)(2,1)} %constant.51.clone.turned_ref) | copy-start | bytes 1572868
  12.9 10.9 %copy-start.4 = (bf16[4,256,240]{2,1,0:T(8,128)(2,1)S(1)}, bf16[4,256,240]{2,1,0:T(8,128)(2,1)}, u32[]{:S(2)}) copy-start(bf16[4,256,240]{2,1,0:T(8,128)(2,1)} %constant.46.clone.rows_ref) | copy-start | bytes 1474564
  19.1 1.3 %collective-permute-start.4 = (f32[40,128]{1,0:T(8,128)S(1)}, f32[40,128]{1,0:T(8,128)S(1)}, u32[]{:S(2)}, u32[]{:S(2)}) collective-permute-start(f32[40,128]{1,0:T(8,128)S(1)} %coherent_fields.1), channel_id=1, source_target_pairs={{0,1},{1,0},{2,3},{3,2},{4,5},{5,4},{6,7},{7,6},{8,9},{9,8},{10,11... | collective-permute-start | bytes 61448 | tf_op jit(solution)/shard_map/ppermute | solution.py:483
  20.4 3.2 %collective-permute-start.5 = (f32[40,128]{1,0:T(8,128)S(1)}, f32[40,128]{1,0:T(8,128)S(1)}, u32[]{:S(2)}, u32[]{:S(2)}) collective-permute-start(f32[40,128]{1,0:T(8,128)S(1)} %add.18), channel_id=1, source_target_pairs={{0,3},{1,2},{2,1},{3,0},{4,7},{5,6},{6,5},{7,4},{8,11},{9,10},{10,... | collective-permute-start | bytes 61448 | tf_op jit(solution)/shard_map/ppermute | solution.py:483
  23.6 4.1 %copy-start.1 = (bf16[4,64,240]{2,1,0:T(8,128)(2,1)S(1)}, bf16[4,64,240]{2,1,0:T(8,128)(2,1)}, u32[]{:S(2)}) copy-start(bf16[4,64,240]{2,1,0:T(8,128)(2,1)} %constant.48.clone.rows_ref) | copy-start | bytes 368644
  23.6 4.1 %collective-permute-start.6 = (f32[40,128]{1,0:T(8,128)S(1)}, f32[40,128]{1,0:T(8,128)S(1)}, u32[]{:S(2)}, u32[]{:S(2)}) collective-permute-start(f32[40,128]{1,0:T(8,128)S(1)} %add.19.sum_ref), channel_id=1, source_target_pairs={{0,1},{3,2},{4,5},{7,6},{8,9},{11,10},{12,13},{15,14},{16,17},{19,... | collective-permute-start | bytes 61448 | tf_op jit(solution)/shard_map/ppermute | solution.py:480

commit v7 on v6

--- a/solution.py
+++ b/solution.py
@@ -266,7 +266,7 @@
 
 def spectrum_kernel(part_ref, theta_ref, column_ref, rows_ref, out_ref):
     across = columns_of(jnp.tanh(mask_steep * theta_ref[...]), column_ref)
-    even, odd = spectrum_of(across, rows_ref[0])
+    even, odd = spectrum_of(across, rows_ref[part_of(part_ref)])
     out_ref[0] = even
     out_ref[1] = odd
 
@@ -276,7 +276,7 @@
     turned = pltpu.roll(rim, FB, 1)
     first = lax.broadcasted_iota(jnp.int32, rim.shape, 1) < FB
     across = jnp.concatenate([jnp.where(first, rim, turned), jnp.where(first, turned, -rim)], axis=1)
-    even, odd = spectrum_of(across, rows_ref[0])
+    even, odd = spectrum_of(across, rows_ref[part_of(part_ref)])
     out_ref[0] = pack(even + spectrum_ref[0], odd + spectrum_ref[1])
 
 
@@ -335,7 +335,8 @@
         high, low = split(jnp.concatenate(parts, axis=1))
         folded[kern] = jnp.concatenate([high, high, low], axis=0)
     total[...] = jnp.zeros_like(total)
-    signs[...] = 1.0 - 2.0 * target_ref[...].astype(F32)
+    own = pl.ds(pl.multiple_of(part_of(part_ref) * ROWS, ROWS), ROWS)
+    signs[...] = 1.0 - 2.0 * target_ref[:, own].astype(F32)
 
     def expose(cond, carry):
         intensity = None
@@ -408,7 +409,7 @@
     part = part_of(part_ref)
     mask = jnp.tanh(mask_steep * theta_ref[...])
     scale = mask_steep * (1.0 - mask * mask)
-    gradient = image_rows(sum_ref[...], rows_ref[0], turned_ref) * scale
+    gradient = image_rows(sum_ref[...], rows_ref[part], turned_ref) * scale
     out_ref[...] = gradient
     last = part == PARTS - 1
     edge_ref[...] = jnp.where(last, gradient[ROWS - HALO :], gradient[:HALO])
@@ -416,7 +417,7 @@
 
 
 def edge_kernel(part_ref, gradient_hbm, edge_ref, scale_ref, near_ref, turned_ref, rows_ref, out_hbm, stage, sem):
-    rim = image_rows(near_ref[...], rows_ref[0], turned_ref) * scale_ref[...]
+    rim = image_rows(near_ref[...], rows_ref[part_of(part_ref)], turned_ref) * scale_ref[...]
     stage[...] = edge_ref[...] + jnp.where(has_adjoint_halo(part_ref), rim, 0.0)
     copy = pltpu.make_async_copy(stage, out_hbm.at[pl.ds(edge_start(part_ref), HALO)], sem)
     copy.start()
@@ -424,13 +425,8 @@
 
 
 def whole_spec(array):
-    rank = len(array.shape)
-    return pl.BlockSpec(array.shape, lambda i, *refs: (0,) * rank)
-
-
-def part_spec(array):
-    rank = len(array.shape)
-    return pl.BlockSpec((1,) + array.shape[1:], lambda i, part, *refs: (part_of(part),) + (0,) * (rank - 1))
+    del array
+    return pl.BlockSpec(memory_space=pltpu.VMEM)
 
 
 def call(kernel, scalars, operands, specs, out_shapes, scratch=(), name=None, flops=1 << 28, out_specs=None, aliases=None):
@@ -528,7 +524,7 @@
         spectrum_kernel,
         (parts,),
         (theta, table["column"], table["spectrum_rows"]),
-        [whole_spec(theta), whole_spec(table["column"]), part_spec(table["spectrum_rows"])],
+        [whole_spec(theta), whole_spec(table["column"]), whole_spec(table["spectrum_rows"])],
         floats(2, FA, 2 * FB),
         name="own_spectrum",
         flops=1 << 31,
@@ -538,7 +534,7 @@
         rim_kernel,
         (parts,),
         (spectrum, rim, table["rim_rows"]),
-        [whole_spec(spectrum), whole_spec(rim), part_spec(table["rim_rows"])],
+        [whole_spec(spectrum), whole_spec(rim), whole_spec(table["rim_rows"])],
         floats(1, FA, 2 * FB),
         name="add_rim",
     )
@@ -551,7 +547,7 @@
             whole_spec(mixed),
             whole_spec(mixed),
             whole_spec(shares),
-            pl.BlockSpec((TP, ROWS), lambda i, part, *refs: (0, part_of(part))),
+            whole_spec(target),
             whole_spec(forward),
             whole_spec(backward),
             whole_spec(table["row"]),
@@ -584,9 +580,14 @@
             whole_spec(theta),
             whole_spec(adjoint),
             whole_spec(table["turned"]),
-            part_spec(table["own_rows"]),
+            whole_spec(table["own_rows"]),
         ],
         [floats(ROWS, TP), floats(HALO, TP), floats(HALO, TP)],
+        out_specs=[
+            pl.BlockSpec((ROWS, TP), lambda i, *refs: (0, 0)),
+            whole_spec(adjoint),
+            whole_spec(adjoint),
+        ],
         name="own_gradient",
         flops=1 << 31,
     )
@@ -600,7 +601,7 @@
             whole_spec(scale),
             whole_spec(near),
             whole_spec(table["turned"]),
-            part_spec(table["halo_rows"]),
+            whole_spec(table["halo_rows"]),
         ],
         floats(ROWS, TP),
         scratch=(pltpu.VMEM((HALO, TP), F32), pltpu.SemaphoreType.DMA),

time: 29.4 us -> 29.4 us (level)
  no operation moved by 1% of the time
where the time goes in v7:
time: 29.4 us; the launch traced here: 28.8 us
  waiting for transfers between devices  12.5 us (43%)
  Pallas kernels  12.2 us (41%)
  starting transfers between devices  3.88 us (13%)
    pallas_call x7, Pallas kernels, call(): pl.pallas_call(kernel, grid_spec=pltpu.PrefetchScalarGridSpec(num_scalar_...  12.2 us
    ppermute x5, waiting for transfers between devices, partner(): return lax.ppermute(value, 'cond', [(i, i ^ step) for i in range(PARTS)])  9.81 us
    ppermute x2, waiting for transfers between devices, across(): return lax.ppermute(value, ('tile', 'cond'), pairs)  2.69 us
    ppermute x5, starting transfers between devices, partner(): return lax.ppermute(value, 'cond', [(i, i ^ step) for i in range(PARTS)])  2.25 us
    ppermute x2, starting transfers between devices, across(): return lax.ppermute(value, ('tile', 'cond'), pairs)  1.63 us
  transfers between devices with their start and end apart: 7, of which 5 were waited for; matrix products, arithmetic and copies ran while one was open for 0% of the time, Pallas kernels for 13%

profile of v7, /device:TPU:24, one launch (start us, length us, event | category | flops | bytes accessed | tf_op | source)
XLA Modules:
  0.0 28.8 jit_solution(3206051834003102486)
XLA Ops:
  0.0 1.2 %edge_columns.1 = f32[32,128]{1,0:T(8,128)S(1)} custom-call(s32[1]{0:T(128)} %bitcast.part_ref, f32[128,512]{1,0:T(8,128)} %theta_ref.3, bf16[2,512,128]{2,1,0:T(8,128)(2,1)} %constant.44.clone.waves_hbm), custom_call_target="tpu_custom_call" | custom-call | flops 268435456 | bytes 1048576 | tf_op jit(solution)/shard_map/edge_columns/pallas_call | solution.py:436
  1.2 1.5 %collective-permute-start.1 = (f32[32,128]{1,0:T(8,128)S(1)}, f32[32,128]{1,0:T(8,128)S(1)}, u32[]{:S(2)}, u32[]{:S(2)}) collective-permute-start(f32[32,128]{1,0:T(8,128)S(1)} %edge_columns.1), channel_id=1, source_target_pairs={{1,2},{2,1},{5,6},{6,5},{9,10},{10,9},{13,14},{14,13},{17,18},{18,... | collective-permute-start | bytes 49160 | tf_op jit(solution)/shard_map/ppermute | solution.py:476
  2.7 0.0 copy-start.3
  2.7 0.0 copy-start.5
  2.7 0.0 copy-start.7
  2.7 1.7 %open_parts.1 = (f32[8,40,128]{2,1,0:T(8,128)S(1)}, f32[8,128]{1,0:T(8,128)S(1)}, bf16[384,256]{1,0:T(8,128)(2,1)S(1)}, bf16[384,256]{1,0:T(8,128)(2,1)S(1)}) custom-call(s32[1]{0:T(128)} %bitcast.part_ref, f32[2,65,2,65]{3,2,1,0:T(2,128)} %bitcast.3, f32[2,65,2,65]{3,2,1,0:T(2,128)} %bitcast.4, f32[2]{0:T(128)} %thresholds_hbm.1, s32[8]{0:T(128)} %weights_hbm.1, ...), custom_call_target="tpu_custom_call" | custom-call | flops 268435456 | bytes 1048576 | tf_op jit(solution)/shard_map/open_parts/pallas_call | solution.py:436
  4.4 0.0 copy-start.9
  4.4 0.8 %collective-permute-start = (f32[8,40,128]{2,1,0:T(8,128)S(1)}, f32[8,40,128]{2,1,0:T(8,128)S(1)}, u32[]{:S(2)}, u32[]{:S(2)}) collective-permute-start(f32[8,40,128]{2,1,0:T(8,128)S(1)} %get-tuple-element.12), channel_id=1, source_target_pairs={{0,3},{1,2},{2,1},{3,0},{4,7},{5,6},{6,5},{7,4},{8,11},{9,10},{10,... | collective-permute-start | bytes 491528 | tf_op jit(solution)/shard_map/ppermute | solution.py:479
  5.2 0.0 copy-done.3
  5.2 0.0 copy-done.5
  5.2 0.0 copy-done.7
  5.2 0.5 %own_spectrum.1.spectrum_ref = f32[2,40,128]{2,1,0:T(8,128)S(1)} custom-call(s32[1]{0:T(128)} %bitcast.part_ref, f32[128,512]{1,0:T(8,128)S(1)} %copy-done.3, bf16[2,512,256]{2,1,0:T(8,128)(2,1)S(1)} %copy-done.5, bf16[4,80,384]{2,1,0:T(8,128)(2,1)S(1)} %copy-done.7), custom_call_target="tpu_custom_call" | custom-call | flops 2147483648 | bytes 1048576 | tf_op jit(solution)/shard_map/own_spectrum/pallas_call | solution.py:436
  5.7 0.0 copy-start.2
  5.7 0.0 collective-permute-done.1.rim_ref
  5.7 0.0 copy-done.9
  5.8 0.3 %add_rim.1 = f32[1,40,128]{2,1,0:T(8,128)S(1)} custom-call(s32[1]{0:T(128)} %bitcast.part_ref, f32[2,40,128]{2,1,0:T(8,128)S(1)} %own_spectrum.1.spectrum_ref, f32[32,128]{1,0:T(8,128)S(1)} %collective-permute-done.1.rim_ref, bf16[4,80,96]{2,1,0:T(8,128)(2,1)S(1)} %copy-done.9), custom_call_target="tpu_custom_call" | custom-call | flops 268435456 | bytes 1048576 | tf_op jit(solution)/shard_map/add_rim/pallas_call | solution.py:436
  6.1 1.0 %collective-permute-start.2 = (f32[1,40,128]{2,1,0:T(8,128)S(1)}, f32[1,40,128]{2,1,0:T(8,128)S(1)}, u32[]{:S(2)}, u32[]{:S(2)}) collective-permute-start(f32[1,40,128]{2,1,0:T(8,128)S(1)} %add_rim.1), channel_id=1, source_target_pairs={{0,3},{1,2},{2,1},{3,0},{4,7},{5,6},{6,5},{7,4},{8,11},{9,10},{10,... | collective-permute-start | bytes 61448 | tf_op jit(solution)/shard_map/ppermute | solution.py:479
  7.1 4.0 %collective-permute-done.2 = f32[1,40,128]{2,1,0:T(8,128)S(1)} collective-permute-done((f32[1,40,128]{2,1,0:T(8,128)S(1)}, f32[1,40,128]{2,1,0:T(8,128)S(1)}, u32[]{:S(2)}, u32[]{:S(2)}) %collective-permute-start.2) | collective-permute-done | bytes 20512 | tf_op jit(solution)/shard_map/ppermute | solution.py:479
  11.1 0.0 copy-start.6
  11.1 0.0 copy-start.8
  11.1 0.0 collective-permute-done
  11.2 0.2 collective-permute-start.3
  11.3 1.5 %collective-permute-done.3.other_ref = f32[17,40,128]{2,1,0:T(8,128)S(1)} collective-permute-done((f32[17,40,128]{2,1,0:T(8,128)S(1)}, f32[17,40,128]{2,1,0:T(8,128)S(1)}, u32[]{:S(2)}, u32[]{:S(2)}) %collective-permute-start.3) | collective-permute-done | bytes 348192 | tf_op jit(solution)/shard_map/ppermute | solution.py:479
  12.9 0.0 copy-done.2
  12.9 0.0 copy-done.6
  12.9 0.0 copy-done.8
  12.9 0.0 copy-start
  12.9 0.0 copy-start.4
  12.9 6.2 %coherent_fields.1 = f32[40,128]{1,0:T(8,128)S(1)} custom-call(s32[1]{0:T(128)} %bitcast.part_ref, f32[17,40,128]{2,1,0:T(8,128)S(1)} %pad_maximum_fusion.mixed_ref, f32[17,40,128]{2,1,0:T(8,128)S(1)} %collective-permute-done.3.other_ref, f32[8,128]{1,0:T(8,128)S(1)} %get-tuple-element.13.shares_ref, s32[512,512]{1,0:T(8,128)S(1)} %copy-done.2, ...), custom_call_target="tpu_custom_call" | custom-call | flops 8589934592 | bytes 1048576 | tf_op jit(solution)/shard_map/coherent_fields/pallas_call | solution.py:436
  19.1 0.2 collective-permute-start.4
  19.3 1.1 %collective-permute-done.4 = f32[40,128]{1,0:T(8,128)S(1)} collective-permute-done((f32[40,128]{1,0:T(8,128)S(1)}, f32[40,128]{1,0:T(8,128)S(1)}, u32[]{:S(2)}, u32[]{:S(2)}) %collective-permute-start.4) | collective-permute-done | bytes 20512 | tf_op jit(solution)/shard_map/ppermute | solution.py:479
  20.4 0.0 collective-permute-start.5
  20.4 3.2 %collective-permute-done.5 = f32[40,128]{1,0:T(8,128)S(1)} collective-permute-done((f32[40,128]{1,0:T(8,128)S(1)}, f32[40,128]{1,0:T(8,128)S(1)}, u32[]{:S(2)}, u32[]{:S(2)}) %collective-permute-start.5) | collective-permute-done | bytes 20512 | tf_op jit(solution)/shard_map/ppermute | solution.py:479
  23.6 0.0 copy-start.1
  23.6 0.2 collective-permute-start.6
  23.8 0.0 copy-done
  23.8 0.0 copy-done.4
  23.8 1.2 %own_gradient.1 = (f32[128,512]{1,0:T(8,128)}, f32[32,512]{1,0:T(8,128)S(1)}, f32[32,512]{1,0:T(8,128)S(1)}) custom-call(s32[1]{0:T(128)} %bitcast.part_ref, f32[128,512]{1,0:T(8,128)S(1)} %copy-done.3, f32[40,128]{1,0:T(8,128)S(1)} %add.19.sum_ref, bf16[2,256,512]{2,1,0:T(8,128)(2,1)S(1)} %copy-done, bf16[4,256,240]{2,1,0:T(8,128)(2,1)S(1)} %copy-done.4), custom_call_target="tpu_custom_call" | custom-call | flops 2147483648 | bytes 1048576 | tf_op jit(solution)/shard_map/own_gradient/pallas_call | solution.py:436
  25.0 2.7 %collective-permute-done.6.near_ref = f32[40,128]{1,0:T(8,128)S(1)} collective-permute-done((f32[40,128]{1,0:T(8,128)S(1)}, f32[40,128]{1,0:T(8,128)S(1)}, u32[]{:S(2)}, u32[]{:S(2)}) %collective-permute-start.6) | collective-permute-done | bytes 20512 | tf_op jit(solution)/shard_map/ppermute | solution.py:476
  27.7 0.0 copy-done.1
  27.7 1.1 %edge_gradient.1 = f32[128,512]{1,0:T(8,128)} custom-call(s32[1]{0:T(128)} %bitcast.part_ref, f32[128,512]{1,0:T(8,128)} %get-tuple-element.16.gradient_hbm, f32[32,512]{1,0:T(8,128)S(1)} %get-tuple-element.17.edge_ref, f32[32,512]{1,0:T(8,128)S(1)} %get-tuple-element.18.scale_ref, ...), custom_call_target="tpu_custom_call", output_to_operand_aliasing={{}: (1, {})} | custom-call | flops 268435456 | bytes 1048576 | tf_op jit(solution)/shard_map/edge_gradient/pallas_call | solution.py:436
  (4 shorter events, 0.0 us)
Async XLA Ops:
  1.2 4.5 %collective-permute-start.1 = (f32[32,128]{1,0:T(8,128)S(1)}, f32[32,128]{1,0:T(8,128)S(1)}, u32[]{:S(2)}, u32[]{:S(2)}) collective-permute-start(f32[32,128]{1,0:T(8,128)S(1)} %edge_columns.1), channel_id=1, source_target_pairs={{1,2},{2,1},{5,6},{6,5},{9,10},{10,9},{13,14},{14,13},{17,18},{18,... | collective-permute-start | bytes 49160 | tf_op jit(solution)/shard_map/ppermute | solution.py:476
  2.7 2.6 %copy-start.3 = (f32[128,512]{1,0:T(8,128)S(1)}, f32[128,512]{1,0:T(8,128)}, u32[]{:S(2)}) copy-start(f32[128,512]{1,0:T(8,128)} %theta_ref.3) | copy-start | bytes 786436
  2.7 2.6 %copy-start.5 = (bf16[2,512,256]{2,1,0:T(8,128)(2,1)S(1)}, bf16[2,512,256]{2,1,0:T(8,128)(2,1)}, u32[]{:S(2)}) copy-start(bf16[2,512,256]{2,1,0:T(8,128)(2,1)} %constant.43.clone.column_ref) | copy-start | bytes 1572868
  2.7 2.6 %copy-start.7 = (bf16[4,80,384]{2,1,0:T(8,128)(2,1)S(1)}, bf16[4,80,384]{2,1,0:T(8,128)(2,1)}, u32[]{:S(2)}) copy-start(bf16[4,80,384]{2,1,0:T(8,128)(2,1)} %constant.45.clone.rows_ref) | copy-start | bytes 737284
  4.4 1.4 %copy-start.9 = (bf16[4,80,96]{2,1,0:T(8,128)(2,1)S(1)}, bf16[4,80,96]{2,1,0:T(8,128)(2,1)}, u32[]{:S(2)}) copy-start(bf16[4,80,96]{2,1,0:T(8,128)(2,1)} %constant.47.clone.rows_ref) | copy-start | bytes 184324
  4.4 6.7 %collective-permute-start = (f32[8,40,128]{2,1,0:T(8,128)S(1)}, f32[8,40,128]{2,1,0:T(8,128)S(1)}, u32[]{:S(2)}, u32[]{:S(2)}) collective-permute-start(f32[8,40,128]{2,1,0:T(8,128)S(1)} %get-tuple-element.12), channel_id=1, source_target_pairs={{0,3},{1,2},{2,1},{3,0},{4,7},{5,6},{6,5},{7,4},{8,11},{9,10},{10,... | collective-permute-start | bytes 491528 | tf_op jit(solution)/shard_map/ppermute | solution.py:479
  5.7 7.2 %copy-start.2 = (s32[512,512]{1,0:T(8,128)S(1)}, s32[512,512]{1,0:T(8,128)}, u32[]{:S(2)}) copy-start(s32[512,512]{1,0:T(8,128)} %target_ref.1) | copy-start | bytes 3145732
  6.1 5.0 %collective-permute-start.2 = (f32[1,40,128]{2,1,0:T(8,128)S(1)}, f32[1,40,128]{2,1,0:T(8,128)S(1)}, u32[]{:S(2)}, u32[]{:S(2)}) collective-permute-start(f32[1,40,128]{2,1,0:T(8,128)S(1)} %add_rim.1), channel_id=1, source_target_pairs={{0,3},{1,2},{2,1},{3,0},{4,7},{5,6},{6,5},{7,4},{8,11},{9,10},{10,... | collective-permute-start | bytes 61448 | tf_op jit(solution)/shard_map/ppermute | solution.py:479
  11.1 1.8 %copy-start.6 = (bf16[512,240]{1,0:T(8,128)(2,1)S(1)}, bf16[512,240]{1,0:T(8,128)(2,1)}, u32[]{:S(2)}) copy-start(bf16[512,240]{1,0:T(8,128)(2,1)} %constant.52.clone.row_ref) | copy-start | bytes 737284
  11.1 1.8 %copy-start.8 = (bf16[160,512]{1,0:T(8,128)(2,1)S(1)}, bf16[160,512]{1,0:T(8,128)(2,1)}, u32[]{:S(2)}) copy-start(bf16[160,512]{1,0:T(8,128)(2,1)} %constant.53.clone.row_turned_ref) | copy-start | bytes 491524
  11.2 1.7 %collective-permute-start.3 = (f32[17,40,128]{2,1,0:T(8,128)S(1)}, f32[17,40,128]{2,1,0:T(8,128)S(1)}, u32[]{:S(2)}, u32[]{:S(2)}) collective-permute-start(f32[17,40,128]{2,1,0:T(8,128)S(1)} %pad_maximum_fusion.mixed_ref), channel_id=1, source_target_pairs={{0,1},{1,0},{2,3},{3,2},{4,5},{5,4},{6,7},{7,6},{8,9},{9,8},{10,11... | collective-permute-start | bytes 1044488 | tf_op jit(solution)/shard_map/ppermute | solution.py:479
  12.9 10.9 %copy-start = (bf16[2,256,512]{2,1,0:T(8,128)(2,1)S(1)}, bf16[2,256,512]{2,1,0:T(8,128)(2,1)}, u32[]{:S(2)}) copy-start(bf16[2,256,512]{2,1,0:T(8,128)(2,1)} %constant.51.clone.turned_ref) | copy-start | bytes 1572868
  12.9 10.9 %copy-start.4 = (bf16[4,256,240]{2,1,0:T(8,128)(2,1)S(1)}, bf16[4,256,240]{2,1,0:T(8,128)(2,1)}, u32[]{:S(2)}) copy-start(bf16[4,256,240]{2,1,0:T(8,128)(2,1)} %constant.46.clone.rows_ref) | copy-start | bytes 1474564
  19.1 1.3 %collective-permute-start.4 = (f32[40,128]{1,0:T(8,128)S(1)}, f32[40,128]{1,0:T(8,128)S(1)}, u32[]{:S(2)}, u32[]{:S(2)}) collective-permute-start(f32[40,128]{1,0:T(8,128)S(1)} %coherent_fields.1), channel_id=1, source_target_pairs={{0,1},{1,0},{2,3},{3,2},{4,5},{5,4},{6,7},{7,6},{8,9},{9,8},{10,11... | collective-permute-start | bytes 61448 | tf_op jit(solution)/shard_map/ppermute | solution.py:479
  20.4 3.2 %collective-permute-start.5 = (f32[40,128]{1,0:T(8,128)S(1)}, f32[40,128]{1,0:T(8,128)S(1)}, u32[]{:S(2)}, u32[]{:S(2)}) collective-permute-start(f32[40,128]{1,0:T(8,128)S(1)} %add.18), channel_id=1, source_target_pairs={{0,3},{1,2},{2,1},{3,0},{4,7},{5,6},{6,5},{7,4},{8,11},{9,10},{10,... | collective-permute-start | bytes 61448 | tf_op jit(solution)/shard_map/ppermute | solution.py:479
  23.6 4.1 %copy-start.1 = (bf16[4,64,240]{2,1,0:T(8,128)(2,1)S(1)}, bf16[4,64,240]{2,1,0:T(8,128)(2,1)}, u32[]{:S(2)}) copy-start(bf16[4,64,240]{2,1,0:T(8,128)(2,1)} %constant.48.clone.rows_ref) | copy-start | bytes 368644
  23.6 4.1 %collective-permute-start.6 = (f32[40,128]{1,0:T(8,128)S(1)}, f32[40,128]{1,0:T(8,128)S(1)}, u32[]{:S(2)}, u32[]{:S(2)}) collective-permute-start(f32[40,128]{1,0:T(8,128)S(1)} %add.19.sum_ref), channel_id=1, source_target_pairs={{0,1},{3,2},{4,5},{7,6},{8,9},{11,10},{12,13},{15,14},{16,17},{19,... | collective-permute-start | bytes 61448 | tf_op jit(solution)/shard_map/ppermute | solution.py:476

commit v8 on v7

--- a/solution.py
+++ b/solution.py
@@ -186,12 +186,6 @@
     local_conds = real_ref.shape[0]
     mats = local_conds * KERNELS * 2
     stage[...] = jnp.zeros_like(stage)
-    for copy in copies[:4]:
-        copy.wait()
-    for cond in range(local_conds):
-        for kern in range(KERNELS):
-            for piece, ref in enumerate((real_ref, imag_ref)):
-                stage[(cond * KERNELS + kern) * 2 + piece, :KSUP, :KSUP] = ref[cond, :, kern, :]
     rows = stage.shape[1]
     source = lax.broadcasted_iota(jnp.int32, (2 * FB, 4 * FB), 0)
     target = lax.broadcasted_iota(jnp.int32, (2 * FB, 4 * FB), 1)
@@ -201,8 +195,6 @@
     freq = jnp.where(lane < HALF, lane + 1, 0)
     used = (lane < HALF) | ((lane == HALF) & (block % 2 == 0))
     pick = (used & (source == jnp.where(plus, HALF + freq, HALF - freq))).astype(F32).astype(BF)
-    high, low = split(stage[...].reshape(mats * rows, 2 * FB))
-    picked = [dot(piece, pick) for piece in (high, low)]
     source = lax.broadcasted_iota(jnp.int32, (FA, 2 * rows), 1) % rows
     target = lax.broadcasted_iota(jnp.int32, (FA, 2 * rows), 0)
     turn = ((source == HALF - target) & (target <= HALF)).astype(F32).astype(BF)
@@ -213,6 +205,14 @@
     keep_top = jnp.where(valid, scale, 0.0)
     keep_bottom = jnp.where((row == 0) & (lane == HALF), 0.0, keep_top)
     first = lane % FB < HALF
+    for copy in copies[:4]:
+        copy.wait()
+    for cond in range(local_conds):
+        for kern in range(KERNELS):
+            for piece, ref in enumerate((real_ref, imag_ref)):
+                stage[(cond * KERNELS + kern) * 2 + piece, :KSUP, :KSUP] = ref[cond, :, kern, :]
+    high, low = split(stage[...].reshape(mats * rows, 2 * FB))
+    picked = [dot(piece, pick) for piece in (high, low)]
     extra = jnp.zeros((FA, 2 * FB), F32)
     blocks = []
     for kern in range(local_conds * KERNELS):
@@ -280,45 +280,76 @@
     out_ref[0] = pack(even + spectrum_ref[0], odd + spectrum_ref[1])
 
 
+def unpack_group(ref, put):
+    lane, row = lanes_and_rows()
+    zero_lane = (lane == HALF) & (row <= HALF)
+    extra = [ref[i][HALF + 1 :] for i in range(SPARE_BLOCKS)]
+    extra = jnp.concatenate(extra + [jnp.zeros((FA - SPARE * SPARE_BLOCKS, 2 * FB), F32)], axis=0)
+    for kern in range(ref.shape[0] // 2):
+        values = []
+        for which in range(2):
+            packed = ref[2 * kern + which]
+            for part, value in enumerate((packed, pltpu.roll(packed, 2 * FB - HALF, 1))):
+                place = kern * 4 + which * 2 + part
+                zeroth = pltpu.roll(extra, (HALF - place) % (2 * FB), 1)
+                values.append(jnp.where(zero_lane, zeroth, value))
+        put(kern, values)
+
+
+def near_kernels_kernel(part_ref, mixed_ref, target_ref, near_ref, signs_ref):
+    local = near_ref.shape[0] // 2
+    for group in range(2):
+        def put(kern, values, group=group):
+            for i, value in enumerate(values):
+                near_ref[group * local + kern, i] = value
+
+        unpack_group(mixed_ref.at[pl.ds(group * 2 * local, 2 * local)], put)
+    own = pl.ds(pl.multiple_of(part_of(part_ref) * ROWS, ROWS), ROWS)
+    signs_ref[...] = 1.0 - 2.0 * target_ref[:, own].astype(F32)
+
+
 def fields_kernel(
-    part_ref, mixed_ref, other_ref, shares_ref, target_ref, forward_ref, backward_ref, row_ref,
-    row_turned_ref, out_ref, kernels_ref, levels_ref, lines, folded, amps, tanhs, total, signs, turned, backs,
+    part_ref, mixed_ref, other_ref, near_ref, signs, shares_ref, forward_ref, backward_ref, row_ref,
+    row_turned_ref, out_ref, far_ref, levels_ref, lines, folded, amps, tanhs, total, turned, backs,
 ):
-    count = kernels_ref.shape[0]
+    count = 2 * far_ref.shape[0]
     local = count // PARTS
     tall = 4 * FA
     each = 2 * local
     even, odd = unpack(mixed_ref[2 * each] + other_ref[2 * each])
-    lane, row = lanes_and_rows()
-    zero_lane = (lane == HALF) & (row <= HALF)
+
+    def put_line(kern, values):
+        he_real, he_imag, ho_real, ho_imag = values
+        start = kern * tall
+        for i, value in enumerate(
+            (
+                even * he_real + odd * ho_imag,
+                odd * he_real - even * ho_imag,
+                even * he_imag - odd * ho_real,
+                odd * he_imag + even * ho_real,
+            )
+        ):
+            lines[start + i * FA : start + (i + 1) * FA] = value
+
+    def arrays_of(kern):
+        ref = near_ref if kern < count // 2 else far_ref
+        return [ref[kern % (count // 2), i] for i in range(4)]
+
     for group in range(PARTS):
         ref = (mixed_ref, other_ref)[group // 2].at[pl.ds(group % 2 * each, each)]
-        extra = [ref[i][HALF + 1 :] for i in range(SPARE_BLOCKS)]
-        extra = jnp.concatenate(extra + [jnp.zeros((FA - SPARE * SPARE_BLOCKS, 2 * FB), F32)], axis=0)
         for i in range(CONDS // PARTS):
             place = group * (CONDS // PARTS) + i
             levels_ref[place : place + 1] = ref[SPARE_BLOCKS + i][FA - 1 :]
-        for kern in range(local):
-            values = []
-            for which in range(2):
-                packed = ref[2 * kern + which]
-                for part, value in enumerate((packed, pltpu.roll(packed, 2 * FB - HALF, 1))):
-                    place = kern * 4 + which * 2 + part
-                    zeroth = pltpu.roll(extra, (HALF - place) % (2 * FB), 1)
-                    value = jnp.where(zero_lane, zeroth, value)
-                    kernels_ref[group * local + kern, which * 2 + part] = value
-                    values.append(value)
-            he_real, he_imag, ho_real, ho_imag = values
-            start = (group * local + kern) * tall
-            for i, value in enumerate(
-                (
-                    even * he_real + odd * ho_imag,
-                    odd * he_real - even * ho_imag,
-                    even * he_imag - odd * ho_real,
-                    odd * he_imag + even * ho_real,
-                )
-            ):
-                lines[start + i * FA : start + (i + 1) * FA] = value
+        if group < 2:
+            for kern in range(group * local, (group + 1) * local):
+                put_line(kern, arrays_of(kern))
+        else:
+            def put(kern, values, group=group):
+                for i, value in enumerate(values):
+                    far_ref[(group - 2) * local + kern, i] = value
+                put_line(group * local + kern, values)
+
+            unpack_group(ref, put)
 
     high, low = split(lines[...])
     lines_folded = dot(jnp.concatenate([high, low], axis=1), forward_ref[: 4 * FB]) + dot(high, forward_ref[4 * FB :])
@@ -335,8 +366,6 @@
         high, low = split(jnp.concatenate(parts, axis=1))
         folded[kern] = jnp.concatenate([high, high, low], axis=0)
     total[...] = jnp.zeros_like(total)
-    own = pl.ds(pl.multiple_of(part_of(part_ref) * ROWS, ROWS), ROWS)
-    signs[...] = 1.0 - 2.0 * target_ref[:, own].astype(F32)
 
     def expose(cond, carry):
         intensity = None
@@ -387,7 +416,7 @@
                 )
             )
         (x_real, y_real), (x_imag, y_imag) = grads
-        he_real, he_imag, ho_real, ho_imag = (kernels_ref[kern, i] for i in range(4))
+        he_real, he_imag, ho_real, ho_imag = arrays_of(kern)
         sum_even = sum_even + x_real * he_real + x_imag * he_imag - y_real * ho_imag + y_imag * ho_real
         sum_odd = sum_odd + x_real * ho_imag - x_imag * ho_real + y_real * he_real + y_imag * he_imag
     out_ref[...] = pack(sum_even, sum_odd)
@@ -417,11 +446,13 @@
 
 
 def edge_kernel(part_ref, gradient_hbm, edge_ref, scale_ref, near_ref, turned_ref, rows_ref, out_hbm, stage, sem):
-    rim = image_rows(near_ref[...], rows_ref[part_of(part_ref)], turned_ref) * scale_ref[...]
-    stage[...] = edge_ref[...] + jnp.where(has_adjoint_halo(part_ref), rim, 0.0)
-    copy = pltpu.make_async_copy(stage, out_hbm.at[pl.ds(edge_start(part_ref), HALO)], sem)
-    copy.start()
-    copy.wait()
+    @pl.when(has_adjoint_halo(part_ref))
+    def _():
+        rim = image_rows(near_ref[...], rows_ref[part_of(part_ref)], turned_ref)
+        stage[...] = edge_ref[...] + rim * scale_ref[...]
+        copy = pltpu.make_async_copy(stage, out_hbm.at[pl.ds(edge_start(part_ref), HALO)], sem)
+        copy.start()
+        copy.wait()
 
 
 def whole_spec(array):
@@ -539,15 +570,27 @@
         name="add_rim",
     )
     mixed = jnp.concatenate([own, side, spectrum + partner(spectrum, 3)], axis=0)
+    near_kernels, signs = call(
+        near_kernels_kernel,
+        (parts,),
+        (mixed, target),
+        [whole_spec(mixed), whole_spec(target)],
+        [floats(count // 2, 4, FA, 2 * FB), floats(TP, ROWS)],
+        name="near_kernels",
+        flops=1 << 30,
+    )
     adjoint = call(
         fields_kernel,
         (parts,),
-        (mixed, partner(mixed, 1), shares, target, forward, backward, table["row"], table["row_turned"]),
+        (
+            mixed, partner(mixed, 1), near_kernels, signs, shares, forward, backward, table["row"], table["row_turned"],
+        ),
         [
             whole_spec(mixed),
             whole_spec(mixed),
+            whole_spec(near_kernels),
+            whole_spec(signs),
             whole_spec(shares),
-            whole_spec(target),
             whole_spec(forward),
             whole_spec(backward),
             whole_spec(table["row"]),
@@ -555,13 +598,12 @@
         ],
         floats(FA, 2 * FB),
         scratch=(
-            pltpu.VMEM((count, 4, FA, 2 * FB), F32),
+            pltpu.VMEM((count // 2, 4, FA, 2 * FB), F32),
             pltpu.VMEM((CONDS, ROWS), F32),
             pltpu.VMEM((count * 4 * FA, 2 * FB), F32),
             pltpu.VMEM((count, 6 * FA, 2 * ROWS), BF),
             pltpu.VMEM((count, TP, 2 * ROWS), F32),
             pltpu.VMEM((CONDS, TP, ROWS), F32),
-            pltpu.VMEM((TP, ROWS), F32),
             pltpu.VMEM((TP, ROWS), F32),
             pltpu.VMEM((count * 2, 2 * FA, ROWS), F32),
             pltpu.VMEM((count * 4 * FA, 4 * FB), F32),

time: 29.4 us -> 29 us (0.986); the launches traced: 28.8 us -> 28.8 us
  Pallas kernels: 12.2 us -> 12.5 us
  waiting for transfers between devices: 12.5 us -> 12.2 us
    ppermute x5, waiting for transfers between devices: 9.81 us -> 9.47 us  [partner(): return lax.ppermute(value, 'cond', [(i, i ^ step) for i in range(PARTS)])]
    pallas_call x7 -> x8, Pallas kernels: 12.2 us -> 12.5 us  [call(): pl.pallas_call(kernel, grid_spec=pltpu.PrefetchScalarGridSpec(num_scalar_...]
  transfers between devices with their start and end apart: 7 -> 7, of which waited for: 5 -> 5; matrix products, arithmetic and copies ran while one was open for 0% -> 0% of each run, Pallas kernels for 13% -> 14%
where the time goes in v8:
time: 29 us; the launch traced here: 28.8 us
  Pallas kernels  12.5 us (43%)
  waiting for transfers between devices  12.2 us (42%)
  starting transfers between devices  3.89 us (13%)
    pallas_call x8, Pallas kernels, call(): pl.pallas_call(kernel, grid_spec=pltpu.PrefetchScalarGridSpec(num_scalar_...  12.5 us
    ppermute x5, waiting for transfers between devices, partner(): return lax.ppermute(value, 'cond', [(i, i ^ step) for i in range(PARTS)])  9.47 us
    ppermute x2, waiting for transfers between devices, across(): return lax.ppermute(value, ('tile', 'cond'), pairs)  2.69 us
    ppermute x5, starting transfers between devices, partner(): return lax.ppermute(value, 'cond', [(i, i ^ step) for i in range(PARTS)])  2.26 us
    ppermute x2, starting transfers between devices, across(): return lax.ppermute(value, ('tile', 'cond'), pairs)  1.63 us
  transfers between devices with their start and end apart: 7, of which 5 were waited for; matrix products, arithmetic and copies ran while one was open for 0% of the time, Pallas kernels for 14%

profile of v8, /device:TPU:24, one launch (start us, length us, event | category | flops | bytes accessed | tf_op | source)
XLA Modules:
  0.0 28.8 jit_solution(10915091652199693907)
XLA Ops:
  0.0 1.2 %edge_columns.1 = f32[32,128]{1,0:T(8,128)S(1)} custom-call(s32[1]{0:T(128)} %bitcast.part_ref, f32[128,512]{1,0:T(8,128)} %theta_ref.3, bf16[2,512,128]{2,1,0:T(8,128)(2,1)} %constant.44.clone.waves_hbm), custom_call_target="tpu_custom_call" | custom-call | flops 268435456 | bytes 1048576 | tf_op jit(solution)/shard_map/edge_columns/pallas_call | solution.py:467
  1.2 1.5 %collective-permute-start.1 = (f32[32,128]{1,0:T(8,128)S(1)}, f32[32,128]{1,0:T(8,128)S(1)}, u32[]{:S(2)}, u32[]{:S(2)}) collective-permute-start(f32[32,128]{1,0:T(8,128)S(1)} %edge_columns.1), channel_id=1, source_target_pairs={{1,2},{2,1},{5,6},{6,5},{9,10},{10,9},{13,14},{14,13},{17,18},{18,... | collective-permute-start | bytes 49160 | tf_op jit(solution)/shard_map/ppermute | solution.py:507
  2.7 0.0 copy-start.3
  2.7 0.0 copy-start.5
  2.7 0.0 copy-start.7
  2.7 1.7 %open_parts.1 = (f32[8,40,128]{2,1,0:T(8,128)S(1)}, f32[8,128]{1,0:T(8,128)S(1)}, bf16[384,256]{1,0:T(8,128)(2,1)S(1)}, bf16[384,256]{1,0:T(8,128)(2,1)S(1)}) custom-call(s32[1]{0:T(128)} %bitcast.part_ref, f32[2,65,2,65]{3,2,1,0:T(2,128)} %bitcast.3, f32[2,65,2,65]{3,2,1,0:T(2,128)} %bitcast.4, f32[2]{0:T(128)} %thresholds_hbm.1, s32[8]{0:T(128)} %weights_hbm.1, ...), custom_call_target="tpu_custom_call" | custom-call | flops 268435456 | bytes 1048576 | tf_op jit(solution)/shard_map/open_parts/pallas_call | solution.py:467
  4.4 0.0 copy-start.9
  4.4 0.8 %collective-permute-start = (f32[8,40,128]{2,1,0:T(8,128)S(1)}, f32[8,40,128]{2,1,0:T(8,128)S(1)}, u32[]{:S(2)}, u32[]{:S(2)}) collective-permute-start(f32[8,40,128]{2,1,0:T(8,128)S(1)} %get-tuple-element.14), channel_id=1, source_target_pairs={{0,3},{1,2},{2,1},{3,0},{4,7},{5,6},{6,5},{7,4},{8,11},{9,10},{10,... | collective-permute-start | bytes 491528 | tf_op jit(solution)/shard_map/ppermute | solution.py:510
  5.2 0.0 copy-done.3
  5.2 0.0 copy-done.5
  5.2 0.0 copy-done.7
  5.2 0.5 %own_spectrum.1.spectrum_ref = f32[2,40,128]{2,1,0:T(8,128)S(1)} custom-call(s32[1]{0:T(128)} %bitcast.part_ref, f32[128,512]{1,0:T(8,128)S(1)} %copy-done.3, bf16[2,512,256]{2,1,0:T(8,128)(2,1)S(1)} %copy-done.5, bf16[4,80,384]{2,1,0:T(8,128)(2,1)S(1)} %copy-done.7), custom_call_target="tpu_custom_call" | custom-call | flops 2147483648 | bytes 1048576 | tf_op jit(solution)/shard_map/own_spectrum/pallas_call | solution.py:467
  5.7 0.0 copy-start.2
  5.7 0.0 collective-permute-done.1.rim_ref
  5.7 0.0 copy-done.9
  5.7 0.3 %add_rim.1 = f32[1,40,128]{2,1,0:T(8,128)S(1)} custom-call(s32[1]{0:T(128)} %bitcast.part_ref, f32[2,40,128]{2,1,0:T(8,128)S(1)} %own_spectrum.1.spectrum_ref, f32[32,128]{1,0:T(8,128)S(1)} %collective-permute-done.1.rim_ref, bf16[4,80,96]{2,1,0:T(8,128)(2,1)S(1)} %copy-done.9), custom_call_target="tpu_custom_call" | custom-call | flops 268435456 | bytes 1048576 | tf_op jit(solution)/shard_map/add_rim/pallas_call | solution.py:467
  6.0 1.0 %collective-permute-start.2 = (f32[1,40,128]{2,1,0:T(8,128)S(1)}, f32[1,40,128]{2,1,0:T(8,128)S(1)}, u32[]{:S(2)}, u32[]{:S(2)}) collective-permute-start(f32[1,40,128]{2,1,0:T(8,128)S(1)} %add_rim.1), channel_id=1, source_target_pairs={{0,3},{1,2},{2,1},{3,0},{4,7},{5,6},{6,5},{7,4},{8,11},{9,10},{10,... | collective-permute-start | bytes 61448 | tf_op jit(solution)/shard_map/ppermute | solution.py:510
  7.1 4.0 %collective-permute-done.2 = f32[1,40,128]{2,1,0:T(8,128)S(1)} collective-permute-done((f32[1,40,128]{2,1,0:T(8,128)S(1)}, f32[1,40,128]{2,1,0:T(8,128)S(1)}, u32[]{:S(2)}, u32[]{:S(2)}) %collective-permute-start.2) | collective-permute-done | bytes 20512 | tf_op jit(solution)/shard_map/ppermute | solution.py:510
  11.1 0.0 collective-permute-done
  11.1 0.0 copy-start.6
  11.2 0.0 copy-start.8
  11.2 0.2 collective-permute-start.3
  11.3 0.0 copy-done.2
  11.3 0.3 %near_kernels.1 = (f32[8,4,40,128]{3,2,1,0:T(8,128)S(1)}, f32[512,128]{1,0:T(8,128)S(1)}) custom-call(s32[1]{0:T(128)} %bitcast.part_ref, f32[17,40,128]{2,1,0:T(8,128)S(1)} %pad_maximum_fusion.mixed_ref, s32[512,512]{1,0:T(8,128)S(1)} %copy-done.2), custom_call_target="tpu_custom_call" | custom-call | flops 1073741824 | bytes 1048576 | tf_op jit(solution)/shard_map/near_kernels/pallas_call | solution.py:467
  11.7 1.2 %collective-permute-done.3.other_ref = f32[17,40,128]{2,1,0:T(8,128)S(1)} collective-permute-done((f32[17,40,128]{2,1,0:T(8,128)S(1)}, f32[17,40,128]{2,1,0:T(8,128)S(1)}, u32[]{:S(2)}, u32[]{:S(2)}) %collective-permute-start.3) | collective-permute-done | bytes 348192 | tf_op jit(solution)/shard_map/ppermute | solution.py:510
  12.9 0.0 copy-done.6
  12.9 0.0 copy-done.8
  12.9 0.0 copy-start
  12.9 0.0 copy-start.4
  12.9 6.2 %coherent_fields.1 = f32[40,128]{1,0:T(8,128)S(1)} custom-call(s32[1]{0:T(128)} %bitcast.part_ref, f32[17,40,128]{2,1,0:T(8,128)S(1)} %pad_maximum_fusion.mixed_ref, f32[17,40,128]{2,1,0:T(8,128)S(1)} %collective-permute-done.3.other_ref, f32[8,4,40,128]{3,2,1,0:T(8,128)S(1)} %get-tuple-element.15.near_ref, f32[512,128]{1,0:T(8,128)S(1)} %get-tuple-element.16.signs, ...), custom_call_target="tpu_custom_call" | custom-call | flops 8589934592 | bytes 1048576 | tf_op jit(solution)/shard_map/coherent_fields/pallas_call | solution.py:467
  19.1 0.2 collective-permute-start.4
  19.3 1.1 %collective-permute-done.4 = f32[40,128]{1,0:T(8,128)S(1)} collective-permute-done((f32[40,128]{1,0:T(8,128)S(1)}, f32[40,128]{1,0:T(8,128)S(1)}, u32[]{:S(2)}, u32[]{:S(2)}) %collective-permute-start.4) | collective-permute-done | bytes 20512 | tf_op jit(solution)/shard_map/ppermute | solution.py:510
  20.4 0.0 collective-permute-start.5
  20.4 3.2 %collective-permute-done.5 = f32[40,128]{1,0:T(8,128)S(1)} collective-permute-done((f32[40,128]{1,0:T(8,128)S(1)}, f32[40,128]{1,0:T(8,128)S(1)}, u32[]{:S(2)}, u32[]{:S(2)}) %collective-permute-start.5) | collective-permute-done | bytes 20512 | tf_op jit(solution)/shard_map/ppermute | solution.py:510
  23.6 0.0 copy-start.1
  23.6 0.2 collective-permute-start.6
  23.7 0.0 copy-done
  23.7 0.0 copy-done.4
  23.7 1.2 %own_gradient.1 = (f32[128,512]{1,0:T(8,128)}, f32[32,512]{1,0:T(8,128)S(1)}, f32[32,512]{1,0:T(8,128)S(1)}) custom-call(s32[1]{0:T(128)} %bitcast.part_ref, f32[128,512]{1,0:T(8,128)S(1)} %copy-done.3, f32[40,128]{1,0:T(8,128)S(1)} %add.19.sum_ref, bf16[2,256,512]{2,1,0:T(8,128)(2,1)S(1)} %copy-done, bf16[4,256,240]{2,1,0:T(8,128)(2,1)S(1)} %copy-done.4), custom_call_target="tpu_custom_call" | custom-call | flops 2147483648 | bytes 1048576 | tf_op jit(solution)/shard_map/own_gradient/pallas_call | solution.py:467
  25.0 2.7 %collective-permute-done.6.near_ref = f32[40,128]{1,0:T(8,128)S(1)} collective-permute-done((f32[40,128]{1,0:T(8,128)S(1)}, f32[40,128]{1,0:T(8,128)S(1)}, u32[]{:S(2)}, u32[]{:S(2)}) %collective-permute-start.6) | collective-permute-done | bytes 20512 | tf_op jit(solution)/shard_map/ppermute | solution.py:507
  27.7 0.0 copy-done.1
  27.7 1.1 %edge_gradient.1 = f32[128,512]{1,0:T(8,128)} custom-call(s32[1]{0:T(128)} %bitcast.part_ref, f32[128,512]{1,0:T(8,128)} %get-tuple-element.20.gradient_hbm, f32[32,512]{1,0:T(8,128)S(1)} %get-tuple-element.21.edge_ref, f32[32,512]{1,0:T(8,128)S(1)} %get-tuple-element.22.scale_ref, ...), custom_call_target="tpu_custom_call", output_to_operand_aliasing={{}: (1, {})} | custom-call | flops 268435456 | bytes 1048576 | tf_op jit(solution)/shard_map/edge_gradient/pallas_call | solution.py:467
  (4 shorter events, 0.0 us)
Async XLA Ops:
  1.2 4.5 %collective-permute-start.1 = (f32[32,128]{1,0:T(8,128)S(1)}, f32[32,128]{1,0:T(8,128)S(1)}, u32[]{:S(2)}, u32[]{:S(2)}) collective-permute-start(f32[32,128]{1,0:T(8,128)S(1)} %edge_columns.1), channel_id=1, source_target_pairs={{1,2},{2,1},{5,6},{6,5},{9,10},{10,9},{13,14},{14,13},{17,18},{18,... | collective-permute-start | bytes 49160 | tf_op jit(solution)/shard_map/ppermute | solution.py:507
  2.7 2.6 %copy-start.3 = (f32[128,512]{1,0:T(8,128)S(1)}, f32[128,512]{1,0:T(8,128)}, u32[]{:S(2)}) copy-start(f32[128,512]{1,0:T(8,128)} %theta_ref.3) | copy-start | bytes 786436
  2.7 2.6 %copy-start.5 = (bf16[2,512,256]{2,1,0:T(8,128)(2,1)S(1)}, bf16[2,512,256]{2,1,0:T(8,128)(2,1)}, u32[]{:S(2)}) copy-start(bf16[2,512,256]{2,1,0:T(8,128)(2,1)} %constant.43.clone.column_ref) | copy-start | bytes 1572868
  2.7 2.6 %copy-start.7 = (bf16[4,80,384]{2,1,0:T(8,128)(2,1)S(1)}, bf16[4,80,384]{2,1,0:T(8,128)(2,1)}, u32[]{:S(2)}) copy-start(bf16[4,80,384]{2,1,0:T(8,128)(2,1)} %constant.45.clone.rows_ref) | copy-start | bytes 737284
  4.4 1.4 %copy-start.9 = (bf16[4,80,96]{2,1,0:T(8,128)(2,1)S(1)}, bf16[4,80,96]{2,1,0:T(8,128)(2,1)}, u32[]{:S(2)}) copy-start(bf16[4,80,96]{2,1,0:T(8,128)(2,1)} %constant.47.clone.rows_ref) | copy-start | bytes 184324
  4.4 6.7 %collective-permute-start = (f32[8,40,128]{2,1,0:T(8,128)S(1)}, f32[8,40,128]{2,1,0:T(8,128)S(1)}, u32[]{:S(2)}, u32[]{:S(2)}) collective-permute-start(f32[8,40,128]{2,1,0:T(8,128)S(1)} %get-tuple-element.14), channel_id=1, source_target_pairs={{0,3},{1,2},{2,1},{3,0},{4,7},{5,6},{6,5},{7,4},{8,11},{9,10},{10,... | collective-permute-start | bytes 491528 | tf_op jit(solution)/shard_map/ppermute | solution.py:510
  5.7 5.6 %copy-start.2 = (s32[512,512]{1,0:T(8,128)S(1)}, s32[512,512]{1,0:T(8,128)}, u32[]{:S(2)}) copy-start(s32[512,512]{1,0:T(8,128)} %target_ref.1) | copy-start | bytes 3145732
  6.0 5.0 %collective-permute-start.2 = (f32[1,40,128]{2,1,0:T(8,128)S(1)}, f32[1,40,128]{2,1,0:T(8,128)S(1)}, u32[]{:S(2)}, u32[]{:S(2)}) collective-permute-start(f32[1,40,128]{2,1,0:T(8,128)S(1)} %add_rim.1), channel_id=1, source_target_pairs={{0,3},{1,2},{2,1},{3,0},{4,7},{5,6},{6,5},{7,4},{8,11},{9,10},{10,... | collective-permute-start | bytes 61448 | tf_op jit(solution)/shard_map/ppermute | solution.py:510
  11.1 1.8 %copy-start.6 = (bf16[512,240]{1,0:T(8,128)(2,1)S(1)}, bf16[512,240]{1,0:T(8,128)(2,1)}, u32[]{:S(2)}) copy-start(bf16[512,240]{1,0:T(8,128)(2,1)} %constant.52.clone.row_ref) | copy-start | bytes 737284
  11.2 1.7 %copy-start.8 = (bf16[160,512]{1,0:T(8,128)(2,1)S(1)}, bf16[160,512]{1,0:T(8,128)(2,1)}, u32[]{:S(2)}) copy-start(bf16[160,512]{1,0:T(8,128)(2,1)} %constant.53.clone.row_turned_ref) | copy-start | bytes 491524
  11.2 1.7 %collective-permute-start.3 = (f32[17,40,128]{2,1,0:T(8,128)S(1)}, f32[17,40,128]{2,1,0:T(8,128)S(1)}, u32[]{:S(2)}, u32[]{:S(2)}) collective-permute-start(f32[17,40,128]{2,1,0:T(8,128)S(1)} %pad_maximum_fusion.mixed_ref), channel_id=1, source_target_pairs={{0,1},{1,0},{2,3},{3,2},{4,5},{5,4},{6,7},{7,6},{8,9},{9,8},{10,11... | collective-permute-start | bytes 1044488 | tf_op jit(solution)/shard_map/ppermute | solution.py:510
  12.9 10.8 %copy-start = (bf16[2,256,512]{2,1,0:T(8,128)(2,1)S(1)}, bf16[2,256,512]{2,1,0:T(8,128)(2,1)}, u32[]{:S(2)}) copy-start(bf16[2,256,512]{2,1,0:T(8,128)(2,1)} %constant.51.clone.turned_ref) | copy-start | bytes 1572868
  12.9 10.8 %copy-start.4 = (bf16[4,256,240]{2,1,0:T(8,128)(2,1)S(1)}, bf16[4,256,240]{2,1,0:T(8,128)(2,1)}, u32[]{:S(2)}) copy-start(bf16[4,256,240]{2,1,0:T(8,128)(2,1)} %constant.46.clone.rows_ref) | copy-start | bytes 1474564
  19.1 1.3 %collective-permute-start.4 = (f32[40,128]{1,0:T(8,128)S(1)}, f32[40,128]{1,0:T(8,128)S(1)}, u32[]{:S(2)}, u32[]{:S(2)}) collective-permute-start(f32[40,128]{1,0:T(8,128)S(1)} %coherent_fields.1), channel_id=1, source_target_pairs={{0,1},{1,0},{2,3},{3,2},{4,5},{5,4},{6,7},{7,6},{8,9},{9,8},{10,11... | collective-permute-start | bytes 61448 | tf_op jit(solution)/shard_map/ppermute | solution.py:510
  20.4 3.2 %collective-permute-start.5 = (f32[40,128]{1,0:T(8,128)S(1)}, f32[40,128]{1,0:T(8,128)S(1)}, u32[]{:S(2)}, u32[]{:S(2)}) collective-permute-start(f32[40,128]{1,0:T(8,128)S(1)} %add.18), channel_id=1, source_target_pairs={{0,3},{1,2},{2,1},{3,0},{4,7},{5,6},{6,5},{7,4},{8,11},{9,10},{10,... | collective-permute-start | bytes 61448 | tf_op jit(solution)/shard_map/ppermute | solution.py:510
  23.6 4.1 %copy-start.1 = (bf16[4,64,240]{2,1,0:T(8,128)(2,1)S(1)}, bf16[4,64,240]{2,1,0:T(8,128)(2,1)}, u32[]{:S(2)}) copy-start(bf16[4,64,240]{2,1,0:T(8,128)(2,1)} %constant.48.clone.rows_ref) | copy-start | bytes 368644
  23.6 4.1 %collective-permute-start.6 = (f32[40,128]{1,0:T(8,128)S(1)}, f32[40,128]{1,0:T(8,128)S(1)}, u32[]{:S(2)}, u32[]{:S(2)}) collective-permute-start(f32[40,128]{1,0:T(8,128)S(1)} %add.19.sum_ref), channel_id=1, source_target_pairs={{0,1},{3,2},{4,5},{7,6},{8,9},{11,10},{12,13},{15,14},{16,17},{19,... | collective-permute-start | bytes 61448 | tf_op jit(solution)/shard_map/ppermute | solution.py:507

commit v9 on v8

--- a/solution.py
+++ b/solution.py
@@ -21,6 +21,8 @@
 FA = 40
 FB = 64
 SPARE = FA - HALF - 1
+DEPTH = 256
+CHUNK = 64
 SPARE_BLOCKS = -(-(HALF + 1) // SPARE)
 BF = jnp.bfloat16
 F32 = jnp.float32
@@ -104,7 +106,7 @@
     out["forward"] = np.stack(forward)
     out["backward"] = np.stack(backward)
     out["turned"] = np.stack([column_high.T, column_low.T])
-    out["row"] = np.concatenate([row_high, row_low, row_high], axis=1)
+    out["row"] = np.concatenate([row_high, row_low, row_high, np.zeros((TP, DEPTH - 6 * FA), row_high.dtype)], axis=1)
     out["row_turned"] = np.concatenate([row_high.T, row_low.T])
     return out
 
@@ -310,7 +312,7 @@
 
 def fields_kernel(
     part_ref, mixed_ref, other_ref, near_ref, signs, shares_ref, forward_ref, backward_ref, row_ref,
-    row_turned_ref, out_ref, far_ref, levels_ref, lines, folded, amps, tanhs, total, turned, backs,
+    row_turned_ref, out_ref, far_ref, levels_ref, lines, folded, amps, highs, lows, tanhs, total, turned, backs,
 ):
     count = 2 * far_ref.shape[0]
     local = count // PARTS
@@ -364,37 +366,45 @@
                 )
             )
         high, low = split(jnp.concatenate(parts, axis=1))
-        folded[kern] = jnp.concatenate([high, high, low], axis=0)
+        folded[kern] = jnp.concatenate([high, high, low, jnp.zeros((DEPTH - 6 * FA, 2 * ROWS), BF)], axis=0)
     total[...] = jnp.zeros_like(total)
 
     def expose(cond, carry):
-        intensity = None
+        for kern in range(KERNELS):
+            amps[cond * KERNELS + kern] = dot(row_ref[...], folded[cond * KERNELS + kern])
+        level = levels_ref[pl.ds(cond, 1), :]
+        for start in range(0, TP, CHUNK):
+            rows = slice(start, start + CHUNK)
+            intensity = None
+            for kern in range(KERNELS):
+                amp = amps[cond * KERNELS + kern, rows]
+                power = amp[:, :ROWS] * amp[:, :ROWS] + amp[:, ROWS:] * amp[:, ROWS:]
+                intensity = power if intensity is None else intensity + power
+            value = jnp.tanh((0.5 * resist_steep) * (intensity - level))
+            tanhs[cond, rows] = value
+            total[rows] += value
+        return carry
+
+    lax.fori_loop(0, CONDS, expose, 0, unroll=4)
+
+    def drive(cond, carry):
+        weight = shares_ref[pl.ds(cond, 1), :]
+        for start in range(0, TP, CHUNK):
+            rows = slice(start, start + CHUNK)
+            value = tanhs[cond, rows]
+            slope = (weight + band_weight / CONDS) * value + weight * signs[rows]
+            slope = slope - total[rows] * (band_weight / (CONDS * CONDS))
+            field = (0.5 * resist_steep) * (1.0 - value * value) * slope
+            field = jnp.concatenate([field, field], axis=1)
+            for kern in range(KERNELS):
+                index = cond * KERNELS + kern
+                high, low = split(field * amps[index, rows])
+                highs[index, rows] = high
+                lows[index, rows] = low
         for kern in range(KERNELS):
             index = cond * KERNELS + kern
-            amp = dot(row_ref[...], folded[index])
-            amps[index] = amp
-            power = amp[:, :ROWS] * amp[:, :ROWS] + amp[:, ROWS:] * amp[:, ROWS:]
-            intensity = power if intensity is None else intensity + power
-        level = levels_ref[pl.ds(cond, 1), :]
-        value = jnp.tanh((0.5 * resist_steep) * (intensity - level))
-        tanhs[cond] = value
-        total[...] += value
-        return carry
-
-    lax.fori_loop(0, CONDS, expose, 0, unroll=4)
-    total[...] = total[...] * (band_weight / (CONDS * CONDS))
-
-    def drive(cond, carry):
-        weight = shares_ref[pl.ds(cond, 1), :]
-        value = tanhs[cond]
-        slope = (weight + band_weight / CONDS) * value + weight * signs[...] - total[...]
-        field = (0.5 * resist_steep) * (1.0 - value * value) * slope
-        field = jnp.concatenate([field, field], axis=1)
-        for kern in range(KERNELS):
-            index = cond * KERNELS + kern
-            high, low = split(field * amps[index])
-            long = dot(row_turned_ref[...], high)
-            back = long[: 2 * FA] + long[2 * FA :] + dot(row_turned_ref[: 2 * FA], low)
+            long = dot(row_turned_ref[...], highs[index])
+            back = long[: 2 * FA] + long[2 * FA :] + dot(row_turned_ref[: 2 * FA], lows[index])
             turned[pl.ds(index * 2, 2)] = jnp.stack([back[:, :ROWS], back[:, ROWS:]])
         return carry
 
@@ -601,8 +611,10 @@
             pltpu.VMEM((count // 2, 4, FA, 2 * FB), F32),
             pltpu.VMEM((CONDS, ROWS), F32),
             pltpu.VMEM((count * 4 * FA, 2 * FB), F32),
-            pltpu.VMEM((count, 6 * FA, 2 * ROWS), BF),
+            pltpu.VMEM((count, DEPTH, 2 * ROWS), BF),
             pltpu.VMEM((count, TP, 2 * ROWS), F32),
+            pltpu.VMEM((count, TP, 2 * ROWS), BF),
+            pltpu.VMEM((count, TP, 2 * ROWS), BF),
             pltpu.VMEM((CONDS, TP, ROWS), F32),
             pltpu.VMEM((TP, ROWS), F32),
             pltpu.VMEM((count * 2, 2 * FA, ROWS), F32),

time: 29 us -> 29.1 us (level)
  no operation moved by 1% of the time
where the time goes in v9:
time: 29.1 us; the launch traced here: 28.9 us
  Pallas kernels  12.7 us (44%)
  waiting for transfers between devices  12.2 us (42%)
  starting transfers between devices  3.89 us (13%)
    pallas_call x8, Pallas kernels, call(): pl.pallas_call(kernel, grid_spec=pltpu.PrefetchScalarGridSpec(num_scalar_...  12.7 us
    ppermute x5, waiting for transfers between devices, partner(): return lax.ppermute(value, 'cond', [(i, i ^ step) for i in range(PARTS)])  9.47 us
    ppermute x2, waiting for transfers between devices, across(): return lax.ppermute(value, ('tile', 'cond'), pairs)  2.69 us
    ppermute x5, starting transfers between devices, partner(): return lax.ppermute(value, 'cond', [(i, i ^ step) for i in range(PARTS)])  2.26 us
    ppermute x2, starting transfers between devices, across(): return lax.ppermute(value, ('tile', 'cond'), pairs)  1.63 us
  transfers between devices with their start and end apart: 7, of which 5 were waited for; matrix products, arithmetic and copies ran while one was open for 0% of the time, Pallas kernels for 14%

profile of v9, /device:TPU:24, one launch (start us, length us, event | category | flops | bytes accessed | tf_op | source)
XLA Modules:
  0.0 28.9 jit_solution(12117737457800531274)
XLA Ops:
  0.0 1.2 %edge_columns.1 = f32[32,128]{1,0:T(8,128)S(1)} custom-call(s32[1]{0:T(128)} %bitcast.part_ref, f32[128,512]{1,0:T(8,128)} %theta_ref.3, bf16[2,512,128]{2,1,0:T(8,128)(2,1)} %constant.44.clone.waves_hbm), custom_call_target="tpu_custom_call" | custom-call | flops 268435456 | bytes 1048576 | tf_op jit(solution)/shard_map/edge_columns/pallas_call | solution.py:477
  1.2 1.5 %collective-permute-start.1 = (f32[32,128]{1,0:T(8,128)S(1)}, f32[32,128]{1,0:T(8,128)S(1)}, u32[]{:S(2)}, u32[]{:S(2)}) collective-permute-start(f32[32,128]{1,0:T(8,128)S(1)} %edge_columns.1), channel_id=1, source_target_pairs={{1,2},{2,1},{5,6},{6,5},{9,10},{10,9},{13,14},{14,13},{17,18},{18,... | collective-permute-start | bytes 49160 | tf_op jit(solution)/shard_map/ppermute | solution.py:517
  2.7 0.0 copy-start.3
  2.7 0.0 copy-start.5
  2.7 0.0 copy-start.7
  2.7 1.7 %open_parts.1 = (f32[8,40,128]{2,1,0:T(8,128)S(1)}, f32[8,128]{1,0:T(8,128)S(1)}, bf16[384,256]{1,0:T(8,128)(2,1)S(1)}, bf16[384,256]{1,0:T(8,128)(2,1)S(1)}) custom-call(s32[1]{0:T(128)} %bitcast.part_ref, f32[2,65,2,65]{3,2,1,0:T(2,128)} %bitcast.3, f32[2,65,2,65]{3,2,1,0:T(2,128)} %bitcast.4, f32[2]{0:T(128)} %thresholds_hbm.1, s32[8]{0:T(128)} %weights_hbm.1, ...), custom_call_target="tpu_custom_call" | custom-call | flops 268435456 | bytes 1048576 | tf_op jit(solution)/shard_map/open_parts/pallas_call | solution.py:477
  4.4 0.0 copy-start.9
  4.4 0.8 %collective-permute-start = (f32[8,40,128]{2,1,0:T(8,128)S(1)}, f32[8,40,128]{2,1,0:T(8,128)S(1)}, u32[]{:S(2)}, u32[]{:S(2)}) collective-permute-start(f32[8,40,128]{2,1,0:T(8,128)S(1)} %get-tuple-element.14), channel_id=1, source_target_pairs={{0,3},{1,2},{2,1},{3,0},{4,7},{5,6},{6,5},{7,4},{8,11},{9,10},{10,... | collective-permute-start | bytes 491528 | tf_op jit(solution)/shard_map/ppermute | solution.py:520
  5.2 0.0 copy-done.3
  5.2 0.0 copy-done.5
  5.2 0.0 copy-done.7
  5.2 0.5 %own_spectrum.1.spectrum_ref = f32[2,40,128]{2,1,0:T(8,128)S(1)} custom-call(s32[1]{0:T(128)} %bitcast.part_ref, f32[128,512]{1,0:T(8,128)S(1)} %copy-done.3, bf16[2,512,256]{2,1,0:T(8,128)(2,1)S(1)} %copy-done.5, bf16[4,80,384]{2,1,0:T(8,128)(2,1)S(1)} %copy-done.7), custom_call_target="tpu_custom_call" | custom-call | flops 2147483648 | bytes 1048576 | tf_op jit(solution)/shard_map/own_spectrum/pallas_call | solution.py:477
  5.7 0.0 copy-start.2
  5.7 0.0 collective-permute-done.1.rim_ref
  5.7 0.0 copy-done.9
  5.7 0.3 %add_rim.1 = f32[1,40,128]{2,1,0:T(8,128)S(1)} custom-call(s32[1]{0:T(128)} %bitcast.part_ref, f32[2,40,128]{2,1,0:T(8,128)S(1)} %own_spectrum.1.spectrum_ref, f32[32,128]{1,0:T(8,128)S(1)} %collective-permute-done.1.rim_ref, bf16[4,80,96]{2,1,0:T(8,128)(2,1)S(1)} %copy-done.9), custom_call_target="tpu_custom_call" | custom-call | flops 268435456 | bytes 1048576 | tf_op jit(solution)/shard_map/add_rim/pallas_call | solution.py:477
  6.0 1.0 %collective-permute-start.2 = (f32[1,40,128]{2,1,0:T(8,128)S(1)}, f32[1,40,128]{2,1,0:T(8,128)S(1)}, u32[]{:S(2)}, u32[]{:S(2)}) collective-permute-start(f32[1,40,128]{2,1,0:T(8,128)S(1)} %add_rim.1), channel_id=1, source_target_pairs={{0,3},{1,2},{2,1},{3,0},{4,7},{5,6},{6,5},{7,4},{8,11},{9,10},{10,... | collective-permute-start | bytes 61448 | tf_op jit(solution)/shard_map/ppermute | solution.py:520
  7.1 4.0 %collective-permute-done.2 = f32[1,40,128]{2,1,0:T(8,128)S(1)} collective-permute-done((f32[1,40,128]{2,1,0:T(8,128)S(1)}, f32[1,40,128]{2,1,0:T(8,128)S(1)}, u32[]{:S(2)}, u32[]{:S(2)}) %collective-permute-start.2) | collective-permute-done | bytes 20512 | tf_op jit(solution)/shard_map/ppermute | solution.py:520
  11.1 0.0 collective-permute-done
  11.1 0.0 copy-start.6
  11.2 0.0 copy-start.8
  11.2 0.2 collective-permute-start.3
  11.3 0.0 copy-done.2
  11.3 0.3 %near_kernels.1 = (f32[8,4,40,128]{3,2,1,0:T(8,128)S(1)}, f32[512,128]{1,0:T(8,128)S(1)}) custom-call(s32[1]{0:T(128)} %bitcast.part_ref, f32[17,40,128]{2,1,0:T(8,128)S(1)} %pad_maximum_fusion.mixed_ref, s32[512,512]{1,0:T(8,128)S(1)} %copy-done.2), custom_call_target="tpu_custom_call" | custom-call | flops 1073741824 | bytes 1048576 | tf_op jit(solution)/shard_map/near_kernels/pallas_call | solution.py:477
  11.7 1.2 %collective-permute-done.3.other_ref = f32[17,40,128]{2,1,0:T(8,128)S(1)} collective-permute-done((f32[17,40,128]{2,1,0:T(8,128)S(1)}, f32[17,40,128]{2,1,0:T(8,128)S(1)}, u32[]{:S(2)}, u32[]{:S(2)}) %collective-permute-start.3) | collective-permute-done | bytes 348192 | tf_op jit(solution)/shard_map/ppermute | solution.py:520
  12.9 0.0 copy-done.6
  12.9 0.0 copy-done.8
  12.9 0.0 copy-start
  12.9 0.0 copy-start.4
  12.9 6.3 %coherent_fields.1 = f32[40,128]{1,0:T(8,128)S(1)} custom-call(s32[1]{0:T(128)} %bitcast.part_ref, f32[17,40,128]{2,1,0:T(8,128)S(1)} %pad_maximum_fusion.mixed_ref, f32[17,40,128]{2,1,0:T(8,128)S(1)} %collective-permute-done.3.other_ref, f32[8,4,40,128]{3,2,1,0:T(8,128)S(1)} %get-tuple-element.15.near_ref, f32[512,128]{1,0:T(8,128)S(1)} %get-tuple-element.16.signs, ...), custom_call_target="tpu_custom_call" | custom-call | flops 8589934592 | bytes 1048576 | tf_op jit(solution)/shard_map/coherent_fields/pallas_call | solution.py:477
  19.2 0.2 collective-permute-start.4
  19.4 1.1 %collective-permute-done.4 = f32[40,128]{1,0:T(8,128)S(1)} collective-permute-done((f32[40,128]{1,0:T(8,128)S(1)}, f32[40,128]{1,0:T(8,128)S(1)}, u32[]{:S(2)}, u32[]{:S(2)}) %collective-permute-start.4) | collective-permute-done | bytes 20512 | tf_op jit(solution)/shard_map/ppermute | solution.py:520
  20.5 0.0 collective-permute-start.5
  20.5 3.2 %collective-permute-done.5 = f32[40,128]{1,0:T(8,128)S(1)} collective-permute-done((f32[40,128]{1,0:T(8,128)S(1)}, f32[40,128]{1,0:T(8,128)S(1)}, u32[]{:S(2)}, u32[]{:S(2)}) %collective-permute-start.5) | collective-permute-done | bytes 20512 | tf_op jit(solution)/shard_map/ppermute | solution.py:520
  23.7 0.0 copy-start.1
  23.7 0.2 collective-permute-start.6
  23.9 0.0 copy-done
  23.9 0.0 copy-done.4
  23.9 1.2 %own_gradient.1 = (f32[128,512]{1,0:T(8,128)}, f32[32,512]{1,0:T(8,128)S(1)}, f32[32,512]{1,0:T(8,128)S(1)}) custom-call(s32[1]{0:T(128)} %bitcast.part_ref, f32[128,512]{1,0:T(8,128)S(1)} %copy-done.3, f32[40,128]{1,0:T(8,128)S(1)} %add.19.sum_ref, bf16[2,256,512]{2,1,0:T(8,128)(2,1)S(1)} %copy-done, bf16[4,256,240]{2,1,0:T(8,128)(2,1)S(1)} %copy-done.4), custom_call_target="tpu_custom_call" | custom-call | flops 2147483648 | bytes 1048576 | tf_op jit(solution)/shard_map/own_gradient/pallas_call | solution.py:477
  25.1 2.7 %collective-permute-done.6.near_ref = f32[40,128]{1,0:T(8,128)S(1)} collective-permute-done((f32[40,128]{1,0:T(8,128)S(1)}, f32[40,128]{1,0:T(8,128)S(1)}, u32[]{:S(2)}, u32[]{:S(2)}) %collective-permute-start.6) | collective-permute-done | bytes 20512 | tf_op jit(solution)/shard_map/ppermute | solution.py:517
  27.8 0.0 copy-done.1
  27.8 1.1 %edge_gradient.1 = f32[128,512]{1,0:T(8,128)} custom-call(s32[1]{0:T(128)} %bitcast.part_ref, f32[128,512]{1,0:T(8,128)} %get-tuple-element.20.gradient_hbm, f32[32,512]{1,0:T(8,128)S(1)} %get-tuple-element.21.edge_ref, f32[32,512]{1,0:T(8,128)S(1)} %get-tuple-element.22.scale_ref, ...), custom_call_target="tpu_custom_call", output_to_operand_aliasing={{}: (1, {})} | custom-call | flops 268435456 | bytes 1048576 | tf_op jit(solution)/shard_map/edge_gradient/pallas_call | solution.py:477
  (4 shorter events, 0.0 us)
Async XLA Ops:
  1.2 4.5 %collective-permute-start.1 = (f32[32,128]{1,0:T(8,128)S(1)}, f32[32,128]{1,0:T(8,128)S(1)}, u32[]{:S(2)}, u32[]{:S(2)}) collective-permute-start(f32[32,128]{1,0:T(8,128)S(1)} %edge_columns.1), channel_id=1, source_target_pairs={{1,2},{2,1},{5,6},{6,5},{9,10},{10,9},{13,14},{14,13},{17,18},{18,... | collective-permute-start | bytes 49160 | tf_op jit(solution)/shard_map/ppermute | solution.py:517
  2.7 2.6 %copy-start.3 = (f32[128,512]{1,0:T(8,128)S(1)}, f32[128,512]{1,0:T(8,128)}, u32[]{:S(2)}) copy-start(f32[128,512]{1,0:T(8,128)} %theta_ref.3) | copy-start | bytes 786436
  2.7 2.6 %copy-start.5 = (bf16[2,512,256]{2,1,0:T(8,128)(2,1)S(1)}, bf16[2,512,256]{2,1,0:T(8,128)(2,1)}, u32[]{:S(2)}) copy-start(bf16[2,512,256]{2,1,0:T(8,128)(2,1)} %constant.43.clone.column_ref) | copy-start | bytes 1572868
  2.7 2.6 %copy-start.7 = (bf16[4,80,384]{2,1,0:T(8,128)(2,1)S(1)}, bf16[4,80,384]{2,1,0:T(8,128)(2,1)}, u32[]{:S(2)}) copy-start(bf16[4,80,384]{2,1,0:T(8,128)(2,1)} %constant.45.clone.rows_ref) | copy-start | bytes 737284
  4.4 1.4 %copy-start.9 = (bf16[4,80,96]{2,1,0:T(8,128)(2,1)S(1)}, bf16[4,80,96]{2,1,0:T(8,128)(2,1)}, u32[]{:S(2)}) copy-start(bf16[4,80,96]{2,1,0:T(8,128)(2,1)} %constant.47.clone.rows_ref) | copy-start | bytes 184324
  4.4 6.7 %collective-permute-start = (f32[8,40,128]{2,1,0:T(8,128)S(1)}, f32[8,40,128]{2,1,0:T(8,128)S(1)}, u32[]{:S(2)}, u32[]{:S(2)}) collective-permute-start(f32[8,40,128]{2,1,0:T(8,128)S(1)} %get-tuple-element.14), channel_id=1, source_target_pairs={{0,3},{1,2},{2,1},{3,0},{4,7},{5,6},{6,5},{7,4},{8,11},{9,10},{10,... | collective-permute-start | bytes 491528 | tf_op jit(solution)/shard_map/ppermute | solution.py:520
  5.7 5.6 %copy-start.2 = (s32[512,512]{1,0:T(8,128)S(1)}, s32[512,512]{1,0:T(8,128)}, u32[]{:S(2)}) copy-start(s32[512,512]{1,0:T(8,128)} %target_ref.1) | copy-start | bytes 3145732
  6.0 5.0 %collective-permute-start.2 = (f32[1,40,128]{2,1,0:T(8,128)S(1)}, f32[1,40,128]{2,1,0:T(8,128)S(1)}, u32[]{:S(2)}, u32[]{:S(2)}) collective-permute-start(f32[1,40,128]{2,1,0:T(8,128)S(1)} %add_rim.1), channel_id=1, source_target_pairs={{0,3},{1,2},{2,1},{3,0},{4,7},{5,6},{6,5},{7,4},{8,11},{9,10},{10,... | collective-permute-start | bytes 61448 | tf_op jit(solution)/shard_map/ppermute | solution.py:520
  11.1 1.8 %copy-start.6 = (bf16[512,256]{1,0:T(8,128)(2,1)S(1)}, bf16[512,256]{1,0:T(8,128)(2,1)}, u32[]{:S(2)}) copy-start(bf16[512,256]{1,0:T(8,128)(2,1)} %constant.52.clone.row_ref) | copy-start | bytes 786436
  11.2 1.7 %copy-start.8 = (bf16[160,512]{1,0:T(8,128)(2,1)S(1)}, bf16[160,512]{1,0:T(8,128)(2,1)}, u32[]{:S(2)}) copy-start(bf16[160,512]{1,0:T(8,128)(2,1)} %constant.53.clone.row_turned_ref) | copy-start | bytes 491524
  11.2 1.7 %collective-permute-start.3 = (f32[17,40,128]{2,1,0:T(8,128)S(1)}, f32[17,40,128]{2,1,0:T(8,128)S(1)}, u32[]{:S(2)}, u32[]{:S(2)}) collective-permute-start(f32[17,40,128]{2,1,0:T(8,128)S(1)} %pad_maximum_fusion.mixed_ref), channel_id=1, source_target_pairs={{0,1},{1,0},{2,3},{3,2},{4,5},{5,4},{6,7},{7,6},{8,9},{9,8},{10,11... | collective-permute-start | bytes 1044488 | tf_op jit(solution)/shard_map/ppermute | solution.py:520
  12.9 11.0 %copy-start = (bf16[2,256,512]{2,1,0:T(8,128)(2,1)S(1)}, bf16[2,256,512]{2,1,0:T(8,128)(2,1)}, u32[]{:S(2)}) copy-start(bf16[2,256,512]{2,1,0:T(8,128)(2,1)} %constant.51.clone.turned_ref) | copy-start | bytes 1572868
  12.9 11.0 %copy-start.4 = (bf16[4,256,240]{2,1,0:T(8,128)(2,1)S(1)}, bf16[4,256,240]{2,1,0:T(8,128)(2,1)}, u32[]{:S(2)}) copy-start(bf16[4,256,240]{2,1,0:T(8,128)(2,1)} %constant.46.clone.rows_ref) | copy-start | bytes 1474564
  19.2 1.3 %collective-permute-start.4 = (f32[40,128]{1,0:T(8,128)S(1)}, f32[40,128]{1,0:T(8,128)S(1)}, u32[]{:S(2)}, u32[]{:S(2)}) collective-permute-start(f32[40,128]{1,0:T(8,128)S(1)} %coherent_fields.1), channel_id=1, source_target_pairs={{0,1},{1,0},{2,3},{3,2},{4,5},{5,4},{6,7},{7,6},{8,9},{9,8},{10,11... | collective-permute-start | bytes 61448 | tf_op jit(solution)/shard_map/ppermute | solution.py:520
  20.5 3.2 %collective-permute-start.5 = (f32[40,128]{1,0:T(8,128)S(1)}, f32[40,128]{1,0:T(8,128)S(1)}, u32[]{:S(2)}, u32[]{:S(2)}) collective-permute-start(f32[40,128]{1,0:T(8,128)S(1)} %add.18), channel_id=1, source_target_pairs={{0,3},{1,2},{2,1},{3,0},{4,7},{5,6},{6,5},{7,4},{8,11},{9,10},{10,... | collective-permute-start | bytes 61448 | tf_op jit(solution)/shard_map/ppermute | solution.py:520
  23.7 4.1 %copy-start.1 = (bf16[4,64,240]{2,1,0:T(8,128)(2,1)S(1)}, bf16[4,64,240]{2,1,0:T(8,128)(2,1)}, u32[]{:S(2)}) copy-start(bf16[4,64,240]{2,1,0:T(8,128)(2,1)} %constant.48.clone.rows_ref) | copy-start | bytes 368644
  23.7 4.1 %collective-permute-start.6 = (f32[40,128]{1,0:T(8,128)S(1)}, f32[40,128]{1,0:T(8,128)S(1)}, u32[]{:S(2)}, u32[]{:S(2)}) collective-permute-start(f32[40,128]{1,0:T(8,128)S(1)} %add.19.sum_ref), channel_id=1, source_target_pairs={{0,1},{3,2},{4,5},{7,6},{8,9},{11,10},{12,13},{15,14},{16,17},{19,... | collective-permute-start | bytes 61448 | tf_op jit(solution)/shard_map/ppermute | solution.py:517

commit v10 on v8

--- a/solution.py
+++ b/solution.py
@@ -364,17 +364,14 @@
                 )
             )
         high, low = split(jnp.concatenate(parts, axis=1))
-        folded[kern] = jnp.concatenate([high, high, low], axis=0)
+        lanes = slice(kern % KERNELS * 2 * ROWS, (kern % KERNELS + 1) * 2 * ROWS)
+        folded[kern // KERNELS, :, lanes] = jnp.concatenate([high, high, low], axis=0)
     total[...] = jnp.zeros_like(total)
 
     def expose(cond, carry):
-        intensity = None
-        for kern in range(KERNELS):
-            index = cond * KERNELS + kern
-            amp = dot(row_ref[...], folded[index])
-            amps[index] = amp
-            power = amp[:, :ROWS] * amp[:, :ROWS] + amp[:, ROWS:] * amp[:, ROWS:]
-            intensity = power if intensity is None else intensity + power
+        amp = dot(row_ref[...], folded[cond])
+        amps[cond] = amp
+        intensity = sum(amp[:, i * ROWS : (i + 1) * ROWS] * amp[:, i * ROWS : (i + 1) * ROWS] for i in range(2 * KERNELS))
         level = levels_ref[pl.ds(cond, 1), :]
         value = jnp.tanh((0.5 * resist_steep) * (intensity - level))
         tanhs[cond] = value
@@ -389,13 +386,11 @@
         value = tanhs[cond]
         slope = (weight + band_weight / CONDS) * value + weight * signs[...] - total[...]
         field = (0.5 * resist_steep) * (1.0 - value * value) * slope
-        field = jnp.concatenate([field, field], axis=1)
-        for kern in range(KERNELS):
-            index = cond * KERNELS + kern
-            high, low = split(field * amps[index])
-            long = dot(row_turned_ref[...], high)
-            back = long[: 2 * FA] + long[2 * FA :] + dot(row_turned_ref[: 2 * FA], low)
-            turned[pl.ds(index * 2, 2)] = jnp.stack([back[:, :ROWS], back[:, ROWS:]])
+        high, low = split(jnp.concatenate([field] * (2 * KERNELS), axis=1) * amps[cond])
+        long = dot(row_turned_ref[...], high)
+        back = long[: 2 * FA] + long[2 * FA :] + dot(row_turned_ref[: 2 * FA], low)
+        for i in range(2 * KERNELS):
+            turned[cond * 2 * KERNELS + i] = back[:, i * ROWS : (i + 1) * ROWS]
         return carry
 
     lax.fori_loop(0, CONDS, drive, 0, unroll=4)
@@ -601,8 +596,8 @@
             pltpu.VMEM((count // 2, 4, FA, 2 * FB), F32),
             pltpu.VMEM((CONDS, ROWS), F32),
             pltpu.VMEM((count * 4 * FA, 2 * FB), F32),
-            pltpu.VMEM((count, 6 * FA, 2 * ROWS), BF),
-            pltpu.VMEM((count, TP, 2 * ROWS), F32),
+            pltpu.VMEM((CONDS, 6 * FA, 2 * KERNELS * ROWS), BF),
+            pltpu.VMEM((CONDS, TP, 2 * KERNELS * ROWS), F32),
             pltpu.VMEM((CONDS, TP, ROWS), F32),
             pltpu.VMEM((TP, ROWS), F32),
             pltpu.VMEM((count * 2, 2 * FA, ROWS), F32),

time: 29 us -> 29 us (level)
  no operation moved by 1% of the time
where the time goes in v10:
time: 29 us; the launch traced here: 28.8 us
  Pallas kernels  12.6 us (43%)
  waiting for transfers between devices  12.2 us (42%)
  starting transfers between devices  3.89 us (13%)
    pallas_call x8, Pallas kernels, call(): pl.pallas_call(kernel, grid_spec=pltpu.PrefetchScalarGridSpec(num_scalar_...  12.6 us
    ppermute x5, waiting for transfers between devices, partner(): return lax.ppermute(value, 'cond', [(i, i ^ step) for i in range(PARTS)])  9.47 us
    ppermute x2, waiting for transfers between devices, across(): return lax.ppermute(value, ('tile', 'cond'), pairs)  2.69 us
    ppermute x5, starting transfers between devices, partner(): return lax.ppermute(value, 'cond', [(i, i ^ step) for i in range(PARTS)])  2.26 us
    ppermute x2, starting transfers between devices, across(): return lax.ppermute(value, ('tile', 'cond'), pairs)  1.63 us
  transfers between devices with their start and end apart: 7, of which 5 were waited for; matrix products, arithmetic and copies ran while one was open for 0% of the time, Pallas kernels for 14%

profile of v10, /device:TPU:24, one launch (start us, length us, event | category | flops | bytes accessed | tf_op | source)
XLA Modules:
  0.0 28.8 jit_solution(6979734666156341870)
XLA Ops:
  0.0 1.2 %edge_columns.1 = f32[32,128]{1,0:T(8,128)S(1)} custom-call(s32[1]{0:T(128)} %bitcast.part_ref, f32[128,512]{1,0:T(8,128)} %theta_ref.3, bf16[2,512,128]{2,1,0:T(8,128)(2,1)} %constant.44.clone.waves_hbm), custom_call_target="tpu_custom_call" | custom-call | flops 268435456 | bytes 1048576 | tf_op jit(solution)/shard_map/edge_columns/pallas_call | solution.py:462
  1.2 1.5 %collective-permute-start.1 = (f32[32,128]{1,0:T(8,128)S(1)}, f32[32,128]{1,0:T(8,128)S(1)}, u32[]{:S(2)}, u32[]{:S(2)}) collective-permute-start(f32[32,128]{1,0:T(8,128)S(1)} %edge_columns.1), channel_id=1, source_target_pairs={{1,2},{2,1},{5,6},{6,5},{9,10},{10,9},{13,14},{14,13},{17,18},{18,... | collective-permute-start | bytes 49160 | tf_op jit(solution)/shard_map/ppermute | solution.py:502
  2.7 0.0 copy-start.3
  2.7 0.0 copy-start.5
  2.7 0.0 copy-start.7
  2.7 1.7 %open_parts.1 = (f32[8,40,128]{2,1,0:T(8,128)S(1)}, f32[8,128]{1,0:T(8,128)S(1)}, bf16[384,256]{1,0:T(8,128)(2,1)S(1)}, bf16[384,256]{1,0:T(8,128)(2,1)S(1)}) custom-call(s32[1]{0:T(128)} %bitcast.part_ref, f32[2,65,2,65]{3,2,1,0:T(2,128)} %bitcast.3, f32[2,65,2,65]{3,2,1,0:T(2,128)} %bitcast.4, f32[2]{0:T(128)} %thresholds_hbm.1, s32[8]{0:T(128)} %weights_hbm.1, ...), custom_call_target="tpu_custom_call" | custom-call | flops 268435456 | bytes 1048576 | tf_op jit(solution)/shard_map/open_parts/pallas_call | solution.py:462
  4.4 0.0 copy-start.9
  4.4 0.8 %collective-permute-start = (f32[8,40,128]{2,1,0:T(8,128)S(1)}, f32[8,40,128]{2,1,0:T(8,128)S(1)}, u32[]{:S(2)}, u32[]{:S(2)}) collective-permute-start(f32[8,40,128]{2,1,0:T(8,128)S(1)} %get-tuple-element.14), channel_id=1, source_target_pairs={{0,3},{1,2},{2,1},{3,0},{4,7},{5,6},{6,5},{7,4},{8,11},{9,10},{10,... | collective-permute-start | bytes 491528 | tf_op jit(solution)/shard_map/ppermute | solution.py:505
  5.2 0.0 copy-done.3
  5.2 0.0 copy-done.5
  5.2 0.0 copy-done.7
  5.2 0.5 %own_spectrum.1.spectrum_ref = f32[2,40,128]{2,1,0:T(8,128)S(1)} custom-call(s32[1]{0:T(128)} %bitcast.part_ref, f32[128,512]{1,0:T(8,128)S(1)} %copy-done.3, bf16[2,512,256]{2,1,0:T(8,128)(2,1)S(1)} %copy-done.5, bf16[4,80,384]{2,1,0:T(8,128)(2,1)S(1)} %copy-done.7), custom_call_target="tpu_custom_call" | custom-call | flops 2147483648 | bytes 1048576 | tf_op jit(solution)/shard_map/own_spectrum/pallas_call | solution.py:462
  5.7 0.0 copy-start.2
  5.7 0.0 collective-permute-done.1.rim_ref
  5.7 0.0 copy-done.9
  5.7 0.3 %add_rim.1 = f32[1,40,128]{2,1,0:T(8,128)S(1)} custom-call(s32[1]{0:T(128)} %bitcast.part_ref, f32[2,40,128]{2,1,0:T(8,128)S(1)} %own_spectrum.1.spectrum_ref, f32[32,128]{1,0:T(8,128)S(1)} %collective-permute-done.1.rim_ref, bf16[4,80,96]{2,1,0:T(8,128)(2,1)S(1)} %copy-done.9), custom_call_target="tpu_custom_call" | custom-call | flops 268435456 | bytes 1048576 | tf_op jit(solution)/shard_map/add_rim/pallas_call | solution.py:462
  6.0 1.0 %collective-permute-start.2 = (f32[1,40,128]{2,1,0:T(8,128)S(1)}, f32[1,40,128]{2,1,0:T(8,128)S(1)}, u32[]{:S(2)}, u32[]{:S(2)}) collective-permute-start(f32[1,40,128]{2,1,0:T(8,128)S(1)} %add_rim.1), channel_id=1, source_target_pairs={{0,3},{1,2},{2,1},{3,0},{4,7},{5,6},{6,5},{7,4},{8,11},{9,10},{10,... | collective-permute-start | bytes 61448 | tf_op jit(solution)/shard_map/ppermute | solution.py:505
  7.1 4.0 %collective-permute-done.2 = f32[1,40,128]{2,1,0:T(8,128)S(1)} collective-permute-done((f32[1,40,128]{2,1,0:T(8,128)S(1)}, f32[1,40,128]{2,1,0:T(8,128)S(1)}, u32[]{:S(2)}, u32[]{:S(2)}) %collective-permute-start.2) | collective-permute-done | bytes 20512 | tf_op jit(solution)/shard_map/ppermute | solution.py:505
  11.1 0.0 collective-permute-done
  11.1 0.0 copy-start.6
  11.2 0.0 copy-start.8
  11.2 0.2 collective-permute-start.3
  11.3 0.0 copy-done.2
  11.3 0.3 %near_kernels.1 = (f32[8,4,40,128]{3,2,1,0:T(8,128)S(1)}, f32[512,128]{1,0:T(8,128)S(1)}) custom-call(s32[1]{0:T(128)} %bitcast.part_ref, f32[17,40,128]{2,1,0:T(8,128)S(1)} %pad_maximum_fusion.mixed_ref, s32[512,512]{1,0:T(8,128)S(1)} %copy-done.2), custom_call_target="tpu_custom_call" | custom-call | flops 1073741824 | bytes 1048576 | tf_op jit(solution)/shard_map/near_kernels/pallas_call | solution.py:462
  11.7 1.2 %collective-permute-done.3.other_ref = f32[17,40,128]{2,1,0:T(8,128)S(1)} collective-permute-done((f32[17,40,128]{2,1,0:T(8,128)S(1)}, f32[17,40,128]{2,1,0:T(8,128)S(1)}, u32[]{:S(2)}, u32[]{:S(2)}) %collective-permute-start.3) | collective-permute-done | bytes 348192 | tf_op jit(solution)/shard_map/ppermute | solution.py:505
  12.9 0.0 copy-done.6
  12.9 0.0 copy-done.8
  12.9 0.0 copy-start
  12.9 0.0 copy-start.4
  12.9 6.2 %coherent_fields.1 = f32[40,128]{1,0:T(8,128)S(1)} custom-call(s32[1]{0:T(128)} %bitcast.part_ref, f32[17,40,128]{2,1,0:T(8,128)S(1)} %pad_maximum_fusion.mixed_ref, f32[17,40,128]{2,1,0:T(8,128)S(1)} %collective-permute-done.3.other_ref, f32[8,4,40,128]{3,2,1,0:T(8,128)S(1)} %get-tuple-element.15.near_ref, f32[512,128]{1,0:T(8,128)S(1)} %get-tuple-element.16.signs, ...), custom_call_target="tpu_custom_call" | custom-call | flops 8589934592 | bytes 1048576 | tf_op jit(solution)/shard_map/coherent_fields/pallas_call | solution.py:462
  19.1 0.2 collective-permute-start.4
  19.3 1.1 %collective-permute-done.4 = f32[40,128]{1,0:T(8,128)S(1)} collective-permute-done((f32[40,128]{1,0:T(8,128)S(1)}, f32[40,128]{1,0:T(8,128)S(1)}, u32[]{:S(2)}, u32[]{:S(2)}) %collective-permute-start.4) | collective-permute-done | bytes 20512 | tf_op jit(solution)/shard_map/ppermute | solution.py:505
  20.4 0.0 collective-permute-start.5
  20.4 3.2 %collective-permute-done.5 = f32[40,128]{1,0:T(8,128)S(1)} collective-permute-done((f32[40,128]{1,0:T(8,128)S(1)}, f32[40,128]{1,0:T(8,128)S(1)}, u32[]{:S(2)}, u32[]{:S(2)}) %collective-permute-start.5) | collective-permute-done | bytes 20512 | tf_op jit(solution)/shard_map/ppermute | solution.py:505
  23.6 0.0 copy-start.1
  23.6 0.2 collective-permute-start.6
  23.7 0.0 copy-done
  23.7 0.0 copy-done.4
  23.7 1.2 %own_gradient.1 = (f32[128,512]{1,0:T(8,128)}, f32[32,512]{1,0:T(8,128)S(1)}, f32[32,512]{1,0:T(8,128)S(1)}) custom-call(s32[1]{0:T(128)} %bitcast.part_ref, f32[128,512]{1,0:T(8,128)S(1)} %copy-done.3, f32[40,128]{1,0:T(8,128)S(1)} %add.19.sum_ref, bf16[2,256,512]{2,1,0:T(8,128)(2,1)S(1)} %copy-done, bf16[4,256,240]{2,1,0:T(8,128)(2,1)S(1)} %copy-done.4), custom_call_target="tpu_custom_call" | custom-call | flops 2147483648 | bytes 1048576 | tf_op jit(solution)/shard_map/own_gradient/pallas_call | solution.py:462
  25.0 2.7 %collective-permute-done.6.near_ref = f32[40,128]{1,0:T(8,128)S(1)} collective-permute-done((f32[40,128]{1,0:T(8,128)S(1)}, f32[40,128]{1,0:T(8,128)S(1)}, u32[]{:S(2)}, u32[]{:S(2)}) %collective-permute-start.6) | collective-permute-done | bytes 20512 | tf_op jit(solution)/shard_map/ppermute | solution.py:502
  27.7 0.0 copy-done.1
  27.7 1.1 %edge_gradient.1 = f32[128,512]{1,0:T(8,128)} custom-call(s32[1]{0:T(128)} %bitcast.part_ref, f32[128,512]{1,0:T(8,128)} %get-tuple-element.20.gradient_hbm, f32[32,512]{1,0:T(8,128)S(1)} %get-tuple-element.21.edge_ref, f32[32,512]{1,0:T(8,128)S(1)} %get-tuple-element.22.scale_ref, ...), custom_call_target="tpu_custom_call", output_to_operand_aliasing={{}: (1, {})} | custom-call | flops 268435456 | bytes 1048576 | tf_op jit(solution)/shard_map/edge_gradient/pallas_call | solution.py:462
  (4 shorter events, 0.0 us)
Async XLA Ops:
  1.2 4.5 %collective-permute-start.1 = (f32[32,128]{1,0:T(8,128)S(1)}, f32[32,128]{1,0:T(8,128)S(1)}, u32[]{:S(2)}, u32[]{:S(2)}) collective-permute-start(f32[32,128]{1,0:T(8,128)S(1)} %edge_columns.1), channel_id=1, source_target_pairs={{1,2},{2,1},{5,6},{6,5},{9,10},{10,9},{13,14},{14,13},{17,18},{18,... | collective-permute-start | bytes 49160 | tf_op jit(solution)/shard_map/ppermute | solution.py:502
  2.7 2.6 %copy-start.3 = (f32[128,512]{1,0:T(8,128)S(1)}, f32[128,512]{1,0:T(8,128)}, u32[]{:S(2)}) copy-start(f32[128,512]{1,0:T(8,128)} %theta_ref.3) | copy-start | bytes 786436
  2.7 2.6 %copy-start.5 = (bf16[2,512,256]{2,1,0:T(8,128)(2,1)S(1)}, bf16[2,512,256]{2,1,0:T(8,128)(2,1)}, u32[]{:S(2)}) copy-start(bf16[2,512,256]{2,1,0:T(8,128)(2,1)} %constant.43.clone.column_ref) | copy-start | bytes 1572868
  2.7 2.6 %copy-start.7 = (bf16[4,80,384]{2,1,0:T(8,128)(2,1)S(1)}, bf16[4,80,384]{2,1,0:T(8,128)(2,1)}, u32[]{:S(2)}) copy-start(bf16[4,80,384]{2,1,0:T(8,128)(2,1)} %constant.45.clone.rows_ref) | copy-start | bytes 737284
  4.4 1.4 %copy-start.9 = (bf16[4,80,96]{2,1,0:T(8,128)(2,1)S(1)}, bf16[4,80,96]{2,1,0:T(8,128)(2,1)}, u32[]{:S(2)}) copy-start(bf16[4,80,96]{2,1,0:T(8,128)(2,1)} %constant.47.clone.rows_ref) | copy-start | bytes 184324
  4.4 6.7 %collective-permute-start = (f32[8,40,128]{2,1,0:T(8,128)S(1)}, f32[8,40,128]{2,1,0:T(8,128)S(1)}, u32[]{:S(2)}, u32[]{:S(2)}) collective-permute-start(f32[8,40,128]{2,1,0:T(8,128)S(1)} %get-tuple-element.14), channel_id=1, source_target_pairs={{0,3},{1,2},{2,1},{3,0},{4,7},{5,6},{6,5},{7,4},{8,11},{9,10},{10,... | collective-permute-start | bytes 491528 | tf_op jit(solution)/shard_map/ppermute | solution.py:505
  5.7 5.6 %copy-start.2 = (s32[512,512]{1,0:T(8,128)S(1)}, s32[512,512]{1,0:T(8,128)}, u32[]{:S(2)}) copy-start(s32[512,512]{1,0:T(8,128)} %target_ref.1) | copy-start | bytes 3145732
  6.0 5.0 %collective-permute-start.2 = (f32[1,40,128]{2,1,0:T(8,128)S(1)}, f32[1,40,128]{2,1,0:T(8,128)S(1)}, u32[]{:S(2)}, u32[]{:S(2)}) collective-permute-start(f32[1,40,128]{2,1,0:T(8,128)S(1)} %add_rim.1), channel_id=1, source_target_pairs={{0,3},{1,2},{2,1},{3,0},{4,7},{5,6},{6,5},{7,4},{8,11},{9,10},{10,... | collective-permute-start | bytes 61448 | tf_op jit(solution)/shard_map/ppermute | solution.py:505
  11.1 1.8 %copy-start.6 = (bf16[512,240]{1,0:T(8,128)(2,1)S(1)}, bf16[512,240]{1,0:T(8,128)(2,1)}, u32[]{:S(2)}) copy-start(bf16[512,240]{1,0:T(8,128)(2,1)} %constant.52.clone.row_ref) | copy-start | bytes 737284
  11.2 1.7 %copy-start.8 = (bf16[160,512]{1,0:T(8,128)(2,1)S(1)}, bf16[160,512]{1,0:T(8,128)(2,1)}, u32[]{:S(2)}) copy-start(bf16[160,512]{1,0:T(8,128)(2,1)} %constant.53.clone.row_turned_ref) | copy-start | bytes 491524
  11.2 1.7 %collective-permute-start.3 = (f32[17,40,128]{2,1,0:T(8,128)S(1)}, f32[17,40,128]{2,1,0:T(8,128)S(1)}, u32[]{:S(2)}, u32[]{:S(2)}) collective-permute-start(f32[17,40,128]{2,1,0:T(8,128)S(1)} %pad_maximum_fusion.mixed_ref), channel_id=1, source_target_pairs={{0,1},{1,0},{2,3},{3,2},{4,5},{5,4},{6,7},{7,6},{8,9},{9,8},{10,11... | collective-permute-start | bytes 1044488 | tf_op jit(solution)/shard_map/ppermute | solution.py:505
  12.9 10.8 %copy-start = (bf16[2,256,512]{2,1,0:T(8,128)(2,1)S(1)}, bf16[2,256,512]{2,1,0:T(8,128)(2,1)}, u32[]{:S(2)}) copy-start(bf16[2,256,512]{2,1,0:T(8,128)(2,1)} %constant.51.clone.turned_ref) | copy-start | bytes 1572868
  12.9 10.8 %copy-start.4 = (bf16[4,256,240]{2,1,0:T(8,128)(2,1)S(1)}, bf16[4,256,240]{2,1,0:T(8,128)(2,1)}, u32[]{:S(2)}) copy-start(bf16[4,256,240]{2,1,0:T(8,128)(2,1)} %constant.46.clone.rows_ref) | copy-start | bytes 1474564
  19.1 1.3 %collective-permute-start.4 = (f32[40,128]{1,0:T(8,128)S(1)}, f32[40,128]{1,0:T(8,128)S(1)}, u32[]{:S(2)}, u32[]{:S(2)}) collective-permute-start(f32[40,128]{1,0:T(8,128)S(1)} %coherent_fields.1), channel_id=1, source_target_pairs={{0,1},{1,0},{2,3},{3,2},{4,5},{5,4},{6,7},{7,6},{8,9},{9,8},{10,11... | collective-permute-start | bytes 61448 | tf_op jit(solution)/shard_map/ppermute | solution.py:505
  20.4 3.2 %collective-permute-start.5 = (f32[40,128]{1,0:T(8,128)S(1)}, f32[40,128]{1,0:T(8,128)S(1)}, u32[]{:S(2)}, u32[]{:S(2)}) collective-permute-start(f32[40,128]{1,0:T(8,128)S(1)} %add.18), channel_id=1, source_target_pairs={{0,3},{1,2},{2,1},{3,0},{4,7},{5,6},{6,5},{7,4},{8,11},{9,10},{10,... | collective-permute-start | bytes 61448 | tf_op jit(solution)/shard_map/ppermute | solution.py:505
  23.6 4.1 %copy-start.1 = (bf16[4,64,240]{2,1,0:T(8,128)(2,1)S(1)}, bf16[4,64,240]{2,1,0:T(8,128)(2,1)}, u32[]{:S(2)}) copy-start(bf16[4,64,240]{2,1,0:T(8,128)(2,1)} %constant.48.clone.rows_ref) | copy-start | bytes 368644
  23.6 4.1 %collective-permute-start.6 = (f32[40,128]{1,0:T(8,128)S(1)}, f32[40,128]{1,0:T(8,128)S(1)}, u32[]{:S(2)}, u32[]{:S(2)}) collective-permute-start(f32[40,128]{1,0:T(8,128)S(1)} %add.19.sum_ref), channel_id=1, source_target_pairs={{0,1},{3,2},{4,5},{7,6},{8,9},{11,10},{12,13},{15,14},{16,17},{19,... | collective-permute-start | bytes 61448 | tf_op jit(solution)/shard_map/ppermute | solution.py:502

commit v11 on v8

--- a/solution.py
+++ b/solution.py
@@ -168,11 +168,15 @@
 
 
 def open_kernel(
-    part_ref, real_hbm, imag_hbm, thresholds_hbm, weights_hbm, forward_hbm, backward_hbm,
-    out_ref, shares_ref, forward_ref, backward_ref, real_ref, imag_ref, thresholds_ref, weights_ref, stage, sems,
+    part_ref, theta_hbm, waves_hbm, real_hbm, imag_hbm, thresholds_hbm, weights_hbm, forward_hbm, backward_hbm,
+    out_ref, rim_ref, shares_ref, forward_ref, backward_ref, theta_ref, waves_ref, real_ref, imag_ref, thresholds_ref,
+    weights_ref, stage, sems,
 ):
     part = part_of(part_ref)
+    edge = pl.ds(pl.multiple_of(jnp.where(part == 0, 0, ROWS - HALO), HALO), HALO)
     moves = [
+        (theta_hbm.at[edge], theta_ref),
+        (waves_hbm, waves_ref),
         (real_hbm, real_ref),
         (imag_hbm, imag_ref),
         (thresholds_hbm, thresholds_ref),
@@ -205,8 +209,9 @@
     keep_top = jnp.where(valid, scale, 0.0)
     keep_bottom = jnp.where((row == 0) & (lane == HALF), 0.0, keep_top)
     first = lane % FB < HALF
-    for copy in copies[:4]:
+    for copy in copies[:6]:
         copy.wait()
+    rim_ref[...] = columns_of(jnp.tanh(mask_steep * theta_ref[...]), waves_ref)
     for cond in range(local_conds):
         for kern in range(KERNELS):
             for piece, ref in enumerate((real_ref, imag_ref)):
@@ -246,22 +251,8 @@
             weight = weights_ref[lax.bitwise_xor(part, step) * local_conds + i]
             shares = jnp.where(row == group * local_conds + i, weight.astype(F32), shares)
     shares_ref[...] = shares / weight_sum.astype(F32)
-    for copy in copies[4:]:
+    for copy in copies[6:]:
         copy.wait()
-
-
-def send_rim_kernel(part_ref, theta_hbm, waves_hbm, out_ref, theta_ref, waves_ref, sems):
-    rows = pl.ds(pl.multiple_of(jnp.where(part_of(part_ref) == 0, 0, ROWS - HALO), HALO), HALO)
-    copies = [
-        pltpu.make_async_copy(theta_hbm.at[rows], theta_ref, sems.at[0]),
-        pltpu.make_async_copy(waves_hbm, waves_ref, sems.at[1]),
-    ]
-    for copy in copies:
-        copy.start()
-    copies[0].wait()
-    mask = jnp.tanh(mask_steep * theta_ref[...])
-    copies[1].wait()
-    out_ref[...] = columns_of(mask, waves_ref)
 
 
 def spectrum_kernel(part_ref, theta_ref, column_ref, rows_ref, out_ref):
@@ -510,45 +501,35 @@
         return lax.ppermute(value, "cond", [(i, i ^ step) for i in range(PARTS)])
 
     kernel_shape = (local_conds, KSUP, KERNELS, KSUP)
-    own, shares, forward, backward = call(
+    own, rim, shares, forward, backward = call(
         open_kernel,
         (parts,),
         tuple(
             pltpu.with_memory_space_constraint(value, pltpu.HBM)
             for value in (
-                kernel_real.transpose(0, 2, 1, 3), kernel_imag.transpose(0, 2, 1, 3), thresholds, weights,
+                theta, table["waves"], kernel_real.transpose(0, 2, 1, 3), kernel_imag.transpose(0, 2, 1, 3), thresholds, weights,
                 table["forward"], table["backward"],
             )
         ),
-        [hbm] * 6,
+        [hbm] * 8,
         [
             floats(2 * local, FA, 2 * FB),
+            floats(HALO, 2 * FB),
             floats(CONDS, ROWS),
             jax.ShapeDtypeStruct(table["forward"].shape[1:], BF),
             jax.ShapeDtypeStruct(table["backward"].shape[1:], BF),
         ],
         scratch=(
+            pltpu.VMEM((HALO, TP), F32),
+            pltpu.VMEM(table["waves"].shape, BF),
             pltpu.VMEM(kernel_shape, F32),
             pltpu.VMEM(kernel_shape, F32),
             pltpu.SMEM(thresholds.shape, F32),
             pltpu.SMEM(weights.shape, jnp.int32),
             pltpu.VMEM((2 * local, 72, 2 * FB), F32),
-            pltpu.SemaphoreType.DMA((6,)),
+            pltpu.SemaphoreType.DMA((8,)),
         ),
         name="open_parts",
-    )
-    rim = call(
-        send_rim_kernel,
-        (parts,),
-        tuple(pltpu.with_memory_space_constraint(value, pltpu.HBM) for value in (theta, table["waves"])),
-        [hbm, hbm],
-        floats(HALO, 2 * FB),
-        scratch=(
-            pltpu.VMEM((HALO, TP), F32),
-            pltpu.VMEM(table["waves"].shape, BF),
-            pltpu.SemaphoreType.DMA((2,)),
-        ),
-        name="edge_columns",
     )
     rim = across(rim, (0, 0), (last, last), [(1, 2), (2, 1)])
     spectrum = call(

time: 29 us -> 27.8 us (0.959)
  Pallas kernels: 12.5 us -> 11.5 us
    ppermute x2, waiting for transfers between devices: 2.69 us -> 3.75 us  [across(): return lax.ppermute(value, ('tile', 'cond'), pairs)]
    pallas_call x8 -> x7, Pallas kernels: 12.5 us -> 11.5 us  [call(): pl.pallas_call(kernel, grid_spec=pltpu.PrefetchScalarGridSpec(num_scalar_...]
    ppermute x5, waiting for transfers between devices: 9.47 us -> 8.59 us  [partner(): return lax.ppermute(value, 'cond', [(i, i ^ step) for i in range(PARTS)])]
  transfers between devices with their start and end apart: 7 -> 7, of which waited for: 5 -> 6; matrix products, arithmetic and copies ran while one was open for 0% -> 0% of each run, Pallas kernels for 14% -> 8%
where the time goes in v11:
time: 27.8 us; the launch traced here: 27.7 us
  waiting for transfers between devices  12.3 us (44%)
  Pallas kernels  11.5 us (41%)
  starting transfers between devices  3.66 us (13%)
    pallas_call x7, Pallas kernels, call(): pl.pallas_call(kernel, grid_spec=pltpu.PrefetchScalarGridSpec(num_scalar_...  11.5 us
    ppermute x5, waiting for transfers between devices, partner(): return lax.ppermute(value, 'cond', [(i, i ^ step) for i in range(PARTS)])  8.59 us
    ppermute x2, waiting for transfers between devices, across(): return lax.ppermute(value, ('tile', 'cond'), pairs)  3.75 us
    ppermute x5, starting transfers between devices, partner(): return lax.ppermute(value, 'cond', [(i, i ^ step) for i in range(PARTS)])  2.03 us
    ppermute x2, starting transfers between devices, across(): return lax.ppermute(value, ('tile', 'cond'), pairs)  1.63 us
  transfers between devices with their start and end apart: 7, of which 6 were waited for; matrix products, arithmetic and copies ran while one was open for 0% of the time, Pallas kernels for 8%

profile of v11, /device:TPU:24, one launch (start us, length us, event | category | flops | bytes accessed | tf_op | source)
XLA Modules:
  0.0 27.7 jit_solution(9244133566598671438)
XLA Ops:
  0.0 0.0 copy-start.1
  0.0 0.0 copy-start.5
  0.0 0.0 copy-start.7
  0.0 1.9 %open_parts.1 = (f32[8,40,128]{2,1,0:T(8,128)S(1)}, f32[32,128]{1,0:T(8,128)S(1)}, f32[8,128]{1,0:T(8,128)S(1)}, bf16[384,256]{1,0:T(8,128)(2,1)S(1)}, bf16[384,256]{1,0:T(8,128)(2,1)S(1)}) custom-call(s32[1]{0:T(128)} %bitcast.part_ref, f32[128,512]{1,0:T(8,128)} %theta_ref.3, bf16[2,512,128]{2,1,0:T(8,128)(2,1)} %constant.44.clone.waves_hbm, ...), custom_call_target="tpu_custom_call" | custom-call | flops 268435456 | bytes 1048576 | tf_op jit(solution)/shard_map/open_parts/pallas_call | solution.py:458
  1.9 1.5 %collective-permute-start.1 = (f32[32,128]{1,0:T(8,128)S(1)}, f32[32,128]{1,0:T(8,128)S(1)}, u32[]{:S(2)}, u32[]{:S(2)}) collective-permute-start(f32[32,128]{1,0:T(8,128)S(1)} %get-tuple-element.16), channel_id=1, source_target_pairs={{1,2},{2,1},{5,6},{6,5},{9,10},{10,9},{13,14},{14,13},{17,18},{18,... | collective-permute-start | bytes 49160 | tf_op jit(solution)/shard_map/ppermute | solution.py:498
  3.3 0.0 copy-start.9
  3.3 0.8 %collective-permute-start = (f32[8,40,128]{2,1,0:T(8,128)S(1)}, f32[8,40,128]{2,1,0:T(8,128)S(1)}, u32[]{:S(2)}, u32[]{:S(2)}) collective-permute-start(f32[8,40,128]{2,1,0:T(8,128)S(1)} %get-tuple-element.15), channel_id=1, source_target_pairs={{0,3},{1,2},{2,1},{3,0},{4,7},{5,6},{6,5},{7,4},{8,11},{9,10},{10,... | collective-permute-start | bytes 491528 | tf_op jit(solution)/shard_map/ppermute | solution.py:501
  4.1 0.0 copy-done.1
  4.1 0.0 copy-done.5
  4.1 0.0 copy-done.7
  4.1 0.5 %own_spectrum.1.spectrum_ref = f32[2,40,128]{2,1,0:T(8,128)S(1)} custom-call(s32[1]{0:T(128)} %bitcast.part_ref, f32[128,512]{1,0:T(8,128)S(1)} %copy-done.1, bf16[2,512,256]{2,1,0:T(8,128)(2,1)S(1)} %copy-done.5, bf16[4,80,384]{2,1,0:T(8,128)(2,1)S(1)} %copy-done.7), custom_call_target="tpu_custom_call" | custom-call | flops 2147483648 | bytes 1048576 | tf_op jit(solution)/shard_map/own_spectrum/pallas_call | solution.py:458
  4.6 0.0 copy-start.3
  4.6 1.1 %collective-permute-done.1.rim_ref = f32[32,128]{1,0:T(8,128)S(1)} collective-permute-done((f32[32,128]{1,0:T(8,128)S(1)}, f32[32,128]{1,0:T(8,128)S(1)}, u32[]{:S(2)}, u32[]{:S(2)}) %collective-permute-start.1) | collective-permute-done | bytes 16416 | tf_op jit(solution)/shard_map/ppermute | solution.py:498
  5.7 0.0 copy-done.9
  5.7 0.3 %add_rim.1 = f32[1,40,128]{2,1,0:T(8,128)S(1)} custom-call(s32[1]{0:T(128)} %bitcast.part_ref, f32[2,40,128]{2,1,0:T(8,128)S(1)} %own_spectrum.1.spectrum_ref, f32[32,128]{1,0:T(8,128)S(1)} %collective-permute-done.1.rim_ref, bf16[4,80,96]{2,1,0:T(8,128)(2,1)S(1)} %copy-done.9), custom_call_target="tpu_custom_call" | custom-call | flops 268435456 | bytes 1048576 | tf_op jit(solution)/shard_map/add_rim/pallas_call | solution.py:458
  6.0 0.7 %collective-permute-start.2 = (f32[1,40,128]{2,1,0:T(8,128)S(1)}, f32[1,40,128]{2,1,0:T(8,128)S(1)}, u32[]{:S(2)}, u32[]{:S(2)}) collective-permute-start(f32[1,40,128]{2,1,0:T(8,128)S(1)} %add_rim.1), channel_id=1, source_target_pairs={{0,3},{1,2},{2,1},{3,0},{4,7},{5,6},{6,5},{7,4},{8,11},{9,10},{10,... | collective-permute-start | bytes 61448 | tf_op jit(solution)/shard_map/ppermute | solution.py:501
  6.7 3.3 %collective-permute-done.2 = f32[1,40,128]{2,1,0:T(8,128)S(1)} collective-permute-done((f32[1,40,128]{2,1,0:T(8,128)S(1)}, f32[1,40,128]{2,1,0:T(8,128)S(1)}, u32[]{:S(2)}, u32[]{:S(2)}) %collective-permute-start.2) | collective-permute-done | bytes 20512 | tf_op jit(solution)/shard_map/ppermute | solution.py:501
  10.0 0.0 collective-permute-done
  10.0 0.0 copy-start.6
  10.0 0.0 copy-start.8
  10.1 0.2 collective-permute-start.3
  10.2 0.0 copy-done.3
  10.2 0.3 %near_kernels.1 = (f32[8,4,40,128]{3,2,1,0:T(8,128)S(1)}, f32[512,128]{1,0:T(8,128)S(1)}) custom-call(s32[1]{0:T(128)} %bitcast.part_ref, f32[17,40,128]{2,1,0:T(8,128)S(1)} %pad_maximum_fusion.mixed_ref, s32[512,512]{1,0:T(8,128)S(1)} %copy-done.3), custom_call_target="tpu_custom_call" | custom-call | flops 1073741824 | bytes 1048576 | tf_op jit(solution)/shard_map/near_kernels/pallas_call | solution.py:458
  10.6 1.2 %collective-permute-done.3.other_ref = f32[17,40,128]{2,1,0:T(8,128)S(1)} collective-permute-done((f32[17,40,128]{2,1,0:T(8,128)S(1)}, f32[17,40,128]{2,1,0:T(8,128)S(1)}, u32[]{:S(2)}, u32[]{:S(2)}) %collective-permute-start.3) | collective-permute-done | bytes 348192 | tf_op jit(solution)/shard_map/ppermute | solution.py:501
  11.8 0.0 copy-done.6
  11.8 0.0 copy-done.8
  11.8 0.0 copy-start
  11.8 0.0 copy-start.4
  11.8 6.2 %coherent_fields.1 = f32[40,128]{1,0:T(8,128)S(1)} custom-call(s32[1]{0:T(128)} %bitcast.part_ref, f32[17,40,128]{2,1,0:T(8,128)S(1)} %pad_maximum_fusion.mixed_ref, f32[17,40,128]{2,1,0:T(8,128)S(1)} %collective-permute-done.3.other_ref, f32[8,4,40,128]{3,2,1,0:T(8,128)S(1)} %get-tuple-element.17.near_ref, f32[512,128]{1,0:T(8,128)S(1)} %get-tuple-element.18.signs, ...), custom_call_target="tpu_custom_call" | custom-call | flops 8589934592 | bytes 1048576 | tf_op jit(solution)/shard_map/coherent_fields/pallas_call | solution.py:458
  18.0 0.2 collective-permute-start.4
  18.2 1.1 %collective-permute-done.4 = f32[40,128]{1,0:T(8,128)S(1)} collective-permute-done((f32[40,128]{1,0:T(8,128)S(1)}, f32[40,128]{1,0:T(8,128)S(1)}, u32[]{:S(2)}, u32[]{:S(2)}) %collective-permute-start.4) | collective-permute-done | bytes 20512 | tf_op jit(solution)/shard_map/ppermute | solution.py:501
  19.2 0.1 collective-permute-start.5
  19.4 3.1 %collective-permute-done.5 = f32[40,128]{1,0:T(8,128)S(1)} collective-permute-done((f32[40,128]{1,0:T(8,128)S(1)}, f32[40,128]{1,0:T(8,128)S(1)}, u32[]{:S(2)}, u32[]{:S(2)}) %collective-permute-start.5) | collective-permute-done | bytes 20512 | tf_op jit(solution)/shard_map/ppermute | solution.py:501
  22.5 0.0 copy-start.2
  22.5 0.2 collective-permute-start.6
  22.6 0.0 copy-done
  22.6 0.0 copy-done.4
  22.6 1.2 %own_gradient.1 = (f32[128,512]{1,0:T(8,128)}, f32[32,512]{1,0:T(8,128)S(1)}, f32[32,512]{1,0:T(8,128)S(1)}) custom-call(s32[1]{0:T(128)} %bitcast.part_ref, f32[128,512]{1,0:T(8,128)S(1)} %copy-done.1, f32[40,128]{1,0:T(8,128)S(1)} %add.19.sum_ref, bf16[2,256,512]{2,1,0:T(8,128)(2,1)S(1)} %copy-done, bf16[4,256,240]{2,1,0:T(8,128)(2,1)S(1)} %copy-done.4), custom_call_target="tpu_custom_call" | custom-call | flops 2147483648 | bytes 1048576 | tf_op jit(solution)/shard_map/own_gradient/pallas_call | solution.py:458
  23.9 2.7 %collective-permute-done.6.near_ref = f32[40,128]{1,0:T(8,128)S(1)} collective-permute-done((f32[40,128]{1,0:T(8,128)S(1)}, f32[40,128]{1,0:T(8,128)S(1)}, u32[]{:S(2)}, u32[]{:S(2)}) %collective-permute-start.6) | collective-permute-done | bytes 20512 | tf_op jit(solution)/shard_map/ppermute | solution.py:498
  26.6 0.0 copy-done.2
  26.6 1.1 %edge_gradient.1 = f32[128,512]{1,0:T(8,128)} custom-call(s32[1]{0:T(128)} %bitcast.part_ref, f32[128,512]{1,0:T(8,128)} %get-tuple-element.22.gradient_hbm, f32[32,512]{1,0:T(8,128)S(1)} %get-tuple-element.23.edge_ref, f32[32,512]{1,0:T(8,128)S(1)} %get-tuple-element.24.scale_ref, ...), custom_call_target="tpu_custom_call", output_to_operand_aliasing={{}: (1, {})} | custom-call | flops 268435456 | bytes 1048576 | tf_op jit(solution)/shard_map/edge_gradient/pallas_call | solution.py:458
  (4 shorter events, 0.0 us)
Async XLA Ops:
  0.0 4.1 %copy-start.1 = (f32[128,512]{1,0:T(8,128)S(1)}, f32[128,512]{1,0:T(8,128)}, u32[]{:S(2)}) copy-start(f32[128,512]{1,0:T(8,128)} %theta_ref.3) | copy-start | bytes 786436
  0.0 4.1 %copy-start.5 = (bf16[2,512,256]{2,1,0:T(8,128)(2,1)S(1)}, bf16[2,512,256]{2,1,0:T(8,128)(2,1)}, u32[]{:S(2)}) copy-start(bf16[2,512,256]{2,1,0:T(8,128)(2,1)} %constant.43.clone.column_ref) | copy-start | bytes 1572868
  0.0 4.1 %copy-start.7 = (bf16[4,80,384]{2,1,0:T(8,128)(2,1)S(1)}, bf16[4,80,384]{2,1,0:T(8,128)(2,1)}, u32[]{:S(2)}) copy-start(bf16[4,80,384]{2,1,0:T(8,128)(2,1)} %constant.45.clone.rows_ref) | copy-start | bytes 737284
  1.9 3.8 %collective-permute-start.1 = (f32[32,128]{1,0:T(8,128)S(1)}, f32[32,128]{1,0:T(8,128)S(1)}, u32[]{:S(2)}, u32[]{:S(2)}) collective-permute-start(f32[32,128]{1,0:T(8,128)S(1)} %get-tuple-element.16), channel_id=1, source_target_pairs={{1,2},{2,1},{5,6},{6,5},{9,10},{10,9},{13,14},{14,13},{17,18},{18,... | collective-permute-start | bytes 49160 | tf_op jit(solution)/shard_map/ppermute | solution.py:498
  3.3 2.3 %copy-start.9 = (bf16[4,80,96]{2,1,0:T(8,128)(2,1)S(1)}, bf16[4,80,96]{2,1,0:T(8,128)(2,1)}, u32[]{:S(2)}) copy-start(bf16[4,80,96]{2,1,0:T(8,128)(2,1)} %constant.47.clone.rows_ref) | copy-start | bytes 184324
  3.3 6.7 %collective-permute-start = (f32[8,40,128]{2,1,0:T(8,128)S(1)}, f32[8,40,128]{2,1,0:T(8,128)S(1)}, u32[]{:S(2)}, u32[]{:S(2)}) collective-permute-start(f32[8,40,128]{2,1,0:T(8,128)S(1)} %get-tuple-element.15), channel_id=1, source_target_pairs={{0,3},{1,2},{2,1},{3,0},{4,7},{5,6},{6,5},{7,4},{8,11},{9,10},{10,... | collective-permute-start | bytes 491528 | tf_op jit(solution)/shard_map/ppermute | solution.py:501
  4.6 5.6 %copy-start.3 = (s32[512,512]{1,0:T(8,128)S(1)}, s32[512,512]{1,0:T(8,128)}, u32[]{:S(2)}) copy-start(s32[512,512]{1,0:T(8,128)} %target_ref.1) | copy-start | bytes 3145732
  6.0 4.0 %collective-permute-start.2 = (f32[1,40,128]{2,1,0:T(8,128)S(1)}, f32[1,40,128]{2,1,0:T(8,128)S(1)}, u32[]{:S(2)}, u32[]{:S(2)}) collective-permute-start(f32[1,40,128]{2,1,0:T(8,128)S(1)} %add_rim.1), channel_id=1, source_target_pairs={{0,3},{1,2},{2,1},{3,0},{4,7},{5,6},{6,5},{7,4},{8,11},{9,10},{10,... | collective-permute-start | bytes 61448 | tf_op jit(solution)/shard_map/ppermute | solution.py:501
  10.0 1.8 %copy-start.6 = (bf16[512,240]{1,0:T(8,128)(2,1)S(1)}, bf16[512,240]{1,0:T(8,128)(2,1)}, u32[]{:S(2)}) copy-start(bf16[512,240]{1,0:T(8,128)(2,1)} %constant.52.clone.row_ref) | copy-start | bytes 737284
  10.0 1.7 %copy-start.8 = (bf16[160,512]{1,0:T(8,128)(2,1)S(1)}, bf16[160,512]{1,0:T(8,128)(2,1)}, u32[]{:S(2)}) copy-start(bf16[160,512]{1,0:T(8,128)(2,1)} %constant.53.clone.row_turned_ref) | copy-start | bytes 491524
  10.1 1.7 %collective-permute-start.3 = (f32[17,40,128]{2,1,0:T(8,128)S(1)}, f32[17,40,128]{2,1,0:T(8,128)S(1)}, u32[]{:S(2)}, u32[]{:S(2)}) collective-permute-start(f32[17,40,128]{2,1,0:T(8,128)S(1)} %pad_maximum_fusion.mixed_ref), channel_id=1, source_target_pairs={{0,1},{1,0},{2,3},{3,2},{4,5},{5,4},{6,7},{7,6},{8,9},{9,8},{10,11... | collective-permute-start | bytes 1044488 | tf_op jit(solution)/shard_map/ppermute | solution.py:501
  11.8 10.8 %copy-start = (bf16[2,256,512]{2,1,0:T(8,128)(2,1)S(1)}, bf16[2,256,512]{2,1,0:T(8,128)(2,1)}, u32[]{:S(2)}) copy-start(bf16[2,256,512]{2,1,0:T(8,128)(2,1)} %constant.51.clone.turned_ref) | copy-start | bytes 1572868
  11.8 10.8 %copy-start.4 = (bf16[4,256,240]{2,1,0:T(8,128)(2,1)S(1)}, bf16[4,256,240]{2,1,0:T(8,128)(2,1)}, u32[]{:S(2)}) copy-start(bf16[4,256,240]{2,1,0:T(8,128)(2,1)} %constant.46.clone.rows_ref) | copy-start | bytes 1474564
  18.0 1.3 %collective-permute-start.4 = (f32[40,128]{1,0:T(8,128)S(1)}, f32[40,128]{1,0:T(8,128)S(1)}, u32[]{:S(2)}, u32[]{:S(2)}) collective-permute-start(f32[40,128]{1,0:T(8,128)S(1)} %coherent_fields.1), channel_id=1, source_target_pairs={{0,1},{1,0},{2,3},{3,2},{4,5},{5,4},{6,7},{7,6},{8,9},{9,8},{10,11... | collective-permute-start | bytes 61448 | tf_op jit(solution)/shard_map/ppermute | solution.py:501
  19.2 3.2 %collective-permute-start.5 = (f32[40,128]{1,0:T(8,128)S(1)}, f32[40,128]{1,0:T(8,128)S(1)}, u32[]{:S(2)}, u32[]{:S(2)}) collective-permute-start(f32[40,128]{1,0:T(8,128)S(1)} %add.18), channel_id=1, source_target_pairs={{0,3},{1,2},{2,1},{3,0},{4,7},{5,6},{6,5},{7,4},{8,11},{9,10},{10,... | collective-permute-start | bytes 61448 | tf_op jit(solution)/shard_map/ppermute | solution.py:501
  22.5 4.1 %copy-start.2 = (bf16[4,64,240]{2,1,0:T(8,128)(2,1)S(1)}, bf16[4,64,240]{2,1,0:T(8,128)(2,1)}, u32[]{:S(2)}) copy-start(bf16[4,64,240]{2,1,0:T(8,128)(2,1)} %constant.48.clone.rows_ref) | copy-start | bytes 368644
  22.5 4.1 %collective-permute-start.6 = (f32[40,128]{1,0:T(8,128)S(1)}, f32[40,128]{1,0:T(8,128)S(1)}, u32[]{:S(2)}, u32[]{:S(2)}) collective-permute-start(f32[40,128]{1,0:T(8,128)S(1)} %add.19.sum_ref), channel_id=1, source_target_pairs={{0,1},{3,2},{4,5},{7,6},{8,9},{11,10},{12,13},{15,14},{16,17},{19,... | collective-permute-start | bytes 61448 | tf_op jit(solution)/shard_map/ppermute | solution.py:498

commit v12 on v11

--- a/solution.py
+++ b/solution.py
@@ -309,46 +309,49 @@
     each = 2 * local
     even, odd = unpack(mixed_ref[2 * each] + other_ref[2 * each])
 
-    def put_line(kern, values):
-        he_real, he_imag, ho_real, ho_imag = values
-        start = kern * tall
-        for i, value in enumerate(
-            (
-                even * he_real + odd * ho_imag,
-                odd * he_real - even * ho_imag,
-                even * he_imag - odd * ho_real,
-                odd * he_imag + even * ho_real,
-            )
-        ):
-            lines[start + i * FA : start + (i + 1) * FA] = value
-
-    def arrays_of(kern):
-        ref = near_ref if kern < count // 2 else far_ref
-        return [ref[kern % (count // 2), i] for i in range(4)]
+    def write_lines(ref, offset):
+        def body(kern, carry):
+            he_real, he_imag, ho_real, ho_imag = (ref[kern, i] for i in range(4))
+            start = (kern + offset) * tall
+            for i, value in enumerate(
+                (
+                    even * he_real + odd * ho_imag,
+                    odd * he_real - even * ho_imag,
+                    even * he_imag - odd * ho_real,
+                    odd * he_imag + even * ho_real,
+                )
+            ):
+                lines[pl.ds(pl.multiple_of(start + i * FA, FA), FA)] = value
+            return carry
+
+        lax.fori_loop(0, count // 2, body, 0, unroll=2)
 
     for group in range(PARTS):
         ref = (mixed_ref, other_ref)[group // 2].at[pl.ds(group % 2 * each, each)]
         for i in range(CONDS // PARTS):
             place = group * (CONDS // PARTS) + i
             levels_ref[place : place + 1] = ref[SPARE_BLOCKS + i][FA - 1 :]
-        if group < 2:
-            for kern in range(group * local, (group + 1) * local):
-                put_line(kern, arrays_of(kern))
-        else:
+        if group >= 2:
+
             def put(kern, values, group=group):
                 for i, value in enumerate(values):
                     far_ref[(group - 2) * local + kern, i] = value
-                put_line(group * local + kern, values)
 
             unpack_group(ref, put)
+    write_lines(near_ref, 0)
+    write_lines(far_ref, count // 2)
 
     high, low = split(lines[...])
-    lines_folded = dot(jnp.concatenate([high, low], axis=1), forward_ref[: 4 * FB]) + dot(high, forward_ref[4 * FB :])
-    for kern in range(count):
+    backs[...] = dot(jnp.concatenate([high, low], axis=1), forward_ref[: 4 * FB]) + dot(high, forward_ref[4 * FB :])
+
+    def rows_of(kern, i):
+        start = kern * tall + 2 * FA * i
+        return (backs[pl.ds(pl.multiple_of(start + j * FA, FA), FA)] for j in range(2))
+
+    def fold(kern, carry):
         parts = []
         for i in range(2):
-            x_part = lines_folded[tall * kern + 2 * FA * i : tall * kern + 2 * FA * i + FA]
-            y_part = lines_folded[tall * kern + 2 * FA * i + FA : tall * kern + 2 * FA * (i + 1)]
+            x_part, y_part = rows_of(kern, i)
             parts.append(
                 jnp.concatenate(
                     [x_part[:, :ROWS] + y_part[:, ROWS:], y_part[:, :ROWS] - x_part[:, ROWS:]], axis=0
@@ -356,6 +359,9 @@
             )
         high, low = split(jnp.concatenate(parts, axis=1))
         folded[kern] = jnp.concatenate([high, high, low], axis=0)
+        return carry
+
+    lax.fori_loop(0, count, fold, 0, unroll=2)
     total[...] = jnp.zeros_like(total)
 
     def expose(cond, carry):
@@ -393,23 +399,28 @@
     high, low = split(turned[...].reshape(count * tall, ROWS))
     backs[...] = dot(jnp.concatenate([high, low], axis=1), backward_ref[: 2 * ROWS]) + dot(high, backward_ref[2 * ROWS :])
 
-    sum_even = jnp.zeros((FA, 2 * FB), F32)
-    sum_odd = jnp.zeros((FA, 2 * FB), F32)
-    for kern in range(count):
-        grads = []
-        for i in range(2):
-            c_part = backs[tall * kern + 2 * FA * i : tall * kern + 2 * FA * i + FA]
-            s_part = backs[tall * kern + 2 * FA * i + FA : tall * kern + 2 * FA * (i + 1)]
-            grads.append(
-                (
-                    c_part[:, : 2 * FB] - s_part[:, 2 * FB :],
-                    s_part[:, : 2 * FB] + c_part[:, 2 * FB :],
+    sums = (jnp.zeros((FA, 2 * FB), F32),) * 2
+    for offset, ref in ((0, near_ref), (count // 2, far_ref)):
+
+        def gather(kern, carry, offset=offset, ref=ref):
+            sum_even, sum_odd = carry
+            grads = []
+            for i in range(2):
+                c_part, s_part = rows_of(kern + offset, i)
+                grads.append(
+                    (
+                        c_part[:, : 2 * FB] - s_part[:, 2 * FB :],
+                        s_part[:, : 2 * FB] + c_part[:, 2 * FB :],
+                    )
                 )
-            )
-        (x_real, y_real), (x_imag, y_imag) = grads
-        he_real, he_imag, ho_real, ho_imag = arrays_of(kern)
-        sum_even = sum_even + x_real * he_real + x_imag * he_imag - y_real * ho_imag + y_imag * ho_real
-        sum_odd = sum_odd + x_real * ho_imag - x_imag * ho_real + y_real * he_real + y_imag * he_imag
+            (x_real, y_real), (x_imag, y_imag) = grads
+            he_real, he_imag, ho_real, ho_imag = (ref[kern, i] for i in range(4))
+            sum_even = sum_even + x_real * he_real + x_imag * he_imag - y_real * ho_imag + y_imag * ho_real
+            sum_odd = sum_odd + x_real * ho_imag - x_imag * ho_real + y_real * he_real + y_imag * he_imag
+            return sum_even, sum_odd
+
+        sums = lax.fori_loop(0, count // 2, gather, sums, unroll=2)
+    sum_even, sum_odd = sums
     out_ref[...] = pack(sum_even, sum_odd)
 
 

time: 27.8 us -> 28.6 us (1.029)
  Pallas kernels: 11.5 us -> 12.3 us
    pallas_call x7, Pallas kernels: 11.5 us -> 12.3 us  [call(): pl.pallas_call(kernel, grid_spec=pltpu.PrefetchScalarGridSpec(num_scalar_...]
where the time goes in v12:
time: 28.6 us; the launch traced here: 28.4 us
  Pallas kernels  12.3 us (43%)
  waiting for transfers between devices  12.3 us (43%)
  starting transfers between devices  3.66 us (13%)
    pallas_call x7, Pallas kernels, call(): pl.pallas_call(kernel, grid_spec=pltpu.PrefetchScalarGridSpec(num_scalar_...  12.3 us
    ppermute x5, waiting for transfers between devices, partner(): return lax.ppermute(value, 'cond', [(i, i ^ step) for i in range(PARTS)])  8.59 us
    ppermute x2, waiting for transfers between devices, across(): return lax.ppermute(value, ('tile', 'cond'), pairs)  3.75 us
    ppermute x5, starting transfers between devices, partner(): return lax.ppermute(value, 'cond', [(i, i ^ step) for i in range(PARTS)])  2.03 us
    ppermute x2, starting transfers between devices, across(): return lax.ppermute(value, ('tile', 'cond'), pairs)  1.63 us
  transfers between devices with their start and end apart: 7, of which 6 were waited for; matrix products, arithmetic and copies ran while one was open for 0% of the time, Pallas kernels for 8%

profile of v12, /device:TPU:24, one launch (start us, length us, event | category | flops | bytes accessed | tf_op | source)
XLA Modules:
  0.0 28.4 jit_solution(11955330274223158381)
XLA Ops:
  0.0 0.0 copy-start.1
  0.0 0.0 copy-start.5
  0.0 0.0 copy-start.7
  0.0 1.9 %open_parts.1 = (f32[8,40,128]{2,1,0:T(8,128)S(1)}, f32[32,128]{1,0:T(8,128)S(1)}, f32[8,128]{1,0:T(8,128)S(1)}, bf16[384,256]{1,0:T(8,128)(2,1)S(1)}, bf16[384,256]{1,0:T(8,128)(2,1)S(1)}) custom-call(s32[1]{0:T(128)} %bitcast.part_ref, f32[128,512]{1,0:T(8,128)} %theta_ref.3, bf16[2,512,128]{2,1,0:T(8,128)(2,1)} %constant.44.clone.waves_hbm, ...), custom_call_target="tpu_custom_call" | custom-call | flops 268435456 | bytes 1048576 | tf_op jit(solution)/shard_map/open_parts/pallas_call | solution.py:469
  1.9 1.5 %collective-permute-start.1 = (f32[32,128]{1,0:T(8,128)S(1)}, f32[32,128]{1,0:T(8,128)S(1)}, u32[]{:S(2)}, u32[]{:S(2)}) collective-permute-start(f32[32,128]{1,0:T(8,128)S(1)} %get-tuple-element.16), channel_id=1, source_target_pairs={{1,2},{2,1},{5,6},{6,5},{9,10},{10,9},{13,14},{14,13},{17,18},{18,... | collective-permute-start | bytes 49160 | tf_op jit(solution)/shard_map/ppermute | solution.py:509
  3.3 0.0 copy-start.9
  3.3 0.8 %collective-permute-start = (f32[8,40,128]{2,1,0:T(8,128)S(1)}, f32[8,40,128]{2,1,0:T(8,128)S(1)}, u32[]{:S(2)}, u32[]{:S(2)}) collective-permute-start(f32[8,40,128]{2,1,0:T(8,128)S(1)} %get-tuple-element.15), channel_id=1, source_target_pairs={{0,3},{1,2},{2,1},{3,0},{4,7},{5,6},{6,5},{7,4},{8,11},{9,10},{10,... | collective-permute-start | bytes 491528 | tf_op jit(solution)/shard_map/ppermute | solution.py:512
  4.1 0.0 copy-done.1
  4.1 0.0 copy-done.5
  4.1 0.0 copy-done.7
  4.1 0.5 %own_spectrum.1.spectrum_ref = f32[2,40,128]{2,1,0:T(8,128)S(1)} custom-call(s32[1]{0:T(128)} %bitcast.part_ref, f32[128,512]{1,0:T(8,128)S(1)} %copy-done.1, bf16[2,512,256]{2,1,0:T(8,128)(2,1)S(1)} %copy-done.5, bf16[4,80,384]{2,1,0:T(8,128)(2,1)S(1)} %copy-done.7), custom_call_target="tpu_custom_call" | custom-call | flops 2147483648 | bytes 1048576 | tf_op jit(solution)/shard_map/own_spectrum/pallas_call | solution.py:469
  4.6 0.0 copy-start.3
  4.6 1.1 %collective-permute-done.1.rim_ref = f32[32,128]{1,0:T(8,128)S(1)} collective-permute-done((f32[32,128]{1,0:T(8,128)S(1)}, f32[32,128]{1,0:T(8,128)S(1)}, u32[]{:S(2)}, u32[]{:S(2)}) %collective-permute-start.1) | collective-permute-done | bytes 16416 | tf_op jit(solution)/shard_map/ppermute | solution.py:509
  5.7 0.0 copy-done.9
  5.7 0.3 %add_rim.1 = f32[1,40,128]{2,1,0:T(8,128)S(1)} custom-call(s32[1]{0:T(128)} %bitcast.part_ref, f32[2,40,128]{2,1,0:T(8,128)S(1)} %own_spectrum.1.spectrum_ref, f32[32,128]{1,0:T(8,128)S(1)} %collective-permute-done.1.rim_ref, bf16[4,80,96]{2,1,0:T(8,128)(2,1)S(1)} %copy-done.9), custom_call_target="tpu_custom_call" | custom-call | flops 268435456 | bytes 1048576 | tf_op jit(solution)/shard_map/add_rim/pallas_call | solution.py:469
  6.0 0.7 %collective-permute-start.2 = (f32[1,40,128]{2,1,0:T(8,128)S(1)}, f32[1,40,128]{2,1,0:T(8,128)S(1)}, u32[]{:S(2)}, u32[]{:S(2)}) collective-permute-start(f32[1,40,128]{2,1,0:T(8,128)S(1)} %add_rim.1), channel_id=1, source_target_pairs={{0,3},{1,2},{2,1},{3,0},{4,7},{5,6},{6,5},{7,4},{8,11},{9,10},{10,... | collective-permute-start | bytes 61448 | tf_op jit(solution)/shard_map/ppermute | solution.py:512
  6.7 3.3 %collective-permute-done.2 = f32[1,40,128]{2,1,0:T(8,128)S(1)} collective-permute-done((f32[1,40,128]{2,1,0:T(8,128)S(1)}, f32[1,40,128]{2,1,0:T(8,128)S(1)}, u32[]{:S(2)}, u32[]{:S(2)}) %collective-permute-start.2) | collective-permute-done | bytes 20512 | tf_op jit(solution)/shard_map/ppermute | solution.py:512
  10.0 0.0 collective-permute-done
  10.0 0.0 copy-start.6
  10.0 0.0 copy-start.8
  10.1 0.2 collective-permute-start.3
  10.2 0.0 copy-done.3
  10.2 0.3 %near_kernels.1 = (f32[8,4,40,128]{3,2,1,0:T(8,128)S(1)}, f32[512,128]{1,0:T(8,128)S(1)}) custom-call(s32[1]{0:T(128)} %bitcast.part_ref, f32[17,40,128]{2,1,0:T(8,128)S(1)} %pad_maximum_fusion.mixed_ref, s32[512,512]{1,0:T(8,128)S(1)} %copy-done.3), custom_call_target="tpu_custom_call" | custom-call | flops 1073741824 | bytes 1048576 | tf_op jit(solution)/shard_map/near_kernels/pallas_call | solution.py:469
  10.6 1.2 %collective-permute-done.3.other_ref = f32[17,40,128]{2,1,0:T(8,128)S(1)} collective-permute-done((f32[17,40,128]{2,1,0:T(8,128)S(1)}, f32[17,40,128]{2,1,0:T(8,128)S(1)}, u32[]{:S(2)}, u32[]{:S(2)}) %collective-permute-start.3) | collective-permute-done | bytes 348192 | tf_op jit(solution)/shard_map/ppermute | solution.py:512
  11.8 0.0 copy-done.6
  11.8 0.0 copy-done.8
  11.8 0.0 copy-start
  11.8 0.0 copy-start.4
  11.8 6.9 %coherent_fields.1 = f32[40,128]{1,0:T(8,128)S(1)} custom-call(s32[1]{0:T(128)} %bitcast.part_ref, f32[17,40,128]{2,1,0:T(8,128)S(1)} %pad_maximum_fusion.mixed_ref, f32[17,40,128]{2,1,0:T(8,128)S(1)} %collective-permute-done.3.other_ref, f32[8,4,40,128]{3,2,1,0:T(8,128)S(1)} %get-tuple-element.17.near_ref, f32[512,128]{1,0:T(8,128)S(1)} %get-tuple-element.18.signs, ...), custom_call_target="tpu_custom_call" | custom-call | flops 8589934592 | bytes 1048576 | tf_op jit(solution)/shard_map/coherent_fields/pallas_call | solution.py:469
  18.7 0.2 collective-permute-start.4
  18.9 1.1 %collective-permute-done.4 = f32[40,128]{1,0:T(8,128)S(1)} collective-permute-done((f32[40,128]{1,0:T(8,128)S(1)}, f32[40,128]{1,0:T(8,128)S(1)}, u32[]{:S(2)}, u32[]{:S(2)}) %collective-permute-start.4) | collective-permute-done | bytes 20512 | tf_op jit(solution)/shard_map/ppermute | solution.py:512
  20.0 0.1 collective-permute-start.5
  20.1 3.1 %collective-permute-done.5 = f32[40,128]{1,0:T(8,128)S(1)} collective-permute-done((f32[40,128]{1,0:T(8,128)S(1)}, f32[40,128]{1,0:T(8,128)S(1)}, u32[]{:S(2)}, u32[]{:S(2)}) %collective-permute-start.5) | collective-permute-done | bytes 20512 | tf_op jit(solution)/shard_map/ppermute | solution.py:512
  23.2 0.0 copy-start.2
  23.2 0.2 collective-permute-start.6
  23.4 0.0 copy-done
  23.4 0.0 copy-done.4
  23.4 1.2 %own_gradient.1 = (f32[128,512]{1,0:T(8,128)}, f32[32,512]{1,0:T(8,128)S(1)}, f32[32,512]{1,0:T(8,128)S(1)}) custom-call(s32[1]{0:T(128)} %bitcast.part_ref, f32[128,512]{1,0:T(8,128)S(1)} %copy-done.1, f32[40,128]{1,0:T(8,128)S(1)} %add.19.sum_ref, bf16[2,256,512]{2,1,0:T(8,128)(2,1)S(1)} %copy-done, bf16[4,256,240]{2,1,0:T(8,128)(2,1)S(1)} %copy-done.4), custom_call_target="tpu_custom_call" | custom-call | flops 2147483648 | bytes 1048576 | tf_op jit(solution)/shard_map/own_gradient/pallas_call | solution.py:469
  24.6 2.7 %collective-permute-done.6.near_ref = f32[40,128]{1,0:T(8,128)S(1)} collective-permute-done((f32[40,128]{1,0:T(8,128)S(1)}, f32[40,128]{1,0:T(8,128)S(1)}, u32[]{:S(2)}, u32[]{:S(2)}) %collective-permute-start.6) | collective-permute-done | bytes 20512 | tf_op jit(solution)/shard_map/ppermute | solution.py:509
  27.3 0.0 copy-done.2
  27.3 1.1 %edge_gradient.1 = f32[128,512]{1,0:T(8,128)} custom-call(s32[1]{0:T(128)} %bitcast.part_ref, f32[128,512]{1,0:T(8,128)} %get-tuple-element.22.gradient_hbm, f32[32,512]{1,0:T(8,128)S(1)} %get-tuple-element.23.edge_ref, f32[32,512]{1,0:T(8,128)S(1)} %get-tuple-element.24.scale_ref, ...), custom_call_target="tpu_custom_call", output_to_operand_aliasing={{}: (1, {})} | custom-call | flops 268435456 | bytes 1048576 | tf_op jit(solution)/shard_map/edge_gradient/pallas_call | solution.py:469
  (4 shorter events, 0.0 us)
Async XLA Ops:
  0.0 4.1 %copy-start.1 = (f32[128,512]{1,0:T(8,128)S(1)}, f32[128,512]{1,0:T(8,128)}, u32[]{:S(2)}) copy-start(f32[128,512]{1,0:T(8,128)} %theta_ref.3) | copy-start | bytes 786436
  0.0 4.1 %copy-start.5 = (bf16[2,512,256]{2,1,0:T(8,128)(2,1)S(1)}, bf16[2,512,256]{2,1,0:T(8,128)(2,1)}, u32[]{:S(2)}) copy-start(bf16[2,512,256]{2,1,0:T(8,128)(2,1)} %constant.43.clone.column_ref) | copy-start | bytes 1572868
  0.0 4.1 %copy-start.7 = (bf16[4,80,384]{2,1,0:T(8,128)(2,1)S(1)}, bf16[4,80,384]{2,1,0:T(8,128)(2,1)}, u32[]{:S(2)}) copy-start(bf16[4,80,384]{2,1,0:T(8,128)(2,1)} %constant.45.clone.rows_ref) | copy-start | bytes 737284
  1.9 3.8 %collective-permute-start.1 = (f32[32,128]{1,0:T(8,128)S(1)}, f32[32,128]{1,0:T(8,128)S(1)}, u32[]{:S(2)}, u32[]{:S(2)}) collective-permute-start(f32[32,128]{1,0:T(8,128)S(1)} %get-tuple-element.16), channel_id=1, source_target_pairs={{1,2},{2,1},{5,6},{6,5},{9,10},{10,9},{13,14},{14,13},{17,18},{18,... | collective-permute-start | bytes 49160 | tf_op jit(solution)/shard_map/ppermute | solution.py:509
  3.3 2.3 %copy-start.9 = (bf16[4,80,96]{2,1,0:T(8,128)(2,1)S(1)}, bf16[4,80,96]{2,1,0:T(8,128)(2,1)}, u32[]{:S(2)}) copy-start(bf16[4,80,96]{2,1,0:T(8,128)(2,1)} %constant.47.clone.rows_ref) | copy-start | bytes 184324
  3.3 6.7 %collective-permute-start = (f32[8,40,128]{2,1,0:T(8,128)S(1)}, f32[8,40,128]{2,1,0:T(8,128)S(1)}, u32[]{:S(2)}, u32[]{:S(2)}) collective-permute-start(f32[8,40,128]{2,1,0:T(8,128)S(1)} %get-tuple-element.15), channel_id=1, source_target_pairs={{0,3},{1,2},{2,1},{3,0},{4,7},{5,6},{6,5},{7,4},{8,11},{9,10},{10,... | collective-permute-start | bytes 491528 | tf_op jit(solution)/shard_map/ppermute | solution.py:512
  4.6 5.6 %copy-start.3 = (s32[512,512]{1,0:T(8,128)S(1)}, s32[512,512]{1,0:T(8,128)}, u32[]{:S(2)}) copy-start(s32[512,512]{1,0:T(8,128)} %target_ref.1) | copy-start | bytes 3145732
  6.0 4.0 %collective-permute-start.2 = (f32[1,40,128]{2,1,0:T(8,128)S(1)}, f32[1,40,128]{2,1,0:T(8,128)S(1)}, u32[]{:S(2)}, u32[]{:S(2)}) collective-permute-start(f32[1,40,128]{2,1,0:T(8,128)S(1)} %add_rim.1), channel_id=1, source_target_pairs={{0,3},{1,2},{2,1},{3,0},{4,7},{5,6},{6,5},{7,4},{8,11},{9,10},{10,... | collective-permute-start | bytes 61448 | tf_op jit(solution)/shard_map/ppermute | solution.py:512
  10.0 1.8 %copy-start.6 = (bf16[512,240]{1,0:T(8,128)(2,1)S(1)}, bf16[512,240]{1,0:T(8,128)(2,1)}, u32[]{:S(2)}) copy-start(bf16[512,240]{1,0:T(8,128)(2,1)} %constant.52.clone.row_ref) | copy-start | bytes 737284
  10.0 1.7 %copy-start.8 = (bf16[160,512]{1,0:T(8,128)(2,1)S(1)}, bf16[160,512]{1,0:T(8,128)(2,1)}, u32[]{:S(2)}) copy-start(bf16[160,512]{1,0:T(8,128)(2,1)} %constant.53.clone.row_turned_ref) | copy-start | bytes 491524
  10.1 1.7 %collective-permute-start.3 = (f32[17,40,128]{2,1,0:T(8,128)S(1)}, f32[17,40,128]{2,1,0:T(8,128)S(1)}, u32[]{:S(2)}, u32[]{:S(2)}) collective-permute-start(f32[17,40,128]{2,1,0:T(8,128)S(1)} %pad_maximum_fusion.mixed_ref), channel_id=1, source_target_pairs={{0,1},{1,0},{2,3},{3,2},{4,5},{5,4},{6,7},{7,6},{8,9},{9,8},{10,11... | collective-permute-start | bytes 1044488 | tf_op jit(solution)/shard_map/ppermute | solution.py:512
  11.8 11.6 %copy-start = (bf16[2,256,512]{2,1,0:T(8,128)(2,1)S(1)}, bf16[2,256,512]{2,1,0:T(8,128)(2,1)}, u32[]{:S(2)}) copy-start(bf16[2,256,512]{2,1,0:T(8,128)(2,1)} %constant.51.clone.turned_ref) | copy-start | bytes 1572868
  11.8 11.6 %copy-start.4 = (bf16[4,256,240]{2,1,0:T(8,128)(2,1)S(1)}, bf16[4,256,240]{2,1,0:T(8,128)(2,1)}, u32[]{:S(2)}) copy-start(bf16[4,256,240]{2,1,0:T(8,128)(2,1)} %constant.46.clone.rows_ref) | copy-start | bytes 1474564
  18.7 1.3 %collective-permute-start.4 = (f32[40,128]{1,0:T(8,128)S(1)}, f32[40,128]{1,0:T(8,128)S(1)}, u32[]{:S(2)}, u32[]{:S(2)}) collective-permute-start(f32[40,128]{1,0:T(8,128)S(1)} %coherent_fields.1), channel_id=1, source_target_pairs={{0,1},{1,0},{2,3},{3,2},{4,5},{5,4},{6,7},{7,6},{8,9},{9,8},{10,11... | collective-permute-start | bytes 61448 | tf_op jit(solution)/shard_map/ppermute | solution.py:512
  20.0 3.2 %collective-permute-start.5 = (f32[40,128]{1,0:T(8,128)S(1)}, f32[40,128]{1,0:T(8,128)S(1)}, u32[]{:S(2)}, u32[]{:S(2)}) collective-permute-start(f32[40,128]{1,0:T(8,128)S(1)} %add.18), channel_id=1, source_target_pairs={{0,3},{1,2},{2,1},{3,0},{4,7},{5,6},{6,5},{7,4},{8,11},{9,10},{10,... | collective-permute-start | bytes 61448 | tf_op jit(solution)/shard_map/ppermute | solution.py:512
  23.2 4.1 %copy-start.2 = (bf16[4,64,240]{2,1,0:T(8,128)(2,1)S(1)}, bf16[4,64,240]{2,1,0:T(8,128)(2,1)}, u32[]{:S(2)}) copy-start(bf16[4,64,240]{2,1,0:T(8,128)(2,1)} %constant.48.clone.rows_ref) | copy-start | bytes 368644
  23.2 4.1 %collective-permute-start.6 = (f32[40,128]{1,0:T(8,128)S(1)}, f32[40,128]{1,0:T(8,128)S(1)}, u32[]{:S(2)}, u32[]{:S(2)}) collective-permute-start(f32[40,128]{1,0:T(8,128)S(1)} %add.19.sum_ref), channel_id=1, source_target_pairs={{0,1},{3,2},{4,5},{7,6},{8,9},{11,10},{12,13},{15,14},{16,17},{19,... | collective-permute-start | bytes 61448 | tf_op jit(solution)/shard_map/ppermute | solution.py:509

commit v13 on v11

--- a/solution.py
+++ b/solution.py
@@ -209,9 +209,11 @@
     keep_top = jnp.where(valid, scale, 0.0)
     keep_bottom = jnp.where((row == 0) & (lane == HALF), 0.0, keep_top)
     first = lane % FB < HALF
-    for copy in copies[:6]:
+    for copy in copies[:2]:
         copy.wait()
     rim_ref[...] = columns_of(jnp.tanh(mask_steep * theta_ref[...]), waves_ref)
+    for copy in copies[2:6]:
+        copy.wait()
     for cond in range(local_conds):
         for kern in range(KERNELS):
             for piece, ref in enumerate((real_ref, imag_ref)):
@@ -372,7 +374,7 @@
         total[...] += value
         return carry
 
-    lax.fori_loop(0, CONDS, expose, 0, unroll=4)
+    lax.fori_loop(0, CONDS, expose, 0, unroll=8)
     total[...] = total[...] * (band_weight / (CONDS * CONDS))
 
     def drive(cond, carry):

time: 27.8 us -> 28.4 us (1.022)
  Pallas kernels: 11.5 us -> 12.1 us
    pallas_call x7, Pallas kernels: 11.5 us -> 12.1 us  [call(): pl.pallas_call(kernel, grid_spec=pltpu.PrefetchScalarGridSpec(num_scalar_...]
where the time goes in v13:
time: 28.4 us; the launch traced here: 28.3 us
  waiting for transfers between devices  12.3 us (43%)
  Pallas kernels  12.1 us (43%)
  starting transfers between devices  3.66 us (13%)
    pallas_call x7, Pallas kernels, call(): pl.pallas_call(kernel, grid_spec=pltpu.PrefetchScalarGridSpec(num_scalar_...  12.1 us
    ppermute x5, waiting for transfers between devices, partner(): return lax.ppermute(value, 'cond', [(i, i ^ step) for i in range(PARTS)])  8.59 us
    ppermute x2, waiting for transfers between devices, across(): return lax.ppermute(value, ('tile', 'cond'), pairs)  3.75 us
    ppermute x5, starting transfers between devices, partner(): return lax.ppermute(value, 'cond', [(i, i ^ step) for i in range(PARTS)])  2.03 us
    ppermute x2, starting transfers between devices, across(): return lax.ppermute(value, ('tile', 'cond'), pairs)  1.63 us
  transfers between devices with their start and end apart: 7, of which 6 were waited for; matrix products, arithmetic and copies ran while one was open for 0% of the time, Pallas kernels for 8%

profile of v13, /device:TPU:24, one launch (start us, length us, event | category | flops | bytes accessed | tf_op | source)
XLA Modules:
  0.0 28.3 jit_solution(1229793344680750702)
XLA Ops:
  0.0 0.0 copy-start.1
  0.0 0.0 copy-start.5
  0.0 0.0 copy-start.7
  0.0 1.9 %open_parts.1 = (f32[8,40,128]{2,1,0:T(8,128)S(1)}, f32[32,128]{1,0:T(8,128)S(1)}, f32[8,128]{1,0:T(8,128)S(1)}, bf16[384,256]{1,0:T(8,128)(2,1)S(1)}, bf16[384,256]{1,0:T(8,128)(2,1)S(1)}) custom-call(s32[1]{0:T(128)} %bitcast.part_ref, f32[128,512]{1,0:T(8,128)} %theta_ref.3, bf16[2,512,128]{2,1,0:T(8,128)(2,1)} %constant.44.clone.waves_hbm, ...), custom_call_target="tpu_custom_call" | custom-call | flops 268435456 | bytes 1048576 | tf_op jit(solution)/shard_map/open_parts/pallas_call | solution.py:460
  2.0 1.5 %collective-permute-start.1 = (f32[32,128]{1,0:T(8,128)S(1)}, f32[32,128]{1,0:T(8,128)S(1)}, u32[]{:S(2)}, u32[]{:S(2)}) collective-permute-start(f32[32,128]{1,0:T(8,128)S(1)} %get-tuple-element.16), channel_id=1, source_target_pairs={{1,2},{2,1},{5,6},{6,5},{9,10},{10,9},{13,14},{14,13},{17,18},{18,... | collective-permute-start | bytes 49160 | tf_op jit(solution)/shard_map/ppermute | solution.py:500
  3.4 0.0 copy-start.9
  3.4 0.8 %collective-permute-start = (f32[8,40,128]{2,1,0:T(8,128)S(1)}, f32[8,40,128]{2,1,0:T(8,128)S(1)}, u32[]{:S(2)}, u32[]{:S(2)}) collective-permute-start(f32[8,40,128]{2,1,0:T(8,128)S(1)} %get-tuple-element.15), channel_id=1, source_target_pairs={{0,3},{1,2},{2,1},{3,0},{4,7},{5,6},{6,5},{7,4},{8,11},{9,10},{10,... | collective-permute-start | bytes 491528 | tf_op jit(solution)/shard_map/ppermute | solution.py:503
  4.2 0.0 copy-done.1
  4.2 0.0 copy-done.5
  4.2 0.0 copy-done.7
  4.2 0.5 %own_spectrum.1.spectrum_ref = f32[2,40,128]{2,1,0:T(8,128)S(1)} custom-call(s32[1]{0:T(128)} %bitcast.part_ref, f32[128,512]{1,0:T(8,128)S(1)} %copy-done.1, bf16[2,512,256]{2,1,0:T(8,128)(2,1)S(1)} %copy-done.5, bf16[4,80,384]{2,1,0:T(8,128)(2,1)S(1)} %copy-done.7), custom_call_target="tpu_custom_call" | custom-call | flops 2147483648 | bytes 1048576 | tf_op jit(solution)/shard_map/own_spectrum/pallas_call | solution.py:460
  4.7 0.0 copy-start.3
  4.7 1.1 %collective-permute-done.1.rim_ref = f32[32,128]{1,0:T(8,128)S(1)} collective-permute-done((f32[32,128]{1,0:T(8,128)S(1)}, f32[32,128]{1,0:T(8,128)S(1)}, u32[]{:S(2)}, u32[]{:S(2)}) %collective-permute-start.1) | collective-permute-done | bytes 16416 | tf_op jit(solution)/shard_map/ppermute | solution.py:500
  5.7 0.0 copy-done.9
  5.8 0.3 %add_rim.1 = f32[1,40,128]{2,1,0:T(8,128)S(1)} custom-call(s32[1]{0:T(128)} %bitcast.part_ref, f32[2,40,128]{2,1,0:T(8,128)S(1)} %own_spectrum.1.spectrum_ref, f32[32,128]{1,0:T(8,128)S(1)} %collective-permute-done.1.rim_ref, bf16[4,80,96]{2,1,0:T(8,128)(2,1)S(1)} %copy-done.9), custom_call_target="tpu_custom_call" | custom-call | flops 268435456 | bytes 1048576 | tf_op jit(solution)/shard_map/add_rim/pallas_call | solution.py:460
  6.0 0.7 %collective-permute-start.2 = (f32[1,40,128]{2,1,0:T(8,128)S(1)}, f32[1,40,128]{2,1,0:T(8,128)S(1)}, u32[]{:S(2)}, u32[]{:S(2)}) collective-permute-start(f32[1,40,128]{2,1,0:T(8,128)S(1)} %add_rim.1), channel_id=1, source_target_pairs={{0,3},{1,2},{2,1},{3,0},{4,7},{5,6},{6,5},{7,4},{8,11},{9,10},{10,... | collective-permute-start | bytes 61448 | tf_op jit(solution)/shard_map/ppermute | solution.py:503
  6.8 3.3 %collective-permute-done.2 = f32[1,40,128]{2,1,0:T(8,128)S(1)} collective-permute-done((f32[1,40,128]{2,1,0:T(8,128)S(1)}, f32[1,40,128]{2,1,0:T(8,128)S(1)}, u32[]{:S(2)}, u32[]{:S(2)}) %collective-permute-start.2) | collective-permute-done | bytes 20512 | tf_op jit(solution)/shard_map/ppermute | solution.py:503
  10.1 0.0 collective-permute-done
  10.1 0.0 copy-start.6
  10.1 0.0 copy-start.8
  10.1 0.2 collective-permute-start.3
  10.3 0.0 copy-done.3
  10.3 0.3 %near_kernels.1 = (f32[8,4,40,128]{3,2,1,0:T(8,128)S(1)}, f32[512,128]{1,0:T(8,128)S(1)}) custom-call(s32[1]{0:T(128)} %bitcast.part_ref, f32[17,40,128]{2,1,0:T(8,128)S(1)} %pad_maximum_fusion.mixed_ref, s32[512,512]{1,0:T(8,128)S(1)} %copy-done.3), custom_call_target="tpu_custom_call" | custom-call | flops 1073741824 | bytes 1048576 | tf_op jit(solution)/shard_map/near_kernels/pallas_call | solution.py:460
  10.7 1.2 %collective-permute-done.3.other_ref = f32[17,40,128]{2,1,0:T(8,128)S(1)} collective-permute-done((f32[17,40,128]{2,1,0:T(8,128)S(1)}, f32[17,40,128]{2,1,0:T(8,128)S(1)}, u32[]{:S(2)}, u32[]{:S(2)}) %collective-permute-start.3) | collective-permute-done | bytes 348192 | tf_op jit(solution)/shard_map/ppermute | solution.py:503
  11.9 0.0 copy-done.6
  11.9 0.0 copy-done.8
  11.9 0.0 copy-start
  11.9 0.0 copy-start.4
  11.9 6.7 %coherent_fields.1 = f32[40,128]{1,0:T(8,128)S(1)} custom-call(s32[1]{0:T(128)} %bitcast.part_ref, f32[17,40,128]{2,1,0:T(8,128)S(1)} %pad_maximum_fusion.mixed_ref, f32[17,40,128]{2,1,0:T(8,128)S(1)} %collective-permute-done.3.other_ref, f32[8,4,40,128]{3,2,1,0:T(8,128)S(1)} %get-tuple-element.17.near_ref, f32[512,128]{1,0:T(8,128)S(1)} %get-tuple-element.18.signs, ...), custom_call_target="tpu_custom_call" | custom-call | flops 8589934592 | bytes 1048576 | tf_op jit(solution)/shard_map/coherent_fields/pallas_call | solution.py:460
  18.6 0.2 collective-permute-start.4
  18.8 1.1 %collective-permute-done.4 = f32[40,128]{1,0:T(8,128)S(1)} collective-permute-done((f32[40,128]{1,0:T(8,128)S(1)}, f32[40,128]{1,0:T(8,128)S(1)}, u32[]{:S(2)}, u32[]{:S(2)}) %collective-permute-start.4) | collective-permute-done | bytes 20512 | tf_op jit(solution)/shard_map/ppermute | solution.py:503
  19.9 0.1 collective-permute-start.5
  20.0 3.1 %collective-permute-done.5 = f32[40,128]{1,0:T(8,128)S(1)} collective-permute-done((f32[40,128]{1,0:T(8,128)S(1)}, f32[40,128]{1,0:T(8,128)S(1)}, u32[]{:S(2)}, u32[]{:S(2)}) %collective-permute-start.5) | collective-permute-done | bytes 20512 | tf_op jit(solution)/shard_map/ppermute | solution.py:503
  23.1 0.0 copy-start.2
  23.1 0.2 collective-permute-start.6
  23.2 0.0 copy-done
  23.2 0.0 copy-done.4
  23.2 1.2 %own_gradient.1 = (f32[128,512]{1,0:T(8,128)}, f32[32,512]{1,0:T(8,128)S(1)}, f32[32,512]{1,0:T(8,128)S(1)}) custom-call(s32[1]{0:T(128)} %bitcast.part_ref, f32[128,512]{1,0:T(8,128)S(1)} %copy-done.1, f32[40,128]{1,0:T(8,128)S(1)} %add.19.sum_ref, bf16[2,256,512]{2,1,0:T(8,128)(2,1)S(1)} %copy-done, bf16[4,256,240]{2,1,0:T(8,128)(2,1)S(1)} %copy-done.4), custom_call_target="tpu_custom_call" | custom-call | flops 2147483648 | bytes 1048576 | tf_op jit(solution)/shard_map/own_gradient/pallas_call | solution.py:460
  24.5 2.7 %collective-permute-done.6.near_ref = f32[40,128]{1,0:T(8,128)S(1)} collective-permute-done((f32[40,128]{1,0:T(8,128)S(1)}, f32[40,128]{1,0:T(8,128)S(1)}, u32[]{:S(2)}, u32[]{:S(2)}) %collective-permute-start.6) | collective-permute-done | bytes 20512 | tf_op jit(solution)/shard_map/ppermute | solution.py:500
  27.2 0.0 copy-done.2
  27.2 1.1 %edge_gradient.1 = f32[128,512]{1,0:T(8,128)} custom-call(s32[1]{0:T(128)} %bitcast.part_ref, f32[128,512]{1,0:T(8,128)} %get-tuple-element.22.gradient_hbm, f32[32,512]{1,0:T(8,128)S(1)} %get-tuple-element.23.edge_ref, f32[32,512]{1,0:T(8,128)S(1)} %get-tuple-element.24.scale_ref, ...), custom_call_target="tpu_custom_call", output_to_operand_aliasing={{}: (1, {})} | custom-call | flops 268435456 | bytes 1048576 | tf_op jit(solution)/shard_map/edge_gradient/pallas_call | solution.py:460
  (4 shorter events, 0.0 us)
Async XLA Ops:
  0.0 4.2 %copy-start.1 = (f32[128,512]{1,0:T(8,128)S(1)}, f32[128,512]{1,0:T(8,128)}, u32[]{:S(2)}) copy-start(f32[128,512]{1,0:T(8,128)} %theta_ref.3) | copy-start | bytes 786436
  0.0 4.2 %copy-start.5 = (bf16[2,512,256]{2,1,0:T(8,128)(2,1)S(1)}, bf16[2,512,256]{2,1,0:T(8,128)(2,1)}, u32[]{:S(2)}) copy-start(bf16[2,512,256]{2,1,0:T(8,128)(2,1)} %constant.43.clone.column_ref) | copy-start | bytes 1572868
  0.0 4.2 %copy-start.7 = (bf16[4,80,384]{2,1,0:T(8,128)(2,1)S(1)}, bf16[4,80,384]{2,1,0:T(8,128)(2,1)}, u32[]{:S(2)}) copy-start(bf16[4,80,384]{2,1,0:T(8,128)(2,1)} %constant.45.clone.rows_ref) | copy-start | bytes 737284
  2.0 3.8 %collective-permute-start.1 = (f32[32,128]{1,0:T(8,128)S(1)}, f32[32,128]{1,0:T(8,128)S(1)}, u32[]{:S(2)}, u32[]{:S(2)}) collective-permute-start(f32[32,128]{1,0:T(8,128)S(1)} %get-tuple-element.16), channel_id=1, source_target_pairs={{1,2},{2,1},{5,6},{6,5},{9,10},{10,9},{13,14},{14,13},{17,18},{18,... | collective-permute-start | bytes 49160 | tf_op jit(solution)/shard_map/ppermute | solution.py:500
  3.4 2.3 %copy-start.9 = (bf16[4,80,96]{2,1,0:T(8,128)(2,1)S(1)}, bf16[4,80,96]{2,1,0:T(8,128)(2,1)}, u32[]{:S(2)}) copy-start(bf16[4,80,96]{2,1,0:T(8,128)(2,1)} %constant.47.clone.rows_ref) | copy-start | bytes 184324
  3.4 6.7 %collective-permute-start = (f32[8,40,128]{2,1,0:T(8,128)S(1)}, f32[8,40,128]{2,1,0:T(8,128)S(1)}, u32[]{:S(2)}, u32[]{:S(2)}) collective-permute-start(f32[8,40,128]{2,1,0:T(8,128)S(1)} %get-tuple-element.15), channel_id=1, source_target_pairs={{0,3},{1,2},{2,1},{3,0},{4,7},{5,6},{6,5},{7,4},{8,11},{9,10},{10,... | collective-permute-start | bytes 491528 | tf_op jit(solution)/shard_map/ppermute | solution.py:503
  4.7 5.6 %copy-start.3 = (s32[512,512]{1,0:T(8,128)S(1)}, s32[512,512]{1,0:T(8,128)}, u32[]{:S(2)}) copy-start(s32[512,512]{1,0:T(8,128)} %target_ref.1) | copy-start | bytes 3145732
  6.0 4.0 %collective-permute-start.2 = (f32[1,40,128]{2,1,0:T(8,128)S(1)}, f32[1,40,128]{2,1,0:T(8,128)S(1)}, u32[]{:S(2)}, u32[]{:S(2)}) collective-permute-start(f32[1,40,128]{2,1,0:T(8,128)S(1)} %add_rim.1), channel_id=1, source_target_pairs={{0,3},{1,2},{2,1},{3,0},{4,7},{5,6},{6,5},{7,4},{8,11},{9,10},{10,... | collective-permute-start | bytes 61448 | tf_op jit(solution)/shard_map/ppermute | solution.py:503
  10.1 1.8 %copy-start.6 = (bf16[512,240]{1,0:T(8,128)(2,1)S(1)}, bf16[512,240]{1,0:T(8,128)(2,1)}, u32[]{:S(2)}) copy-start(bf16[512,240]{1,0:T(8,128)(2,1)} %constant.52.clone.row_ref) | copy-start | bytes 737284
  10.1 1.7 %copy-start.8 = (bf16[160,512]{1,0:T(8,128)(2,1)S(1)}, bf16[160,512]{1,0:T(8,128)(2,1)}, u32[]{:S(2)}) copy-start(bf16[160,512]{1,0:T(8,128)(2,1)} %constant.53.clone.row_turned_ref) | copy-start | bytes 491524
  10.1 1.7 %collective-permute-start.3 = (f32[17,40,128]{2,1,0:T(8,128)S(1)}, f32[17,40,128]{2,1,0:T(8,128)S(1)}, u32[]{:S(2)}, u32[]{:S(2)}) collective-permute-start(f32[17,40,128]{2,1,0:T(8,128)S(1)} %pad_maximum_fusion.mixed_ref), channel_id=1, source_target_pairs={{0,1},{1,0},{2,3},{3,2},{4,5},{5,4},{6,7},{7,6},{8,9},{9,8},{10,11... | collective-permute-start | bytes 1044488 | tf_op jit(solution)/shard_map/ppermute | solution.py:503
  11.9 11.4 %copy-start = (bf16[2,256,512]{2,1,0:T(8,128)(2,1)S(1)}, bf16[2,256,512]{2,1,0:T(8,128)(2,1)}, u32[]{:S(2)}) copy-start(bf16[2,256,512]{2,1,0:T(8,128)(2,1)} %constant.51.clone.turned_ref) | copy-start | bytes 1572868
  11.9 11.4 %copy-start.4 = (bf16[4,256,240]{2,1,0:T(8,128)(2,1)S(1)}, bf16[4,256,240]{2,1,0:T(8,128)(2,1)}, u32[]{:S(2)}) copy-start(bf16[4,256,240]{2,1,0:T(8,128)(2,1)} %constant.46.clone.rows_ref) | copy-start | bytes 1474564
  18.6 1.3 %collective-permute-start.4 = (f32[40,128]{1,0:T(8,128)S(1)}, f32[40,128]{1,0:T(8,128)S(1)}, u32[]{:S(2)}, u32[]{:S(2)}) collective-permute-start(f32[40,128]{1,0:T(8,128)S(1)} %coherent_fields.1), channel_id=1, source_target_pairs={{0,1},{1,0},{2,3},{3,2},{4,5},{5,4},{6,7},{7,6},{8,9},{9,8},{10,11... | collective-permute-start | bytes 61448 | tf_op jit(solution)/shard_map/ppermute | solution.py:503
  19.9 3.2 %collective-permute-start.5 = (f32[40,128]{1,0:T(8,128)S(1)}, f32[40,128]{1,0:T(8,128)S(1)}, u32[]{:S(2)}, u32[]{:S(2)}) collective-permute-start(f32[40,128]{1,0:T(8,128)S(1)} %add.18), channel_id=1, source_target_pairs={{0,3},{1,2},{2,1},{3,0},{4,7},{5,6},{6,5},{7,4},{8,11},{9,10},{10,... | collective-permute-start | bytes 61448 | tf_op jit(solution)/shard_map/ppermute | solution.py:503
  23.1 4.1 %copy-start.2 = (bf16[4,64,240]{2,1,0:T(8,128)(2,1)S(1)}, bf16[4,64,240]{2,1,0:T(8,128)(2,1)}, u32[]{:S(2)}) copy-start(bf16[4,64,240]{2,1,0:T(8,128)(2,1)} %constant.48.clone.rows_ref) | copy-start | bytes 368644
  23.1 4.1 %collective-permute-start.6 = (f32[40,128]{1,0:T(8,128)S(1)}, f32[40,128]{1,0:T(8,128)S(1)}, u32[]{:S(2)}, u32[]{:S(2)}) collective-permute-start(f32[40,128]{1,0:T(8,128)S(1)} %add.19.sum_ref), channel_id=1, source_target_pairs={{0,1},{3,2},{4,5},{7,6},{8,9},{11,10},{12,13},{15,14},{16,17},{19,... | collective-permute-start | bytes 61448 | tf_op jit(solution)/shard_map/ppermute | solution.py:500

commit v14 on v11

--- a/solution.py
+++ b/solution.py
@@ -372,7 +372,7 @@
         total[...] += value
         return carry
 
-    lax.fori_loop(0, CONDS, expose, 0, unroll=4)
+    lax.fori_loop(0, CONDS, expose, 0, unroll=2)
     total[...] = total[...] * (band_weight / (CONDS * CONDS))
 
     def drive(cond, carry):

time: 27.8 us -> 28.2 us (1.014)
  Pallas kernels: 11.5 us -> 11.8 us
    pallas_call x7, Pallas kernels: 11.5 us -> 11.8 us  [call(): pl.pallas_call(kernel, grid_spec=pltpu.PrefetchScalarGridSpec(num_scalar_...]
where the time goes in v14:
time: 28.2 us; the launch traced here: 28 us
  waiting for transfers between devices  12.3 us (44%)
  Pallas kernels  11.8 us (42%)
  starting transfers between devices  3.67 us (13%)
    pallas_call x7, Pallas kernels, call(): pl.pallas_call(kernel, grid_spec=pltpu.PrefetchScalarGridSpec(num_scalar_...  11.8 us
    ppermute x5, waiting for transfers between devices, partner(): return lax.ppermute(value, 'cond', [(i, i ^ step) for i in range(PARTS)])  8.58 us
    ppermute x2, waiting for transfers between devices, across(): return lax.ppermute(value, ('tile', 'cond'), pairs)  3.75 us
    ppermute x5, starting transfers between devices, partner(): return lax.ppermute(value, 'cond', [(i, i ^ step) for i in range(PARTS)])  2.04 us
    ppermute x2, starting transfers between devices, across(): return lax.ppermute(value, ('tile', 'cond'), pairs)  1.63 us
  transfers between devices with their start and end apart: 7, of which 6 were waited for; matrix products, arithmetic and copies ran while one was open for 0% of the time, Pallas kernels for 8%

profile of v14, /device:TPU:24, one launch (start us, length us, event | category | flops | bytes accessed | tf_op | source)
XLA Modules:
  0.0 28.0 jit_solution(12825551624065717004)
XLA Ops:
  0.0 0.0 copy-start.1
  0.0 0.0 copy-start.5
  0.0 0.0 copy-start.7
  0.0 1.9 %open_parts.1 = (f32[8,40,128]{2,1,0:T(8,128)S(1)}, f32[32,128]{1,0:T(8,128)S(1)}, f32[8,128]{1,0:T(8,128)S(1)}, bf16[384,256]{1,0:T(8,128)(2,1)S(1)}, bf16[384,256]{1,0:T(8,128)(2,1)S(1)}) custom-call(s32[1]{0:T(128)} %bitcast.part_ref, f32[128,512]{1,0:T(8,128)} %theta_ref.3, bf16[2,512,128]{2,1,0:T(8,128)(2,1)} %constant.44.clone.waves_hbm, ...), custom_call_target="tpu_custom_call" | custom-call | flops 268435456 | bytes 1048576 | tf_op jit(solution)/shard_map/open_parts/pallas_call | solution.py:458
  1.9 1.5 %collective-permute-start.1 = (f32[32,128]{1,0:T(8,128)S(1)}, f32[32,128]{1,0:T(8,128)S(1)}, u32[]{:S(2)}, u32[]{:S(2)}) collective-permute-start(f32[32,128]{1,0:T(8,128)S(1)} %get-tuple-element.16), channel_id=1, source_target_pairs={{1,2},{2,1},{5,6},{6,5},{9,10},{10,9},{13,14},{14,13},{17,18},{18,... | collective-permute-start | bytes 49160 | tf_op jit(solution)/shard_map/ppermute | solution.py:498
  3.3 0.0 copy-start.9
  3.3 0.8 %collective-permute-start = (f32[8,40,128]{2,1,0:T(8,128)S(1)}, f32[8,40,128]{2,1,0:T(8,128)S(1)}, u32[]{:S(2)}, u32[]{:S(2)}) collective-permute-start(f32[8,40,128]{2,1,0:T(8,128)S(1)} %get-tuple-element.15), channel_id=1, source_target_pairs={{0,3},{1,2},{2,1},{3,0},{4,7},{5,6},{6,5},{7,4},{8,11},{9,10},{10,... | collective-permute-start | bytes 491528 | tf_op jit(solution)/shard_map/ppermute | solution.py:501
  4.1 0.0 copy-done.1
  4.1 0.0 copy-done.5
  4.1 0.0 copy-done.7
  4.1 0.5 %own_spectrum.1.spectrum_ref = f32[2,40,128]{2,1,0:T(8,128)S(1)} custom-call(s32[1]{0:T(128)} %bitcast.part_ref, f32[128,512]{1,0:T(8,128)S(1)} %copy-done.1, bf16[2,512,256]{2,1,0:T(8,128)(2,1)S(1)} %copy-done.5, bf16[4,80,384]{2,1,0:T(8,128)(2,1)S(1)} %copy-done.7), custom_call_target="tpu_custom_call" | custom-call | flops 2147483648 | bytes 1048576 | tf_op jit(solution)/shard_map/own_spectrum/pallas_call | solution.py:458
  4.6 0.0 copy-start.3
  4.6 1.1 %collective-permute-done.1.rim_ref = f32[32,128]{1,0:T(8,128)S(1)} collective-permute-done((f32[32,128]{1,0:T(8,128)S(1)}, f32[32,128]{1,0:T(8,128)S(1)}, u32[]{:S(2)}, u32[]{:S(2)}) %collective-permute-start.1) | collective-permute-done | bytes 16416 | tf_op jit(solution)/shard_map/ppermute | solution.py:498
  5.7 0.0 copy-done.9
  5.7 0.3 %add_rim.1 = f32[1,40,128]{2,1,0:T(8,128)S(1)} custom-call(s32[1]{0:T(128)} %bitcast.part_ref, f32[2,40,128]{2,1,0:T(8,128)S(1)} %own_spectrum.1.spectrum_ref, f32[32,128]{1,0:T(8,128)S(1)} %collective-permute-done.1.rim_ref, bf16[4,80,96]{2,1,0:T(8,128)(2,1)S(1)} %copy-done.9), custom_call_target="tpu_custom_call" | custom-call | flops 268435456 | bytes 1048576 | tf_op jit(solution)/shard_map/add_rim/pallas_call | solution.py:458
  6.0 0.7 %collective-permute-start.2 = (f32[1,40,128]{2,1,0:T(8,128)S(1)}, f32[1,40,128]{2,1,0:T(8,128)S(1)}, u32[]{:S(2)}, u32[]{:S(2)}) collective-permute-start(f32[1,40,128]{2,1,0:T(8,128)S(1)} %add_rim.1), channel_id=1, source_target_pairs={{0,3},{1,2},{2,1},{3,0},{4,7},{5,6},{6,5},{7,4},{8,11},{9,10},{10,... | collective-permute-start | bytes 61448 | tf_op jit(solution)/shard_map/ppermute | solution.py:501
  6.7 3.3 %collective-permute-done.2 = f32[1,40,128]{2,1,0:T(8,128)S(1)} collective-permute-done((f32[1,40,128]{2,1,0:T(8,128)S(1)}, f32[1,40,128]{2,1,0:T(8,128)S(1)}, u32[]{:S(2)}, u32[]{:S(2)}) %collective-permute-start.2) | collective-permute-done | bytes 20512 | tf_op jit(solution)/shard_map/ppermute | solution.py:501
  10.0 0.0 collective-permute-done
  10.0 0.0 copy-start.6
  10.0 0.0 copy-start.8
  10.1 0.2 collective-permute-start.3
  10.2 0.0 copy-done.3
  10.2 0.3 %near_kernels.1 = (f32[8,4,40,128]{3,2,1,0:T(8,128)S(1)}, f32[512,128]{1,0:T(8,128)S(1)}) custom-call(s32[1]{0:T(128)} %bitcast.part_ref, f32[17,40,128]{2,1,0:T(8,128)S(1)} %pad_maximum_fusion.mixed_ref, s32[512,512]{1,0:T(8,128)S(1)} %copy-done.3), custom_call_target="tpu_custom_call" | custom-call | flops 1073741824 | bytes 1048576 | tf_op jit(solution)/shard_map/near_kernels/pallas_call | solution.py:458
  10.6 1.2 %collective-permute-done.3.other_ref = f32[17,40,128]{2,1,0:T(8,128)S(1)} collective-permute-done((f32[17,40,128]{2,1,0:T(8,128)S(1)}, f32[17,40,128]{2,1,0:T(8,128)S(1)}, u32[]{:S(2)}, u32[]{:S(2)}) %collective-permute-start.3) | collective-permute-done | bytes 348192 | tf_op jit(solution)/shard_map/ppermute | solution.py:501
  11.8 0.0 copy-done.6
  11.8 0.0 copy-done.8
  11.8 0.0 copy-start
  11.8 0.0 copy-start.4
  11.8 6.5 %coherent_fields.1 = f32[40,128]{1,0:T(8,128)S(1)} custom-call(s32[1]{0:T(128)} %bitcast.part_ref, f32[17,40,128]{2,1,0:T(8,128)S(1)} %pad_maximum_fusion.mixed_ref, f32[17,40,128]{2,1,0:T(8,128)S(1)} %collective-permute-done.3.other_ref, f32[8,4,40,128]{3,2,1,0:T(8,128)S(1)} %get-tuple-element.17.near_ref, f32[512,128]{1,0:T(8,128)S(1)} %get-tuple-element.18.signs, ...), custom_call_target="tpu_custom_call" | custom-call | flops 8589934592 | bytes 1048576 | tf_op jit(solution)/shard_map/coherent_fields/pallas_call | solution.py:458
  18.3 0.2 collective-permute-start.4
  18.5 1.1 %collective-permute-done.4 = f32[40,128]{1,0:T(8,128)S(1)} collective-permute-done((f32[40,128]{1,0:T(8,128)S(1)}, f32[40,128]{1,0:T(8,128)S(1)}, u32[]{:S(2)}, u32[]{:S(2)}) %collective-permute-start.4) | collective-permute-done | bytes 20512 | tf_op jit(solution)/shard_map/ppermute | solution.py:501
  19.6 0.1 collective-permute-start.5
  19.7 3.1 %collective-permute-done.5 = f32[40,128]{1,0:T(8,128)S(1)} collective-permute-done((f32[40,128]{1,0:T(8,128)S(1)}, f32[40,128]{1,0:T(8,128)S(1)}, u32[]{:S(2)}, u32[]{:S(2)}) %collective-permute-start.5) | collective-permute-done | bytes 20512 | tf_op jit(solution)/shard_map/ppermute | solution.py:501
  22.8 0.0 copy-start.2
  22.8 0.2 collective-permute-start.6
  23.0 0.0 copy-done
  23.0 0.0 copy-done.4
  23.0 1.2 %own_gradient.1 = (f32[128,512]{1,0:T(8,128)}, f32[32,512]{1,0:T(8,128)S(1)}, f32[32,512]{1,0:T(8,128)S(1)}) custom-call(s32[1]{0:T(128)} %bitcast.part_ref, f32[128,512]{1,0:T(8,128)S(1)} %copy-done.1, f32[40,128]{1,0:T(8,128)S(1)} %add.19.sum_ref, bf16[2,256,512]{2,1,0:T(8,128)(2,1)S(1)} %copy-done, bf16[4,256,240]{2,1,0:T(8,128)(2,1)S(1)} %copy-done.4), custom_call_target="tpu_custom_call" | custom-call | flops 2147483648 | bytes 1048576 | tf_op jit(solution)/shard_map/own_gradient/pallas_call | solution.py:458
  24.2 2.7 %collective-permute-done.6.near_ref = f32[40,128]{1,0:T(8,128)S(1)} collective-permute-done((f32[40,128]{1,0:T(8,128)S(1)}, f32[40,128]{1,0:T(8,128)S(1)}, u32[]{:S(2)}, u32[]{:S(2)}) %collective-permute-start.6) | collective-permute-done | bytes 20512 | tf_op jit(solution)/shard_map/ppermute | solution.py:498
  26.9 0.0 copy-done.2
  26.9 1.1 %edge_gradient.1 = f32[128,512]{1,0:T(8,128)} custom-call(s32[1]{0:T(128)} %bitcast.part_ref, f32[128,512]{1,0:T(8,128)} %get-tuple-element.22.gradient_hbm, f32[32,512]{1,0:T(8,128)S(1)} %get-tuple-element.23.edge_ref, f32[32,512]{1,0:T(8,128)S(1)} %get-tuple-element.24.scale_ref, ...), custom_call_target="tpu_custom_call", output_to_operand_aliasing={{}: (1, {})} | custom-call | flops 268435456 | bytes 1048576 | tf_op jit(solution)/shard_map/edge_gradient/pallas_call | solution.py:458
  (4 shorter events, 0.0 us)
Async XLA Ops:
  0.0 4.1 %copy-start.1 = (f32[128,512]{1,0:T(8,128)S(1)}, f32[128,512]{1,0:T(8,128)}, u32[]{:S(2)}) copy-start(f32[128,512]{1,0:T(8,128)} %theta_ref.3) | copy-start | bytes 786436
  0.0 4.1 %copy-start.5 = (bf16[2,512,256]{2,1,0:T(8,128)(2,1)S(1)}, bf16[2,512,256]{2,1,0:T(8,128)(2,1)}, u32[]{:S(2)}) copy-start(bf16[2,512,256]{2,1,0:T(8,128)(2,1)} %constant.43.clone.column_ref) | copy-start | bytes 1572868
  0.0 4.1 %copy-start.7 = (bf16[4,80,384]{2,1,0:T(8,128)(2,1)S(1)}, bf16[4,80,384]{2,1,0:T(8,128)(2,1)}, u32[]{:S(2)}) copy-start(bf16[4,80,384]{2,1,0:T(8,128)(2,1)} %constant.45.clone.rows_ref) | copy-start | bytes 737284
  1.9 3.8 %collective-permute-start.1 = (f32[32,128]{1,0:T(8,128)S(1)}, f32[32,128]{1,0:T(8,128)S(1)}, u32[]{:S(2)}, u32[]{:S(2)}) collective-permute-start(f32[32,128]{1,0:T(8,128)S(1)} %get-tuple-element.16), channel_id=1, source_target_pairs={{1,2},{2,1},{5,6},{6,5},{9,10},{10,9},{13,14},{14,13},{17,18},{18,... | collective-permute-start | bytes 49160 | tf_op jit(solution)/shard_map/ppermute | solution.py:498
  3.3 2.3 %copy-start.9 = (bf16[4,80,96]{2,1,0:T(8,128)(2,1)S(1)}, bf16[4,80,96]{2,1,0:T(8,128)(2,1)}, u32[]{:S(2)}) copy-start(bf16[4,80,96]{2,1,0:T(8,128)(2,1)} %constant.47.clone.rows_ref) | copy-start | bytes 184324
  3.3 6.7 %collective-permute-start = (f32[8,40,128]{2,1,0:T(8,128)S(1)}, f32[8,40,128]{2,1,0:T(8,128)S(1)}, u32[]{:S(2)}, u32[]{:S(2)}) collective-permute-start(f32[8,40,128]{2,1,0:T(8,128)S(1)} %get-tuple-element.15), channel_id=1, source_target_pairs={{0,3},{1,2},{2,1},{3,0},{4,7},{5,6},{6,5},{7,4},{8,11},{9,10},{10,... | collective-permute-start | bytes 491528 | tf_op jit(solution)/shard_map/ppermute | solution.py:501
  4.6 5.6 %copy-start.3 = (s32[512,512]{1,0:T(8,128)S(1)}, s32[512,512]{1,0:T(8,128)}, u32[]{:S(2)}) copy-start(s32[512,512]{1,0:T(8,128)} %target_ref.1) | copy-start | bytes 3145732
  6.0 4.0 %collective-permute-start.2 = (f32[1,40,128]{2,1,0:T(8,128)S(1)}, f32[1,40,128]{2,1,0:T(8,128)S(1)}, u32[]{:S(2)}, u32[]{:S(2)}) collective-permute-start(f32[1,40,128]{2,1,0:T(8,128)S(1)} %add_rim.1), channel_id=1, source_target_pairs={{0,3},{1,2},{2,1},{3,0},{4,7},{5,6},{6,5},{7,4},{8,11},{9,10},{10,... | collective-permute-start | bytes 61448 | tf_op jit(solution)/shard_map/ppermute | solution.py:501
  10.0 1.8 %copy-start.6 = (bf16[512,240]{1,0:T(8,128)(2,1)S(1)}, bf16[512,240]{1,0:T(8,128)(2,1)}, u32[]{:S(2)}) copy-start(bf16[512,240]{1,0:T(8,128)(2,1)} %constant.52.clone.row_ref) | copy-start | bytes 737284
  10.0 1.7 %copy-start.8 = (bf16[160,512]{1,0:T(8,128)(2,1)S(1)}, bf16[160,512]{1,0:T(8,128)(2,1)}, u32[]{:S(2)}) copy-start(bf16[160,512]{1,0:T(8,128)(2,1)} %constant.53.clone.row_turned_ref) | copy-start | bytes 491524
  10.1 1.7 %collective-permute-start.3 = (f32[17,40,128]{2,1,0:T(8,128)S(1)}, f32[17,40,128]{2,1,0:T(8,128)S(1)}, u32[]{:S(2)}, u32[]{:S(2)}) collective-permute-start(f32[17,40,128]{2,1,0:T(8,128)S(1)} %pad_maximum_fusion.mixed_ref), channel_id=1, source_target_pairs={{0,1},{1,0},{2,3},{3,2},{4,5},{5,4},{6,7},{7,6},{8,9},{9,8},{10,11... | collective-permute-start | bytes 1044488 | tf_op jit(solution)/shard_map/ppermute | solution.py:501
  11.8 11.2 %copy-start = (bf16[2,256,512]{2,1,0:T(8,128)(2,1)S(1)}, bf16[2,256,512]{2,1,0:T(8,128)(2,1)}, u32[]{:S(2)}) copy-start(bf16[2,256,512]{2,1,0:T(8,128)(2,1)} %constant.51.clone.turned_ref) | copy-start | bytes 1572868
  11.8 11.2 %copy-start.4 = (bf16[4,256,240]{2,1,0:T(8,128)(2,1)S(1)}, bf16[4,256,240]{2,1,0:T(8,128)(2,1)}, u32[]{:S(2)}) copy-start(bf16[4,256,240]{2,1,0:T(8,128)(2,1)} %constant.46.clone.rows_ref) | copy-start | bytes 1474564
  18.3 1.3 %collective-permute-start.4 = (f32[40,128]{1,0:T(8,128)S(1)}, f32[40,128]{1,0:T(8,128)S(1)}, u32[]{:S(2)}, u32[]{:S(2)}) collective-permute-start(f32[40,128]{1,0:T(8,128)S(1)} %coherent_fields.1), channel_id=1, source_target_pairs={{0,1},{1,0},{2,3},{3,2},{4,5},{5,4},{6,7},{7,6},{8,9},{9,8},{10,11... | collective-permute-start | bytes 61448 | tf_op jit(solution)/shard_map/ppermute | solution.py:501
  19.6 3.2 %collective-permute-start.5 = (f32[40,128]{1,0:T(8,128)S(1)}, f32[40,128]{1,0:T(8,128)S(1)}, u32[]{:S(2)}, u32[]{:S(2)}) collective-permute-start(f32[40,128]{1,0:T(8,128)S(1)} %add.18), channel_id=1, source_target_pairs={{0,3},{1,2},{2,1},{3,0},{4,7},{5,6},{6,5},{7,4},{8,11},{9,10},{10,... | collective-permute-start | bytes 61448 | tf_op jit(solution)/shard_map/ppermute | solution.py:501
  22.8 4.1 %copy-start.2 = (bf16[4,64,240]{2,1,0:T(8,128)(2,1)S(1)}, bf16[4,64,240]{2,1,0:T(8,128)(2,1)}, u32[]{:S(2)}) copy-start(bf16[4,64,240]{2,1,0:T(8,128)(2,1)} %constant.48.clone.rows_ref) | copy-start | bytes 368644
  22.8 4.1 %collective-permute-start.6 = (f32[40,128]{1,0:T(8,128)S(1)}, f32[40,128]{1,0:T(8,128)S(1)}, u32[]{:S(2)}, u32[]{:S(2)}) collective-permute-start(f32[40,128]{1,0:T(8,128)S(1)} %add.19.sum_ref), channel_id=1, source_target_pairs={{0,1},{3,2},{4,5},{7,6},{8,9},{11,10},{12,13},{15,14},{16,17},{19,... | collective-permute-start | bytes 61448 | tf_op jit(solution)/shard_map/ppermute | solution.py:498

commit v15 on v11

--- a/solution.py
+++ b/solution.py
@@ -389,7 +389,7 @@
             turned[pl.ds(index * 2, 2)] = jnp.stack([back[:, :ROWS], back[:, ROWS:]])
         return carry
 
-    lax.fori_loop(0, CONDS, drive, 0, unroll=4)
+    lax.fori_loop(0, CONDS, drive, 0, unroll=8)
     high, low = split(turned[...].reshape(count * tall, ROWS))
     backs[...] = dot(jnp.concatenate([high, low], axis=1), backward_ref[: 2 * ROWS]) + dot(high, backward_ref[2 * ROWS :])
 

time: 27.8 us -> 27.6 us (level)
  Pallas kernels: 11.5 us -> 11.2 us
  transfers between devices with their start and end apart: 7 -> 7, of which waited for: 6 -> 6; matrix products, arithmetic and copies ran while one was open for 0% -> 0% of each run, Pallas kernels for 8% -> 9%
where the time goes in v15:
time: 27.6 us; the launch traced here: 27.4 us
  waiting for transfers between devices  12.3 us (45%)
  Pallas kernels  11.2 us (41%)
  starting transfers between devices  3.68 us (13%)
    pallas_call x7, Pallas kernels, call(): pl.pallas_call(kernel, grid_spec=pltpu.PrefetchScalarGridSpec(num_scalar_...  11.2 us
    ppermute x5, waiting for transfers between devices, partner(): return lax.ppermute(value, 'cond', [(i, i ^ step) for i in range(PARTS)])  8.58 us
    ppermute x2, waiting for transfers between devices, across(): return lax.ppermute(value, ('tile', 'cond'), pairs)  3.75 us
    ppermute x5, starting transfers between devices, partner(): return lax.ppermute(value, 'cond', [(i, i ^ step) for i in range(PARTS)])  2.05 us
    ppermute x2, starting transfers between devices, across(): return lax.ppermute(value, ('tile', 'cond'), pairs)  1.63 us
  transfers between devices with their start and end apart: 7, of which 6 were waited for; matrix products, arithmetic and copies ran while one was open for 0% of the time, Pallas kernels for 9%

profile of v15, /device:TPU:24, one launch (start us, length us, event | category | flops | bytes accessed | tf_op | source)
XLA Modules:
  0.0 27.4 jit_solution(15108495964617039945)
XLA Ops:
  0.0 0.0 copy-start.1
  0.0 0.0 copy-start.5
  0.0 0.0 copy-start.7
  0.0 1.9 %open_parts.1 = (f32[8,40,128]{2,1,0:T(8,128)S(1)}, f32[32,128]{1,0:T(8,128)S(1)}, f32[8,128]{1,0:T(8,128)S(1)}, bf16[384,256]{1,0:T(8,128)(2,1)S(1)}, bf16[384,256]{1,0:T(8,128)(2,1)S(1)}) custom-call(s32[1]{0:T(128)} %bitcast.part_ref, f32[128,512]{1,0:T(8,128)} %theta_ref.3, bf16[2,512,128]{2,1,0:T(8,128)(2,1)} %constant.44.clone.waves_hbm, ...), custom_call_target="tpu_custom_call" | custom-call | flops 268435456 | bytes 1048576 | tf_op jit(solution)/shard_map/open_parts/pallas_call | solution.py:458
  1.9 1.5 %collective-permute-start.1 = (f32[32,128]{1,0:T(8,128)S(1)}, f32[32,128]{1,0:T(8,128)S(1)}, u32[]{:S(2)}, u32[]{:S(2)}) collective-permute-start(f32[32,128]{1,0:T(8,128)S(1)} %get-tuple-element.16), channel_id=1, source_target_pairs={{1,2},{2,1},{5,6},{6,5},{9,10},{10,9},{13,14},{14,13},{17,18},{18,... | collective-permute-start | bytes 49160 | tf_op jit(solution)/shard_map/ppermute | solution.py:498
  3.3 0.0 copy-start.9
  3.3 0.8 %collective-permute-start = (f32[8,40,128]{2,1,0:T(8,128)S(1)}, f32[8,40,128]{2,1,0:T(8,128)S(1)}, u32[]{:S(2)}, u32[]{:S(2)}) collective-permute-start(f32[8,40,128]{2,1,0:T(8,128)S(1)} %get-tuple-element.15), channel_id=1, source_target_pairs={{0,3},{1,2},{2,1},{3,0},{4,7},{5,6},{6,5},{7,4},{8,11},{9,10},{10,... | collective-permute-start | bytes 491528 | tf_op jit(solution)/shard_map/ppermute | solution.py:501
  4.1 0.0 copy-done.1
  4.1 0.0 copy-done.5
  4.1 0.0 copy-done.7
  4.1 0.5 %own_spectrum.1.spectrum_ref = f32[2,40,128]{2,1,0:T(8,128)S(1)} custom-call(s32[1]{0:T(128)} %bitcast.part_ref, f32[128,512]{1,0:T(8,128)S(1)} %copy-done.1, bf16[2,512,256]{2,1,0:T(8,128)(2,1)S(1)} %copy-done.5, bf16[4,80,384]{2,1,0:T(8,128)(2,1)S(1)} %copy-done.7), custom_call_target="tpu_custom_call" | custom-call | flops 2147483648 | bytes 1048576 | tf_op jit(solution)/shard_map/own_spectrum/pallas_call | solution.py:458
  4.6 0.0 copy-start.3
  4.6 1.1 %collective-permute-done.1.rim_ref = f32[32,128]{1,0:T(8,128)S(1)} collective-permute-done((f32[32,128]{1,0:T(8,128)S(1)}, f32[32,128]{1,0:T(8,128)S(1)}, u32[]{:S(2)}, u32[]{:S(2)}) %collective-permute-start.1) | collective-permute-done | bytes 16416 | tf_op jit(solution)/shard_map/ppermute | solution.py:498
  5.7 0.0 copy-done.9
  5.7 0.3 %add_rim.1 = f32[1,40,128]{2,1,0:T(8,128)S(1)} custom-call(s32[1]{0:T(128)} %bitcast.part_ref, f32[2,40,128]{2,1,0:T(8,128)S(1)} %own_spectrum.1.spectrum_ref, f32[32,128]{1,0:T(8,128)S(1)} %collective-permute-done.1.rim_ref, bf16[4,80,96]{2,1,0:T(8,128)(2,1)S(1)} %copy-done.9), custom_call_target="tpu_custom_call" | custom-call | flops 268435456 | bytes 1048576 | tf_op jit(solution)/shard_map/add_rim/pallas_call | solution.py:458
  6.0 0.7 %collective-permute-start.2 = (f32[1,40,128]{2,1,0:T(8,128)S(1)}, f32[1,40,128]{2,1,0:T(8,128)S(1)}, u32[]{:S(2)}, u32[]{:S(2)}) collective-permute-start(f32[1,40,128]{2,1,0:T(8,128)S(1)} %add_rim.1), channel_id=1, source_target_pairs={{0,3},{1,2},{2,1},{3,0},{4,7},{5,6},{6,5},{7,4},{8,11},{9,10},{10,... | collective-permute-start | bytes 61448 | tf_op jit(solution)/shard_map/ppermute | solution.py:501
  6.7 3.3 %collective-permute-done.2 = f32[1,40,128]{2,1,0:T(8,128)S(1)} collective-permute-done((f32[1,40,128]{2,1,0:T(8,128)S(1)}, f32[1,40,128]{2,1,0:T(8,128)S(1)}, u32[]{:S(2)}, u32[]{:S(2)}) %collective-permute-start.2) | collective-permute-done | bytes 20512 | tf_op jit(solution)/shard_map/ppermute | solution.py:501
  10.0 0.0 collective-permute-done
  10.0 0.0 copy-start.6
  10.0 0.0 copy-start.8
  10.1 0.2 collective-permute-start.3
  10.2 0.0 copy-done.3
  10.2 0.3 %near_kernels.1 = (f32[8,4,40,128]{3,2,1,0:T(8,128)S(1)}, f32[512,128]{1,0:T(8,128)S(1)}) custom-call(s32[1]{0:T(128)} %bitcast.part_ref, f32[17,40,128]{2,1,0:T(8,128)S(1)} %pad_maximum_fusion.mixed_ref, s32[512,512]{1,0:T(8,128)S(1)} %copy-done.3), custom_call_target="tpu_custom_call" | custom-call | flops 1073741824 | bytes 1048576 | tf_op jit(solution)/shard_map/near_kernels/pallas_call | solution.py:458
  10.6 1.2 %collective-permute-done.3.other_ref = f32[17,40,128]{2,1,0:T(8,128)S(1)} collective-permute-done((f32[17,40,128]{2,1,0:T(8,128)S(1)}, f32[17,40,128]{2,1,0:T(8,128)S(1)}, u32[]{:S(2)}, u32[]{:S(2)}) %collective-permute-start.3) | collective-permute-done | bytes 348192 | tf_op jit(solution)/shard_map/ppermute | solution.py:501
  11.8 0.0 copy-done.6
  11.8 0.0 copy-done.8
  11.8 0.0 copy-start
  11.8 0.0 copy-start.4
  11.8 5.9 %coherent_fields.1 = f32[40,128]{1,0:T(8,128)S(1)} custom-call(s32[1]{0:T(128)} %bitcast.part_ref, f32[17,40,128]{2,1,0:T(8,128)S(1)} %pad_maximum_fusion.mixed_ref, f32[17,40,128]{2,1,0:T(8,128)S(1)} %collective-permute-done.3.other_ref, f32[8,4,40,128]{3,2,1,0:T(8,128)S(1)} %get-tuple-element.17.near_ref, f32[512,128]{1,0:T(8,128)S(1)} %get-tuple-element.18.signs, ...), custom_call_target="tpu_custom_call" | custom-call | flops 8589934592 | bytes 1048576 | tf_op jit(solution)/shard_map/coherent_fields/pallas_call | solution.py:458
  17.7 0.2 collective-permute-start.4
  17.9 1.1 %collective-permute-done.4 = f32[40,128]{1,0:T(8,128)S(1)} collective-permute-done((f32[40,128]{1,0:T(8,128)S(1)}, f32[40,128]{1,0:T(8,128)S(1)}, u32[]{:S(2)}, u32[]{:S(2)}) %collective-permute-start.4) | collective-permute-done | bytes 20512 | tf_op jit(solution)/shard_map/ppermute | solution.py:501
  19.0 0.2 collective-permute-start.5
  19.1 3.1 %collective-permute-done.5 = f32[40,128]{1,0:T(8,128)S(1)} collective-permute-done((f32[40,128]{1,0:T(8,128)S(1)}, f32[40,128]{1,0:T(8,128)S(1)}, u32[]{:S(2)}, u32[]{:S(2)}) %collective-permute-start.5) | collective-permute-done | bytes 20512 | tf_op jit(solution)/shard_map/ppermute | solution.py:501
  22.2 0.0 copy-start.2
  22.2 0.2 collective-permute-start.6
  22.4 0.0 copy-done
  22.4 0.0 copy-done.4
  22.4 1.2 %own_gradient.1 = (f32[128,512]{1,0:T(8,128)}, f32[32,512]{1,0:T(8,128)S(1)}, f32[32,512]{1,0:T(8,128)S(1)}) custom-call(s32[1]{0:T(128)} %bitcast.part_ref, f32[128,512]{1,0:T(8,128)S(1)} %copy-done.1, f32[40,128]{1,0:T(8,128)S(1)} %add.19.sum_ref, bf16[2,256,512]{2,1,0:T(8,128)(2,1)S(1)} %copy-done, bf16[4,256,240]{2,1,0:T(8,128)(2,1)S(1)} %copy-done.4), custom_call_target="tpu_custom_call" | custom-call | flops 2147483648 | bytes 1048576 | tf_op jit(solution)/shard_map/own_gradient/pallas_call | solution.py:458
  23.6 2.7 %collective-permute-done.6.near_ref = f32[40,128]{1,0:T(8,128)S(1)} collective-permute-done((f32[40,128]{1,0:T(8,128)S(1)}, f32[40,128]{1,0:T(8,128)S(1)}, u32[]{:S(2)}, u32[]{:S(2)}) %collective-permute-start.6) | collective-permute-done | bytes 20512 | tf_op jit(solution)/shard_map/ppermute | solution.py:498
  26.3 0.0 copy-done.2
  26.3 1.1 %edge_gradient.1 = f32[128,512]{1,0:T(8,128)} custom-call(s32[1]{0:T(128)} %bitcast.part_ref, f32[128,512]{1,0:T(8,128)} %get-tuple-element.22.gradient_hbm, f32[32,512]{1,0:T(8,128)S(1)} %get-tuple-element.23.edge_ref, f32[32,512]{1,0:T(8,128)S(1)} %get-tuple-element.24.scale_ref, ...), custom_call_target="tpu_custom_call", output_to_operand_aliasing={{}: (1, {})} | custom-call | flops 268435456 | bytes 1048576 | tf_op jit(solution)/shard_map/edge_gradient/pallas_call | solution.py:458
  (4 shorter events, 0.0 us)
Async XLA Ops:
  0.0 4.1 %copy-start.1 = (f32[128,512]{1,0:T(8,128)S(1)}, f32[128,512]{1,0:T(8,128)}, u32[]{:S(2)}) copy-start(f32[128,512]{1,0:T(8,128)} %theta_ref.3) | copy-start | bytes 786436
  0.0 4.1 %copy-start.5 = (bf16[2,512,256]{2,1,0:T(8,128)(2,1)S(1)}, bf16[2,512,256]{2,1,0:T(8,128)(2,1)}, u32[]{:S(2)}) copy-start(bf16[2,512,256]{2,1,0:T(8,128)(2,1)} %constant.43.clone.column_ref) | copy-start | bytes 1572868
  0.0 4.1 %copy-start.7 = (bf16[4,80,384]{2,1,0:T(8,128)(2,1)S(1)}, bf16[4,80,384]{2,1,0:T(8,128)(2,1)}, u32[]{:S(2)}) copy-start(bf16[4,80,384]{2,1,0:T(8,128)(2,1)} %constant.45.clone.rows_ref) | copy-start | bytes 737284
  1.9 3.8 %collective-permute-start.1 = (f32[32,128]{1,0:T(8,128)S(1)}, f32[32,128]{1,0:T(8,128)S(1)}, u32[]{:S(2)}, u32[]{:S(2)}) collective-permute-start(f32[32,128]{1,0:T(8,128)S(1)} %get-tuple-element.16), channel_id=1, source_target_pairs={{1,2},{2,1},{5,6},{6,5},{9,10},{10,9},{13,14},{14,13},{17,18},{18,... | collective-permute-start | bytes 49160 | tf_op jit(solution)/shard_map/ppermute | solution.py:498
  3.3 2.3 %copy-start.9 = (bf16[4,80,96]{2,1,0:T(8,128)(2,1)S(1)}, bf16[4,80,96]{2,1,0:T(8,128)(2,1)}, u32[]{:S(2)}) copy-start(bf16[4,80,96]{2,1,0:T(8,128)(2,1)} %constant.47.clone.rows_ref) | copy-start | bytes 184324
  3.3 6.7 %collective-permute-start = (f32[8,40,128]{2,1,0:T(8,128)S(1)}, f32[8,40,128]{2,1,0:T(8,128)S(1)}, u32[]{:S(2)}, u32[]{:S(2)}) collective-permute-start(f32[8,40,128]{2,1,0:T(8,128)S(1)} %get-tuple-element.15), channel_id=1, source_target_pairs={{0,3},{1,2},{2,1},{3,0},{4,7},{5,6},{6,5},{7,4},{8,11},{9,10},{10,... | collective-permute-start | bytes 491528 | tf_op jit(solution)/shard_map/ppermute | solution.py:501
  4.6 5.6 %copy-start.3 = (s32[512,512]{1,0:T(8,128)S(1)}, s32[512,512]{1,0:T(8,128)}, u32[]{:S(2)}) copy-start(s32[512,512]{1,0:T(8,128)} %target_ref.1) | copy-start | bytes 3145732
  6.0 4.0 %collective-permute-start.2 = (f32[1,40,128]{2,1,0:T(8,128)S(1)}, f32[1,40,128]{2,1,0:T(8,128)S(1)}, u32[]{:S(2)}, u32[]{:S(2)}) collective-permute-start(f32[1,40,128]{2,1,0:T(8,128)S(1)} %add_rim.1), channel_id=1, source_target_pairs={{0,3},{1,2},{2,1},{3,0},{4,7},{5,6},{6,5},{7,4},{8,11},{9,10},{10,... | collective-permute-start | bytes 61448 | tf_op jit(solution)/shard_map/ppermute | solution.py:501
  10.0 1.8 %copy-start.6 = (bf16[512,240]{1,0:T(8,128)(2,1)S(1)}, bf16[512,240]{1,0:T(8,128)(2,1)}, u32[]{:S(2)}) copy-start(bf16[512,240]{1,0:T(8,128)(2,1)} %constant.52.clone.row_ref) | copy-start | bytes 737284
  10.0 1.7 %copy-start.8 = (bf16[160,512]{1,0:T(8,128)(2,1)S(1)}, bf16[160,512]{1,0:T(8,128)(2,1)}, u32[]{:S(2)}) copy-start(bf16[160,512]{1,0:T(8,128)(2,1)} %constant.53.clone.row_turned_ref) | copy-start | bytes 491524
  10.1 1.7 %collective-permute-start.3 = (f32[17,40,128]{2,1,0:T(8,128)S(1)}, f32[17,40,128]{2,1,0:T(8,128)S(1)}, u32[]{:S(2)}, u32[]{:S(2)}) collective-permute-start(f32[17,40,128]{2,1,0:T(8,128)S(1)} %pad_maximum_fusion.mixed_ref), channel_id=1, source_target_pairs={{0,1},{1,0},{2,3},{3,2},{4,5},{5,4},{6,7},{7,6},{8,9},{9,8},{10,11... | collective-permute-start | bytes 1044488 | tf_op jit(solution)/shard_map/ppermute | solution.py:501
  11.8 10.6 %copy-start = (bf16[2,256,512]{2,1,0:T(8,128)(2,1)S(1)}, bf16[2,256,512]{2,1,0:T(8,128)(2,1)}, u32[]{:S(2)}) copy-start(bf16[2,256,512]{2,1,0:T(8,128)(2,1)} %constant.51.clone.turned_ref) | copy-start | bytes 1572868
  11.8 10.6 %copy-start.4 = (bf16[4,256,240]{2,1,0:T(8,128)(2,1)S(1)}, bf16[4,256,240]{2,1,0:T(8,128)(2,1)}, u32[]{:S(2)}) copy-start(bf16[4,256,240]{2,1,0:T(8,128)(2,1)} %constant.46.clone.rows_ref) | copy-start | bytes 1474564
  17.7 1.3 %collective-permute-start.4 = (f32[40,128]{1,0:T(8,128)S(1)}, f32[40,128]{1,0:T(8,128)S(1)}, u32[]{:S(2)}, u32[]{:S(2)}) collective-permute-start(f32[40,128]{1,0:T(8,128)S(1)} %coherent_fields.1), channel_id=1, source_target_pairs={{0,1},{1,0},{2,3},{3,2},{4,5},{5,4},{6,7},{7,6},{8,9},{9,8},{10,11... | collective-permute-start | bytes 61448 | tf_op jit(solution)/shard_map/ppermute | solution.py:501
  19.0 3.2 %collective-permute-start.5 = (f32[40,128]{1,0:T(8,128)S(1)}, f32[40,128]{1,0:T(8,128)S(1)}, u32[]{:S(2)}, u32[]{:S(2)}) collective-permute-start(f32[40,128]{1,0:T(8,128)S(1)} %add.18), channel_id=1, source_target_pairs={{0,3},{1,2},{2,1},{3,0},{4,7},{5,6},{6,5},{7,4},{8,11},{9,10},{10,... | collective-permute-start | bytes 61448 | tf_op jit(solution)/shard_map/ppermute | solution.py:501
  22.2 4.1 %copy-start.2 = (bf16[4,64,240]{2,1,0:T(8,128)(2,1)S(1)}, bf16[4,64,240]{2,1,0:T(8,128)(2,1)}, u32[]{:S(2)}) copy-start(bf16[4,64,240]{2,1,0:T(8,128)(2,1)} %constant.48.clone.rows_ref) | copy-start | bytes 368644
  22.2 4.1 %collective-permute-start.6 = (f32[40,128]{1,0:T(8,128)S(1)}, f32[40,128]{1,0:T(8,128)S(1)}, u32[]{:S(2)}, u32[]{:S(2)}) collective-permute-start(f32[40,128]{1,0:T(8,128)S(1)} %add.19.sum_ref), channel_id=1, source_target_pairs={{0,1},{3,2},{4,5},{7,6},{8,9},{11,10},{12,13},{15,14},{16,17},{19,... | collective-permute-start | bytes 61448 | tf_op jit(solution)/shard_map/ppermute | solution.py:498

commit v16 on v15

--- a/solution.py
+++ b/solution.py
@@ -355,17 +355,14 @@
                 )
             )
         high, low = split(jnp.concatenate(parts, axis=1))
-        folded[kern] = jnp.concatenate([high, high, low], axis=0)
+        lanes = slice(kern % KERNELS * 2 * ROWS, (kern % KERNELS + 1) * 2 * ROWS)
+        folded[kern // KERNELS, :, lanes] = jnp.concatenate([high, high, low], axis=0)
     total[...] = jnp.zeros_like(total)
 
     def expose(cond, carry):
-        intensity = None
-        for kern in range(KERNELS):
-            index = cond * KERNELS + kern
-            amp = dot(row_ref[...], folded[index])
-            amps[index] = amp
-            power = amp[:, :ROWS] * amp[:, :ROWS] + amp[:, ROWS:] * amp[:, ROWS:]
-            intensity = power if intensity is None else intensity + power
+        amp = dot(row_ref[...], folded[cond])
+        amps[cond] = amp
+        intensity = sum(amp[:, i * ROWS : (i + 1) * ROWS] * amp[:, i * ROWS : (i + 1) * ROWS] for i in range(2 * KERNELS))
         level = levels_ref[pl.ds(cond, 1), :]
         value = jnp.tanh((0.5 * resist_steep) * (intensity - level))
         tanhs[cond] = value
@@ -380,13 +377,11 @@
         value = tanhs[cond]
         slope = (weight + band_weight / CONDS) * value + weight * signs[...] - total[...]
         field = (0.5 * resist_steep) * (1.0 - value * value) * slope
-        field = jnp.concatenate([field, field], axis=1)
-        for kern in range(KERNELS):
-            index = cond * KERNELS + kern
-            high, low = split(field * amps[index])
-            long = dot(row_turned_ref[...], high)
-            back = long[: 2 * FA] + long[2 * FA :] + dot(row_turned_ref[: 2 * FA], low)
-            turned[pl.ds(index * 2, 2)] = jnp.stack([back[:, :ROWS], back[:, ROWS:]])
+        high, low = split(jnp.concatenate([field] * (2 * KERNELS), axis=1) * amps[cond])
+        long = dot(row_turned_ref[...], high)
+        back = long[: 2 * FA] + long[2 * FA :] + dot(row_turned_ref[: 2 * FA], low)
+        for i in range(2 * KERNELS):
+            turned[cond * 2 * KERNELS + i] = back[:, i * ROWS : (i + 1) * ROWS]
         return carry
 
     lax.fori_loop(0, CONDS, drive, 0, unroll=8)
@@ -582,8 +577,8 @@
             pltpu.VMEM((count // 2, 4, FA, 2 * FB), F32),
             pltpu.VMEM((CONDS, ROWS), F32),
             pltpu.VMEM((count * 4 * FA, 2 * FB), F32),
-            pltpu.VMEM((count, 6 * FA, 2 * ROWS), BF),
-            pltpu.VMEM((count, TP, 2 * ROWS), F32),
+            pltpu.VMEM((CONDS, 6 * FA, 2 * KERNELS * ROWS), BF),
+            pltpu.VMEM((CONDS, TP, 2 * KERNELS * ROWS), F32),
             pltpu.VMEM((CONDS, TP, ROWS), F32),
             pltpu.VMEM((TP, ROWS), F32),
             pltpu.VMEM((count * 2, 2 * FA, ROWS), F32),

time: 27.6 us -> 27.6 us (level)
  no operation moved by 1% of the time
where the time goes in v16:
time: 27.6 us; the launch traced here: 27.4 us
  waiting for transfers between devices  12.3 us (45%)
  Pallas kernels  11.2 us (41%)
  starting transfers between devices  3.67 us (13%)
    pallas_call x7, Pallas kernels, call(): pl.pallas_call(kernel, grid_spec=pltpu.PrefetchScalarGridSpec(num_scalar_...  11.2 us
    ppermute x5, waiting for transfers between devices, partner(): return lax.ppermute(value, 'cond', [(i, i ^ step) for i in range(PARTS)])  8.58 us
    ppermute x2, waiting for transfers between devices, across(): return lax.ppermute(value, ('tile', 'cond'), pairs)  3.75 us
    ppermute x5, starting transfers between devices, partner(): return lax.ppermute(value, 'cond', [(i, i ^ step) for i in range(PARTS)])  2.04 us
    ppermute x2, starting transfers between devices, across(): return lax.ppermute(value, ('tile', 'cond'), pairs)  1.63 us
  transfers between devices with their start and end apart: 7, of which 6 were waited for; matrix products, arithmetic and copies ran while one was open for 0% of the time, Pallas kernels for 9%

profile of v16, /device:TPU:24, one launch (start us, length us, event | category | flops | bytes accessed | tf_op | source)
XLA Modules:
  0.0 27.4 jit_solution(8974177239800637296)
XLA Ops:
  0.0 0.0 copy-start.1
  0.0 0.0 copy-start.5
  0.0 0.0 copy-start.7
  0.0 1.9 %open_parts.1 = (f32[8,40,128]{2,1,0:T(8,128)S(1)}, f32[32,128]{1,0:T(8,128)S(1)}, f32[8,128]{1,0:T(8,128)S(1)}, bf16[384,256]{1,0:T(8,128)(2,1)S(1)}, bf16[384,256]{1,0:T(8,128)(2,1)S(1)}) custom-call(s32[1]{0:T(128)} %bitcast.part_ref, f32[128,512]{1,0:T(8,128)} %theta_ref.3, bf16[2,512,128]{2,1,0:T(8,128)(2,1)} %constant.44.clone.waves_hbm, ...), custom_call_target="tpu_custom_call" | custom-call | flops 268435456 | bytes 1048576 | tf_op jit(solution)/shard_map/open_parts/pallas_call | solution.py:453
  1.9 1.5 %collective-permute-start.1 = (f32[32,128]{1,0:T(8,128)S(1)}, f32[32,128]{1,0:T(8,128)S(1)}, u32[]{:S(2)}, u32[]{:S(2)}) collective-permute-start(f32[32,128]{1,0:T(8,128)S(1)} %get-tuple-element.16), channel_id=1, source_target_pairs={{1,2},{2,1},{5,6},{6,5},{9,10},{10,9},{13,14},{14,13},{17,18},{18,... | collective-permute-start | bytes 49160 | tf_op jit(solution)/shard_map/ppermute | solution.py:493
  3.3 0.0 copy-start.9
  3.3 0.8 %collective-permute-start = (f32[8,40,128]{2,1,0:T(8,128)S(1)}, f32[8,40,128]{2,1,0:T(8,128)S(1)}, u32[]{:S(2)}, u32[]{:S(2)}) collective-permute-start(f32[8,40,128]{2,1,0:T(8,128)S(1)} %get-tuple-element.15), channel_id=1, source_target_pairs={{0,3},{1,2},{2,1},{3,0},{4,7},{5,6},{6,5},{7,4},{8,11},{9,10},{10,... | collective-permute-start | bytes 491528 | tf_op jit(solution)/shard_map/ppermute | solution.py:496
  4.1 0.0 copy-done.1
  4.1 0.0 copy-done.5
  4.1 0.0 copy-done.7
  4.1 0.5 %own_spectrum.1.spectrum_ref = f32[2,40,128]{2,1,0:T(8,128)S(1)} custom-call(s32[1]{0:T(128)} %bitcast.part_ref, f32[128,512]{1,0:T(8,128)S(1)} %copy-done.1, bf16[2,512,256]{2,1,0:T(8,128)(2,1)S(1)} %copy-done.5, bf16[4,80,384]{2,1,0:T(8,128)(2,1)S(1)} %copy-done.7), custom_call_target="tpu_custom_call" | custom-call | flops 2147483648 | bytes 1048576 | tf_op jit(solution)/shard_map/own_spectrum/pallas_call | solution.py:453
  4.6 0.0 copy-start.3
  4.6 1.1 %collective-permute-done.1.rim_ref = f32[32,128]{1,0:T(8,128)S(1)} collective-permute-done((f32[32,128]{1,0:T(8,128)S(1)}, f32[32,128]{1,0:T(8,128)S(1)}, u32[]{:S(2)}, u32[]{:S(2)}) %collective-permute-start.1) | collective-permute-done | bytes 16416 | tf_op jit(solution)/shard_map/ppermute | solution.py:493
  5.7 0.0 copy-done.9
  5.7 0.3 %add_rim.1 = f32[1,40,128]{2,1,0:T(8,128)S(1)} custom-call(s32[1]{0:T(128)} %bitcast.part_ref, f32[2,40,128]{2,1,0:T(8,128)S(1)} %own_spectrum.1.spectrum_ref, f32[32,128]{1,0:T(8,128)S(1)} %collective-permute-done.1.rim_ref, bf16[4,80,96]{2,1,0:T(8,128)(2,1)S(1)} %copy-done.9), custom_call_target="tpu_custom_call" | custom-call | flops 268435456 | bytes 1048576 | tf_op jit(solution)/shard_map/add_rim/pallas_call | solution.py:453
  6.0 0.7 %collective-permute-start.2 = (f32[1,40,128]{2,1,0:T(8,128)S(1)}, f32[1,40,128]{2,1,0:T(8,128)S(1)}, u32[]{:S(2)}, u32[]{:S(2)}) collective-permute-start(f32[1,40,128]{2,1,0:T(8,128)S(1)} %add_rim.1), channel_id=1, source_target_pairs={{0,3},{1,2},{2,1},{3,0},{4,7},{5,6},{6,5},{7,4},{8,11},{9,10},{10,... | collective-permute-start | bytes 61448 | tf_op jit(solution)/shard_map/ppermute | solution.py:496
  6.7 3.3 %collective-permute-done.2 = f32[1,40,128]{2,1,0:T(8,128)S(1)} collective-permute-done((f32[1,40,128]{2,1,0:T(8,128)S(1)}, f32[1,40,128]{2,1,0:T(8,128)S(1)}, u32[]{:S(2)}, u32[]{:S(2)}) %collective-permute-start.2) | collective-permute-done | bytes 20512 | tf_op jit(solution)/shard_map/ppermute | solution.py:496
  10.0 0.0 collective-permute-done
  10.0 0.0 copy-start.6
  10.0 0.0 copy-start.8
  10.1 0.2 collective-permute-start.3
  10.2 0.0 copy-done.3
  10.2 0.3 %near_kernels.1 = (f32[8,4,40,128]{3,2,1,0:T(8,128)S(1)}, f32[512,128]{1,0:T(8,128)S(1)}) custom-call(s32[1]{0:T(128)} %bitcast.part_ref, f32[17,40,128]{2,1,0:T(8,128)S(1)} %pad_maximum_fusion.mixed_ref, s32[512,512]{1,0:T(8,128)S(1)} %copy-done.3), custom_call_target="tpu_custom_call" | custom-call | flops 1073741824 | bytes 1048576 | tf_op jit(solution)/shard_map/near_kernels/pallas_call | solution.py:453
  10.6 1.2 %collective-permute-done.3.other_ref = f32[17,40,128]{2,1,0:T(8,128)S(1)} collective-permute-done((f32[17,40,128]{2,1,0:T(8,128)S(1)}, f32[17,40,128]{2,1,0:T(8,128)S(1)}, u32[]{:S(2)}, u32[]{:S(2)}) %collective-permute-start.3) | collective-permute-done | bytes 348192 | tf_op jit(solution)/shard_map/ppermute | solution.py:496
  11.8 0.0 copy-done.6
  11.8 0.0 copy-done.8
  11.8 0.0 copy-start
  11.8 0.0 copy-start.4
  11.8 5.9 %coherent_fields.1 = f32[40,128]{1,0:T(8,128)S(1)} custom-call(s32[1]{0:T(128)} %bitcast.part_ref, f32[17,40,128]{2,1,0:T(8,128)S(1)} %pad_maximum_fusion.mixed_ref, f32[17,40,128]{2,1,0:T(8,128)S(1)} %collective-permute-done.3.other_ref, f32[8,4,40,128]{3,2,1,0:T(8,128)S(1)} %get-tuple-element.17.near_ref, f32[512,128]{1,0:T(8,128)S(1)} %get-tuple-element.18.signs, ...), custom_call_target="tpu_custom_call" | custom-call | flops 8589934592 | bytes 1048576 | tf_op jit(solution)/shard_map/coherent_fields/pallas_call | solution.py:453
  17.7 0.2 collective-permute-start.4
  17.9 1.1 %collective-permute-done.4 = f32[40,128]{1,0:T(8,128)S(1)} collective-permute-done((f32[40,128]{1,0:T(8,128)S(1)}, f32[40,128]{1,0:T(8,128)S(1)}, u32[]{:S(2)}, u32[]{:S(2)}) %collective-permute-start.4) | collective-permute-done | bytes 20512 | tf_op jit(solution)/shard_map/ppermute | solution.py:496
  19.0 0.1 collective-permute-start.5
  19.1 3.1 %collective-permute-done.5 = f32[40,128]{1,0:T(8,128)S(1)} collective-permute-done((f32[40,128]{1,0:T(8,128)S(1)}, f32[40,128]{1,0:T(8,128)S(1)}, u32[]{:S(2)}, u32[]{:S(2)}) %collective-permute-start.5) | collective-permute-done | bytes 20512 | tf_op jit(solution)/shard_map/ppermute | solution.py:496
  22.2 0.0 copy-start.2
  22.2 0.2 collective-permute-start.6
  22.4 0.0 copy-done
  22.4 0.0 copy-done.4
  22.4 1.2 %own_gradient.1 = (f32[128,512]{1,0:T(8,128)}, f32[32,512]{1,0:T(8,128)S(1)}, f32[32,512]{1,0:T(8,128)S(1)}) custom-call(s32[1]{0:T(128)} %bitcast.part_ref, f32[128,512]{1,0:T(8,128)S(1)} %copy-done.1, f32[40,128]{1,0:T(8,128)S(1)} %add.19.sum_ref, bf16[2,256,512]{2,1,0:T(8,128)(2,1)S(1)} %copy-done, bf16[4,256,240]{2,1,0:T(8,128)(2,1)S(1)} %copy-done.4), custom_call_target="tpu_custom_call" | custom-call | flops 2147483648 | bytes 1048576 | tf_op jit(solution)/shard_map/own_gradient/pallas_call | solution.py:453
  23.6 2.7 %collective-permute-done.6.near_ref = f32[40,128]{1,0:T(8,128)S(1)} collective-permute-done((f32[40,128]{1,0:T(8,128)S(1)}, f32[40,128]{1,0:T(8,128)S(1)}, u32[]{:S(2)}, u32[]{:S(2)}) %collective-permute-start.6) | collective-permute-done | bytes 20512 | tf_op jit(solution)/shard_map/ppermute | solution.py:493
  26.3 0.0 copy-done.2
  26.3 1.1 %edge_gradient.1 = f32[128,512]{1,0:T(8,128)} custom-call(s32[1]{0:T(128)} %bitcast.part_ref, f32[128,512]{1,0:T(8,128)} %get-tuple-element.22.gradient_hbm, f32[32,512]{1,0:T(8,128)S(1)} %get-tuple-element.23.edge_ref, f32[32,512]{1,0:T(8,128)S(1)} %get-tuple-element.24.scale_ref, ...), custom_call_target="tpu_custom_call", output_to_operand_aliasing={{}: (1, {})} | custom-call | flops 268435456 | bytes 1048576 | tf_op jit(solution)/shard_map/edge_gradient/pallas_call | solution.py:453
  (4 shorter events, 0.0 us)
Async XLA Ops:
  0.0 4.1 %copy-start.1 = (f32[128,512]{1,0:T(8,128)S(1)}, f32[128,512]{1,0:T(8,128)}, u32[]{:S(2)}) copy-start(f32[128,512]{1,0:T(8,128)} %theta_ref.3) | copy-start | bytes 786436
  0.0 4.1 %copy-start.5 = (bf16[2,512,256]{2,1,0:T(8,128)(2,1)S(1)}, bf16[2,512,256]{2,1,0:T(8,128)(2,1)}, u32[]{:S(2)}) copy-start(bf16[2,512,256]{2,1,0:T(8,128)(2,1)} %constant.43.clone.column_ref) | copy-start | bytes 1572868
  0.0 4.1 %copy-start.7 = (bf16[4,80,384]{2,1,0:T(8,128)(2,1)S(1)}, bf16[4,80,384]{2,1,0:T(8,128)(2,1)}, u32[]{:S(2)}) copy-start(bf16[4,80,384]{2,1,0:T(8,128)(2,1)} %constant.45.clone.rows_ref) | copy-start | bytes 737284
  1.9 3.8 %collective-permute-start.1 = (f32[32,128]{1,0:T(8,128)S(1)}, f32[32,128]{1,0:T(8,128)S(1)}, u32[]{:S(2)}, u32[]{:S(2)}) collective-permute-start(f32[32,128]{1,0:T(8,128)S(1)} %get-tuple-element.16), channel_id=1, source_target_pairs={{1,2},{2,1},{5,6},{6,5},{9,10},{10,9},{13,14},{14,13},{17,18},{18,... | collective-permute-start | bytes 49160 | tf_op jit(solution)/shard_map/ppermute | solution.py:493
  3.3 2.3 %copy-start.9 = (bf16[4,80,96]{2,1,0:T(8,128)(2,1)S(1)}, bf16[4,80,96]{2,1,0:T(8,128)(2,1)}, u32[]{:S(2)}) copy-start(bf16[4,80,96]{2,1,0:T(8,128)(2,1)} %constant.47.clone.rows_ref) | copy-start | bytes 184324
  3.3 6.7 %collective-permute-start = (f32[8,40,128]{2,1,0:T(8,128)S(1)}, f32[8,40,128]{2,1,0:T(8,128)S(1)}, u32[]{:S(2)}, u32[]{:S(2)}) collective-permute-start(f32[8,40,128]{2,1,0:T(8,128)S(1)} %get-tuple-element.15), channel_id=1, source_target_pairs={{0,3},{1,2},{2,1},{3,0},{4,7},{5,6},{6,5},{7,4},{8,11},{9,10},{10,... | collective-permute-start | bytes 491528 | tf_op jit(solution)/shard_map/ppermute | solution.py:496
  4.6 5.6 %copy-start.3 = (s32[512,512]{1,0:T(8,128)S(1)}, s32[512,512]{1,0:T(8,128)}, u32[]{:S(2)}) copy-start(s32[512,512]{1,0:T(8,128)} %target_ref.1) | copy-start | bytes 3145732
  6.0 4.0 %collective-permute-start.2 = (f32[1,40,128]{2,1,0:T(8,128)S(1)}, f32[1,40,128]{2,1,0:T(8,128)S(1)}, u32[]{:S(2)}, u32[]{:S(2)}) collective-permute-start(f32[1,40,128]{2,1,0:T(8,128)S(1)} %add_rim.1), channel_id=1, source_target_pairs={{0,3},{1,2},{2,1},{3,0},{4,7},{5,6},{6,5},{7,4},{8,11},{9,10},{10,... | collective-permute-start | bytes 61448 | tf_op jit(solution)/shard_map/ppermute | solution.py:496
  10.0 1.8 %copy-start.6 = (bf16[512,240]{1,0:T(8,128)(2,1)S(1)}, bf16[512,240]{1,0:T(8,128)(2,1)}, u32[]{:S(2)}) copy-start(bf16[512,240]{1,0:T(8,128)(2,1)} %constant.52.clone.row_ref) | copy-start | bytes 737284
  10.0 1.7 %copy-start.8 = (bf16[160,512]{1,0:T(8,128)(2,1)S(1)}, bf16[160,512]{1,0:T(8,128)(2,1)}, u32[]{:S(2)}) copy-start(bf16[160,512]{1,0:T(8,128)(2,1)} %constant.53.clone.row_turned_ref) | copy-start | bytes 491524
  10.1 1.7 %collective-permute-start.3 = (f32[17,40,128]{2,1,0:T(8,128)S(1)}, f32[17,40,128]{2,1,0:T(8,128)S(1)}, u32[]{:S(2)}, u32[]{:S(2)}) collective-permute-start(f32[17,40,128]{2,1,0:T(8,128)S(1)} %pad_maximum_fusion.mixed_ref), channel_id=1, source_target_pairs={{0,1},{1,0},{2,3},{3,2},{4,5},{5,4},{6,7},{7,6},{8,9},{9,8},{10,11... | collective-permute-start | bytes 1044488 | tf_op jit(solution)/shard_map/ppermute | solution.py:496
  11.8 10.6 %copy-start = (bf16[2,256,512]{2,1,0:T(8,128)(2,1)S(1)}, bf16[2,256,512]{2,1,0:T(8,128)(2,1)}, u32[]{:S(2)}) copy-start(bf16[2,256,512]{2,1,0:T(8,128)(2,1)} %constant.51.clone.turned_ref) | copy-start | bytes 1572868
  11.8 10.6 %copy-start.4 = (bf16[4,256,240]{2,1,0:T(8,128)(2,1)S(1)}, bf16[4,256,240]{2,1,0:T(8,128)(2,1)}, u32[]{:S(2)}) copy-start(bf16[4,256,240]{2,1,0:T(8,128)(2,1)} %constant.46.clone.rows_ref) | copy-start | bytes 1474564
  17.7 1.3 %collective-permute-start.4 = (f32[40,128]{1,0:T(8,128)S(1)}, f32[40,128]{1,0:T(8,128)S(1)}, u32[]{:S(2)}, u32[]{:S(2)}) collective-permute-start(f32[40,128]{1,0:T(8,128)S(1)} %coherent_fields.1), channel_id=1, source_target_pairs={{0,1},{1,0},{2,3},{3,2},{4,5},{5,4},{6,7},{7,6},{8,9},{9,8},{10,11... | collective-permute-start | bytes 61448 | tf_op jit(solution)/shard_map/ppermute | solution.py:496
  19.0 3.2 %collective-permute-start.5 = (f32[40,128]{1,0:T(8,128)S(1)}, f32[40,128]{1,0:T(8,128)S(1)}, u32[]{:S(2)}, u32[]{:S(2)}) collective-permute-start(f32[40,128]{1,0:T(8,128)S(1)} %add.18), channel_id=1, source_target_pairs={{0,3},{1,2},{2,1},{3,0},{4,7},{5,6},{6,5},{7,4},{8,11},{9,10},{10,... | collective-permute-start | bytes 61448 | tf_op jit(solution)/shard_map/ppermute | solution.py:496
  22.2 4.1 %copy-start.2 = (bf16[4,64,240]{2,1,0:T(8,128)(2,1)S(1)}, bf16[4,64,240]{2,1,0:T(8,128)(2,1)}, u32[]{:S(2)}) copy-start(bf16[4,64,240]{2,1,0:T(8,128)(2,1)} %constant.48.clone.rows_ref) | copy-start | bytes 368644
  22.2 4.1 %collective-permute-start.6 = (f32[40,128]{1,0:T(8,128)S(1)}, f32[40,128]{1,0:T(8,128)S(1)}, u32[]{:S(2)}, u32[]{:S(2)}) collective-permute-start(f32[40,128]{1,0:T(8,128)S(1)} %add.19.sum_ref), channel_id=1, source_target_pairs={{0,1},{3,2},{4,5},{7,6},{8,9},{11,10},{12,13},{15,14},{16,17},{19,... | collective-permute-start | bytes 61448 | tf_op jit(solution)/shard_map/ppermute | solution.py:493

commit v17 on v15

--- a/solution.py
+++ b/solution.py
@@ -389,9 +389,13 @@
             turned[pl.ds(index * 2, 2)] = jnp.stack([back[:, :ROWS], back[:, ROWS:]])
         return carry
 
-    lax.fori_loop(0, CONDS, drive, 0, unroll=8)
-    high, low = split(turned[...].reshape(count * tall, ROWS))
-    backs[...] = dot(jnp.concatenate([high, low], axis=1), backward_ref[: 2 * ROWS]) + dot(high, backward_ref[2 * ROWS :])
+    for half in range(2):
+        for cond in range(half * CONDS // 2, (half + 1) * CONDS // 2):
+            drive(cond, 0)
+        high, low = split(turned[half * count : (half + 1) * count].reshape(count // 2 * tall, ROWS))
+        backs[half * count // 2 * tall : (half + 1) * count // 2 * tall] = dot(
+            jnp.concatenate([high, low], axis=1), backward_ref[: 2 * ROWS]
+        ) + dot(high, backward_ref[2 * ROWS :])
 
     sum_even = jnp.zeros((FA, 2 * FB), F32)
     sum_odd = jnp.zeros((FA, 2 * FB), F32)

time: 27.6 us -> 27.5 us (level)
  no operation moved by 1% of the time
where the time goes in v17:
time: 27.5 us; the launch traced here: 27.3 us
  waiting for transfers between devices  12.3 us (45%)
  Pallas kernels  11.2 us (41%)
  starting transfers between devices  3.68 us (13%)
    pallas_call x7, Pallas kernels, call(): pl.pallas_call(kernel, grid_spec=pltpu.PrefetchScalarGridSpec(num_scalar_...  11.2 us
    ppermute x5, waiting for transfers between devices, partner(): return lax.ppermute(value, 'cond', [(i, i ^ step) for i in range(PARTS)])  8.58 us
    ppermute x2, waiting for transfers between devices, across(): return lax.ppermute(value, ('tile', 'cond'), pairs)  3.75 us
    ppermute x5, starting transfers between devices, partner(): return lax.ppermute(value, 'cond', [(i, i ^ step) for i in range(PARTS)])  2.05 us
    ppermute x2, starting transfers between devices, across(): return lax.ppermute(value, ('tile', 'cond'), pairs)  1.63 us
  transfers between devices with their start and end apart: 7, of which 6 were waited for; matrix products, arithmetic and copies ran while one was open for 0% of the time, Pallas kernels for 9%

profile of v17, /device:TPU:24, one launch (start us, length us, event | category | flops | bytes accessed | tf_op | source)
XLA Modules:
  0.0 27.3 jit_solution(12018808148874201466)
XLA Ops:
  0.0 0.0 copy-start.1
  0.0 0.0 copy-start.5
  0.0 0.0 copy-start.7
  0.0 1.9 %open_parts.1 = (f32[8,40,128]{2,1,0:T(8,128)S(1)}, f32[32,128]{1,0:T(8,128)S(1)}, f32[8,128]{1,0:T(8,128)S(1)}, bf16[384,256]{1,0:T(8,128)(2,1)S(1)}, bf16[384,256]{1,0:T(8,128)(2,1)S(1)}) custom-call(s32[1]{0:T(128)} %bitcast.part_ref, f32[128,512]{1,0:T(8,128)} %theta_ref.3, bf16[2,512,128]{2,1,0:T(8,128)(2,1)} %constant.44.clone.waves_hbm, ...), custom_call_target="tpu_custom_call" | custom-call | flops 268435456 | bytes 1048576 | tf_op jit(solution)/shard_map/open_parts/pallas_call | solution.py:462
  1.9 1.5 %collective-permute-start.1 = (f32[32,128]{1,0:T(8,128)S(1)}, f32[32,128]{1,0:T(8,128)S(1)}, u32[]{:S(2)}, u32[]{:S(2)}) collective-permute-start(f32[32,128]{1,0:T(8,128)S(1)} %get-tuple-element.16), channel_id=1, source_target_pairs={{1,2},{2,1},{5,6},{6,5},{9,10},{10,9},{13,14},{14,13},{17,18},{18,... | collective-permute-start | bytes 49160 | tf_op jit(solution)/shard_map/ppermute | solution.py:502
  3.3 0.0 copy-start.9
  3.3 0.8 %collective-permute-start = (f32[8,40,128]{2,1,0:T(8,128)S(1)}, f32[8,40,128]{2,1,0:T(8,128)S(1)}, u32[]{:S(2)}, u32[]{:S(2)}) collective-permute-start(f32[8,40,128]{2,1,0:T(8,128)S(1)} %get-tuple-element.15), channel_id=1, source_target_pairs={{0,3},{1,2},{2,1},{3,0},{4,7},{5,6},{6,5},{7,4},{8,11},{9,10},{10,... | collective-permute-start | bytes 491528 | tf_op jit(solution)/shard_map/ppermute | solution.py:505
  4.1 0.0 copy-done.1
  4.1 0.0 copy-done.5
  4.1 0.0 copy-done.7
  4.1 0.5 %own_spectrum.1.spectrum_ref = f32[2,40,128]{2,1,0:T(8,128)S(1)} custom-call(s32[1]{0:T(128)} %bitcast.part_ref, f32[128,512]{1,0:T(8,128)S(1)} %copy-done.1, bf16[2,512,256]{2,1,0:T(8,128)(2,1)S(1)} %copy-done.5, bf16[4,80,384]{2,1,0:T(8,128)(2,1)S(1)} %copy-done.7), custom_call_target="tpu_custom_call" | custom-call | flops 2147483648 | bytes 1048576 | tf_op jit(solution)/shard_map/own_spectrum/pallas_call | solution.py:462
  4.6 0.0 copy-start.3
  4.6 1.1 %collective-permute-done.1.rim_ref = f32[32,128]{1,0:T(8,128)S(1)} collective-permute-done((f32[32,128]{1,0:T(8,128)S(1)}, f32[32,128]{1,0:T(8,128)S(1)}, u32[]{:S(2)}, u32[]{:S(2)}) %collective-permute-start.1) | collective-permute-done | bytes 16416 | tf_op jit(solution)/shard_map/ppermute | solution.py:502
  5.7 0.0 copy-done.9
  5.7 0.3 %add_rim.1 = f32[1,40,128]{2,1,0:T(8,128)S(1)} custom-call(s32[1]{0:T(128)} %bitcast.part_ref, f32[2,40,128]{2,1,0:T(8,128)S(1)} %own_spectrum.1.spectrum_ref, f32[32,128]{1,0:T(8,128)S(1)} %collective-permute-done.1.rim_ref, bf16[4,80,96]{2,1,0:T(8,128)(2,1)S(1)} %copy-done.9), custom_call_target="tpu_custom_call" | custom-call | flops 268435456 | bytes 1048576 | tf_op jit(solution)/shard_map/add_rim/pallas_call | solution.py:462
  6.0 0.7 %collective-permute-start.2 = (f32[1,40,128]{2,1,0:T(8,128)S(1)}, f32[1,40,128]{2,1,0:T(8,128)S(1)}, u32[]{:S(2)}, u32[]{:S(2)}) collective-permute-start(f32[1,40,128]{2,1,0:T(8,128)S(1)} %add_rim.1), channel_id=1, source_target_pairs={{0,3},{1,2},{2,1},{3,0},{4,7},{5,6},{6,5},{7,4},{8,11},{9,10},{10,... | collective-permute-start | bytes 61448 | tf_op jit(solution)/shard_map/ppermute | solution.py:505
  6.7 3.3 %collective-permute-done.2 = f32[1,40,128]{2,1,0:T(8,128)S(1)} collective-permute-done((f32[1,40,128]{2,1,0:T(8,128)S(1)}, f32[1,40,128]{2,1,0:T(8,128)S(1)}, u32[]{:S(2)}, u32[]{:S(2)}) %collective-permute-start.2) | collective-permute-done | bytes 20512 | tf_op jit(solution)/shard_map/ppermute | solution.py:505
  10.0 0.0 collective-permute-done
  10.0 0.0 copy-start.6
  10.0 0.0 copy-start.8
  10.1 0.2 collective-permute-start.3
  10.2 0.0 copy-done.3
  10.2 0.3 %near_kernels.1 = (f32[8,4,40,128]{3,2,1,0:T(8,128)S(1)}, f32[512,128]{1,0:T(8,128)S(1)}) custom-call(s32[1]{0:T(128)} %bitcast.part_ref, f32[17,40,128]{2,1,0:T(8,128)S(1)} %pad_maximum_fusion.mixed_ref, s32[512,512]{1,0:T(8,128)S(1)} %copy-done.3), custom_call_target="tpu_custom_call" | custom-call | flops 1073741824 | bytes 1048576 | tf_op jit(solution)/shard_map/near_kernels/pallas_call | solution.py:462
  10.6 1.2 %collective-permute-done.3.other_ref = f32[17,40,128]{2,1,0:T(8,128)S(1)} collective-permute-done((f32[17,40,128]{2,1,0:T(8,128)S(1)}, f32[17,40,128]{2,1,0:T(8,128)S(1)}, u32[]{:S(2)}, u32[]{:S(2)}) %collective-permute-start.3) | collective-permute-done | bytes 348192 | tf_op jit(solution)/shard_map/ppermute | solution.py:505
  11.8 0.0 copy-done.6
  11.8 0.0 copy-done.8
  11.8 0.0 copy-start
  11.8 0.0 copy-start.4
  11.8 5.8 %coherent_fields.1 = f32[40,128]{1,0:T(8,128)S(1)} custom-call(s32[1]{0:T(128)} %bitcast.part_ref, f32[17,40,128]{2,1,0:T(8,128)S(1)} %pad_maximum_fusion.mixed_ref, f32[17,40,128]{2,1,0:T(8,128)S(1)} %collective-permute-done.3.other_ref, f32[8,4,40,128]{3,2,1,0:T(8,128)S(1)} %get-tuple-element.17.near_ref, f32[512,128]{1,0:T(8,128)S(1)} %get-tuple-element.18.signs, ...), custom_call_target="tpu_custom_call" | custom-call | flops 8589934592 | bytes 1048576 | tf_op jit(solution)/shard_map/coherent_fields/pallas_call | solution.py:462
  17.6 0.2 collective-permute-start.4
  17.8 1.1 %collective-permute-done.4 = f32[40,128]{1,0:T(8,128)S(1)} collective-permute-done((f32[40,128]{1,0:T(8,128)S(1)}, f32[40,128]{1,0:T(8,128)S(1)}, u32[]{:S(2)}, u32[]{:S(2)}) %collective-permute-start.4) | collective-permute-done | bytes 20512 | tf_op jit(solution)/shard_map/ppermute | solution.py:505
  18.9 0.2 collective-permute-start.5
  19.0 3.1 %collective-permute-done.5 = f32[40,128]{1,0:T(8,128)S(1)} collective-permute-done((f32[40,128]{1,0:T(8,128)S(1)}, f32[40,128]{1,0:T(8,128)S(1)}, u32[]{:S(2)}, u32[]{:S(2)}) %collective-permute-start.5) | collective-permute-done | bytes 20512 | tf_op jit(solution)/shard_map/ppermute | solution.py:505
  22.1 0.0 copy-start.2
  22.1 0.2 collective-permute-start.6
  22.3 0.0 copy-done
  22.3 0.0 copy-done.4
  22.3 1.2 %own_gradient.1 = (f32[128,512]{1,0:T(8,128)}, f32[32,512]{1,0:T(8,128)S(1)}, f32[32,512]{1,0:T(8,128)S(1)}) custom-call(s32[1]{0:T(128)} %bitcast.part_ref, f32[128,512]{1,0:T(8,128)S(1)} %copy-done.1, f32[40,128]{1,0:T(8,128)S(1)} %add.19.sum_ref, bf16[2,256,512]{2,1,0:T(8,128)(2,1)S(1)} %copy-done, bf16[4,256,240]{2,1,0:T(8,128)(2,1)S(1)} %copy-done.4), custom_call_target="tpu_custom_call" | custom-call | flops 2147483648 | bytes 1048576 | tf_op jit(solution)/shard_map/own_gradient/pallas_call | solution.py:462
  23.5 2.7 %collective-permute-done.6.near_ref = f32[40,128]{1,0:T(8,128)S(1)} collective-permute-done((f32[40,128]{1,0:T(8,128)S(1)}, f32[40,128]{1,0:T(8,128)S(1)}, u32[]{:S(2)}, u32[]{:S(2)}) %collective-permute-start.6) | collective-permute-done | bytes 20512 | tf_op jit(solution)/shard_map/ppermute | solution.py:502
  26.2 0.0 copy-done.2
  26.2 1.1 %edge_gradient.1 = f32[128,512]{1,0:T(8,128)} custom-call(s32[1]{0:T(128)} %bitcast.part_ref, f32[128,512]{1,0:T(8,128)} %get-tuple-element.22.gradient_hbm, f32[32,512]{1,0:T(8,128)S(1)} %get-tuple-element.23.edge_ref, f32[32,512]{1,0:T(8,128)S(1)} %get-tuple-element.24.scale_ref, ...), custom_call_target="tpu_custom_call", output_to_operand_aliasing={{}: (1, {})} | custom-call | flops 268435456 | bytes 1048576 | tf_op jit(solution)/shard_map/edge_gradient/pallas_call | solution.py:462
  (4 shorter events, 0.0 us)
Async XLA Ops:
  0.0 4.1 %copy-start.1 = (f32[128,512]{1,0:T(8,128)S(1)}, f32[128,512]{1,0:T(8,128)}, u32[]{:S(2)}) copy-start(f32[128,512]{1,0:T(8,128)} %theta_ref.3) | copy-start | bytes 786436
  0.0 4.1 %copy-start.5 = (bf16[2,512,256]{2,1,0:T(8,128)(2,1)S(1)}, bf16[2,512,256]{2,1,0:T(8,128)(2,1)}, u32[]{:S(2)}) copy-start(bf16[2,512,256]{2,1,0:T(8,128)(2,1)} %constant.43.clone.column_ref) | copy-start | bytes 1572868
  0.0 4.1 %copy-start.7 = (bf16[4,80,384]{2,1,0:T(8,128)(2,1)S(1)}, bf16[4,80,384]{2,1,0:T(8,128)(2,1)}, u32[]{:S(2)}) copy-start(bf16[4,80,384]{2,1,0:T(8,128)(2,1)} %constant.45.clone.rows_ref) | copy-start | bytes 737284
  1.9 3.8 %collective-permute-start.1 = (f32[32,128]{1,0:T(8,128)S(1)}, f32[32,128]{1,0:T(8,128)S(1)}, u32[]{:S(2)}, u32[]{:S(2)}) collective-permute-start(f32[32,128]{1,0:T(8,128)S(1)} %get-tuple-element.16), channel_id=1, source_target_pairs={{1,2},{2,1},{5,6},{6,5},{9,10},{10,9},{13,14},{14,13},{17,18},{18,... | collective-permute-start | bytes 49160 | tf_op jit(solution)/shard_map/ppermute | solution.py:502
  3.3 2.3 %copy-start.9 = (bf16[4,80,96]{2,1,0:T(8,128)(2,1)S(1)}, bf16[4,80,96]{2,1,0:T(8,128)(2,1)}, u32[]{:S(2)}) copy-start(bf16[4,80,96]{2,1,0:T(8,128)(2,1)} %constant.47.clone.rows_ref) | copy-start | bytes 184324
  3.3 6.7 %collective-permute-start = (f32[8,40,128]{2,1,0:T(8,128)S(1)}, f32[8,40,128]{2,1,0:T(8,128)S(1)}, u32[]{:S(2)}, u32[]{:S(2)}) collective-permute-start(f32[8,40,128]{2,1,0:T(8,128)S(1)} %get-tuple-element.15), channel_id=1, source_target_pairs={{0,3},{1,2},{2,1},{3,0},{4,7},{5,6},{6,5},{7,4},{8,11},{9,10},{10,... | collective-permute-start | bytes 491528 | tf_op jit(solution)/shard_map/ppermute | solution.py:505
  4.6 5.6 %copy-start.3 = (s32[512,512]{1,0:T(8,128)S(1)}, s32[512,512]{1,0:T(8,128)}, u32[]{:S(2)}) copy-start(s32[512,512]{1,0:T(8,128)} %target_ref.1) | copy-start | bytes 3145732
  6.0 4.0 %collective-permute-start.2 = (f32[1,40,128]{2,1,0:T(8,128)S(1)}, f32[1,40,128]{2,1,0:T(8,128)S(1)}, u32[]{:S(2)}, u32[]{:S(2)}) collective-permute-start(f32[1,40,128]{2,1,0:T(8,128)S(1)} %add_rim.1), channel_id=1, source_target_pairs={{0,3},{1,2},{2,1},{3,0},{4,7},{5,6},{6,5},{7,4},{8,11},{9,10},{10,... | collective-permute-start | bytes 61448 | tf_op jit(solution)/shard_map/ppermute | solution.py:505
  10.0 1.8 %copy-start.6 = (bf16[512,240]{1,0:T(8,128)(2,1)S(1)}, bf16[512,240]{1,0:T(8,128)(2,1)}, u32[]{:S(2)}) copy-start(bf16[512,240]{1,0:T(8,128)(2,1)} %constant.52.clone.row_ref) | copy-start | bytes 737284
  10.0 1.7 %copy-start.8 = (bf16[160,512]{1,0:T(8,128)(2,1)S(1)}, bf16[160,512]{1,0:T(8,128)(2,1)}, u32[]{:S(2)}) copy-start(bf16[160,512]{1,0:T(8,128)(2,1)} %constant.53.clone.row_turned_ref) | copy-start | bytes 491524
  10.1 1.7 %collective-permute-start.3 = (f32[17,40,128]{2,1,0:T(8,128)S(1)}, f32[17,40,128]{2,1,0:T(8,128)S(1)}, u32[]{:S(2)}, u32[]{:S(2)}) collective-permute-start(f32[17,40,128]{2,1,0:T(8,128)S(1)} %pad_maximum_fusion.mixed_ref), channel_id=1, source_target_pairs={{0,1},{1,0},{2,3},{3,2},{4,5},{5,4},{6,7},{7,6},{8,9},{9,8},{10,11... | collective-permute-start | bytes 1044488 | tf_op jit(solution)/shard_map/ppermute | solution.py:505
  11.8 10.5 %copy-start = (bf16[2,256,512]{2,1,0:T(8,128)(2,1)S(1)}, bf16[2,256,512]{2,1,0:T(8,128)(2,1)}, u32[]{:S(2)}) copy-start(bf16[2,256,512]{2,1,0:T(8,128)(2,1)} %constant.51.clone.turned_ref) | copy-start | bytes 1572868
  11.8 10.5 %copy-start.4 = (bf16[4,256,240]{2,1,0:T(8,128)(2,1)S(1)}, bf16[4,256,240]{2,1,0:T(8,128)(2,1)}, u32[]{:S(2)}) copy-start(bf16[4,256,240]{2,1,0:T(8,128)(2,1)} %constant.46.clone.rows_ref) | copy-start | bytes 1474564
  17.6 1.3 %collective-permute-start.4 = (f32[40,128]{1,0:T(8,128)S(1)}, f32[40,128]{1,0:T(8,128)S(1)}, u32[]{:S(2)}, u32[]{:S(2)}) collective-permute-start(f32[40,128]{1,0:T(8,128)S(1)} %coherent_fields.1), channel_id=1, source_target_pairs={{0,1},{1,0},{2,3},{3,2},{4,5},{5,4},{6,7},{7,6},{8,9},{9,8},{10,11... | collective-permute-start | bytes 61448 | tf_op jit(solution)/shard_map/ppermute | solution.py:505
  18.9 3.2 %collective-permute-start.5 = (f32[40,128]{1,0:T(8,128)S(1)}, f32[40,128]{1,0:T(8,128)S(1)}, u32[]{:S(2)}, u32[]{:S(2)}) collective-permute-start(f32[40,128]{1,0:T(8,128)S(1)} %add.18), channel_id=1, source_target_pairs={{0,3},{1,2},{2,1},{3,0},{4,7},{5,6},{6,5},{7,4},{8,11},{9,10},{10,... | collective-permute-start | bytes 61448 | tf_op jit(solution)/shard_map/ppermute | solution.py:505
  22.1 4.1 %copy-start.2 = (bf16[4,64,240]{2,1,0:T(8,128)(2,1)S(1)}, bf16[4,64,240]{2,1,0:T(8,128)(2,1)}, u32[]{:S(2)}) copy-start(bf16[4,64,240]{2,1,0:T(8,128)(2,1)} %constant.48.clone.rows_ref) | copy-start | bytes 368644
  22.1 4.1 %collective-permute-start.6 = (f32[40,128]{1,0:T(8,128)S(1)}, f32[40,128]{1,0:T(8,128)S(1)}, u32[]{:S(2)}, u32[]{:S(2)}) collective-permute-start(f32[40,128]{1,0:T(8,128)S(1)} %add.19.sum_ref), channel_id=1, source_target_pairs={{0,1},{3,2},{4,5},{7,6},{8,9},{11,10},{12,13},{15,14},{16,17},{19,... | collective-permute-start | bytes 61448 | tf_op jit(solution)/shard_map/ppermute | solution.py:502

commit v18 on v17

--- a/solution.py
+++ b/solution.py
@@ -342,13 +342,20 @@
 
             unpack_group(ref, put)
 
-    high, low = split(lines[...])
-    lines_folded = dot(jnp.concatenate([high, low], axis=1), forward_ref[: 4 * FB]) + dot(high, forward_ref[4 * FB :])
+    deep = count // 2 * tall
+    line_products = []
+    for half in range(2):
+        high, low = split(lines[half * deep : (half + 1) * deep])
+        line_products.append(
+            dot(jnp.concatenate([high, low], axis=1), forward_ref[: 4 * FB]) + dot(high, forward_ref[4 * FB :])
+        )
     for kern in range(count):
+        lines_folded = line_products[kern // (count // 2)]
         parts = []
+        base = tall * (kern % (count // 2))
         for i in range(2):
-            x_part = lines_folded[tall * kern + 2 * FA * i : tall * kern + 2 * FA * i + FA]
-            y_part = lines_folded[tall * kern + 2 * FA * i + FA : tall * kern + 2 * FA * (i + 1)]
+            x_part = lines_folded[base + 2 * FA * i : base + 2 * FA * i + FA]
+            y_part = lines_folded[base + 2 * FA * i + FA : base + 2 * FA * (i + 1)]
             parts.append(
                 jnp.concatenate(
                     [x_part[:, :ROWS] + y_part[:, ROWS:], y_part[:, :ROWS] - x_part[:, ROWS:]], axis=0

time: 27.5 us -> 27.4 us (level)
  no operation moved by 1% of the time
where the time goes in v18:
time: 27.4 us; the launch traced here: 27.3 us
  waiting for transfers between devices  12.3 us (45%)
  Pallas kernels  11.1 us (41%)
  starting transfers between devices  3.66 us (13%)
    pallas_call x7, Pallas kernels, call(): pl.pallas_call(kernel, grid_spec=pltpu.PrefetchScalarGridSpec(num_scalar_...  11.1 us
    ppermute x5, waiting for transfers between devices, partner(): return lax.ppermute(value, 'cond', [(i, i ^ step) for i in range(PARTS)])  8.59 us
    ppermute x2, waiting for transfers between devices, across(): return lax.ppermute(value, ('tile', 'cond'), pairs)  3.75 us
    ppermute x5, starting transfers between devices, partner(): return lax.ppermute(value, 'cond', [(i, i ^ step) for i in range(PARTS)])  2.03 us
    ppermute x2, starting transfers between devices, across(): return lax.ppermute(value, ('tile', 'cond'), pairs)  1.63 us
  transfers between devices with their start and end apart: 7, of which 6 were waited for; matrix products, arithmetic and copies ran while one was open for 0% of the time, Pallas kernels for 9%

profile of v18, /device:TPU:24, one launch (start us, length us, event | category | flops | bytes accessed | tf_op | source)
XLA Modules:
  0.0 27.3 jit_solution(2476859442012102966)
XLA Ops:
  0.0 0.0 copy-start.1
  0.0 0.0 copy-start.5
  0.0 0.0 copy-start.7
  0.0 1.9 %open_parts.1 = (f32[8,40,128]{2,1,0:T(8,128)S(1)}, f32[32,128]{1,0:T(8,128)S(1)}, f32[8,128]{1,0:T(8,128)S(1)}, bf16[384,256]{1,0:T(8,128)(2,1)S(1)}, bf16[384,256]{1,0:T(8,128)(2,1)S(1)}) custom-call(s32[1]{0:T(128)} %bitcast.part_ref, f32[128,512]{1,0:T(8,128)} %theta_ref.3, bf16[2,512,128]{2,1,0:T(8,128)(2,1)} %constant.44.clone.waves_hbm, ...), custom_call_target="tpu_custom_call" | custom-call | flops 268435456 | bytes 1048576 | tf_op jit(solution)/shard_map/open_parts/pallas_call | solution.py:469
  1.9 1.5 %collective-permute-start.1 = (f32[32,128]{1,0:T(8,128)S(1)}, f32[32,128]{1,0:T(8,128)S(1)}, u32[]{:S(2)}, u32[]{:S(2)}) collective-permute-start(f32[32,128]{1,0:T(8,128)S(1)} %get-tuple-element.16), channel_id=1, source_target_pairs={{1,2},{2,1},{5,6},{6,5},{9,10},{10,9},{13,14},{14,13},{17,18},{18,... | collective-permute-start | bytes 49160 | tf_op jit(solution)/shard_map/ppermute | solution.py:509
  3.3 0.0 copy-start.9
  3.3 0.8 %collective-permute-start = (f32[8,40,128]{2,1,0:T(8,128)S(1)}, f32[8,40,128]{2,1,0:T(8,128)S(1)}, u32[]{:S(2)}, u32[]{:S(2)}) collective-permute-start(f32[8,40,128]{2,1,0:T(8,128)S(1)} %get-tuple-element.15), channel_id=1, source_target_pairs={{0,3},{1,2},{2,1},{3,0},{4,7},{5,6},{6,5},{7,4},{8,11},{9,10},{10,... | collective-permute-start | bytes 491528 | tf_op jit(solution)/shard_map/ppermute | solution.py:512
  4.1 0.0 copy-done.1
  4.1 0.0 copy-done.5
  4.1 0.0 copy-done.7
  4.1 0.5 %own_spectrum.1.spectrum_ref = f32[2,40,128]{2,1,0:T(8,128)S(1)} custom-call(s32[1]{0:T(128)} %bitcast.part_ref, f32[128,512]{1,0:T(8,128)S(1)} %copy-done.1, bf16[2,512,256]{2,1,0:T(8,128)(2,1)S(1)} %copy-done.5, bf16[4,80,384]{2,1,0:T(8,128)(2,1)S(1)} %copy-done.7), custom_call_target="tpu_custom_call" | custom-call | flops 2147483648 | bytes 1048576 | tf_op jit(solution)/shard_map/own_spectrum/pallas_call | solution.py:469
  4.6 0.0 copy-start.3
  4.6 1.1 %collective-permute-done.1.rim_ref = f32[32,128]{1,0:T(8,128)S(1)} collective-permute-done((f32[32,128]{1,0:T(8,128)S(1)}, f32[32,128]{1,0:T(8,128)S(1)}, u32[]{:S(2)}, u32[]{:S(2)}) %collective-permute-start.1) | collective-permute-done | bytes 16416 | tf_op jit(solution)/shard_map/ppermute | solution.py:509
  5.7 0.0 copy-done.9
  5.7 0.3 %add_rim.1 = f32[1,40,128]{2,1,0:T(8,128)S(1)} custom-call(s32[1]{0:T(128)} %bitcast.part_ref, f32[2,40,128]{2,1,0:T(8,128)S(1)} %own_spectrum.1.spectrum_ref, f32[32,128]{1,0:T(8,128)S(1)} %collective-permute-done.1.rim_ref, bf16[4,80,96]{2,1,0:T(8,128)(2,1)S(1)} %copy-done.9), custom_call_target="tpu_custom_call" | custom-call | flops 268435456 | bytes 1048576 | tf_op jit(solution)/shard_map/add_rim/pallas_call | solution.py:469
  6.0 0.7 %collective-permute-start.2 = (f32[1,40,128]{2,1,0:T(8,128)S(1)}, f32[1,40,128]{2,1,0:T(8,128)S(1)}, u32[]{:S(2)}, u32[]{:S(2)}) collective-permute-start(f32[1,40,128]{2,1,0:T(8,128)S(1)} %add_rim.1), channel_id=1, source_target_pairs={{0,3},{1,2},{2,1},{3,0},{4,7},{5,6},{6,5},{7,4},{8,11},{9,10},{10,... | collective-permute-start | bytes 61448 | tf_op jit(solution)/shard_map/ppermute | solution.py:512
  6.7 3.3 %collective-permute-done.2 = f32[1,40,128]{2,1,0:T(8,128)S(1)} collective-permute-done((f32[1,40,128]{2,1,0:T(8,128)S(1)}, f32[1,40,128]{2,1,0:T(8,128)S(1)}, u32[]{:S(2)}, u32[]{:S(2)}) %collective-permute-start.2) | collective-permute-done | bytes 20512 | tf_op jit(solution)/shard_map/ppermute | solution.py:512
  10.0 0.0 collective-permute-done
  10.0 0.0 copy-start.6
  10.0 0.0 copy-start.8
  10.1 0.2 collective-permute-start.3
  10.2 0.0 copy-done.3
  10.2 0.3 %near_kernels.1 = (f32[8,4,40,128]{3,2,1,0:T(8,128)S(1)}, f32[512,128]{1,0:T(8,128)S(1)}) custom-call(s32[1]{0:T(128)} %bitcast.part_ref, f32[17,40,128]{2,1,0:T(8,128)S(1)} %pad_maximum_fusion.mixed_ref, s32[512,512]{1,0:T(8,128)S(1)} %copy-done.3), custom_call_target="tpu_custom_call" | custom-call | flops 1073741824 | bytes 1048576 | tf_op jit(solution)/shard_map/near_kernels/pallas_call | solution.py:469
  10.6 1.2 %collective-permute-done.3.other_ref = f32[17,40,128]{2,1,0:T(8,128)S(1)} collective-permute-done((f32[17,40,128]{2,1,0:T(8,128)S(1)}, f32[17,40,128]{2,1,0:T(8,128)S(1)}, u32[]{:S(2)}, u32[]{:S(2)}) %collective-permute-start.3) | collective-permute-done | bytes 348192 | tf_op jit(solution)/shard_map/ppermute | solution.py:512
  11.8 0.0 copy-done.6
  11.8 0.0 copy-done.8
  11.8 0.0 copy-start
  11.8 0.0 copy-start.4
  11.8 5.8 %coherent_fields.1 = f32[40,128]{1,0:T(8,128)S(1)} custom-call(s32[1]{0:T(128)} %bitcast.part_ref, f32[17,40,128]{2,1,0:T(8,128)S(1)} %pad_maximum_fusion.mixed_ref, f32[17,40,128]{2,1,0:T(8,128)S(1)} %collective-permute-done.3.other_ref, f32[8,4,40,128]{3,2,1,0:T(8,128)S(1)} %get-tuple-element.17.near_ref, f32[512,128]{1,0:T(8,128)S(1)} %get-tuple-element.18.signs, ...), custom_call_target="tpu_custom_call" | custom-call | flops 8589934592 | bytes 1048576 | tf_op jit(solution)/shard_map/coherent_fields/pallas_call | solution.py:469
  17.6 0.2 collective-permute-start.4
  17.8 1.1 %collective-permute-done.4 = f32[40,128]{1,0:T(8,128)S(1)} collective-permute-done((f32[40,128]{1,0:T(8,128)S(1)}, f32[40,128]{1,0:T(8,128)S(1)}, u32[]{:S(2)}, u32[]{:S(2)}) %collective-permute-start.4) | collective-permute-done | bytes 20512 | tf_op jit(solution)/shard_map/ppermute | solution.py:512
  18.9 0.1 collective-permute-start.5
  19.0 3.1 %collective-permute-done.5 = f32[40,128]{1,0:T(8,128)S(1)} collective-permute-done((f32[40,128]{1,0:T(8,128)S(1)}, f32[40,128]{1,0:T(8,128)S(1)}, u32[]{:S(2)}, u32[]{:S(2)}) %collective-permute-start.5) | collective-permute-done | bytes 20512 | tf_op jit(solution)/shard_map/ppermute | solution.py:512
  22.1 0.0 copy-start.2
  22.1 0.2 collective-permute-start.6
  22.2 0.0 copy-done
  22.2 0.0 copy-done.4
  22.2 1.2 %own_gradient.1 = (f32[128,512]{1,0:T(8,128)}, f32[32,512]{1,0:T(8,128)S(1)}, f32[32,512]{1,0:T(8,128)S(1)}) custom-call(s32[1]{0:T(128)} %bitcast.part_ref, f32[128,512]{1,0:T(8,128)S(1)} %copy-done.1, f32[40,128]{1,0:T(8,128)S(1)} %add.19.sum_ref, bf16[2,256,512]{2,1,0:T(8,128)(2,1)S(1)} %copy-done, bf16[4,256,240]{2,1,0:T(8,128)(2,1)S(1)} %copy-done.4), custom_call_target="tpu_custom_call" | custom-call | flops 2147483648 | bytes 1048576 | tf_op jit(solution)/shard_map/own_gradient/pallas_call | solution.py:469
  23.5 2.7 %collective-permute-done.6.near_ref = f32[40,128]{1,0:T(8,128)S(1)} collective-permute-done((f32[40,128]{1,0:T(8,128)S(1)}, f32[40,128]{1,0:T(8,128)S(1)}, u32[]{:S(2)}, u32[]{:S(2)}) %collective-permute-start.6) | collective-permute-done | bytes 20512 | tf_op jit(solution)/shard_map/ppermute | solution.py:509
  26.2 0.0 copy-done.2
  26.2 1.1 %edge_gradient.1 = f32[128,512]{1,0:T(8,128)} custom-call(s32[1]{0:T(128)} %bitcast.part_ref, f32[128,512]{1,0:T(8,128)} %get-tuple-element.22.gradient_hbm, f32[32,512]{1,0:T(8,128)S(1)} %get-tuple-element.23.edge_ref, f32[32,512]{1,0:T(8,128)S(1)} %get-tuple-element.24.scale_ref, ...), custom_call_target="tpu_custom_call", output_to_operand_aliasing={{}: (1, {})} | custom-call | flops 268435456 | bytes 1048576 | tf_op jit(solution)/shard_map/edge_gradient/pallas_call | solution.py:469
  (4 shorter events, 0.0 us)
Async XLA Ops:
  0.0 4.1 %copy-start.1 = (f32[128,512]{1,0:T(8,128)S(1)}, f32[128,512]{1,0:T(8,128)}, u32[]{:S(2)}) copy-start(f32[128,512]{1,0:T(8,128)} %theta_ref.3) | copy-start | bytes 786436
  0.0 4.1 %copy-start.5 = (bf16[2,512,256]{2,1,0:T(8,128)(2,1)S(1)}, bf16[2,512,256]{2,1,0:T(8,128)(2,1)}, u32[]{:S(2)}) copy-start(bf16[2,512,256]{2,1,0:T(8,128)(2,1)} %constant.43.clone.column_ref) | copy-start | bytes 1572868
  0.0 4.1 %copy-start.7 = (bf16[4,80,384]{2,1,0:T(8,128)(2,1)S(1)}, bf16[4,80,384]{2,1,0:T(8,128)(2,1)}, u32[]{:S(2)}) copy-start(bf16[4,80,384]{2,1,0:T(8,128)(2,1)} %constant.45.clone.rows_ref) | copy-start | bytes 737284
  1.9 3.8 %collective-permute-start.1 = (f32[32,128]{1,0:T(8,128)S(1)}, f32[32,128]{1,0:T(8,128)S(1)}, u32[]{:S(2)}, u32[]{:S(2)}) collective-permute-start(f32[32,128]{1,0:T(8,128)S(1)} %get-tuple-element.16), channel_id=1, source_target_pairs={{1,2},{2,1},{5,6},{6,5},{9,10},{10,9},{13,14},{14,13},{17,18},{18,... | collective-permute-start | bytes 49160 | tf_op jit(solution)/shard_map/ppermute | solution.py:509
  3.3 2.3 %copy-start.9 = (bf16[4,80,96]{2,1,0:T(8,128)(2,1)S(1)}, bf16[4,80,96]{2,1,0:T(8,128)(2,1)}, u32[]{:S(2)}) copy-start(bf16[4,80,96]{2,1,0:T(8,128)(2,1)} %constant.47.clone.rows_ref) | copy-start | bytes 184324
  3.3 6.7 %collective-permute-start = (f32[8,40,128]{2,1,0:T(8,128)S(1)}, f32[8,40,128]{2,1,0:T(8,128)S(1)}, u32[]{:S(2)}, u32[]{:S(2)}) collective-permute-start(f32[8,40,128]{2,1,0:T(8,128)S(1)} %get-tuple-element.15), channel_id=1, source_target_pairs={{0,3},{1,2},{2,1},{3,0},{4,7},{5,6},{6,5},{7,4},{8,11},{9,10},{10,... | collective-permute-start | bytes 491528 | tf_op jit(solution)/shard_map/ppermute | solution.py:512
  4.6 5.6 %copy-start.3 = (s32[512,512]{1,0:T(8,128)S(1)}, s32[512,512]{1,0:T(8,128)}, u32[]{:S(2)}) copy-start(s32[512,512]{1,0:T(8,128)} %target_ref.1) | copy-start | bytes 3145732
  6.0 4.0 %collective-permute-start.2 = (f32[1,40,128]{2,1,0:T(8,128)S(1)}, f32[1,40,128]{2,1,0:T(8,128)S(1)}, u32[]{:S(2)}, u32[]{:S(2)}) collective-permute-start(f32[1,40,128]{2,1,0:T(8,128)S(1)} %add_rim.1), channel_id=1, source_target_pairs={{0,3},{1,2},{2,1},{3,0},{4,7},{5,6},{6,5},{7,4},{8,11},{9,10},{10,... | collective-permute-start | bytes 61448 | tf_op jit(solution)/shard_map/ppermute | solution.py:512
  10.0 1.8 %copy-start.6 = (bf16[512,240]{1,0:T(8,128)(2,1)S(1)}, bf16[512,240]{1,0:T(8,128)(2,1)}, u32[]{:S(2)}) copy-start(bf16[512,240]{1,0:T(8,128)(2,1)} %constant.52.clone.row_ref) | copy-start | bytes 737284
  10.0 1.7 %copy-start.8 = (bf16[160,512]{1,0:T(8,128)(2,1)S(1)}, bf16[160,512]{1,0:T(8,128)(2,1)}, u32[]{:S(2)}) copy-start(bf16[160,512]{1,0:T(8,128)(2,1)} %constant.53.clone.row_turned_ref) | copy-start | bytes 491524
  10.1 1.7 %collective-permute-start.3 = (f32[17,40,128]{2,1,0:T(8,128)S(1)}, f32[17,40,128]{2,1,0:T(8,128)S(1)}, u32[]{:S(2)}, u32[]{:S(2)}) collective-permute-start(f32[17,40,128]{2,1,0:T(8,128)S(1)} %pad_maximum_fusion.mixed_ref), channel_id=1, source_target_pairs={{0,1},{1,0},{2,3},{3,2},{4,5},{5,4},{6,7},{7,6},{8,9},{9,8},{10,11... | collective-permute-start | bytes 1044488 | tf_op jit(solution)/shard_map/ppermute | solution.py:512
  11.8 10.4 %copy-start = (bf16[2,256,512]{2,1,0:T(8,128)(2,1)S(1)}, bf16[2,256,512]{2,1,0:T(8,128)(2,1)}, u32[]{:S(2)}) copy-start(bf16[2,256,512]{2,1,0:T(8,128)(2,1)} %constant.51.clone.turned_ref) | copy-start | bytes 1572868
  11.8 10.4 %copy-start.4 = (bf16[4,256,240]{2,1,0:T(8,128)(2,1)S(1)}, bf16[4,256,240]{2,1,0:T(8,128)(2,1)}, u32[]{:S(2)}) copy-start(bf16[4,256,240]{2,1,0:T(8,128)(2,1)} %constant.46.clone.rows_ref) | copy-start | bytes 1474564
  17.6 1.3 %collective-permute-start.4 = (f32[40,128]{1,0:T(8,128)S(1)}, f32[40,128]{1,0:T(8,128)S(1)}, u32[]{:S(2)}, u32[]{:S(2)}) collective-permute-start(f32[40,128]{1,0:T(8,128)S(1)} %coherent_fields.1), channel_id=1, source_target_pairs={{0,1},{1,0},{2,3},{3,2},{4,5},{5,4},{6,7},{7,6},{8,9},{9,8},{10,11... | collective-permute-start | bytes 61448 | tf_op jit(solution)/shard_map/ppermute | solution.py:512
  18.9 3.2 %collective-permute-start.5 = (f32[40,128]{1,0:T(8,128)S(1)}, f32[40,128]{1,0:T(8,128)S(1)}, u32[]{:S(2)}, u32[]{:S(2)}) collective-permute-start(f32[40,128]{1,0:T(8,128)S(1)} %add.18), channel_id=1, source_target_pairs={{0,3},{1,2},{2,1},{3,0},{4,7},{5,6},{6,5},{7,4},{8,11},{9,10},{10,... | collective-permute-start | bytes 61448 | tf_op jit(solution)/shard_map/ppermute | solution.py:512
  22.1 4.1 %copy-start.2 = (bf16[4,64,240]{2,1,0:T(8,128)(2,1)S(1)}, bf16[4,64,240]{2,1,0:T(8,128)(2,1)}, u32[]{:S(2)}) copy-start(bf16[4,64,240]{2,1,0:T(8,128)(2,1)} %constant.48.clone.rows_ref) | copy-start | bytes 368644
  22.1 4.1 %collective-permute-start.6 = (f32[40,128]{1,0:T(8,128)S(1)}, f32[40,128]{1,0:T(8,128)S(1)}, u32[]{:S(2)}, u32[]{:S(2)}) collective-permute-start(f32[40,128]{1,0:T(8,128)S(1)} %add.19.sum_ref), channel_id=1, source_target_pairs={{0,1},{3,2},{4,5},{7,6},{8,9},{11,10},{12,13},{15,14},{16,17},{19,... | collective-permute-start | bytes 61448 | tf_op jit(solution)/shard_map/ppermute | solution.py:509
